TPU v7x, 32 devices: a whole 2x2x4 slice. The times are simulated.
32 devices in a mesh: ctx: 8 (over z, x), tp: 4 (over y, core).
Axes of the slice: x: 2, y: 2, z: 4, core: 2. Of those that a mesh axis runs over, the one named last changes fastest.
Arguments:
- prompt_embeds: bfloat16 [2048, 2048], P('ctx', 'tp'), may hold values from -6 to 6
- decode_ids: int32 [128, 4], P('ctx'), may hold values from 0 to 32767, as said below
- embed_table: bfloat16 [32768, 2048], P('ctx', 'tp'), may hold values from -6 to 6
- norm_gain: float32 [2048], replicated, may hold values from 0.5 to 1.5
- x_weight: bfloat16 [2048, 4096], P(None, 'tp'), may hold values from -0.125 to 0.125
- bc_weight: bfloat16 [2048, 4, 2, 64], P(None, 'tp'), may hold values from -0.125 to 0.125
- dt_weight: bfloat16 [2048, 64], P(None, 'tp'), may hold values from -0.125 to 0.125
- dt_bias: float32 [64], P('tp'), may hold values from -4.91 to -1.75
- decay_log: float32 [64], P('tp'), may hold values from -8 to -0.68
- conv_x: float32 [4, 4096], P(None, 'tp'), may hold values from -3 to 3
- conv_bc: float32 [4, 4, 2, 64], P(None, 'tp'), may hold values from -3 to 3
- skip_gain: float32 [64], P('tp'), may hold values from 0.5 to 2
- out_gain: float32 [4096], P('tp'), may hold values from 0.5 to 1.5
- out_weight: bfloat16 [4096, 2048], P('tp'), may hold values from -0.09375 to 0.09375
Outputs:
- prompt_out: bfloat16 [2048, 2048], P('ctx', 'tp')
- decode_out: bfloat16 [128, 4, 2048], P('ctx', None, 'tp')
Inputs may be any that keep to these rules, and one draw needn't show every extreme that they name: `decode_ids`: in every draw, all 64 ids of some sampler group lie in one of the 8 equal parts of the vocabulary.
All inputs are finite; a program needn't handle non-finite values.
Results may differ from a plain program's by a relative error of at most 0.0075.
Values may be sent and summed in bfloat16 or wider, within the bound.
No kernel may reach another device: no remote copies, remote signals or barrier semaphores. Data moves between devices by JAX's collectives and lax.ppermute only.
A program may use at most 128 MiB of HBM per device.

v0:
```python
import jax
import jax.numpy as jnp
from jax import lax
from jax.sharding import PartitionSpec as P

SPAN = 256


EPS = 1e-05


def passed_along(value, axis, steps):
    count = lax.axis_size(axis)
    leading, last = (max(0, -steps), min(count, count - steps))
    return lax.ppermute(value, axis, [(source, source + steps) for source in range(leading, last)])


def spread(value, axis, root):
    mine = lax.axis_index(axis) == root
    return lax.psum(jnp.where(mine, value, jnp.zeros_like(value)), axis)


def rms_rows(values, gain_row):
    widened = values.astype(jnp.float32)
    factor = lax.rsqrt(jnp.mean(widened * widened, axis=-1, keepdims=True) + EPS)
    return (widened * factor * gain_row).astype(jnp.bfloat16)


def project(normed, x_weight, bc_weight, dt_weight, dt_bias):
    flat_weight = bc_weight.reshape(bc_weight.shape[0], -1)
    x_raw = jnp.dot(normed, x_weight, preferred_element_type=jnp.float32).astype(jnp.bfloat16)
    bc_raw = jnp.dot(normed, flat_weight, preferred_element_type=jnp.float32).astype(jnp.bfloat16)
    step_size = jax.nn.softplus(
        jnp.dot(normed, dt_weight, preferred_element_type=jnp.float32) + dt_bias
    )
    return (x_raw, bc_raw, step_size)


def causal_conv(stream, kernel_rows, rim_rows):
    rim_rows = jnp.broadcast_to(rim_rows, stream.shape[:-2] + rim_rows.shape[-2:])
    joined = jnp.concatenate([rim_rows, stream], axis=-2).astype(jnp.float32)
    length = stream.shape[-2]
    summed = jnp.zeros(stream.shape, jnp.float32)
    for offset in range(kernel_rows.shape[0]):
        summed = summed + kernel_rows[offset] * lax.slice_in_dim(
            joined, offset, offset + length, axis=joined.ndim - 2
        )
    return jax.nn.silu(summed).astype(jnp.bfloat16)


def intra_block(x_conv, b_rows, c_rows, step_size, decay_rate):
    length, head_count, head_width = x_conv.shape
    groups = b_rows.shape[1]
    per_group = head_count // groups
    cum_log = jnp.cumsum(step_size * decay_rate, axis=0)
    scores = jnp.einsum("tgn,sgn->gts", c_rows, b_rows, preferred_element_type=jnp.float32)
    scores = jnp.repeat(scores, per_group, axis=0)
    log_gaps = cum_log.T[:, :, None] - cum_log.T[:, None, :]
    causal = jnp.arange(length)[:, None] >= jnp.arange(length)[None, :]
    decays = jnp.where(causal, jnp.exp(jnp.where(causal, log_gaps, 0.0)), 0.0)
    mixing = (scores * decays * step_size.T[:, None, :]).astype(jnp.bfloat16)
    within = jnp.einsum("hts,shp->thp", mixing, x_conv, preferred_element_type=jnp.float32)
    to_end = jnp.exp(cum_log[-1] - cum_log) * step_size
    weighted = (x_conv.astype(jnp.float32) * to_end[:, :, None]).astype(jnp.bfloat16)
    fresh_state = jnp.einsum(
        "sgkp,sgn->gkpn",
        weighted.reshape(length, groups, per_group, head_width),
        b_rows,
        preferred_element_type=jnp.float32,
    )
    return (within, fresh_state.reshape(head_count, head_width, -1), cum_log)


def carried(c_rows, cum_log, state_in):
    length, groups, _ = c_rows.shape
    head_count, head_width, _ = state_in.shape
    grouped = state_in.reshape(groups, head_count // groups, head_width, -1)
    reaches = jnp.einsum(
        "tgn,gkpn->tgkp", c_rows.astype(jnp.float32), grouped, precision=lax.Precision.HIGHEST
    )
    return reaches.reshape(length, head_count, head_width) * jnp.exp(cum_log)[:, :, None]


def finish(y_sum, x_conv, skip_gain, out_gain, groups):
    length, head_count, head_width = y_sum.shape
    full = y_sum + skip_gain[:, None] * x_conv.astype(jnp.float32)
    grouped = full.reshape(length, groups, -1)
    factor = lax.rsqrt(jnp.mean(grouped * grouped, axis=-1, keepdims=True) + EPS)
    return ((grouped * factor).reshape(length, -1) * out_gain).astype(jnp.bfloat16)


def decode_rows(x_conv, b_rows, c_rows, step_size, decay_rate, state_in):

    def one_row(x_row, b_row, c_row, step_row):
        within, fresh_state, cum_log = intra_block(x_row, b_row, c_row, step_row, decay_rate)
        return within + carried(c_row, cum_log, state_in)

    return jax.vmap(one_row)(x_conv, b_rows, c_rows, step_size)


def on_device(
    prompt_embeds,
    decode_ids,
    embed_table,
    norm_gain,
    x_weight,
    bc_weight,
    dt_weight,
    dt_bias,
    decay_log,
    conv_x,
    conv_bc,
    skip_gain,
    out_gain,
    out_weight,
):
    heads_here = dt_weight.shape[1]
    groups_here = bc_weight.shape[1]
    head_width = x_weight.shape[1] // heads_here
    kernel_taps = conv_x.shape[0]
    margin = kernel_taps - 1
    channels = x_weight.shape[1]
    decay_rate = -jnp.exp(decay_log)
    kernel_bc = conv_bc.reshape(kernel_taps, -1)
    gathered_ids = lax.all_gather(decode_ids, "ctx", axis=0, tiled=True)
    vocab_here = embed_table.shape[0]
    first_word = lax.axis_index("ctx") * vocab_here
    rows_here = decode_ids.shape[0]
    steps_here = decode_ids.shape[1]
    wanted = gathered_ids - first_word
    inside = jnp.logical_and(wanted >= 0, wanted < vocab_here)
    picked = jnp.take(embed_table, jnp.clip(wanted, 0, vocab_here - 1), axis=0)
    kept = jnp.where(inside[:, :, None], picked, jnp.zeros((), jnp.bfloat16))
    looked = lax.psum_scatter(kept.astype(jnp.float32), "ctx", scatter_dimension=0, tiled=True)
    gathered = lax.all_gather(prompt_embeds, "tp", axis=1, tiled=True)
    normed = rms_rows(gathered, norm_gain)
    x_raw, bc_raw, step_size = project(normed, x_weight, bc_weight, dt_weight, dt_bias)
    conv_edge = jnp.concatenate([x_raw[-margin:], bc_raw[-margin:]], axis=1)
    before = passed_along(conv_edge, "ctx", 1)
    x_conv = causal_conv(x_raw, conv_x, before[:, :channels])
    bc_conv = causal_conv(bc_raw, kernel_bc, before[:, channels:])
    tokens_here = x_conv.shape[0]
    blocks = tokens_here // SPAN
    x_blocks = x_conv.reshape(blocks, SPAN, heads_here, head_width)
    bc_blocks = bc_conv.reshape(blocks, SPAN, groups_here, 2, -1)
    state_width = bc_blocks.shape[-1]
    step_blocks = step_size.reshape(blocks, SPAN, heads_here)

    def local_step(running, pieces):
        prefix, logged = running
        x_block, b_block, c_block, step_block = pieces
        within, fresh_state, cum_log = intra_block(
            x_block, b_block, c_block, step_block, decay_rate
        )
        partial_y = within + carried(c_block, cum_log, prefix)
        prefix = jnp.exp(cum_log[-1])[:, None, None] * prefix + fresh_state
        return ((prefix, logged + cum_log[-1]), (partial_y, cum_log + logged))

    start_state = jnp.zeros((heads_here, head_width, state_width), jnp.float32)
    start_log = jnp.zeros((heads_here,), jnp.float32)
    (local_state, log_total), (partial_y, reaches) = lax.scan(
        local_step,
        (start_state, start_log),
        (x_blocks, bc_blocks[:, :, :, 0], bc_blocks[:, :, :, 1], step_blocks),
    )
    decay_total = jnp.exp(log_total)

    def turn(turn_index, incoming):
        return passed_along(decay_total[:, None, None] * incoming + local_state, "ctx", 1)

    incoming = lax.fori_loop(0, lax.axis_size("ctx") - 1, turn, jnp.zeros_like(local_state))
    c_flat = bc_blocks[:, :, :, 1].reshape(tokens_here, groups_here, state_width)
    prompt_y = partial_y.reshape(tokens_here, heads_here, head_width) + carried(
        c_flat, reaches.reshape(tokens_here, heads_here), incoming
    )
    prompt_mixed = finish(
        prompt_y,
        x_conv.reshape(tokens_here, heads_here, head_width),
        skip_gain,
        out_gain,
        groups_here,
    )
    prompt_terms = jnp.dot(prompt_mixed, out_weight, preferred_element_type=jnp.float32)
    prompt_out = lax.psum_scatter(prompt_terms, "tp", scatter_dimension=1, tiled=True).astype(
        jnp.bfloat16
    )
    tail_here = conv_edge.astype(jnp.float32)
    final_here = decay_total[:, None, None] * incoming + local_state
    final_state, conv_tail = (
        spread(final_here, "ctx", lax.axis_size("ctx") - 1),
        spread(tail_here, "ctx", lax.axis_size("ctx") - 1),
    )
    conv_tail = conv_tail.astype(jnp.bfloat16)
    dec_gathered = lax.all_gather(looked.astype(jnp.bfloat16), "tp", axis=2, tiled=True)
    dec_normed = rms_rows(dec_gathered, norm_gain).reshape(rows_here * steps_here, -1)
    dx_raw, dbc_raw, dec_step = project(dec_normed, x_weight, bc_weight, dt_weight, dt_bias)
    dec_x_conv = causal_conv(
        dx_raw.reshape(rows_here, steps_here, -1), conv_x, conv_tail[:, :channels]
    )
    dec_bc = causal_conv(
        dbc_raw.reshape(rows_here, steps_here, -1), kernel_bc, conv_tail[:, channels:]
    )
    dec_x_conv = dec_x_conv.reshape(rows_here, steps_here, heads_here, head_width)
    dec_bc = dec_bc.reshape(rows_here, steps_here, groups_here, 2, state_width)
    dec_y = decode_rows(
        dec_x_conv,
        dec_bc[:, :, :, 0],
        dec_bc[:, :, :, 1],
        dec_step.reshape(rows_here, steps_here, heads_here),
        decay_rate,
        final_state,
    )
    dec_mixed = finish(
        dec_y.reshape(rows_here * steps_here, heads_here, head_width),
        dec_x_conv.reshape(rows_here * steps_here, heads_here, head_width),
        skip_gain,
        out_gain,
        groups_here,
    )
    dec_terms = jnp.dot(dec_mixed, out_weight, preferred_element_type=jnp.float32).reshape(
        rows_here, steps_here, -1
    )
    decode_out = lax.psum_scatter(dec_terms, "tp", scatter_dimension=2, tiled=True).astype(
        jnp.bfloat16
    )
    return (prompt_out, decode_out)


def solution(mesh):
    return jax.shard_map(
        on_device,
        mesh=mesh,
        in_specs=(
            P("ctx", "tp"),
            P("ctx", None),
            P("ctx", "tp"),
            P(),
            P(None, "tp"),
            P(None, "tp", None, None),
            P(None, "tp"),
            P("tp"),
            P("tp"),
            P(None, "tp"),
            P(None, "tp", None, None),
            P("tp"),
            P("tp"),
            P("tp", None),
        ),
        out_specs=(P("ctx", "tp"), P("ctx", None, "tp")),
        check_vma=False,
    )
```

profile of v0, /device:TPU:0, one launch (start us, length us, event | category | flops | bytes accessed | tf_op | source)
XLA Modules:
  0.0 391.8 jit_solution(13459118670505620245)
XLA Ops:
  8.0 27.9 %all-gather = s32[8,16,4]{1,2,0:T(4,128)S(1)} all-gather(s32[1,16,4]{1,2,0:T(4,128)} %bitcast.172), channel_id=1, replica_groups=mesh['ctx'=8,'tp'=4] {'ctx'}, dimensions={0}, use_global_device_ids=true | all-gather | bytes 2304 | tf_op jit(solution)/shard_map/all_gather | solution.py:125
  36.3 4.7 %gather_fusion = bf16[512,512]{1,0:T(8,128)(2,1)S(1)} fusion(bf16[4096,512]{1,0:T(8,128)(2,1)} %param.18, s32[1024]{0:T(1024)S(1)} %pad_clamp_fusion), kind=kCustom, calls=%fused_computation | custom fusion | bytes 1050624 | tf_op jit(solution)/shard_map/jit(_take)/gather | solution.py:132
  48.9 3.8 convolution_convert_fusion
  52.8 71.3 %all-reduce.6 = (bf16[128,4,512]{2,1,0:T(4,128)(2,1)S(1)}, bf16[3,1152]{1,0:T(4,128)(2,1)S(1)}) all-reduce(f32[128,4,512]{2,1,0:T(4,128)S(1)} %select_convert_fusion, f32[3,1152]{1,0:T(4,128)S(1)} %convert_select_fusion), channel_id=3, replica_groups=mesh['ctx'=8,'tp'=4] {'ctx'}, use_global_device_ids=true, to_apply=%region_8.9.clone | all-reduce | flops 265600 | bytes 1593600
  124.1 5.9 %all_gather.11 = bf16[16,4,2048]{2,1,0:T(4,128)(2,1)S(1)} all-gather(bf16[16,4,512]{2,1,0:T(4,128)(2,1)S(1)} %dynamic-slice_convert_fusion), channel_id=1, replica_groups=mesh['ctx'=8,'tp'=4] {'tp'}, dimensions={2}, use_global_device_ids=true | all-gather | bytes 327680 | tf_op jit(solution)/shard_map/all_gather | solution.py:194
  130.8 3.0 convolution_convert_fusion.1
  146.8 94.3 %while.2 = (s32[]{:T(128)}, f32[16,64,64]{2,1,0:T(8,128)S(1)}, f32[16]{0:T(128)S(1)}, f32[16,64,64]{2,1,0:T(8,128)S(1)}, s32[]{:T(128)}) while((s32[]{:T(128)}, f32[16,64,64]{2,1,0:T(8,128)S(1)}, f32[16]{0:T(128)S(1)}, f32[16,64,64]{2,1,0:T(8,128)S(1)}, s32[]{:T(128)}) %tuple.43), condition=%wide.region_4.5_spmd, body=%wide.region_3.4_spmd.sunk | while | flops 131074 | bytes 1835173 | solution.py:171
  149.7 11.4 %collective-permute-done = f32[16,64,64]{2,1,0:T(8,128)S(1)} collective-permute-done((f32[16,64,64]{2,1,0:T(8,128)S(1)}, f32[16,64,64]{2,1,0:T(8,128)S(1)}, u32[]{:S(2)}, u32[]{:S(2)}) %collective-permute-start) | collective-permute-done | bytes 262176 | tf_op jit(solution)/shard_map/while/body/eval_jaxpr/ppermute | solution.py:15
  161.1 4.4 %collective-permute-start = (f32[16,64,64]{2,1,0:T(8,128)S(1)}, f32[16,64,64]{2,1,0:T(8,128)S(1)}, u32[]{:S(2)}, u32[]{:S(2)}) collective-permute-start(f32[16,64,64]{2,1,0:T(8,128)S(1)} %multiply_add_fusion.2), channel_id=1, source_target_pairs={{0,4},{4,8},{8,12},{12,16},{16,20},{20,24},{24,28},{1,5},{5,9},{9,... | collective-permute-start | bytes 786440 | tf_op jit(solution)/shard_map/while/body/eval_jaxpr/ppermute | solution.py:15
  165.6 10.5 %collective-permute-done = f32[16,64,64]{2,1,0:T(8,128)S(1)} collective-permute-done((f32[16,64,64]{2,1,0:T(8,128)S(1)}, f32[16,64,64]{2,1,0:T(8,128)S(1)}, u32[]{:S(2)}, u32[]{:S(2)}) %collective-permute-start) | collective-permute-done | bytes 262176 | tf_op jit(solution)/shard_map/while/body/eval_jaxpr/ppermute | solution.py:15
  176.2 4.4 %collective-permute-start = (f32[16,64,64]{2,1,0:T(8,128)S(1)}, f32[16,64,64]{2,1,0:T(8,128)S(1)}, u32[]{:S(2)}, u32[]{:S(2)}) collective-permute-start(f32[16,64,64]{2,1,0:T(8,128)S(1)} %multiply_add_fusion.2), channel_id=1, source_target_pairs={{0,4},{4,8},{8,12},{12,16},{16,20},{20,24},{24,28},{1,5},{5,9},{9,... | collective-permute-start | bytes 786440 | tf_op jit(solution)/shard_map/while/body/eval_jaxpr/ppermute | solution.py:15
  180.6 9.6 %collective-permute-done = f32[16,64,64]{2,1,0:T(8,128)S(1)} collective-permute-done((f32[16,64,64]{2,1,0:T(8,128)S(1)}, f32[16,64,64]{2,1,0:T(8,128)S(1)}, u32[]{:S(2)}, u32[]{:S(2)}) %collective-permute-start) | collective-permute-done | bytes 262176 | tf_op jit(solution)/shard_map/while/body/eval_jaxpr/ppermute | solution.py:15
  190.3 4.4 %collective-permute-start = (f32[16,64,64]{2,1,0:T(8,128)S(1)}, f32[16,64,64]{2,1,0:T(8,128)S(1)}, u32[]{:S(2)}, u32[]{:S(2)}) collective-permute-start(f32[16,64,64]{2,1,0:T(8,128)S(1)} %multiply_add_fusion.2), channel_id=1, source_target_pairs={{0,4},{4,8},{8,12},{12,16},{16,20},{20,24},{24,28},{1,5},{5,9},{9,... | collective-permute-start | bytes 786440 | tf_op jit(solution)/shard_map/while/body/eval_jaxpr/ppermute | solution.py:15
  194.8 8.7 %collective-permute-done = f32[16,64,64]{2,1,0:T(8,128)S(1)} collective-permute-done((f32[16,64,64]{2,1,0:T(8,128)S(1)}, f32[16,64,64]{2,1,0:T(8,128)S(1)}, u32[]{:S(2)}, u32[]{:S(2)}) %collective-permute-start) | collective-permute-done | bytes 262176 | tf_op jit(solution)/shard_map/while/body/eval_jaxpr/ppermute | solution.py:15
  203.6 5.2 %collective-permute-start = (f32[16,64,64]{2,1,0:T(8,128)S(1)}, f32[16,64,64]{2,1,0:T(8,128)S(1)}, u32[]{:S(2)}, u32[]{:S(2)}) collective-permute-start(f32[16,64,64]{2,1,0:T(8,128)S(1)} %multiply_add_fusion.2), channel_id=1, source_target_pairs={{0,4},{4,8},{8,12},{12,16},{16,20},{20,24},{24,28},{1,5},{5,9},{9,... | collective-permute-start | bytes 786440 | tf_op jit(solution)/shard_map/while/body/eval_jaxpr/ppermute | solution.py:15
  208.8 7.8 %collective-permute-done = f32[16,64,64]{2,1,0:T(8,128)S(1)} collective-permute-done((f32[16,64,64]{2,1,0:T(8,128)S(1)}, f32[16,64,64]{2,1,0:T(8,128)S(1)}, u32[]{:S(2)}, u32[]{:S(2)}) %collective-permute-start) | collective-permute-done | bytes 262176 | tf_op jit(solution)/shard_map/while/body/eval_jaxpr/ppermute | solution.py:15
  216.8 5.3 %collective-permute-start = (f32[16,64,64]{2,1,0:T(8,128)S(1)}, f32[16,64,64]{2,1,0:T(8,128)S(1)}, u32[]{:S(2)}, u32[]{:S(2)}) collective-permute-start(f32[16,64,64]{2,1,0:T(8,128)S(1)} %multiply_add_fusion.2), channel_id=1, source_target_pairs={{0,4},{4,8},{8,12},{12,16},{16,20},{20,24},{24,28},{1,5},{5,9},{9,... | collective-permute-start | bytes 786440 | tf_op jit(solution)/shard_map/while/body/eval_jaxpr/ppermute | solution.py:15
  222.1 6.9 %collective-permute-done = f32[16,64,64]{2,1,0:T(8,128)S(1)} collective-permute-done((f32[16,64,64]{2,1,0:T(8,128)S(1)}, f32[16,64,64]{2,1,0:T(8,128)S(1)}, u32[]{:S(2)}, u32[]{:S(2)}) %collective-permute-start) | collective-permute-done | bytes 262176 | tf_op jit(solution)/shard_map/while/body/eval_jaxpr/ppermute | solution.py:15
  229.1 5.3 %collective-permute-start = (f32[16,64,64]{2,1,0:T(8,128)S(1)}, f32[16,64,64]{2,1,0:T(8,128)S(1)}, u32[]{:S(2)}, u32[]{:S(2)}) collective-permute-start(f32[16,64,64]{2,1,0:T(8,128)S(1)} %multiply_add_fusion.2), channel_id=1, source_target_pairs={{0,4},{4,8},{8,12},{12,16},{16,20},{20,24},{24,28},{1,5},{5,9},{9,... | collective-permute-start | bytes 786440 | tf_op jit(solution)/shard_map/while/body/eval_jaxpr/ppermute | solution.py:15
  234.5 6.6 %collective-permute-done = f32[16,64,64]{2,1,0:T(8,128)S(1)} collective-permute-done((f32[16,64,64]{2,1,0:T(8,128)S(1)}, f32[16,64,64]{2,1,0:T(8,128)S(1)}, u32[]{:S(2)}, u32[]{:S(2)}) %collective-permute-start) | collective-permute-done | bytes 262176 | tf_op jit(solution)/shard_map/while/body/eval_jaxpr/ppermute | solution.py:15
  244.5 75.3 %all-reduce.5.cloned.1.call-done = f32[16,64,64]{2,1,0:T(8,128)} async-done(((f32[16,64,64]{2,1,0:T(8,128)}), f32[16,64,64]{2,1,0:T(8,128)}) %all-reduce.5.cloned.1.call-update) | async-done | bytes 262160 | tf_op jit(solution)/shard_map/psum | solution.py:20
  324.7 3.9 fusion
  340.1 9.6 %reduce-scatter.5.cloned.1.call-done = f32[16,4,512]{2,0,1:T(8,128)} async-done(((f32[16,4,2048]{2,0,1:T(8,128)}), f32[16,4,512]{2,0,1:T(8,128)}) %reduce-scatter.5.cloned.1.call-update) | async-done | bytes 131088 | tf_op jit(solution)/shard_map/reduce_scatter | solution.py:223
  351.3 32.2 %reduce-scatter.3.cloned.1.call-done = f32[256,512]{1,0:T(8,128)} async-done(((f32[256,2048]{1,0:T(8,128)}), f32[256,512]{1,0:T(8,128)}) %reduce-scatter.3.cloned.1.call-update) | async-done | bytes 524304 | tf_op jit(solution)/shard_map/reduce_scatter | solution.py:184
  (165 shorter events, 48.3 us)
Async XLA Ops:
  7.2 40.0 %copy-start = (bf16[2048,1,2,64]{0,3,2,1:T(8,128)(2,1)S(1)}, bf16[2048,1,2,64]{0,3,2,1:T(8,128)(2,1)}, u32[]{:S(2)}) copy-start(bf16[2048,1,2,64]{0,3,2,1:T(8,128)(2,1)} %param.21) | copy-start | bytes 1572868
  7.2 38.3 %copy-start.17 = (f32[16]{0:T(128)S(1)}, f32[16]{0:T(128)}, u32[]{:S(2)}) copy-start(f32[16]{0:T(128)} %param.24) | copy-start | bytes 196
  7.2 38.3 %copy-start.12 = (f32[4,1024]{1,0:T(4,128)S(1)}, f32[4,1024]{1,0:T(4,128)}, u32[]{:S(2)}) copy-start(f32[4,1024]{1,0:T(4,128)} %param.25) | copy-start | bytes 49156
  7.2 38.4 %all-gather.3.cloned.1.call-start = ((), (), s32[]{:S(2)}) async-start(), calls=%async_computation.2 | async-start | bytes 1310720 | tf_op jit(solution)/shard_map/all_gather | solution.py:135
  8.0 311.8 %all-reduce.5.cloned.1.call-start = ((), (), s32[]{:S(2)}) async-start(), calls=%async_computation.4 | async-start | bytes 1048576 | tf_op jit(solution)/shard_map/psum | solution.py:20
  52.7 81.4 %copy-start.16 = (bf16[2048,16]{0,1:T(8,128)(2,1)S(1)}, bf16[2048,16]{0,1:T(8,128)(2,1)}, u32[]{:S(2)}) copy-start(bf16[2048,16]{0,1:T(8,128)(2,1)} %param.22) | copy-start | bytes 196612
  52.7 81.4 %copy-start.18 = (f32[16]{0:T(128)S(1)}, f32[16]{0:T(128)}, u32[]{:S(2)}) copy-start(f32[16]{0:T(128)} %param.23) | copy-start | bytes 196
  137.2 7.7 %collective-permute-start.1 = (bf16[3,1152]{1,0:T(4,128)(2,1)S(1)}, bf16[3,1152]{1,0:T(4,128)(2,1)S(1)}, u32[]{:S(2)}, u32[]{:S(2)}) collective-permute-start(bf16[3,1152]{1,0:T(4,128)(2,1)S(1)} %pad_maximum_fusion), channel_id=1, source_target_pairs={{0,4},{4,8},{8,12},{12,16},{16,20},{20,24},{24,28},{1,5},{5,9},{9,... | collective-permute-start | bytes 20744 | tf_op jit(solution)/shard_map/ppermute | solution.py:15
  146.2 97.7 %copy-start.3 = (bf16[256,128]{0,1:T(8,128)(2,1)}, bf16[256,128]{0,1:T(8,128)(2,1)S(1)}, u32[]{:S(2)}) copy-start(bf16[256,128]{0,1:T(8,128)(2,1)S(1)} %copy.123) | copy-start | bytes 196612
  146.8 95.7 %copy-start.9 = (pred[256,256]{1,0:T(8,128)(4,1)S(1)}, pred[256,256]{1,0:T(8,128)(4,1)}, u32[]{:S(2)}) copy-start(pred[256,256]{1,0:T(8,128)(4,1)} %iota_compare_fusion) | copy-start | bytes 196612
  146.8 95.7 %copy-start.10 = (f32[16,256]{1,0:T(8,128)S(1)}, f32[16,256]{1,0:T(8,128)}, u32[]{:S(2)}) copy-start(f32[16,256]{1,0:T(8,128)} %get-tuple-element.85) | copy-start | bytes 49156
  146.8 95.7 %copy-start.11 = (f32[16,256]{1,0:T(8,128)S(1)}, f32[16,256]{1,0:T(8,128)}, u32[]{:S(2)}) copy-start(f32[16,256]{1,0:T(8,128)} %get-tuple-element.83) | copy-start | bytes 49156
  146.9 14.1 %collective-permute-start = (f32[16,64,64]{2,1,0:T(8,128)S(1)}, f32[16,64,64]{2,1,0:T(8,128)S(1)}, u32[]{:S(2)}, u32[]{:S(2)}) collective-permute-start(f32[16,64,64]{2,1,0:T(8,128)S(1)} %multiply_add_fusion.2), channel_id=1, source_target_pairs={{0,4},{4,8},{8,12},{12,16},{16,20},{20,24},{24,28},{1,5},{5,9},{9,... | collective-permute-start | bytes 786440 | tf_op jit(solution)/shard_map/while/body/eval_jaxpr/ppermute | solution.py:15
  161.1 14.9 %collective-permute-start = (f32[16,64,64]{2,1,0:T(8,128)S(1)}, f32[16,64,64]{2,1,0:T(8,128)S(1)}, u32[]{:S(2)}, u32[]{:S(2)}) collective-permute-start(f32[16,64,64]{2,1,0:T(8,128)S(1)} %multiply_add_fusion.2), channel_id=1, source_target_pairs={{0,4},{4,8},{8,12},{12,16},{16,20},{20,24},{24,28},{1,5},{5,9},{9,... | collective-permute-start | bytes 786440 | tf_op jit(solution)/shard_map/while/body/eval_jaxpr/ppermute | solution.py:15
  176.2 14.0 %collective-permute-start = (f32[16,64,64]{2,1,0:T(8,128)S(1)}, f32[16,64,64]{2,1,0:T(8,128)S(1)}, u32[]{:S(2)}, u32[]{:S(2)}) collective-permute-start(f32[16,64,64]{2,1,0:T(8,128)S(1)} %multiply_add_fusion.2), channel_id=1, source_target_pairs={{0,4},{4,8},{8,12},{12,16},{16,20},{20,24},{24,28},{1,5},{5,9},{9,... | collective-permute-start | bytes 786440 | tf_op jit(solution)/shard_map/while/body/eval_jaxpr/ppermute | solution.py:15
  190.3 13.1 %collective-permute-start = (f32[16,64,64]{2,1,0:T(8,128)S(1)}, f32[16,64,64]{2,1,0:T(8,128)S(1)}, u32[]{:S(2)}, u32[]{:S(2)}) collective-permute-start(f32[16,64,64]{2,1,0:T(8,128)S(1)} %multiply_add_fusion.2), channel_id=1, source_target_pairs={{0,4},{4,8},{8,12},{12,16},{16,20},{20,24},{24,28},{1,5},{5,9},{9,... | collective-permute-start | bytes 786440 | tf_op jit(solution)/shard_map/while/body/eval_jaxpr/ppermute | solution.py:15
  203.6 13.1 %collective-permute-start = (f32[16,64,64]{2,1,0:T(8,128)S(1)}, f32[16,64,64]{2,1,0:T(8,128)S(1)}, u32[]{:S(2)}, u32[]{:S(2)}) collective-permute-start(f32[16,64,64]{2,1,0:T(8,128)S(1)} %multiply_add_fusion.2), channel_id=1, source_target_pairs={{0,4},{4,8},{8,12},{12,16},{16,20},{20,24},{24,28},{1,5},{5,9},{9,... | collective-permute-start | bytes 786440 | tf_op jit(solution)/shard_map/while/body/eval_jaxpr/ppermute | solution.py:15
  216.8 12.2 %collective-permute-start = (f32[16,64,64]{2,1,0:T(8,128)S(1)}, f32[16,64,64]{2,1,0:T(8,128)S(1)}, u32[]{:S(2)}, u32[]{:S(2)}) collective-permute-start(f32[16,64,64]{2,1,0:T(8,128)S(1)} %multiply_add_fusion.2), channel_id=1, source_target_pairs={{0,4},{4,8},{8,12},{12,16},{16,20},{20,24},{24,28},{1,5},{5,9},{9,... | collective-permute-start | bytes 786440 | tf_op jit(solution)/shard_map/while/body/eval_jaxpr/ppermute | solution.py:15
  229.1 12.0 %collective-permute-start = (f32[16,64,64]{2,1,0:T(8,128)S(1)}, f32[16,64,64]{2,1,0:T(8,128)S(1)}, u32[]{:S(2)}, u32[]{:S(2)}) collective-permute-start(f32[16,64,64]{2,1,0:T(8,128)S(1)} %multiply_add_fusion.2), channel_id=1, source_target_pairs={{0,4},{4,8},{8,12},{12,16},{16,20},{20,24},{24,28},{1,5},{5,9},{9,... | collective-permute-start | bytes 786440 | tf_op jit(solution)/shard_map/while/body/eval_jaxpr/ppermute | solution.py:15
  242.0 107.6 %reduce-scatter.5.cloned.1.call-start = ((), (), s32[]{:S(2)}) async-start(), calls=%async_computation.5 | async-start | bytes 655360 | tf_op jit(solution)/shard_map/reduce_scatter | solution.py:223
  242.5 79.2 %copy-start.5 = (bf16[16,4,16,64]{3,2,0,1:T(8,128)(2,1)S(1)}, bf16[16,4,16,64]{3,2,0,1:T(8,128)(2,1)}, u32[]{:S(2)}) copy-start(bf16[16,4,16,64]{3,2,0,1:T(8,128)(2,1)} %reshape.315) | copy-start | bytes 393220
  244.5 80.2 %copy-start.7 = (f32[1024]{0:T(1024)S(1)}, f32[1024]{0:T(1024)}, u32[]{:S(2)}) copy-start(f32[1024]{0:T(1024)} %mul.457) | copy-start | bytes 12292
  244.5 80.2 %copy-start.8 = (f32[1024]{0:T(1024)S(1)}, f32[1024]{0:T(1024)}, u32[]{:S(2)}) copy-start(f32[1024]{0:T(1024)} %param.28) | copy-start | bytes 12292
  328.6 54.9 %reduce-scatter.3.cloned.1.call-start = ((), (), s32[]{:S(2)}) async-start(), calls=%async_computation.3 | async-start | bytes 2621440 | tf_op jit(solution)/shard_map/reduce_scatter | solution.py:184
  (8 other events, 139.7 us)
Sparse Core Ops, SparseCore 0:
  9.6 19.4 all-gather.2
  242.2 77.5 all-reduce.4
  328.7 20.9 reduce-scatter.4
  352.0 31.4 reduce-scatter.2
where the time goes:
time: 393 us; the launch traced here: 392 us
  waiting for transfers between devices  179 us (46%)
  blocking collectives  105 us (27%)
  starting transfers between devices  33.5 us (9%)
  matrix products  25.2 us (6%)
  local copies, waits for them, and re-layouts  19.5 us (5%)
  between operations  15.1 us (4%)
  other arithmetic  13.8 us (4%)
    psum x1, waiting for transfers between devices, spread(): return lax.psum(jnp.where(mine, value, jnp.zeros_like(value)), axis)  75.3 us
    unnamed x1, blocking collectives  71.3 us
    ppermute x8, waiting for transfers between devices, passed_along(): lax.ppermute(value, axis, [(source, source + steps) for source in range(l...  61.5 us
    ppermute x8, starting transfers between devices, passed_along(): lax.ppermute(value, axis, [(source, source + steps) for source in range(l...  33.1 us
    reduce_scatter x1, waiting for transfers between devices, on_device(): lax.psum_scatter(prompt_terms, 'tp', scatter_dimension=1, tiled=True)  32.2 us
    all_gather x1, blocking collectives, on_device(): gathered_ids = lax.all_gather(decode_ids, 'ctx', axis=0, tiled=True)  27.9 us
    reduce_scatter x1, waiting for transfers between devices, on_device(): lax.psum_scatter(dec_terms, 'tp', scatter_dimension=2, tiled=True)  9.57 us
  transfers between devices with their start and end apart: 12, of which 10 were waited for; matrix products, arithmetic and copies ran while one was open for 8% of the time, Pallas kernels for 0%

commit v1 on v0

v1 whole, which is shorter than its diff:
```python
import jax
import jax.numpy as jnp
from jax import lax
from jax.sharding import PartitionSpec as P

EPS = 1e-05
BF16 = jnp.bfloat16
F32 = jnp.float32


def swapped(value, axis, bit):
    count = lax.axis_size(axis)
    return lax.ppermute(value, axis, [(i, i ^ bit) for i in range(count)])


def bits_of(axis):
    count = lax.axis_size(axis)
    assert count & (count - 1) == 0
    return [1 << k for k in range(count.bit_length() - 1)]


def relative(blocks, axis):
    bits = bits_of(axis)
    me = lax.axis_index(axis)
    tail = blocks.shape[1:]
    cube = blocks.reshape((2,) * len(bits) + tail)
    for at, bit in enumerate(reversed(bits)):
        cube = jnp.where((me & bit) != 0, jnp.flip(cube, axis=at), cube)
    order = tuple(reversed(range(len(bits)))) + tuple(range(len(bits), cube.ndim))
    return cube.transpose(order).reshape(blocks.shape)


def rms_rows(values, gain_row):
    widened = values.astype(F32)
    factor = lax.rsqrt(jnp.mean(widened * widened, axis=-1, keepdims=True) + EPS)
    return (widened * factor * gain_row).astype(BF16)


def dot(a, b):
    return jnp.dot(a, b, preferred_element_type=F32)


def expand(per_head, width):
    return jnp.repeat(per_head, width, axis=-1)


def project(normed, x_weight, bc_weight, dt_weight, dt_bias):
    x_raw = dot(normed, x_weight).astype(BF16)
    bc_raw = dot(normed, bc_weight).astype(BF16)
    step_size = jax.nn.softplus(dot(normed, dt_weight) + dt_bias)
    return x_raw, bc_raw, step_size


def conv_rows(joined, kernel_rows, stride, length):
    joined = joined.astype(F32)
    summed = jnp.zeros((length, joined.shape[1]), F32)
    for offset in range(kernel_rows.shape[0]):
        start = offset * stride
        summed = summed + kernel_rows[offset] * joined[start : start + length]
    return jax.nn.silu(summed).astype(BF16)


def local_part(x_conv, bc_conv, step_size, decay_rate, mask, heads):
    length = x_conv.shape[0]
    state_width = bc_conv.shape[1] // 2
    width = x_conv.shape[1] // heads
    b_rows, c_rows = bc_conv[:, :state_width], bc_conv[:, state_width:]
    cum_log = jnp.dot(mask.astype(F32), step_size * decay_rate, precision=lax.Precision.HIGHEST)
    scores = lax.dot_general(c_rows, b_rows, (((1,), (1,)), ((), ())), preferred_element_type=F32)
    gaps = cum_log.T[:, :, None] - cum_log.T[:, None, :]
    decays = jnp.where(mask, jnp.exp(jnp.where(mask, gaps, 0.0)), 0.0)
    mixing = (scores[None] * decays * step_size.T[:, None, :]).astype(BF16)
    x_heads = x_conv.reshape(length, heads, width)
    within = jnp.einsum("hts,shp->thp", mixing, x_heads, preferred_element_type=F32)
    return within.reshape(length, -1), cum_log, b_rows, c_rows


def reach(c_rows, state):
    high = state.astype(BF16)
    low = (state - high.astype(F32)).astype(BF16)
    return dot(jnp.concatenate([c_rows, c_rows], axis=1), jnp.concatenate([high, low], axis=0))


def finish(y_sum, x_conv, skip_row, out_gain):
    full = y_sum + skip_row * x_conv.astype(F32)
    factor = lax.rsqrt(jnp.mean(full * full, axis=-1, keepdims=True) + EPS)
    return (full * factor * out_gain).astype(BF16)


def on_device(
    prompt_embeds,
    decode_ids,
    embed_table,
    norm_gain,
    x_weight,
    bc_weight,
    dt_weight,
    dt_bias,
    decay_log,
    conv_x,
    conv_bc,
    skip_gain,
    out_gain,
    out_weight,
):
    heads = dt_weight.shape[1]
    assert bc_weight.shape[1] == 1 and lax.axis_size("tp") == 4
    width = x_weight.shape[1] // heads
    taps = conv_x.shape[0]
    margin = taps - 1
    decay_rate = -jnp.exp(decay_log)
    kernel_bc = conv_bc.reshape(taps, -1)
    flat_bc = bc_weight.reshape(bc_weight.shape[0], -1)
    state_width = flat_bc.shape[1] // 2
    tokens, part = prompt_embeds.shape
    rows, steps = decode_ids.shape
    asked = rows * steps
    groups = lax.axis_size("ctx")
    me_c = lax.axis_index("ctx")
    me_t = lax.axis_index("tp")
    vocab_here = embed_table.shape[0]

    e2 = swapped(prompt_embeds, "tp", 2)
    e1 = swapped(prompt_embeds, "tp", 1)

    ids = decode_ids.T.reshape(-1)
    digits = jnp.stack([ids & 255, (ids >> 8) & 255, ids >> 16]).astype(BF16).reshape(-1)
    extra = -(-digits.shape[0] // part)
    digits = jnp.pad(digits, (0, extra * part - digits.shape[0])).reshape(extra, part)
    note = jnp.concatenate([prompt_embeds[-margin:], digits], axis=0)
    devices = groups * 4
    notes = lax.all_to_all(
        jnp.broadcast_to(note[None], (devices,) + note.shape), ("ctx", "tp"), 0, 0
    ).reshape(groups, 4, margin + extra, part)
    digits = notes[:, 0, margin:].reshape(groups, -1)[:, : 3 * asked].reshape(groups, 3, asked)
    digits = digits.astype(jnp.int32)
    all_ids = digits[:, 0] + digits[:, 1] * 256 + digits[:, 2] * 65536
    edges = notes[:, :, :margin].transpose(0, 2, 1, 3).reshape(groups, margin, 4 * part)
    before = lax.dynamic_index_in_dim(edges, jnp.maximum(me_c - 1, 0), 0, keepdims=False)
    before = jnp.where(me_c > 0, before, jnp.zeros_like(before))
    tail = edges[-1]

    e3 = swapped(e2, "tp", 1)

    wanted = relative(all_ids, "ctx").reshape(-1) - me_c * vocab_here
    inside = jnp.logical_and(wanted >= 0, wanted < vocab_here)
    picked = jnp.take(embed_table, jnp.clip(wanted, 0, vocab_here - 1), axis=0)
    kept = jnp.where(inside[:, None], picked, jnp.zeros((), BF16))
    for bit in bits_of("ctx"):
        half = kept.shape[0] // 2
        kept = kept[:half] + swapped(kept[half:], "ctx", bit)
    dec2 = jnp.concatenate([kept, swapped(kept, "tp", 2)], axis=0)
    dec4 = jnp.concatenate([dec2, swapped(dec2, "tp", 1)], axis=0).reshape(4, asked, part)

    def in_order(r0, r1, r2, r3):
        cube = jnp.stack([r0, r1, r2, r3])
        cube = jnp.where((me_t & 1) != 0, cube[jnp.array([1, 0, 3, 2])], cube)
        cube = jnp.where((me_t & 2) != 0, cube[jnp.array([2, 3, 0, 1])], cube)
        return jnp.concatenate([cube[0], cube[1], cube[2], cube[3]], axis=1)

    pad = 8 - margin
    features = in_order(prompt_embeds, e1, e2, e3)
    features = jnp.concatenate([jnp.zeros((pad, features.shape[1]), BF16), before, features], axis=0)
    normed = rms_rows(features, norm_gain)
    x_raw, bc_raw, step_size = project(normed, x_weight, flat_bc, dt_weight, dt_bias)
    step_size = step_size[8:]
    x_conv = conv_rows(x_raw[pad:], conv_x, 1, tokens)
    bc_conv = conv_rows(bc_raw[pad:], kernel_bc, 1, tokens)
    mask = jnp.arange(tokens)[:, None] >= jnp.arange(tokens)[None, :]
    y_local, cum_log, b_rows, c_rows = local_part(
        x_conv, bc_conv, step_size, decay_rate, mask, heads
    )
    to_end = jnp.exp(cum_log[-1] - cum_log) * step_size
    weighted = (x_conv.astype(F32) * expand(to_end, width)).astype(BF16)
    state = lax.dot_general(b_rows, weighted, (((0,), (0,)), ((), ())), preferred_element_type=F32)
    decay = expand(jnp.exp(cum_log[-1:]), width)

    came = jnp.zeros_like(state)
    since = jnp.ones_like(decay)
    for bit in bits_of("ctx"):
        high = decay.astype(BF16)
        low = (decay - high.astype(F32)).astype(BF16)
        message = jnp.concatenate([state.astype(BF16), high, low], axis=0)
        message = swapped(message, "ctx", bit).astype(F32)
        other = message[:state_width]
        other_decay = message[state_width : state_width + 1] + message[state_width + 1 :]
        later = (me_c & bit) != 0
        came = jnp.where(later, since * other + came, came)
        since = jnp.where(later, since * other_decay, since)
        state = jnp.where(later, decay * other + state, other_decay * state + other)
        decay = decay * other_decay

    dec_features = in_order(dec4[0], dec4[2], dec4[1], dec4[3])
    dec_features = jnp.concatenate([dec_features, tail], axis=0)
    dec_normed = rms_rows(dec_features, norm_gain)
    dx_raw, dbc_raw, dec_step = project(dec_normed, x_weight, flat_bc, dt_weight, dt_bias)
    dec_step = dec_step[:asked]

    def stepped(raw):
        ahead = jnp.repeat(raw[asked:], rows, axis=0)
        return jnp.concatenate([ahead, raw[:asked]], axis=0)

    dec_x = conv_rows(stepped(dx_raw), conv_x, rows, asked)
    dec_bc = conv_rows(stepped(dbc_raw), kernel_bc, rows, asked)
    at = jnp.arange(asked)
    dec_mask = jnp.logical_and(
        (at % rows)[:, None] == (at % rows)[None, :], at[:, None] >= at[None, :]
    )
    dec_y, dec_cum, _, dec_c = local_part(dec_x, dec_bc, dec_step, decay_rate, dec_mask, heads)

    skip_row = expand(skip_gain, width)
    y = y_local + reach(c_rows, came) * expand(jnp.exp(cum_log), width)
    mixed = finish(y, x_conv, skip_row, out_gain)
    dec_y = dec_y + reach(dec_c, state) * expand(jnp.exp(dec_cum), width)
    dec_mixed = finish(dec_y, dec_x, skip_row, out_gain)
    both = jnp.concatenate([mixed, dec_mixed], axis=0)

    def terms(r):
        columns = lax.dynamic_slice_in_dim(out_weight, (me_t ^ r) * part, part, axis=1)
        return dot(both, columns)

    got3 = swapped(terms(3).astype(BF16), "tp", 1)
    got1 = swapped(terms(1).astype(BF16), "tp", 1)
    far = terms(2) + got3.astype(F32)
    got2 = swapped(far.astype(BF16), "tp", 2)
    total = terms(0) + got1.astype(F32) + got2.astype(F32)
    total = total.astype(BF16)
    decode_out = total[tokens:].reshape(steps, rows, part).transpose(1, 0, 2)
    return (total[:tokens], decode_out)


def solution(mesh):
    return jax.shard_map(
        on_device,
        mesh=mesh,
        in_specs=(
            P("ctx", "tp"),
            P("ctx", None),
            P("ctx", "tp"),
            P(),
            P(None, "tp"),
            P(None, "tp", None, None),
            P(None, "tp"),
            P("tp"),
            P("tp"),
            P(None, "tp"),
            P(None, "tp", None, None),
            P("tp"),
            P("tp"),
            P("tp", None),
        ),
        out_specs=(P("ctx", "tp"), P("ctx", None, "tp")),
        check_vma=False,
    )
```

time: 393 us -> 113 us (0.29)
  waiting for transfers between devices: 179 us -> 15.7 us
  blocking collectives: 105 us -> 0 us
  between operations: 15.1 us -> 1.86 us
  local copies, waits for them, and re-layouts: 19.5 us -> 32.3 us
  starting transfers between devices: 33.5 us -> 21.1 us
  other arithmetic: 13.8 us -> 23 us
  matrix products: 25.2 us -> 17.5 us
    psum x1 -> x0, waiting for transfers between devices: 75.3 us -> none  [spread(): return lax.psum(jnp.where(mine, value, jnp.zeros_like(value)), axis)]
    unnamed x1 -> x0, blocking collectives: 71.3 us -> none
    ppermute x8 -> x14, waiting for transfers between devices: 61.5 us -> 15.7 us  [swapped(): return lax.ppermute(value, axis, [(i, i ^ bit) for i in range(count)])]
    reduce_scatter x2 -> x0, waiting for transfers between devices: 41.8 us -> none  [the longest x1 32.2 us: on_device(): lax.psum_scatter(prompt_terms, 'tp', scatter_dimension=1, tiled=True)]
    all_gather x2 -> x0, blocking collectives: 33.8 us -> none  [the longest x1 27.9 us: on_device(): gathered_ids = lax.all_gather(decode_ids, 'ctx', axis=0, tiled=True)]
    ppermute x8 -> x14, starting transfers between devices: 33.1 us -> 16.1 us  [swapped(): return lax.ppermute(value, axis, [(i, i ^ bit) for i in range(count)])]
    dot_general x16 -> x19, matrix products: 25.2 us -> 17.5 us  [the longest x12 14 us: dot(): return jnp.dot(a, b, preferred_element_type=F32)]
    slice x10 -> x18, local copies, waits for them, and re-layouts: 0.28 us -> 6.09 us  [the longest x2 2.21 us: conv_rows(): summed = summed + kernel_rows[offset] * joined[start:start + length]]
  transfers between devices with their start and end apart: 12 -> 15, of which waited for: 10 -> 4; matrix products, arithmetic and copies ran while one was open for 8% -> 58% of each run, Pallas kernels for 0% -> 0%
where the time goes in v1:
time: 113 us; the launch traced here: 111 us
  local copies, waits for them, and re-layouts  32.3 us (29%)
  other arithmetic  23 us (20%)
  starting transfers between devices  21.1 us (19%)
  matrix products  17.5 us (15%)
  waiting for transfers between devices  15.7 us (14%)
  between operations  1.86 us (2%)
    ppermute x14, starting transfers between devices, swapped(): return lax.ppermute(value, axis, [(i, i ^ bit) for i in range(count)])  16.1 us
    ppermute x14, waiting for transfers between devices, swapped(): return lax.ppermute(value, axis, [(i, i ^ bit) for i in range(count)])  15.7 us
    dot_general x12, matrix products, dot(): return jnp.dot(a, b, preferred_element_type=F32)  14 us
    all_to_all x1, starting transfers between devices, on_device(): lax.all_to_all(jnp.broadcast_to(note[None], (devices,) + note.shape), ('c...  4.98 us
    gather x1, local copies, waits for them, and re-layouts, on_device(): picked = jnp.take(embed_table, jnp.clip(wanted, 0, vocab_here - 1), axis=0)  4.89 us
    reshape x3, local copies, waits for them, and re-layouts, expand(): return jnp.repeat(per_head, width, axis=-1)  3.59 us
    select_n x2, other arithmetic, in_order(): cube = jnp.where(me_t & 1 != 0, cube[jnp.array([1, 0, 3, 2])], cube)  3.03 us
    gather x2, local copies, waits for them, and re-layouts, in_order(): cube = jnp.where(me_t & 2 != 0, cube[jnp.array([2, 3, 0, 1])], cube)  2.78 us
  transfers between devices with their start and end apart: 15, of which 4 were waited for; matrix products, arithmetic and copies ran while one was open for 58% of the time, Pallas kernels for 0%

profile of v1, /device:TPU:0, one launch (start us, length us, event | category | flops | bytes accessed | tf_op | source)
XLA Modules:
  0.0 111.5 jit_solution(1613883217668683525)
XLA Ops:
  0.6 3.0 %collective-permute-start.1 = (bf16[256,512]{1,0:T(8,128)(2,1)}, bf16[256,512]{1,0:T(8,128)(2,1)S(1)}, u32[]{:S(2)}, u32[]{:S(2)}) collective-permute-start(bf16[256,512]{1,0:T(8,128)(2,1)} %param.18), channel_id=1, source_target_pairs={{0,2},{1,3},{2,0},{3,1},{4,6},{5,7},{6,4},{7,5},{8,10},{9,11},{10,... | collective-permute-start | bytes 786440 | tf_op jit(solution)/shard_map/ppermute | solution.py:13
  6.2 5.0 %all-to-all-start = ((bf16[32,4,512]{2,1,0:T(4,128)(2,1)}), bf16[32,4,512]{2,1,0:T(4,128)(2,1)S(1)}, u32[]{:S(2)}, u32[]{:S(2)}) async-start(bf16[32,4,512]{2,1,0:T(4,128)(2,1)} %broadcast_in_dim.129), calls=%async_computation | async-start | bytes 262144 | tf_op jit(solution)/shard_map/all_to_all | solution.py:132
  21.4 1.5 %fusion.107 = (f32[1,1024]{1,0:T(1,128)}, f32[1,1024]{1,0:T(1,128)}, f32[1,1024]{1,0:T(1,128)}, f32[1,1024]{1,0:T(1,128)}) fusion(f32[4,1024]{1,0:T(4,128)} %param.27), kind=kLoop, calls=%fused_computation.226 | loop fusion | bytes 32768 | tf_op jit(solution)/shard_map/slice | solution.py:59
  23.4 4.9 %gather_fusion.2 = bf16[512,512]{1,0:T(8,128)(2,1)S(1)} fusion(bf16[4096,512]{1,0:T(8,128)(2,1)} %param.20, s32[1024]{0:T(1024)S(1)} %pad_clamp_fusion), kind=kCustom, calls=%fused_computation.2 | custom fusion | bytes 1050624 | tf_op jit(solution)/shard_map/jit(_take)/gather | solution.py:147
  28.5 1.8 %collective-permute-start.6 = (bf16[256,512]{1,0:T(8,128)(2,1)S(1)}, bf16[256,512]{1,0:T(8,128)(2,1)S(1)}, u32[]{:S(2)}, u32[]{:S(2)}) collective-permute-start(bf16[256,512]{1,0:T(8,128)(2,1)S(1)} %slice.364), channel_id=1, source_target_pairs={{0,4},{4,0},{8,12},{12,8},{16,20},{20,16},{24,28},{28,24},{1,5},{5... | collective-permute-start | bytes 786440 | tf_op jit(solution)/shard_map/ppermute | solution.py:13
  31.3 5.8 %collective-permute-done.6 = bf16[256,512]{1,0:T(8,128)(2,1)S(1)} collective-permute-done((bf16[256,512]{1,0:T(8,128)(2,1)S(1)}, bf16[256,512]{1,0:T(8,128)(2,1)S(1)}, u32[]{:S(2)}, u32[]{:S(2)}) %collective-permute-start.6) | collective-permute-done | bytes 262176 | tf_op jit(solution)/shard_map/ppermute | solution.py:13
  37.8 1.7 %collective-permute-start.7 = (bf16[128,512]{1,0:T(8,128)(2,1)}, bf16[128,512]{1,0:T(8,128)(2,1)S(1)}, u32[]{:S(2)}, u32[]{:S(2)}) collective-permute-start(bf16[128,512]{1,0:T(8,128)(2,1)} %slice.366), channel_id=1, source_target_pairs={{0,8},{4,12},{8,0},{12,4},{16,24},{20,28},{24,16},{28,20},{1,9},{5... | collective-permute-start | bytes 393224 | tf_op jit(solution)/shard_map/ppermute | solution.py:13
  41.1 2.1 %broadcast_select_fusion = bf16[4,256,512]{2,1,0:T(8,128)(2,1)} fusion(bf16[4,256,512]{2,1,0:T(8,128)(2,1)S(1)} %gather_fusion, pred[]{:T(512)S(6)} %ne.60, bf16[1,256,512]{2,1,0:T(8,128)(2,1)} %bitcast.106, bf16[1,256,512]{2,1,0:T(8,128)(2,1)S(1)} %bitcast.100, bf16[1,256,512]{2,1,0:T(8,128)(2,1)S(1)} %bitcast.103, bf16[1,256,512]{2,1,0:T(8,128)(2,1)S(1)} %bitcast.97), kind=kLoop, calls=%fused_computation.52 | loop fusion | flops 2097152 | bytes 3145729 | tf_op jit(solution)/shard_map/jit(_where)/select_n | solution.py:157
  43.2 2.0 %gather_fusion.1 = bf16[4,256,512]{2,1,0:T(8,128)(2,1)S(1)} fusion(bf16[4,256,512]{2,1,0:T(8,128)(2,1)} %broadcast_select_fusion, s32[1024]{0:T(1024)} %pad_clamp_fusion.1), kind=kCustom, calls=%fused_computation.1 | custom fusion | bytes 2097168 | tf_op jit(solution)/shard_map/gather | solution.py:158
  49.1 3.6 %fusion.98 = bf16[264,1024]{1,0:T(8,128)(2,1)S(1)} fusion(bf16[2048,1024]{1,0:T(8,128)(2,1)} %param.22, bf16[264,2048]{1,0:T(8,128)(2,1)S(1)} %get-tuple-element.19, f32[2048]{0:T(1024)S(1)} %copy-done.47, f32[264]{0:T(512)S(1)} %add_rsqrt_fusion), kind=kOutput, calls=%fused_computation.222 | convolution fusion | flops 1109458944 | bytes 5825568 | tf_op jit(solution)/shard_map/dot_general | solution.py:40
  56.2 1.5 %collective-permute-start.3 = (bf16[66,1024]{1,0:T(8,128)(2,1)S(1)}, bf16[66,1024]{1,0:T(8,128)(2,1)S(1)}, u32[]{:S(2)}, u32[]{:S(2)}) collective-permute-start(bf16[66,1024]{1,0:T(8,128)(2,1)S(1)} %pad_maximum_fusion.4), channel_id=1, source_target_pairs={{0,4},{4,0},{8,12},{12,8},{16,20},{20,16},{24,28},{28,24},{1,5},{5... | collective-permute-start | bytes 405512 | tf_op jit(solution)/shard_map/ppermute | solution.py:13
  58.0 2.5 %collective-permute-start.8 = (bf16[64,512]{1,0:T(8,128)(2,1)S(1)}, bf16[64,512]{1,0:T(8,128)(2,1)S(1)}, u32[]{:S(2)}, u32[]{:S(2)}) collective-permute-start(bf16[64,512]{1,0:T(8,128)(2,1)S(1)} %slice.368), channel_id=1, source_target_pairs={{0,16},{4,20},{8,24},{12,28},{16,0},{20,4},{24,8},{28,12},{1,17},{... | collective-permute-start | bytes 196616 | tf_op jit(solution)/shard_map/ppermute | solution.py:13
  62.6 1.5 %collective-permute-done.8 = bf16[64,512]{1,0:T(8,128)(2,1)S(1)} collective-permute-done((bf16[64,512]{1,0:T(8,128)(2,1)S(1)}, bf16[64,512]{1,0:T(8,128)(2,1)S(1)}, u32[]{:S(2)}, u32[]{:S(2)}) %collective-permute-start.8) | collective-permute-done | bytes 65568 | tf_op jit(solution)/shard_map/ppermute | solution.py:13
  64.1 1.5 %collective-permute-start.9 = (bf16[64,512]{1,0:T(8,128)(2,1)S(1)}, bf16[64,512]{1,0:T(8,128)(2,1)}, u32[]{:S(2)}, u32[]{:S(2)}) collective-permute-start(bf16[64,512]{1,0:T(8,128)(2,1)S(1)} %slice_add_fusion.2), channel_id=1, source_target_pairs={{0,2},{1,3},{2,0},{3,1},{4,6},{5,7},{6,4},{7,5},{8,10},{9,11},{10,... | collective-permute-start | bytes 196616 | tf_op jit(solution)/shard_map/ppermute | solution.py:13
  65.6 1.4 %fusion.3 = f32[16,64,256]{2,1,0:T(8,128)S(1)} fusion(bf16[256,16,64]{0,2,1:T(8,128)(2,1)S(1)} %bitcast.115, f32[16,256]{1,0:T(8,128)S(1)} %copy-done.31, f32[16,256]{1,0:T(8,128)S(1)} %bitcast.139, f32[256,256]{1,0:T(8,128)S(1)} %fusion.55, pred[256,256]{1,0:T(8,128)(4,1)S(1)} %copy-done.15), kind=kOutput, calls=%fused_computation.11 | convolution fusion | flops 140509184 | bytes 1933312 | tf_op jit(solution)/shard_map/hts,shp->thp/dot_general | solution.py:74
  68.2 1.4 %copy.42 = f32[256,1024]{1,0:T(8,128)} copy(f32[256,1024]{0,1:T(8,128)S(1)} %bitcast.95) | data formatting | bytes 2097152 | tf_op jit(solution)/shard_map/reshape | solution.py:44
  72.1 1.8 %fusion.104 = (bf16[64,1024]{1,0:T(8,128)(2,1)S(1)}, f32[64,1024]{1,0:T(8,128)}) fusion(f32[1024]{0:T(1024)S(1)} %bitcast.137, f32[64,1024]{1,0:T(8,128)} %copy-done.3, f32[1024]{0:T(1024)S(1)} %bitcast.121, f32[66,1024]{1,0:T(8,128)S(1)} %convert_element_type.213, f32[1024]{0:T(1024)S(1)} %copy-done.17, pred[]{:T(512)S(6)} %ne.64, ...), kind=kLoop, calls=%fused_computation.223 | loop fusion | flops 720896 | bytes 1196034 | tf_op jit(solution)/shard_map/convert_element_type | solution.py:183
  74.6 2.3 %collective-permute-start.5 = (bf16[66,1024]{1,0:T(8,128)(2,1)}, bf16[66,1024]{1,0:T(8,128)(2,1)}, u32[]{:S(2)}, u32[]{:S(2)}) collective-permute-start(bf16[66,1024]{1,0:T(8,128)(2,1)} %pad_maximum_fusion.6), channel_id=1, source_target_pairs={{0,16},{4,20},{8,24},{12,28},{16,0},{20,4},{24,8},{28,12},{1,17},{... | collective-permute-start | bytes 405512 | tf_op jit(solution)/shard_map/ppermute | solution.py:13
  88.5 1.9 %reshape.302 = f32[64,1024]{1,0:T(8,128)} reshape(f32[64,16,64]{2,1,0:T(8,128)} %broadcast_in_dim.153) | data formatting | bytes 524288 | tf_op jit(solution)/shard_map/reshape | solution.py:44
  94.2 1.7 %convolution_convert_fusion = bf16[320,512]{1,0:T(8,128)(2,1)S(1)} fusion(bf16[1024,2048]{1,0:T(8,128)(2,1)} %param.31, s32[]{:T(128)S(6)} %select_n.246, bf16[64,1024]{1,0:T(8,128)(2,1)S(1)} %multiply_convert_fusion.6, bf16[256,1024]{1,0:T(8,128)(2,1)S(1)} %multiply_convert_fusion.2), kind=kOutput, calls=%fused_computation.23 | convolution fusion | flops 337018880 | bytes 2031620 | tf_op jit(solution)/shard_map/dot_general | solution.py:40
  96.2 1.7 %convolution_convert_fusion.1 = bf16[320,512]{1,0:T(8,128)(2,1)S(1)} fusion(bf16[1024,2048]{1,0:T(8,128)(2,1)} %param.31, s32[]{:T(128)S(6)} %select_n.244, bf16[64,1024]{1,0:T(8,128)(2,1)S(1)} %multiply_convert_fusion.6, bf16[256,1024]{1,0:T(8,128)(2,1)S(1)} %multiply_convert_fusion.2), kind=kOutput, calls=%fused_computation.24 | convolution fusion | flops 337018880 | bytes 2031620 | tf_op jit(solution)/shard_map/dot_general | solution.py:40
  98.3 1.7 %add_convert_fusion.1 = bf16[320,512]{1,0:T(8,128)(2,1)S(1)} fusion(bf16[320,512]{1,0:T(8,128)(2,1)S(1)} %collective-permute-done.12, bf16[1024,2048]{1,0:T(8,128)(2,1)} %param.31, s32[]{:T(128)S(6)} %select_n.245, bf16[64,1024]{1,0:T(8,128)(2,1)S(1)} %multiply_convert_fusion.6, bf16[256,1024]{1,0:T(8,128)(2,1)S(1)} %multiply_convert_fusion.2), kind=kOutput, calls=%fused_computation.58 | convolution fusion | flops 337346560 | bytes 2359300 | tf_op jit(solution)/shard_map/dot_general | solution.py:40
  100.6 1.7 %fusion.22 = f32[320,512]{1,0:T(8,128)S(1)} fusion(bf16[1024,2048]{1,0:T(8,128)(2,1)} %param.31, s32[]{:T(128)S(6)} %select_n.243, bf16[64,1024]{1,0:T(8,128)(2,1)S(1)} %multiply_convert_fusion.6, bf16[256,1024]{1,0:T(8,128)(2,1)S(1)} %multiply_convert_fusion.2), kind=kOutput, calls=%fused_computation.47 | convolution fusion | flops 336855040 | bytes 2359300 | tf_op jit(solution)/shard_map/dot_general | solution.py:40
  102.4 7.6 %collective-permute-done.13 = bf16[320,512]{1,0:T(8,128)(2,1)S(1)} collective-permute-done((bf16[320,512]{1,0:T(8,128)(2,1)S(1)}, bf16[320,512]{1,0:T(8,128)(2,1)S(1)}, u32[]{:S(2)}, u32[]{:S(2)}) %collective-permute-start.13) | collective-permute-done | bytes 327712 | tf_op jit(solution)/shard_map/ppermute | solution.py:13
  (265 shorter events, 48.1 us)
Async XLA Ops:
  0.6 47.8 %copy-start = (bf16[2048,1,2,64]{0,3,2,1:T(8,128)(2,1)S(1)}, bf16[2048,1,2,64]{0,3,2,1:T(8,128)(2,1)}, u32[]{:S(2)}) copy-start(bf16[2048,1,2,64]{0,3,2,1:T(8,128)(2,1)} %param.23) | copy-start | bytes 1572868
  0.6 29.9 %collective-permute-start.1 = (bf16[256,512]{1,0:T(8,128)(2,1)}, bf16[256,512]{1,0:T(8,128)(2,1)S(1)}, u32[]{:S(2)}, u32[]{:S(2)}) collective-permute-start(bf16[256,512]{1,0:T(8,128)(2,1)} %param.18), channel_id=1, source_target_pairs={{0,2},{1,3},{2,0},{3,1},{4,6},{5,7},{6,4},{7,5},{8,10},{9,11},{10,... | collective-permute-start | bytes 786440 | tf_op jit(solution)/shard_map/ppermute | solution.py:13
  3.7 35.8 %collective-permute-start = (bf16[256,512]{1,0:T(8,128)(2,1)}, bf16[256,512]{1,0:T(8,128)(2,1)S(1)}, u32[]{:S(2)}, u32[]{:S(2)}) collective-permute-start(bf16[256,512]{1,0:T(8,128)(2,1)} %param.18), channel_id=1, source_target_pairs={{0,1},{1,0},{2,3},{3,2},{4,5},{5,4},{6,7},{7,6},{8,9},{9,8},{10,11... | collective-permute-start | bytes 786440 | tf_op jit(solution)/shard_map/ppermute | solution.py:13
  6.2 16.7 %all-to-all-start = ((bf16[32,4,512]{2,1,0:T(4,128)(2,1)}), bf16[32,4,512]{2,1,0:T(4,128)(2,1)S(1)}, u32[]{:S(2)}, u32[]{:S(2)}) async-start(bf16[32,4,512]{2,1,0:T(4,128)(2,1)} %broadcast_in_dim.129), calls=%async_computation | async-start | bytes 262144 | tf_op jit(solution)/shard_map/all_to_all | solution.py:132
  11.8 7.6 %copy-start.42 = (s32[64]{0:T(128)}, s32[64]{0:T(128)S(1)}, u32[]{:S(2)}) copy-start(s32[64]{0:T(128)S(1)} %and_select_fusion) | copy-start | bytes 772
  28.3 11.9 %copy-start.2 = (bf16[256,512]{1,0:T(8,128)(2,1)S(1)}, bf16[256,512]{1,0:T(8,128)(2,1)}, u32[]{:S(2)}) copy-start(bf16[256,512]{1,0:T(8,128)(2,1)} %param.18) | copy-start | bytes 786436
  28.5 8.5 %collective-permute-start.6 = (bf16[256,512]{1,0:T(8,128)(2,1)S(1)}, bf16[256,512]{1,0:T(8,128)(2,1)S(1)}, u32[]{:S(2)}, u32[]{:S(2)}) collective-permute-start(bf16[256,512]{1,0:T(8,128)(2,1)S(1)} %slice.364), channel_id=1, source_target_pairs={{0,4},{4,0},{8,12},{12,8},{16,20},{20,16},{24,28},{28,24},{1,5},{5... | collective-permute-start | bytes 786440 | tf_op jit(solution)/shard_map/ppermute | solution.py:13
  30.5 8.9 %collective-permute-start.2 = (bf16[256,512]{1,0:T(8,128)(2,1)S(1)}, bf16[256,512]{1,0:T(8,128)(2,1)S(1)}, u32[]{:S(2)}, u32[]{:S(2)}) collective-permute-start(bf16[256,512]{1,0:T(8,128)(2,1)S(1)} %collective-permute-done.1), channel_id=1, source_target_pairs={{0,1},{1,0},{2,3},{3,2},{4,5},{5,4},{6,7},{7,6},{8,9},{9,8},{10,11... | collective-permute-start | bytes 786440 | tf_op jit(solution)/shard_map/ppermute | solution.py:13
  37.8 20.2 %collective-permute-start.7 = (bf16[128,512]{1,0:T(8,128)(2,1)}, bf16[128,512]{1,0:T(8,128)(2,1)S(1)}, u32[]{:S(2)}, u32[]{:S(2)}) collective-permute-start(bf16[128,512]{1,0:T(8,128)(2,1)} %slice.366), channel_id=1, source_target_pairs={{0,8},{4,12},{8,0},{12,4},{16,24},{20,28},{24,16},{28,20},{1,9},{5... | collective-permute-start | bytes 393224 | tf_op jit(solution)/shard_map/ppermute | solution.py:13
  48.4 13.1 %copy-start.16 = (f32[1024]{0:T(1024)}, f32[1024]{0:T(1024)S(1)}, u32[]{:S(2)}) copy-start(f32[1024]{0:T(1024)S(1)} %broadcast_in_dim.139) | copy-start | bytes 12292
  55.9 9.7 %copy-start.12 = (bf16[256,1024]{0,1:T(8,128)(2,1)S(1)}, bf16[256,1024]{0,1:T(8,128)(2,1)}, u32[]{:S(2)}) copy-start(bf16[256,1024]{0,1:T(8,128)(2,1)} %copy.40) | copy-start | bytes 1572868
  55.9 9.7 %copy-start.15 = (pred[256,256]{1,0:T(8,128)(4,1)S(1)}, pred[256,256]{1,0:T(8,128)(4,1)}, u32[]{:S(2)}) copy-start(pred[256,256]{1,0:T(8,128)(4,1)} %iota_compare_fusion) | copy-start | bytes 196612
  55.9 9.7 %copy-start.28 = (f32[256,16]{0,1:T(8,128)S(1)}, f32[256,16]{0,1:T(8,128)}, u32[]{:S(2)}) copy-start(f32[256,16]{0,1:T(8,128)} %copy-done.27) | copy-start | bytes 49156
  55.9 9.7 %copy-start.31 = (f32[16,256]{1,0:T(8,128)S(1)}, f32[16,256]{1,0:T(8,128)}, u32[]{:S(2)}) copy-start(f32[16,256]{1,0:T(8,128)} %get-tuple-element.31) | copy-start | bytes 49156
  56.2 5.2 %collective-permute-start.3 = (bf16[66,1024]{1,0:T(8,128)(2,1)S(1)}, bf16[66,1024]{1,0:T(8,128)(2,1)S(1)}, u32[]{:S(2)}, u32[]{:S(2)}) collective-permute-start(bf16[66,1024]{1,0:T(8,128)(2,1)S(1)} %pad_maximum_fusion.4), channel_id=1, source_target_pairs={{0,4},{4,0},{8,12},{12,8},{16,20},{20,16},{24,28},{28,24},{1,5},{5... | collective-permute-start | bytes 405512 | tf_op jit(solution)/shard_map/ppermute | solution.py:13
  58.0 6.0 %collective-permute-start.8 = (bf16[64,512]{1,0:T(8,128)(2,1)S(1)}, bf16[64,512]{1,0:T(8,128)(2,1)S(1)}, u32[]{:S(2)}, u32[]{:S(2)}) collective-permute-start(bf16[64,512]{1,0:T(8,128)(2,1)S(1)} %slice.368), channel_id=1, source_target_pairs={{0,16},{4,20},{8,24},{12,28},{16,0},{20,4},{24,8},{28,12},{1,17},{... | collective-permute-start | bytes 196616 | tf_op jit(solution)/shard_map/ppermute | solution.py:13
  62.2 8.2 %collective-permute-start.4 = (bf16[66,1024]{1,0:T(8,128)(2,1)}, bf16[66,1024]{1,0:T(8,128)(2,1)}, u32[]{:S(2)}, u32[]{:S(2)}) collective-permute-start(bf16[66,1024]{1,0:T(8,128)(2,1)} %pad_maximum_fusion.5), channel_id=1, source_target_pairs={{0,8},{4,12},{8,0},{12,4},{16,24},{20,28},{24,16},{28,20},{1,9},{5... | collective-permute-start | bytes 405512 | tf_op jit(solution)/shard_map/ppermute | solution.py:13
  64.1 5.5 %collective-permute-start.9 = (bf16[64,512]{1,0:T(8,128)(2,1)S(1)}, bf16[64,512]{1,0:T(8,128)(2,1)}, u32[]{:S(2)}, u32[]{:S(2)}) collective-permute-start(bf16[64,512]{1,0:T(8,128)(2,1)S(1)} %slice_add_fusion.2), channel_id=1, source_target_pairs={{0,2},{1,3},{2,0},{3,1},{4,6},{5,7},{6,4},{7,5},{8,10},{9,11},{10,... | collective-permute-start | bytes 196616 | tf_op jit(solution)/shard_map/ppermute | solution.py:13
  70.4 6.5 %collective-permute-start.10 = (bf16[128,512]{1,0:T(8,128)(2,1)S(1)}, bf16[128,512]{1,0:T(8,128)(2,1)S(1)}, u32[]{:S(2)}, u32[]{:S(2)}) collective-permute-start(bf16[128,512]{1,0:T(8,128)(2,1)S(1)} %pad_maximum_fusion.7), channel_id=1, source_target_pairs={{0,1},{1,0},{2,3},{3,2},{4,5},{5,4},{6,7},{7,6},{8,9},{9,8},{10,11... | collective-permute-start | bytes 393224 | tf_op jit(solution)/shard_map/ppermute | solution.py:13
  74.6 6.7 %copy-start.14 = (bf16[1,3,4,512]{3,1,2,0:T(4,128)(2,1)S(1)}, bf16[1,3,4,512]{3,1,2,0:T(4,128)(2,1)}, u32[]{:S(2)}) copy-start(bf16[1,3,4,512]{3,1,2,0:T(4,128)(2,1)} %slice.375) | copy-start | bytes 36868
  74.6 15.7 %collective-permute-start.5 = (bf16[66,1024]{1,0:T(8,128)(2,1)}, bf16[66,1024]{1,0:T(8,128)(2,1)}, u32[]{:S(2)}, u32[]{:S(2)}) collective-permute-start(bf16[66,1024]{1,0:T(8,128)(2,1)} %pad_maximum_fusion.6), channel_id=1, source_target_pairs={{0,16},{4,20},{8,24},{12,28},{16,0},{20,4},{24,8},{28,12},{1,17},{... | collective-permute-start | bytes 405512 | tf_op jit(solution)/shard_map/ppermute | solution.py:13
  95.9 2.4 %collective-permute-start.12 = (bf16[320,512]{1,0:T(8,128)(2,1)S(1)}, bf16[320,512]{1,0:T(8,128)(2,1)S(1)}, u32[]{:S(2)}, u32[]{:S(2)}) collective-permute-start(bf16[320,512]{1,0:T(8,128)(2,1)S(1)} %convolution_convert_fusion), channel_id=1, source_target_pairs={{0,1},{1,0},{2,3},{3,2},{4,5},{5,4},{6,7},{7,6},{8,9},{9,8},{10,11... | collective-permute-start | bytes 983048 | tf_op jit(solution)/shard_map/ppermute | solution.py:13
  97.9 4.4 %collective-permute-start.11 = (bf16[320,512]{1,0:T(8,128)(2,1)S(1)}, bf16[320,512]{1,0:T(8,128)(2,1)S(1)}, u32[]{:S(2)}, u32[]{:S(2)}) collective-permute-start(bf16[320,512]{1,0:T(8,128)(2,1)S(1)} %convolution_convert_fusion.1), channel_id=1, source_target_pairs={{0,1},{1,0},{2,3},{3,2},{4,5},{5,4},{6,7},{7,6},{8,9},{9,8},{10,11... | collective-permute-start | bytes 983048 | tf_op jit(solution)/shard_map/ppermute | solution.py:13
  100.0 9.9 %collective-permute-start.13 = (bf16[320,512]{1,0:T(8,128)(2,1)S(1)}, bf16[320,512]{1,0:T(8,128)(2,1)S(1)}, u32[]{:S(2)}, u32[]{:S(2)}) collective-permute-start(bf16[320,512]{1,0:T(8,128)(2,1)S(1)} %add_convert_fusion.1), channel_id=1, source_target_pairs={{0,2},{1,3},{2,0},{3,1},{4,6},{5,7},{6,4},{7,5},{8,10},{9,11},{10,... | collective-permute-start | bytes 983048 | tf_op jit(solution)/shard_map/ppermute | solution.py:13
  (44 other events, 105.4 us)

commit v2 on v1

v2 whole, which is shorter than its diff:
```python
import functools

import jax
import jax.numpy as jnp
from jax import lax
from jax.experimental import pallas as pl
from jax.experimental.pallas import tpu as pltpu
from jax.sharding import PartitionSpec as P

EPS = 1e-05
BF16 = jnp.bfloat16
F32 = jnp.float32
LANES = 128
PARTS = 4
EDGE = 8
MEBI = 1024 * 1024


def swapped(value, axis, bit):
    count = lax.axis_size(axis)
    return lax.ppermute(value, axis, [(i, i ^ bit) for i in range(count)])


def bits_of(axis):
    count = lax.axis_size(axis)
    assert count & (count - 1) == 0
    return [1 << k for k in range(count.bit_length() - 1)]


def relative(blocks, axis):
    bits = bits_of(axis)
    me = lax.axis_index(axis)
    tail = blocks.shape[1:]
    cube = blocks.reshape((2,) * len(bits) + tail)
    for at, bit in enumerate(reversed(bits)):
        cube = jnp.where((me & bit) != 0, jnp.flip(cube, axis=at), cube)
    order = tuple(reversed(range(len(bits)))) + tuple(range(len(bits), cube.ndim))
    return cube.transpose(order).reshape(blocks.shape)


def dot(a, b):
    return jnp.dot(a, b, preferred_element_type=F32)


def across(a, b, axis):
    return lax.dot_general(a, b, (((axis,), (axis,)), ((), ())), preferred_element_type=F32)


def halves(value):
    high = value.astype(BF16)
    low = (value - high.astype(F32)).astype(BF16)
    return high, low


def iota(shape, axis):
    return lax.broadcasted_iota(jnp.int32, shape, axis)


def spreader(width, channels):
    head = iota((2 * LANES, channels), 0) & (LANES - 1)
    return jnp.where(head == iota((2 * LANES, channels), 1) // width, 1.0, 0.0).astype(BF16)


def widened(per_head, spread):
    high, low = halves(per_head)
    return dot(jnp.concatenate([high, low], axis=1), spread)


def padded(row):
    return jnp.concatenate([row, jnp.zeros((row.shape[0], LANES - row.shape[1]), F32)], axis=1)


def silu(value):
    return value / (1.0 + jnp.exp(-value))


def front_kernel(
    decode,
    rows,
    heads,
    place,
    notes,
    own,
    over1,
    over2,
    over3,
    gain,
    x_weight,
    bc_weight,
    dt_weight,
    dt_bias,
    decay_log,
    conv_x,
    conv_bc,
    skip_gain,
    y_out,
    bc_out,
    reach_out,
    *rest,
):
    if decode:
        normed, x_conv, joined = rest
    else:
        message_out, state_out, decay_out, normed, x_conv, joined = rest
    tokens, part = own.shape
    channels = x_weight.shape[1]
    width = channels // heads
    state_width = bc_weight.shape[1] // 2
    taps = conv_x.shape[0]
    margin = taps - 1
    me, edge_at, edge_on = place[0], place[1], place[2]

    blocks = [ref[...].astype(F32) for ref in (own, over1, over2, over3)]
    square = sum(jnp.sum(b * b, axis=1, keepdims=True) for b in blocks)
    factor = lax.rsqrt(square / (PARTS * part) + EPS)
    for r in range(PARTS):
        normed[me ^ r, :tokens, :] = (blocks[r] * factor * gain[me ^ r]).astype(BF16)
    valid = jnp.logical_and(iota((EDGE, part), 0) >= EDGE - margin, edge_on > 0)
    edges = [jnp.where(valid, notes[edge_at * PARTS + j].astype(F32), 0.0) for j in range(PARTS)]
    square = sum(jnp.sum(e * e, axis=1, keepdims=True) for e in edges)
    factor = lax.rsqrt(square / (PARTS * part) + EPS)
    for j in range(PARTS):
        edge = edges[j] * factor * gain[j]
        normed[j, tokens:, :] = jnp.concatenate([edge, jnp.zeros_like(edge)], axis=0).astype(BF16)

    def projected(weight_of):
        return sum(dot(normed[j], weight_of(j)) for j in range(PARTS))

    def convolved(raw, taps_of):
        raw = raw.astype(BF16).astype(F32)
        lanes = raw.shape[1]
        edge = raw[tokens : tokens + EDGE]
        if decode:
            for m in range(margin):
                one = edge[EDGE - margin + m : EDGE - margin + m + 1]
                joined[m * rows : (m + 1) * rows, :lanes] = jnp.broadcast_to(one, (rows, lanes))
            joined[margin * rows : margin * rows + tokens, :lanes] = raw[:tokens]
            starts = [k * rows for k in range(taps)]
        else:
            joined[:EDGE, :lanes] = edge
            joined[EDGE : EDGE + tokens, :lanes] = raw[:tokens]
            starts = [EDGE - margin + k for k in range(taps)]
        total = sum(taps_of(k) * joined[s : s + tokens, :lanes] for k, s in enumerate(starts))
        return silu(total)

    step_lanes = 2 * LANES
    for lane in range(0, channels, step_lanes):
        raw = projected(lambda j: x_weight[j * part : (j + 1) * part, lane : lane + step_lanes])
        x_conv[:, lane : lane + step_lanes] = convolved(
            raw, lambda k: conv_x[k : k + 1, lane : lane + step_lanes]
        ).astype(BF16)

    def side(j):
        here = slice(j * part, (j + 1) * part)
        fill = jnp.zeros((part, LANES - heads), BF16)
        return jnp.concatenate([bc_weight[here], dt_weight[here], fill], axis=1)

    raw = projected(side)
    bc_conv = convolved(raw[:, : 2 * state_width], lambda k: conv_bc[k : k + 1])
    bc_out[...] = bc_conv.astype(BF16)
    pre = raw[:tokens, 2 * state_width :] + padded(dt_bias[...])
    step_size = jnp.maximum(pre, 0.0) + jnp.log1p(jnp.exp(-jnp.abs(pre)))
    b_rows = bc_conv[:, :state_width].astype(BF16)
    c_rows = bc_conv[:, state_width:].astype(BF16)

    t_at = iota((tokens, tokens), 0)
    s_at = iota((tokens, tokens), 1)
    mask = t_at >= s_at
    if decode:
        mask = jnp.logical_and(mask, t_at % rows == s_at % rows)
    logs = step_size * -jnp.exp(padded(decay_log[...]))
    high, low = halves(logs)
    lowest = (logs - high.astype(F32) - low.astype(F32)).astype(BF16)
    sums = dot(
        jnp.where(mask, 1.0, 0.0).astype(BF16), jnp.concatenate([high, low, lowest], axis=1)
    )
    cum_log = sums[:, :LANES] + sums[:, LANES : 2 * LANES] + sums[:, 2 * LANES :]
    reach_out[...] = jnp.exp(cum_log)
    cum_across = cum_log.T
    step_across = step_size.T
    scores = across(c_rows, b_rows, 1)
    spread = spreader(width, channels)
    skip_row = widened(jnp.broadcast_to(padded(skip_gain[...]), (EDGE, LANES)), spread)[:1]

    per_tile = LANES // width
    lane_head = iota((tokens, LANES), 1) // width
    for tile in range(channels // LANES):
        lanes = slice(tile * LANES, (tile + 1) * LANES)
        x_tile = x_conv[:, lanes].astype(F32)
        left, right = [], []
        for k in range(per_tile):
            h = tile * per_tile + k
            gaps = cum_log[:, h : h + 1] - cum_across[h : h + 1, :]
            decays = jnp.exp(jnp.where(mask, gaps, -1e30))
            left.append((scores * decays * step_across[h : h + 1, :]).astype(BF16))
            right.append(jnp.where(lane_head == k, x_tile, 0.0).astype(BF16))
        within = sum(dot(a, b) for a, b in zip(left, right))
        y_out[:, lanes] = within + skip_row[:, lanes] * x_tile

    if not decode:
        last = cum_log[tokens - 1 : tokens]
        to_end = jnp.exp(last - cum_log) * step_size
        b_turned = bc_conv.T[:state_width].astype(BF16)
        decay = widened(jnp.broadcast_to(jnp.exp(last), (EDGE, LANES)), spread)
        decay_out[...] = decay
        high, low = halves(decay[:1])
        at = iota((2 * EDGE, channels), 0)
        message_out[state_width:, :] = jnp.where(
            at == 0, high.astype(F32), jnp.where(at == 1, low.astype(F32), 0.0)
        ).astype(BF16)
        for lane in range(0, channels, step_lanes):
            lanes = slice(lane, lane + step_lanes)
            scale = widened(to_end, spread[:, lanes])
            weighted = (x_conv[:, lanes].astype(F32) * scale).astype(BF16)
            state = dot(b_turned, weighted)
            state_out[:, lanes] = state
            message_out[:state_width, lanes] = state.astype(BF16)


def unpacked(message, state_width):
    other = message[:state_width, :].astype(F32)
    tail = message[state_width:, :].astype(F32)
    return other, tail[0:1] + tail[1:2]


def step_kernel(first, place, message, state, decay, came, since, message_out, state_out, decay_out, came_out, since_out):
    later = place[0] > 0
    state_width = state.shape[0]
    other, other_decay = unpacked(message, state_width)
    mine, my_decay = state[...], decay[0:1, :]
    before = jnp.zeros_like(mine) if first else came[...]
    passed = jnp.ones_like(my_decay) if first else since[0:1, :]
    came_out[...] = jnp.where(later, passed * other + before, before)
    since_out[...] = jnp.broadcast_to(jnp.where(later, passed * other_decay, passed), since_out.shape)
    total = jnp.where(later, my_decay * other + mine, other_decay * mine + other)
    decayed = my_decay * other_decay
    state_out[...] = total
    decay_out[...] = jnp.broadcast_to(decayed, decay_out.shape)
    message_out[:state_width, :] = total.astype(BF16)
    high, low = halves(decayed)
    at = iota((2 * EDGE, state.shape[1]), 0)
    message_out[state_width:, :] = jnp.where(
        at == 0, high.astype(F32), jnp.where(at == 1, low.astype(F32), 0.0)
    ).astype(BF16)


def back_kernel(decode, heads, place, message, state, decay, came, since, y, bc, reach, gain, weight, sent_out, kept_out, full, mixed):
    me, later = place[0], place[1] > 0
    state_width = state.shape[0]
    tokens, channels = y.shape
    part = weight.shape[1] // PARTS
    other, other_decay = unpacked(message, state_width)
    if decode:
        incoming = jnp.where(later, decay[0:1, :] * other + state[...], other_decay * state[...] + other)
    else:
        incoming = jnp.where(later, since[0:1, :] * other + came[...], came[...])
    high, low = halves(incoming)
    blank = jnp.zeros_like(high)
    table = jnp.concatenate([blank, high, blank, low], axis=0)
    twice = jnp.concatenate([bc[...], bc[...]], axis=1)
    spread = spreader(channels // heads, channels)
    step_lanes = 2 * LANES
    square = jnp.zeros((tokens, 1), F32)
    for lane in range(0, channels, step_lanes):
        lanes = slice(lane, lane + step_lanes)
        total = y[:, lanes] + dot(twice, table[:, lanes]) * widened(reach[...], spread[:, lanes])
        full[:, lanes] = total
        square = square + jnp.sum(total * total, axis=1, keepdims=True)
    factor = lax.rsqrt(square / channels + EPS)
    mixed[...] = (full[...] * factor * gain[...]).astype(BF16)
    for at, r in enumerate((3, 1)):
        columns = pl.ds(pl.multiple_of((me ^ r) * part, part), part)
        sent_out[at] = dot(mixed[...], weight[:, columns]).astype(BF16)
    for at, r in enumerate((2, 0)):
        columns = pl.ds(pl.multiple_of((me ^ r) * part, part), part)
        kept_out[at] = dot(mixed[...], weight[:, columns])


VMEM = pl.BlockSpec(memory_space=pltpu.VMEM)
SMEM = pl.BlockSpec(memory_space=pltpu.SMEM)


def called(kernel, inputs, outs, scratch, flops, limit):
    moved = sum(v.size * v.dtype.itemsize for v in inputs) + sum(
        o.size * o.dtype.itemsize for o in outs
    )
    return pl.pallas_call(
        kernel,
        out_shape=outs,
        in_specs=[SMEM] + [VMEM] * (len(inputs) - 1),
        out_specs=[VMEM] * len(outs),
        scratch_shapes=scratch,
        compiler_params=pltpu.CompilerParams(vmem_limit_bytes=limit * MEBI),
        cost_estimate=pl.CostEstimate(flops=flops, bytes_accessed=moved, transcendentals=0),
    )(*inputs)


def shaped(shape, dtype):
    return jax.ShapeDtypeStruct(shape, dtype)


def on_device(
    prompt_embeds,
    decode_ids,
    embed_table,
    norm_gain,
    x_weight,
    bc_weight,
    dt_weight,
    dt_bias,
    decay_log,
    conv_x,
    conv_bc,
    skip_gain,
    out_gain,
    out_weight,
):
    heads = dt_weight.shape[1]
    assert bc_weight.shape[1] == 1 and lax.axis_size("tp") == PARTS
    channels = x_weight.shape[1]
    taps = conv_x.shape[0]
    margin = taps - 1
    flat_bc = bc_weight.reshape(bc_weight.shape[0], -1)
    state_width = flat_bc.shape[1] // 2
    assert flat_bc.shape[1] == LANES
    tokens, part = prompt_embeds.shape
    rows, steps = decode_ids.shape
    asked = rows * steps
    groups = lax.axis_size("ctx")
    me_c = lax.axis_index("ctx")
    me_t = lax.axis_index("tp")
    vocab_here = embed_table.shape[0]
    bits = bits_of("ctx")
    assert len(bits) >= 2

    e2 = swapped(prompt_embeds, "tp", 2)
    e1 = swapped(prompt_embeds, "tp", 1)

    ids = decode_ids.T.reshape(-1)
    digits = jnp.stack([ids & 255, (ids >> 8) & 255, ids >> 16]).astype(BF16).reshape(-1)
    extra = EDGE - margin
    digits = jnp.pad(digits, (0, extra * part - digits.shape[0])).reshape(extra, part)
    note = jnp.concatenate([digits, prompt_embeds[-margin:]], axis=0)
    devices = groups * PARTS
    notes = lax.all_to_all(
        jnp.broadcast_to(note[None], (devices,) + note.shape), ("ctx", "tp"), 0, 0
    )
    digits = notes.reshape(groups, PARTS, EDGE, part)[:, 0, :extra].reshape(groups, -1)
    digits = digits[:, : 3 * asked].reshape(groups, 3, asked).astype(jnp.int32)
    all_ids = digits[:, 0] + digits[:, 1] * 256 + digits[:, 2] * 65536

    e3 = swapped(e2, "tp", 1)

    wanted = relative(all_ids, "ctx").reshape(-1) - me_c * vocab_here
    inside = jnp.logical_and(wanted >= 0, wanted < vocab_here)
    picked = jnp.take(embed_table, jnp.clip(wanted, 0, vocab_here - 1), axis=0)
    kept = jnp.where(inside[:, None], picked, jnp.zeros((), BF16))
    for bit in bits:
        half = kept.shape[0] // 2
        kept = kept[:half] + swapped(kept[half:], "ctx", bit)
    near = swapped(kept, "tp", 2)
    over = swapped(jnp.concatenate([kept, near], axis=0), "tp", 1)

    weights = [
        norm_gain.reshape(PARTS, 1, part),
        x_weight,
        flat_bc,
        dt_weight,
        dt_bias.reshape(1, -1),
        decay_log.reshape(1, -1),
        conv_x,
        conv_bc.reshape(taps, -1),
        skip_gain.reshape(1, -1),
    ]
    packed = state_width + 2 * EDGE

    def front(decode, place, blocks, count):
        outs = [
            shaped((count, channels), F32),
            shaped((count, LANES), BF16),
            shaped((count, LANES), F32),
        ]
        if not decode:
            outs += [
                shaped((packed, channels), BF16),
                shaped((state_width, channels), F32),
                shaped((EDGE, channels), F32),
            ]
        joined = margin * rows if decode else EDGE
        scratch = [
            pltpu.VMEM((PARTS, count + 2 * EDGE, part), BF16),
            pltpu.VMEM((count, channels), BF16),
            pltpu.VMEM((joined + count, 2 * LANES), F32),
        ]
        return called(
            functools.partial(front_kernel, decode, rows, heads),
            [place, notes] + blocks + weights,
            outs,
            scratch,
            2 * count * PARTS * part * (channels + 2 * LANES),
            24,
        )

    ones = jnp.ones((), jnp.int32)
    place = jnp.stack([me_t, jnp.maximum(me_c - 1, 0), (me_c > 0).astype(jnp.int32)])
    y, bc, reach, message, state, decay = front(
        False, place.astype(jnp.int32), [prompt_embeds, e1, e2, e3], tokens
    )

    came, since = state, decay
    for bit in bits[:-1]:
        got = swapped(message, "ctx", bit)
        later = ((me_c & bit) != 0).astype(jnp.int32).reshape(1)
        message, state, decay, came, since = called(
            functools.partial(step_kernel, bit == bits[0]),
            [later, got, state, decay, came, since],
            [
                shaped((packed, channels), BF16),
                shaped((state_width, channels), F32),
                shaped((EDGE, channels), F32),
                shaped((state_width, channels), F32),
                shaped((EDGE, channels), F32),
            ],
            [],
            8 * state_width * channels,
            8,
        )
    got = swapped(message, "ctx", bits[-1])
    later = ((me_c & bits[-1]) != 0).astype(jnp.int32)
    back_place = jnp.stack([me_t.astype(jnp.int32), later])

    def back(decode, y, bc, reach):
        count = y.shape[0]
        sent, held = called(
            functools.partial(back_kernel, decode, heads),
            [back_place, got, state, decay, came, since, y, bc, reach, out_gain.reshape(1, -1), out_weight],
            [shaped((2, count, part), BF16), shaped((2, count, part), F32)],
            [pltpu.VMEM((count, channels), F32), pltpu.VMEM((count, channels), BF16)],
            2 * count * channels * PARTS * part,
            24,
        )
        got_near = swapped(sent, "tp", 1).astype(F32)
        far = swapped((held[0] + got_near[0]).astype(BF16), "tp", 2)
        return (held[1] + got_near[1] + far.astype(F32)).astype(BF16)

    prompt_out = back(False, y, bc, reach)

    place = jnp.stack([me_t.astype(jnp.int32), ones * (groups - 1), ones])
    blocks = [kept, over[:asked], near, over[asked:]]
    dec_y, dec_bc, dec_reach = front(True, place, blocks, asked)
    decode_out = back(True, dec_y, dec_bc, dec_reach)
    decode_out = decode_out.reshape(steps, rows, part).transpose(1, 0, 2)
    return (prompt_out, decode_out)


def solution(mesh):
    return jax.shard_map(
        on_device,
        mesh=mesh,
        in_specs=(
            P("ctx", "tp"),
            P("ctx", None),
            P("ctx", "tp"),
            P(),
            P(None, "tp"),
            P(None, "tp", None, None),
            P(None, "tp"),
            P("tp"),
            P("tp"),
            P(None, "tp"),
            P(None, "tp", None, None),
            P("tp"),
            P("tp"),
            P("tp", None),
        ),
        out_specs=(P("ctx", "tp"), P("ctx", None, "tp")),
        check_vma=False,
    )
```

time: 113 us -> 97.2 us (0.86)
  other arithmetic: 23 us -> 4.76 us
  waiting for transfers between devices: 15.7 us -> 33.8 us
  matrix products: 17.5 us -> 0 us
  Pallas kernels: 0 us -> 13 us
  local copies, waits for them, and re-layouts: 32.3 us -> 23.8 us
    dot_general x19 -> x0, matrix products: 17.5 us -> none  [the longest x12 14 us: dot(): return jnp.dot(a, b, preferred_element_type=F32)]
    pallas_call x0 -> x6, Pallas kernels: none -> 13 us  [called(): pl.pallas_call(kernel, out_shape=outs, in_specs=[SMEM] + [VMEM] * (len(in...]
    unnamed x108 -> x62, local copies, waits for them, and re-layouts: 2.16 us -> 13.9 us
    ppermute x14 -> x15, waiting for transfers between devices: 15.7 us -> 24.9 us  [swapped(): return lax.ppermute(value, axis, [(i, i ^ bit) for i in range(count)])]
    all_to_all x1, waiting for transfers between devices: 0.01 us -> 8.87 us  [on_device(): lax.all_to_all(jnp.broadcast_to(note[None], (devices,) + note.shape), ('c...]
    select_n x7 -> x0, other arithmetic: 5.83 us -> none  [the longest x2 3.03 us: in_order(): cube = jnp.where(me_t & 1 != 0, cube[jnp.array([1, 0, 3, 2])], cube)]
    convert_element_type x24 -> x7, other arithmetic: 6.44 us -> 1.12 us  [the longest x2 0.86 us: back(): return (held[1] + got_near[1] + far.astype(F32)).astype(BF16)]
    slice x15 -> x3, local copies, waits for them, and re-layouts: 5.37 us -> 0.72 us  [the longest x1 0.71 us: on_device(): note = jnp.concatenate([digits, prompt_embeds[-margin:]], axis=0)]
  transfers between devices with their start and end apart: 15 -> 16, of which waited for: 4 -> 10; matrix products, arithmetic and copies ran while one was open for 58% -> 12% of each run, Pallas kernels for 0% -> 13%
where the time goes in v2:
time: 97.2 us; the launch traced here: 96.5 us
  waiting for transfers between devices  33.8 us (35%)
  local copies, waits for them, and re-layouts  23.8 us (24%)
  starting transfers between devices  20.1 us (21%)
  Pallas kernels  13 us (13%)
  other arithmetic  4.76 us (5%)
  between operations  1.02 us (1%)
    ppermute x15, waiting for transfers between devices, swapped(): return lax.ppermute(value, axis, [(i, i ^ bit) for i in range(count)])  24.9 us
    unnamed x62, local copies, waits for them, and re-layouts  13.9 us
    pallas_call x6, Pallas kernels, called(): pl.pallas_call(kernel, out_shape=outs, in_specs=[SMEM] + [VMEM] * (len(in...  13 us
    ppermute x15, starting transfers between devices, swapped(): return lax.ppermute(value, axis, [(i, i ^ bit) for i in range(count)])  12.9 us
    all_to_all x1, waiting for transfers between devices, on_device(): lax.all_to_all(jnp.broadcast_to(note[None], (devices,) + note.shape), ('c...  8.87 us
    all_to_all x1, starting transfers between devices, on_device(): lax.all_to_all(jnp.broadcast_to(note[None], (devices,) + note.shape), ('c...  7.3 us
    gather x1, local copies, waits for them, and re-layouts, on_device(): picked = jnp.take(embed_table, jnp.clip(wanted, 0, vocab_here - 1), axis=0)  4.74 us
  transfers between devices with their start and end apart: 16, of which 10 were waited for; matrix products, arithmetic and copies ran while one was open for 12% of the time, Pallas kernels for 13%

profile of v2, /device:TPU:0, one launch (start us, length us, event | category | flops | bytes accessed | tf_op | source)
XLA Modules:
  0.0 96.5 jit_solution(6110943596998372475)
XLA Ops:
  3.2 7.3 %all-to-all-start = ((bf16[32,8,512]{2,1,0:T(8,128)(2,1)}), bf16[32,8,512]{2,1,0:T(8,128)(2,1)S(1)}, u32[]{:S(2)}, u32[]{:S(2)}) async-start(bf16[32,8,512]{2,1,0:T(8,128)(2,1)} %broadcast_in_dim.29), calls=%async_computation | async-start | bytes 524288 | tf_op jit(solution)/shard_map/all_to_all | solution.py:345
  10.5 1.8 %collective-permute-start.1 = (bf16[256,512]{1,0:T(8,128)(2,1)}, bf16[256,512]{1,0:T(8,128)(2,1)S(1)}, u32[]{:S(2)}, u32[]{:S(2)}) collective-permute-start(bf16[256,512]{1,0:T(8,128)(2,1)} %own.1), channel_id=1, source_target_pairs={{0,2},{1,3},{2,0},{3,1},{4,6},{5,7},{6,4},{7,5},{8,10},{9,11},{10,... | collective-permute-start | bytes 786440 | tf_op jit(solution)/shard_map/ppermute | solution.py:21
  12.3 8.9 %all-to-all-done.notes = bf16[32,8,512]{2,1,0:T(8,128)(2,1)S(1)} async-done(((bf16[32,8,512]{2,1,0:T(8,128)(2,1)}), bf16[32,8,512]{2,1,0:T(8,128)(2,1)S(1)}, u32[]{:S(2)}, u32[]{:S(2)}) %all-to-all-start) | async-done | bytes 262176 | tf_op jit(solution)/shard_map/all_to_all | solution.py:345
  21.8 4.7 %gather_fusion = bf16[512,512]{1,0:T(8,128)(2,1)S(1)} fusion(bf16[4096,512]{1,0:T(8,128)(2,1)} %param.16, s32[1024]{0:T(1024)S(1)} %pad_clamp_fusion), kind=kCustom, calls=%fused_computation | custom fusion | bytes 1050624 | tf_op jit(solution)/shard_map/jit(_take)/gather | solution.py:356
  26.7 1.0 %collective-permute-start.8 = (bf16[256,512]{1,0:T(8,128)(2,1)S(1)}, bf16[256,512]{1,0:T(8,128)(2,1)S(1)}, u32[]{:S(2)}, u32[]{:S(2)}) collective-permute-start(bf16[256,512]{1,0:T(8,128)(2,1)S(1)} %slice.98), channel_id=1, source_target_pairs={{0,4},{4,0},{8,12},{12,8},{16,20},{20,16},{24,28},{28,24},{1,5},{5... | collective-permute-start | bytes 786440 | tf_op jit(solution)/shard_map/ppermute | solution.py:21
  28.2 6.7 %collective-permute-done.8 = bf16[256,512]{1,0:T(8,128)(2,1)S(1)} collective-permute-done((bf16[256,512]{1,0:T(8,128)(2,1)S(1)}, bf16[256,512]{1,0:T(8,128)(2,1)S(1)}, u32[]{:S(2)}, u32[]{:S(2)}) %collective-permute-start.8) | collective-permute-done | bytes 262176 | tf_op jit(solution)/shard_map/ppermute | solution.py:21
  38.3 2.2 %copy-done = bf16[2048,1024]{1,0:T(8,128)(2,1)S(1)} copy-done((bf16[2048,1024]{1,0:T(8,128)(2,1)S(1)}, bf16[2048,1024]{1,0:T(8,128)(2,1)}, u32[]{:S(2)}) %copy-start) | copy-done | bytes 4194328
  40.5 0.9 copy-done.6
  45.4 6.3 %shard_map.149 = (f32[256,1024]{1,0:T(8,128)S(1)}, bf16[256,128]{1,0:T(8,128)(2,1)S(1)}, f32[256,128]{1,0:T(8,128)S(1)}, bf16[80,1024]{1,0:T(8,128)(2,1)}, f32[6...) custom-call(s32[3]{0:T(128)S(1)} %copy-done.23, bf16[32,8,512]{2,1,0:T(8,128)(2,1)S(1)} %all-to-all-done.notes, ...), custom_call_target="tpu_custom_call" | custom-call | flops 1342177280 | bytes 7825612 | tf_op jit(solution)/shard_map/pallas_call | solution.py:287
  53.0 1.5 %collective-permute-start.3 = (bf16[80,1024]{1,0:T(8,128)(2,1)}, bf16[80,1024]{1,0:T(8,128)(2,1)S(1)}, u32[]{:S(2)}, u32[]{:S(2)}) collective-permute-start(bf16[80,1024]{1,0:T(8,128)(2,1)} %get-tuple-element.25), channel_id=1, source_target_pairs={{0,4},{4,0},{8,12},{12,8},{16,20},{20,16},{24,28},{28,24},{1,5},{5... | collective-permute-start | bytes 491528 | tf_op jit(solution)/shard_map/ppermute | solution.py:21
  54.5 0.9 slice_add_fusion.5
  57.0 1.6 %collective-permute-done.3.message = bf16[80,1024]{1,0:T(8,128)(2,1)S(1)} collective-permute-done((bf16[80,1024]{1,0:T(8,128)(2,1)}, bf16[80,1024]{1,0:T(8,128)(2,1)S(1)}, u32[]{:S(2)}, u32[]{:S(2)}) %collective-permute-start.3) | collective-permute-done | bytes 163872 | tf_op jit(solution)/shard_map/ppermute | solution.py:21
  59.4 2.1 %collective-permute-start.4 = (bf16[80,1024]{1,0:T(8,128)(2,1)S(1)}, bf16[80,1024]{1,0:T(8,128)(2,1)S(1)}, u32[]{:S(2)}, u32[]{:S(2)}) collective-permute-start(bf16[80,1024]{1,0:T(8,128)(2,1)S(1)} %get-tuple-element.28), channel_id=1, source_target_pairs={{0,8},{4,12},{8,0},{12,4},{16,24},{20,28},{24,16},{28,20},{1,9},{5... | collective-permute-start | bytes 491528 | tf_op jit(solution)/shard_map/ppermute | solution.py:21
  63.6 1.2 %collective-permute-done.4.message = bf16[80,1024]{1,0:T(8,128)(2,1)S(1)} collective-permute-done((bf16[80,1024]{1,0:T(8,128)(2,1)S(1)}, bf16[80,1024]{1,0:T(8,128)(2,1)S(1)}, u32[]{:S(2)}, u32[]{:S(2)}) %collective-permute-start.4) | collective-permute-done | bytes 163872 | tf_op jit(solution)/shard_map/ppermute | solution.py:21
  64.9 1.7 %collective-permute-start.5 = (bf16[80,1024]{1,0:T(8,128)(2,1)S(1)}, bf16[80,1024]{1,0:T(8,128)(2,1)S(1)}, u32[]{:S(2)}, u32[]{:S(2)}) collective-permute-start(bf16[80,1024]{1,0:T(8,128)(2,1)S(1)} %get-tuple-element.33), channel_id=1, source_target_pairs={{0,16},{4,20},{8,24},{12,28},{16,0},{20,4},{24,8},{28,12},{1,17},{... | collective-permute-start | bytes 491528 | tf_op jit(solution)/shard_map/ppermute | solution.py:21
  67.6 5.4 %collective-permute-done.5.message = bf16[80,1024]{1,0:T(8,128)(2,1)S(1)} collective-permute-done((bf16[80,1024]{1,0:T(8,128)(2,1)S(1)}, bf16[80,1024]{1,0:T(8,128)(2,1)S(1)}, u32[]{:S(2)}, u32[]{:S(2)}) %collective-permute-start.5) | collective-permute-done | bytes 163872 | tf_op jit(solution)/shard_map/ppermute | solution.py:21
  73.0 2.2 %copy-done.2 = bf16[1024,2048]{1,0:T(8,128)(2,1)S(1)} copy-done((bf16[1024,2048]{1,0:T(8,128)(2,1)S(1)}, bf16[1024,2048]{1,0:T(8,128)(2,1)}, u32[]{:S(2)}) %copy-start.2) | copy-done | bytes 4194328
  76.7 2.3 %shard_map.152 = (bf16[2,256,512]{2,1,0:T(8,128)(2,1)S(1)}, f32[2,256,512]{2,1,0:T(8,128)S(1)}) custom-call(s32[2]{0:T(128)S(1)} %pad_add_fusion.place, bf16[80,1024]{1,0:T(8,128)(2,1)S(1)} %collective-permute-done.5.message, f32[64,1024]{1,0:T(8,128)S(1)} %get-tuple-element.34.state, f32[8,1024]{1,0:T(8,128)S(1)} %get-tuple-element.35.decay, ...), custom_call_target="tpu_custom_call" | custom-call | flops 1073741824 | bytes 7770120 | tf_op jit(solution)/shard_map/pallas_call | solution.py:287
  79.1 2.4 %shard_map.153 = (f32[64,1024]{1,0:T(8,128)S(1)}, bf16[64,128]{1,0:T(8,128)(2,1)S(1)}, f32[64,128]{1,0:T(8,128)S(1)}) custom-call(s32[3]{0:T(128)S(1)} %pad_add_fusion.2.place, bf16[32,8,512]{2,1,0:T(8,128)(2,1)S(1)} %all-to-all-done.notes, bf16[64,512]{1,0:T(8,128)(2,1)S(1)} %slice_add_fusion.6.own, bf16[64,512]{1,0:T(8,128)(2,1)S(1)} %get-tuple-element.49.over1, ...), custom_call_target="tpu_custom_call" | custom-call | flops 335544320 | bytes 5646540 | tf_op jit(solution)/shard_map/pallas_call | solution.py:287
  81.6 1.7 %shard_map.154 = (bf16[2,64,512]{2,1,0:T(8,128)(2,1)S(1)}, f32[2,64,512]{2,1,0:T(8,128)S(1)}) custom-call(s32[2]{0:T(128)S(1)} %pad_add_fusion.place, bf16[80,1024]{1,0:T(8,128)(2,1)S(1)} %collective-permute-done.5.message, f32[64,1024]{1,0:T(8,128)S(1)} %get-tuple-element.34.state, f32[8,1024]{1,0:T(8,128)S(1)} %get-tuple-element.35.decay, ...), custom_call_target="tpu_custom_call" | custom-call | flops 268435456 | bytes 5656584 | tf_op jit(solution)/shard_map/pallas_call | solution.py:287
  83.8 1.0 %collective-permute-done.13 = bf16[2,64,512]{2,1,0:T(8,128)(2,1)S(1)} collective-permute-done((bf16[2,64,512]{2,1,0:T(8,128)(2,1)S(1)}, bf16[2,64,512]{2,1,0:T(8,128)(2,1)S(1)}, u32[]{:S(2)}, u32[]{:S(2)}) %collective-permute-start.13) | collective-permute-done | bytes 131104 | tf_op jit(solution)/shard_map/ppermute | solution.py:21
  84.9 2.2 %collective-permute-start.14 = (bf16[64,512]{1,0:T(8,128)(2,1)S(1)}, bf16[64,512]{1,0:T(8,128)(2,1)S(1)}, u32[]{:S(2)}, u32[]{:S(2)}) collective-permute-start(bf16[64,512]{1,0:T(8,128)(2,1)S(1)} %fusion.9), channel_id=1, source_target_pairs={{0,2},{1,3},{2,0},{3,1},{4,6},{5,7},{6,4},{7,5},{8,10},{9,11},{10,... | collective-permute-start | bytes 196616 | tf_op jit(solution)/shard_map/ppermute | solution.py:21
  87.4 2.3 %collective-permute-done.14 = bf16[64,512]{1,0:T(8,128)(2,1)S(1)} collective-permute-done((bf16[64,512]{1,0:T(8,128)(2,1)S(1)}, bf16[64,512]{1,0:T(8,128)(2,1)S(1)}, u32[]{:S(2)}, u32[]{:S(2)}) %collective-permute-start.14) | collective-permute-done | bytes 65568 | tf_op jit(solution)/shard_map/ppermute | solution.py:21
  90.4 5.3 %collective-permute-done.7 = bf16[256,512]{1,0:T(8,128)(2,1)S(1)} collective-permute-done((bf16[256,512]{1,0:T(8,128)(2,1)S(1)}, bf16[256,512]{1,0:T(8,128)(2,1)S(1)}, u32[]{:S(2)}, u32[]{:S(2)}) %collective-permute-start.7) | collective-permute-done | bytes 262176 | tf_op jit(solution)/shard_map/ppermute | solution.py:21
  (125 shorter events, 21.9 us)
Async XLA Ops:
  0.6 27.1 %copy-start.4 = (bf16[256,512]{1,0:T(8,128)(2,1)S(1)}, bf16[256,512]{1,0:T(8,128)(2,1)}, u32[]{:S(2)}) copy-start(bf16[256,512]{1,0:T(8,128)(2,1)} %own.1) | copy-start | bytes 786436
  3.2 33.1 %copy-start.29 = (f32[4,1,2,64]{3,2,1,0:T(2,128)S(1)}, f32[4,1,2,64]{3,2,1,0:T(2,128)}, u32[]{:S(2)}) copy-start(f32[4,1,2,64]{3,2,1,0:T(2,128)} %param.24) | copy-start | bytes 6148
  3.2 33.8 %copy-start.27 = (bf16[2048,1,2,64]{0,3,2,1:T(8,128)(2,1)S(1)}, bf16[2048,1,2,64]{0,3,2,1:T(8,128)(2,1)}, u32[]{:S(2)}) copy-start(bf16[2048,1,2,64]{0,3,2,1:T(8,128)(2,1)} %param.19) | copy-start | bytes 1572868
  3.2 18.0 %all-to-all-start = ((bf16[32,8,512]{2,1,0:T(8,128)(2,1)}), bf16[32,8,512]{2,1,0:T(8,128)(2,1)S(1)}, u32[]{:S(2)}, u32[]{:S(2)}) async-start(bf16[32,8,512]{2,1,0:T(8,128)(2,1)} %broadcast_in_dim.29), calls=%async_computation | async-start | bytes 524288 | tf_op jit(solution)/shard_map/all_to_all | solution.py:345
  10.5 17.2 %collective-permute-start.1 = (bf16[256,512]{1,0:T(8,128)(2,1)}, bf16[256,512]{1,0:T(8,128)(2,1)S(1)}, u32[]{:S(2)}, u32[]{:S(2)}) collective-permute-start(bf16[256,512]{1,0:T(8,128)(2,1)} %own.1), channel_id=1, source_target_pairs={{0,2},{1,3},{2,0},{3,1},{4,6},{5,7},{6,4},{7,5},{8,10},{9,11},{10,... | collective-permute-start | bytes 786440 | tf_op jit(solution)/shard_map/ppermute | solution.py:21
  26.7 8.2 %collective-permute-start.8 = (bf16[256,512]{1,0:T(8,128)(2,1)S(1)}, bf16[256,512]{1,0:T(8,128)(2,1)S(1)}, u32[]{:S(2)}, u32[]{:S(2)}) collective-permute-start(bf16[256,512]{1,0:T(8,128)(2,1)S(1)} %slice.98), channel_id=1, source_target_pairs={{0,4},{4,0},{8,12},{12,8},{16,20},{20,16},{24,28},{28,24},{1,5},{5... | collective-permute-start | bytes 786440 | tf_op jit(solution)/shard_map/ppermute | solution.py:21
  27.7 9.9 %collective-permute-start = (bf16[256,512]{1,0:T(8,128)(2,1)S(1)}, bf16[256,512]{1,0:T(8,128)(2,1)S(1)}, u32[]{:S(2)}, u32[]{:S(2)}) collective-permute-start(bf16[256,512]{1,0:T(8,128)(2,1)S(1)} %copy-done.4), channel_id=1, source_target_pairs={{0,1},{1,0},{2,3},{3,2},{4,5},{5,4},{6,7},{7,6},{8,9},{9,8},{10,11... | collective-permute-start | bytes 786440 | tf_op jit(solution)/shard_map/ppermute | solution.py:21
  27.7 9.9 %collective-permute-start.2 = (bf16[256,512]{1,0:T(8,128)(2,1)S(1)}, bf16[256,512]{1,0:T(8,128)(2,1)S(1)}, u32[]{:S(2)}, u32[]{:S(2)}) collective-permute-start(bf16[256,512]{1,0:T(8,128)(2,1)S(1)} %collective-permute-done.1.over2), channel_id=1, source_target_pairs={{0,1},{1,0},{2,3},{3,2},{4,5},{5,4},{6,7},{7,6},{8,9},{9,8},{10,11... | collective-permute-start | bytes 786440 | tf_op jit(solution)/shard_map/ppermute | solution.py:21
  35.7 18.8 %collective-permute-start.9 = (bf16[128,512]{1,0:T(8,128)(2,1)}, bf16[128,512]{1,0:T(8,128)(2,1)}, u32[]{:S(2)}, u32[]{:S(2)}) collective-permute-start(bf16[128,512]{1,0:T(8,128)(2,1)} %slice.100), channel_id=1, source_target_pairs={{0,8},{4,12},{8,0},{12,4},{16,24},{20,28},{24,16},{28,20},{1,9},{5... | collective-permute-start | bytes 393224 | tf_op jit(solution)/shard_map/ppermute | solution.py:21
  53.0 5.5 %collective-permute-start.3 = (bf16[80,1024]{1,0:T(8,128)(2,1)}, bf16[80,1024]{1,0:T(8,128)(2,1)S(1)}, u32[]{:S(2)}, u32[]{:S(2)}) collective-permute-start(bf16[80,1024]{1,0:T(8,128)(2,1)} %get-tuple-element.25), channel_id=1, source_target_pairs={{0,4},{4,0},{8,12},{12,8},{16,20},{20,16},{24,28},{28,24},{1,5},{5... | collective-permute-start | bytes 491528 | tf_op jit(solution)/shard_map/ppermute | solution.py:21
  55.4 23.7 %copy-start.22 = (f32[16]{0:T(128)S(1)}, f32[16]{0:T(128)}, u32[]{:S(2)}) copy-start(f32[16]{0:T(128)} %param.25) | copy-start | bytes 196
  56.1 6.2 %collective-permute-start.10 = (bf16[64,512]{1,0:T(8,128)(2,1)}, bf16[64,512]{1,0:T(8,128)(2,1)S(1)}, u32[]{:S(2)}, u32[]{:S(2)}) collective-permute-start(bf16[64,512]{1,0:T(8,128)(2,1)} %slice.102), channel_id=1, source_target_pairs={{0,16},{4,20},{8,24},{12,28},{16,0},{20,4},{24,8},{28,12},{1,17},{... | collective-permute-start | bytes 196616 | tf_op jit(solution)/shard_map/ppermute | solution.py:21
  57.0 22.1 %copy-start.15 = (f32[4,128]{1,0:T(4,128)S(1)}, f32[4,128]{1,0:T(4,128)}, u32[]{:S(2)}) copy-start(f32[4,128]{1,0:T(4,128)} %reshape.171.conv_bc) | copy-start | bytes 6148
  57.0 22.1 %copy-start.13 = (f32[2048]{0:T(1024)S(1)}, f32[2048]{0:T(1024)}, u32[]{:S(2)}) copy-start(f32[2048]{0:T(1024)} %param.17) | copy-start | bytes 24580
  58.5 20.6 %copy-start.18 = (f32[16]{0:T(128)S(1)}, f32[16]{0:T(128)}, u32[]{:S(2)}) copy-start(f32[16]{0:T(128)} %param.21) | copy-start | bytes 196
  58.5 20.6 %copy-start.20 = (f32[16]{0:T(128)S(1)}, f32[16]{0:T(128)}, u32[]{:S(2)}) copy-start(f32[16]{0:T(128)} %param.22) | copy-start | bytes 196
  59.4 5.4 %collective-permute-start.4 = (bf16[80,1024]{1,0:T(8,128)(2,1)S(1)}, bf16[80,1024]{1,0:T(8,128)(2,1)S(1)}, u32[]{:S(2)}, u32[]{:S(2)}) collective-permute-start(bf16[80,1024]{1,0:T(8,128)(2,1)S(1)} %get-tuple-element.28), channel_id=1, source_target_pairs={{0,8},{4,12},{8,0},{12,4},{16,24},{20,28},{24,16},{28,20},{1,9},{5... | collective-permute-start | bytes 491528 | tf_op jit(solution)/shard_map/ppermute | solution.py:21
  63.1 4.3 %collective-permute-start.11 = (bf16[64,512]{1,0:T(8,128)(2,1)S(1)}, bf16[64,512]{1,0:T(8,128)(2,1)S(1)}, u32[]{:S(2)}, u32[]{:S(2)}) collective-permute-start(bf16[64,512]{1,0:T(8,128)(2,1)S(1)} %slice_add_fusion.6.own), channel_id=1, source_target_pairs={{0,2},{1,3},{2,0},{3,1},{4,6},{5,7},{6,4},{7,5},{8,10},{9,11},{10,... | collective-permute-start | bytes 196616 | tf_op jit(solution)/shard_map/ppermute | solution.py:21
  64.9 8.0 %collective-permute-start.5 = (bf16[80,1024]{1,0:T(8,128)(2,1)S(1)}, bf16[80,1024]{1,0:T(8,128)(2,1)S(1)}, u32[]{:S(2)}, u32[]{:S(2)}) collective-permute-start(bf16[80,1024]{1,0:T(8,128)(2,1)S(1)} %get-tuple-element.33), channel_id=1, source_target_pairs={{0,16},{4,20},{8,24},{12,28},{16,0},{20,4},{24,8},{28,12},{1,17},{... | collective-permute-start | bytes 491528 | tf_op jit(solution)/shard_map/ppermute | solution.py:21
  67.4 11.6 %collective-permute-start.12 = (bf16[128,512]{1,0:T(8,128)(2,1)S(1)}, bf16[128,512]{1,0:T(8,128)(2,1)S(1)}, u32[]{:S(2)}, u32[]{:S(2)}) collective-permute-start(bf16[128,512]{1,0:T(8,128)(2,1)S(1)} %pad_maximum_fusion), channel_id=1, source_target_pairs={{0,1},{1,0},{2,3},{3,2},{4,5},{5,4},{6,7},{7,6},{8,9},{9,8},{10,11... | collective-permute-start | bytes 393224 | tf_op jit(solution)/shard_map/ppermute | solution.py:21
  79.0 8.1 %collective-permute-start.6 = (bf16[2,256,512]{2,1,0:T(8,128)(2,1)S(1)}, bf16[2,256,512]{2,1,0:T(8,128)(2,1)S(1)}, u32[]{:S(2)}, u32[]{:S(2)}) collective-permute-start(bf16[2,256,512]{2,1,0:T(8,128)(2,1)S(1)} %get-tuple-element.42), channel_id=1, source_target_pairs={{0,1},{1,0},{2,3},{3,2},{4,5},{5,4},{6,7},{7,6},{8,9},{9,8},{10,11... | collective-permute-start | bytes 1572872 | tf_op jit(solution)/shard_map/ppermute | solution.py:21
  83.3 1.5 %collective-permute-start.13 = (bf16[2,64,512]{2,1,0:T(8,128)(2,1)S(1)}, bf16[2,64,512]{2,1,0:T(8,128)(2,1)S(1)}, u32[]{:S(2)}, u32[]{:S(2)}) collective-permute-start(bf16[2,64,512]{2,1,0:T(8,128)(2,1)S(1)} %get-tuple-element.47), channel_id=1, source_target_pairs={{0,1},{1,0},{2,3},{3,2},{4,5},{5,4},{6,7},{7,6},{8,9},{9,8},{10,11... | collective-permute-start | bytes 393224 | tf_op jit(solution)/shard_map/ppermute | solution.py:21
  84.9 4.8 %collective-permute-start.14 = (bf16[64,512]{1,0:T(8,128)(2,1)S(1)}, bf16[64,512]{1,0:T(8,128)(2,1)S(1)}, u32[]{:S(2)}, u32[]{:S(2)}) collective-permute-start(bf16[64,512]{1,0:T(8,128)(2,1)S(1)} %fusion.9), channel_id=1, source_target_pairs={{0,2},{1,3},{2,0},{3,1},{4,6},{5,7},{6,4},{7,5},{8,10},{9,11},{10,... | collective-permute-start | bytes 196616 | tf_op jit(solution)/shard_map/ppermute | solution.py:21
  87.3 8.3 %collective-permute-start.7 = (bf16[256,512]{1,0:T(8,128)(2,1)S(1)}, bf16[256,512]{1,0:T(8,128)(2,1)S(1)}, u32[]{:S(2)}, u32[]{:S(2)}) collective-permute-start(bf16[256,512]{1,0:T(8,128)(2,1)S(1)} %fusion.4), channel_id=1, source_target_pairs={{0,2},{1,3},{2,0},{3,1},{4,6},{5,7},{6,4},{7,5},{8,10},{9,11},{10,... | collective-permute-start | bytes 786440 | tf_op jit(solution)/shard_map/ppermute | solution.py:21
  (22 other events, 82.3 us)

commit v3 on v2

v3 whole, which is shorter than its diff:
```python
import functools

import jax
import jax.numpy as jnp
from jax import lax
from jax.experimental import pallas as pl
from jax.experimental.pallas import tpu as pltpu
from jax.sharding import PartitionSpec as P

EPS = 1e-05
BF16 = jnp.bfloat16
F32 = jnp.float32
LANES = 128
PARTS = 4
EDGE = 8
MEBI = 1024 * 1024


def swapped(value, axis, bit):
    count = lax.axis_size(axis)
    return lax.ppermute(value, axis, [(i, i ^ bit) for i in range(count)])


def bits_of(axis):
    count = lax.axis_size(axis)
    assert count & (count - 1) == 0
    return [1 << k for k in range(count.bit_length() - 1)]


def dot(a, b):
    return jnp.dot(a, b, preferred_element_type=F32)


def across(a, b, axis):
    return lax.dot_general(a, b, (((axis,), (axis,)), ((), ())), preferred_element_type=F32)


def halves(value):
    high = value.astype(BF16)
    low = (value - high.astype(F32)).astype(BF16)
    return high, low


def iota(shape, axis):
    return lax.broadcasted_iota(jnp.int32, shape, axis)


def spreader(width, channels):
    head = iota((2 * LANES, channels), 0) & (LANES - 1)
    return jnp.where(head == iota((2 * LANES, channels), 1) // width, 1.0, 0.0).astype(BF16)


def widened(per_head, spread):
    high, low = halves(per_head)
    return dot(jnp.concatenate([high, low], axis=1), spread)


def padded(row):
    return jnp.concatenate([row, jnp.zeros((row.shape[0], LANES - row.shape[1]), F32)], axis=1)


def silu(value):
    return value / (1.0 + jnp.exp(-value))


def started(pairs, sems, first=0):
    copies = [
        pltpu.make_async_copy(source, target, sems.at[first + at])
        for at, (source, target) in enumerate(pairs)
    ]
    for copy in copies:
        copy.start()
    return copies


def front_kernel(
    decode,
    rows,
    heads,
    place,
    edge0,
    edge1,
    edge2,
    edge3,
    own_in,
    over1,
    over2,
    over3,
    gain_in,
    x_weight_in,
    bc_weight_in,
    dt_weight_in,
    dt_bias_in,
    decay_log_in,
    conv_x_in,
    conv_bc_in,
    skip_gain_in,
    y_out,
    bc_out,
    reach_out,
    *rest,
):
    if not decode:
        message_out, state_out, own = rest[:3]
        rest = rest[3:]
    (
        normed,
        x_conv,
        joined,
        gain,
        x_weight,
        bc_weight,
        dt_weight,
        dt_bias,
        decay_log,
        conv_x,
        conv_bc,
        skip_gain,
        sems,
    ) = rest
    tokens, part = over1.shape
    chunks, _, step_lanes = x_weight.shape
    channels = chunks * step_lanes
    width = channels // heads
    state_width = bc_weight.shape[0] // 2
    taps = conv_x.shape[0]
    margin = taps - 1
    me, edge_on = place[0], place[1]
    if decode:
        own = own_in
        early = []
    else:
        early = started([(own_in, own)], sems)
    early += started([(gain_in, gain)], sems, 1)
    chunk_copies = started(
        [(x_weight_in.at[:, pl.ds(c * step_lanes, step_lanes)], x_weight.at[c]) for c in range(chunks)],
        sems,
        2,
    )
    late = started(
        [
            (conv_x_in, conv_x),
            (bc_weight_in, bc_weight),
            (dt_weight_in, dt_weight),
            (dt_bias_in, dt_bias),
            (decay_log_in, decay_log),
            (conv_bc_in, conv_bc),
            (skip_gain_in, skip_gain),
        ],
        sems,
        2 + chunks,
    )
    for copy in early:
        copy.wait()

    blocks = [ref[...].astype(F32) for ref in (own, over1, over2, over3)]
    square = sum(jnp.sum(b * b, axis=1, keepdims=True) for b in blocks)
    factor = lax.rsqrt(square / (PARTS * part) + EPS)
    for r in range(PARTS):
        normed[me ^ r, :tokens, :] = (blocks[r] * factor * gain[me ^ r]).astype(BF16)
    valid = jnp.logical_and(iota((EDGE, part), 0) >= EDGE - margin, edge_on > 0)
    at = EDGE if decode else 0
    edges = [
        jnp.where(valid, ref[...].astype(F32)[at : at + EDGE], 0.0)
        for ref in (edge0, edge1, edge2, edge3)
    ]
    square = sum(jnp.sum(e * e, axis=1, keepdims=True) for e in edges)
    factor = lax.rsqrt(square / (PARTS * part) + EPS)
    for r in range(PARTS):
        edge = edges[r] * factor * gain[me ^ r]
        normed[me ^ r, tokens:, :] = jnp.concatenate([edge, jnp.zeros_like(edge)], axis=0).astype(BF16)

    def projected(weight_of):
        return sum(dot(normed[j], weight_of(j)) for j in range(PARTS))

    def convolved(raw, taps_of):
        raw = raw.astype(BF16).astype(F32)
        lanes = raw.shape[1]
        edge = raw[tokens : tokens + EDGE]
        if decode:
            for m in range(margin):
                one = edge[EDGE - margin + m : EDGE - margin + m + 1]
                joined[m * rows : (m + 1) * rows, :lanes] = jnp.broadcast_to(one, (rows, lanes))
            joined[margin * rows : margin * rows + tokens, :lanes] = raw[:tokens]
            starts = [k * rows for k in range(taps)]
        else:
            joined[:EDGE, :lanes] = edge
            joined[EDGE : EDGE + tokens, :lanes] = raw[:tokens]
            starts = [EDGE - margin + k for k in range(taps)]
        total = sum(taps_of(k) * joined[s : s + tokens, :lanes] for k, s in enumerate(starts))
        return silu(total)

    late[0].wait()
    for c in range(chunks):
        chunk_copies[c].wait()
        lane = c * step_lanes
        raw = projected(lambda j: x_weight[c, j * part : (j + 1) * part, :])
        x_conv[:, lane : lane + step_lanes] = convolved(
            raw, lambda k: conv_x[k : k + 1, lane : lane + step_lanes]
        ).astype(BF16)

    for copy in late[1:]:
        copy.wait()
    fill = jnp.zeros((LANES - heads, PARTS * part), BF16)
    side = jnp.concatenate([bc_weight[...], dt_weight[...], fill], axis=0)
    raw = sum(across(normed[j], side[:, j * part : (j + 1) * part], 1) for j in range(PARTS))
    bc_taps = jnp.concatenate([conv_bc[:, 0, :], conv_bc[:, 1, :]], axis=1)
    bc_conv = convolved(raw[:, : 2 * state_width], lambda k: bc_taps[k : k + 1])
    bc_out[...] = bc_conv.astype(BF16)
    pre = raw[:tokens, 2 * state_width :] + padded(dt_bias[...])
    step_size = jnp.maximum(pre, 0.0) + jnp.log1p(jnp.exp(-jnp.abs(pre)))
    b_rows = bc_conv[:, :state_width].astype(BF16)
    c_rows = bc_conv[:, state_width:].astype(BF16)

    t_at = iota((tokens, tokens), 0)
    s_at = iota((tokens, tokens), 1)
    mask = t_at >= s_at
    if decode:
        mask = jnp.logical_and(mask, t_at % rows == s_at % rows)
    logs = step_size * -jnp.exp(padded(decay_log[...]))
    high, low = halves(logs)
    lowest = (logs - high.astype(F32) - low.astype(F32)).astype(BF16)
    sums = dot(
        jnp.where(mask, 1.0, 0.0).astype(BF16), jnp.concatenate([high, low, lowest], axis=1)
    )
    cum_log = sums[:, :LANES] + sums[:, LANES : 2 * LANES] + sums[:, 2 * LANES :]
    reach_out[...] = jnp.exp(cum_log)
    cum_across = cum_log.T
    step_across = step_size.T
    scores = across(c_rows, b_rows, 1)
    spread = spreader(width, channels)
    skip_row = widened(jnp.broadcast_to(padded(skip_gain[...]), (EDGE, LANES)), spread)[:1]

    per_tile = LANES // width
    lane_head = iota((tokens, LANES), 1) // width
    for tile in range(channels // LANES):
        lanes = slice(tile * LANES, (tile + 1) * LANES)
        x_tile = x_conv[:, lanes].astype(F32)
        left, right = [], []
        for k in range(per_tile):
            h = tile * per_tile + k
            gaps = cum_log[:, h : h + 1] - cum_across[h : h + 1, :]
            decays = jnp.exp(jnp.where(mask, gaps, -1e30))
            left.append((scores * decays * step_across[h : h + 1, :]).astype(BF16))
            right.append(jnp.where(lane_head == k, x_tile, 0.0).astype(BF16))
        within = sum(dot(a, b) for a, b in zip(left, right))
        y_out[:, lanes] = within + skip_row[:, lanes] * x_tile

    if not decode:
        last = cum_log[tokens - 1 : tokens]
        to_end = jnp.exp(last - cum_log) * step_size
        b_turned = bc_conv.T[:state_width].astype(BF16)
        decay = widened(jnp.broadcast_to(jnp.exp(last), (EDGE, LANES)), spread)
        state_out[state_width:, :] = decay
        high, low = halves(decay[:1])
        at = iota((2 * EDGE, channels), 0)
        message_out[state_width:, :] = jnp.where(
            at == 0, high.astype(F32), jnp.where(at == 1, low.astype(F32), 0.0)
        ).astype(BF16)
        for lane in range(0, channels, step_lanes):
            lanes = slice(lane, lane + step_lanes)
            scale = widened(to_end, spread[:, lanes])
            weighted = (x_conv[:, lanes].astype(F32) * scale).astype(BF16)
            state = dot(b_turned, weighted)
            state_out[:state_width, lanes] = state
            message_out[:state_width, lanes] = state.astype(BF16)


def unpacked(message, state_width):
    other = message[:state_width, :].astype(F32)
    tail = message[state_width:, :].astype(F32)
    return other, tail[0:1] + tail[1:2]


def step_kernel(first, place, message, state, came, message_out, state_out, came_out):
    later = place[0] > 0
    state_width = state.shape[0] - EDGE
    channels = state.shape[1]
    other, other_decay = unpacked(message, state_width)
    mine, my_decay = state[:state_width, :], state[state_width : state_width + 1, :]
    if first:
        before, passed = jnp.zeros_like(mine), jnp.ones_like(my_decay)
    else:
        before, passed = came[:state_width, :], came[state_width : state_width + 1, :]
    came_out[:state_width, :] = jnp.where(later, passed * other + before, before)
    passed = jnp.where(later, passed * other_decay, passed)
    came_out[state_width:, :] = jnp.broadcast_to(passed, (EDGE, channels))
    total = jnp.where(later, my_decay * other + mine, other_decay * mine + other)
    decayed = my_decay * other_decay
    state_out[:state_width, :] = total
    state_out[state_width:, :] = jnp.broadcast_to(decayed, (EDGE, channels))
    message_out[:state_width, :] = total.astype(BF16)
    high, low = halves(decayed)
    at = iota((2 * EDGE, channels), 0)
    message_out[state_width:, :] = jnp.where(
        at == 0, high.astype(F32), jnp.where(at == 1, low.astype(F32), 0.0)
    ).astype(BF16)


def back_kernel(
    decode,
    heads,
    place,
    message,
    held,
    y,
    bc,
    reach,
    gain_in,
    weight_in,
    sent3,
    sent1,
    kept2,
    kept0,
    full,
    mixed,
    gain,
    weight,
    sems,
):
    me, later = place[0], place[1] > 0
    state_width = held.shape[0] - EDGE
    tokens, channels = y.shape
    part = weight.shape[2]
    order = (3, 1, 2, 0)
    copies = started(
        [(gain_in, gain)]
        + [
            (weight_in.at[:, pl.ds(pl.multiple_of((me ^ r) * part, part), part)], weight.at[at])
            for at, r in enumerate(order)
        ],
        sems,
    )
    other, other_decay = unpacked(message, state_width)
    mine, my_decay = held[:state_width, :], held[state_width : state_width + 1, :]
    if decode:
        incoming = jnp.where(later, my_decay * other + mine, other_decay * mine + other)
    else:
        incoming = jnp.where(later, my_decay * other + mine, mine)
    high, low = halves(incoming)
    blank = jnp.zeros_like(high)
    table = jnp.concatenate([blank, high, blank, low], axis=0)
    twice = jnp.concatenate([bc[...], bc[...]], axis=1)
    spread = spreader(channels // heads, channels)
    step_lanes = 2 * LANES
    square = jnp.zeros((tokens, 1), F32)
    for lane in range(0, channels, step_lanes):
        lanes = slice(lane, lane + step_lanes)
        total = y[:, lanes] + dot(twice, table[:, lanes]) * widened(reach[...], spread[:, lanes])
        full[:, lanes] = total
        square = square + jnp.sum(total * total, axis=1, keepdims=True)
    factor = lax.rsqrt(square / channels + EPS)
    copies[0].wait()
    mixed[...] = (full[...] * factor * gain[...]).astype(BF16)
    for at, out in enumerate((sent3, sent1, kept2, kept0)):
        copies[1 + at].wait()
        out[...] = dot(mixed[...], weight[at]).astype(out.dtype)


def far_kernel(place, kept, got, out):
    out[...] = (kept[...] + got[...].astype(F32)).astype(BF16)


def total_kernel(place, kept, got, far, out):
    out[...] = (kept[...] + got[...].astype(F32) + far[...].astype(F32)).astype(BF16)


def note_kernel(margin, place, ids_in, embeds_in, note, ids, embeds, sems):
    steps = ids_in.shape[0]
    for copy in started(
        [(ids_in, ids), (embeds_in.at[pl.ds(embeds_in.shape[0] - 2 * EDGE, 2 * EDGE), :], embeds)], sems
    ):
        copy.wait()
    ids = ids[...]
    part = embeds.shape[1]
    digits = [padded(d.astype(F32)) for d in (ids & 255, (ids >> 8) & 255, ids >> 16)]
    blank = jnp.zeros((steps, part - 3 * LANES), F32)
    top = jnp.concatenate(digits + [blank], axis=1)
    middle = jnp.zeros((EDGE - margin - steps, part), F32)
    last = embeds[...].astype(F32)[2 * EDGE - margin :]
    note[...] = jnp.concatenate([top, middle, last], axis=0).astype(BF16)


def join_kernel(place, mine, got, out):
    out[...] = jnp.concatenate([mine[...].astype(F32), got[...].astype(F32)], axis=0).astype(BF16)


def last_join_kernel(place, mine, got, out, picked, held):
    count = mine.shape[0]
    held[:count, :] = mine[...].astype(F32)
    held[count:, :] = got[...].astype(F32)
    out[...] = held[...].astype(BF16)
    edges = [held[pl.ds(pl.multiple_of(place[k] * EDGE, EDGE), EDGE), :] for k in range(2)]
    picked[...] = jnp.concatenate(edges, axis=0).astype(BF16)


def lookup_kernel(steps, rows, place, notes, table_in, kept_out, sent_out, table, wanted, found, sems):
    chunks, chunk, _ = table.shape
    copies = started(
        [(table_in.at[pl.ds(c * chunk, chunk), :], table.at[c]) for c in range(chunks)], sems
    )
    first = (place[0] * (chunks * chunk)).astype(F32)
    held = notes[...].astype(F32)
    groups = held.shape[0] // EDGE
    digits = held[:, :LANES] + held[:, LANES : 2 * LANES] * 256.0 + held[:, 2 * LANES : 3 * LANES] * 65536.0
    same = iota((rows, LANES), 0) == iota((rows, LANES), 1)
    for q in range(groups):
        for s in range(steps):
            line = jnp.broadcast_to(digits[q * EDGE + s : q * EDGE + s + 1], (rows, LANES))
            column = jnp.sum(jnp.where(same, line, 0.0), axis=1, keepdims=True) - first
            at = (q * steps + s) * rows
            wanted[at : at + rows, :] = jnp.broadcast_to(column, (rows, LANES))
    asked = groups * steps * rows
    block = min(asked, 256)
    lane = iota((block, LANES), 1).astype(F32)
    for c in range(chunks):
        copies[c].wait()
        for at in range(0, asked, block):
            gap = wanted[at : at + block, :] - lane
            hot = [
                jnp.where(gap == float(c * chunk + k), 1.0, 0.0).astype(BF16)
                for k in range(0, chunk, LANES)
            ]
            term = dot(jnp.concatenate(hot, axis=1), table[c])
            if c == 0:
                found[at : at + block, :] = term
            else:
                found[at : at + block, :] += term
    kept_out[...] = found[: asked // 2, :].astype(BF16)
    sent_out[...] = found[asked // 2 :, :].astype(BF16)


def fold_kernel(place, kept, got, kept_out, *sent_out):
    total = (kept[...].astype(F32) + got[...].astype(F32)).astype(BF16)
    if sent_out:
        half = kept_out.shape[0]
        kept_out[...] = total[:half]
        sent_out[0][...] = total[half:]
    else:
        kept_out[...] = total


VMEM = pl.BlockSpec(memory_space=pltpu.VMEM)
SMEM = pl.BlockSpec(memory_space=pltpu.SMEM)
ANY = pl.BlockSpec(memory_space=pl.ANY)


def called(kernel, place, inputs, outs, scratch=(), flops=1000, limit=4, far=()):
    moved = sum(v.size * v.dtype.itemsize for v in inputs)
    moved += sum(o.size * o.dtype.itemsize for o in outs)
    return pl.pallas_call(
        kernel,
        out_shape=outs,
        in_specs=[SMEM] + [ANY if at in far else VMEM for at in range(len(inputs))],
        out_specs=[VMEM] * len(outs),
        scratch_shapes=list(scratch),
        compiler_params=pltpu.CompilerParams(vmem_limit_bytes=limit * MEBI),
        cost_estimate=pl.CostEstimate(flops=flops, bytes_accessed=moved, transcendentals=0),
    )(place, *inputs)


def shaped(shape, dtype):
    return jax.ShapeDtypeStruct(shape, dtype)


def on_device(
    prompt_embeds,
    decode_ids,
    embed_table,
    norm_gain,
    x_weight,
    bc_weight,
    dt_weight,
    dt_bias,
    decay_log,
    conv_x,
    conv_bc,
    skip_gain,
    out_gain,
    out_weight,
):
    heads = dt_weight.shape[1]
    assert bc_weight.shape[1] == 1 and lax.axis_size("tp") == PARTS
    channels = x_weight.shape[1]
    taps = conv_x.shape[0]
    margin = taps - 1
    turned_bc = bc_weight.transpose(1, 2, 3, 0).reshape(-1, bc_weight.shape[0])
    turned_dt = dt_weight.T
    state_width = turned_bc.shape[0] // 2
    assert turned_bc.shape[0] == LANES
    tokens, part = prompt_embeds.shape
    rows, steps = decode_ids.shape
    assert steps + margin <= EDGE and rows <= LANES and part >= 3 * LANES
    asked = rows * steps
    groups = lax.axis_size("ctx")
    me_c = lax.axis_index("ctx").astype(jnp.int32)
    me_t = lax.axis_index("tp").astype(jnp.int32)
    vocab_here = embed_table.shape[0]
    bits = bits_of("ctx")
    assert len(bits) >= 2
    none = jnp.zeros((1,), jnp.int32)

    e2 = swapped(prompt_embeds, "tp", 2)
    e1 = swapped(prompt_embeds, "tp", 1)

    (notes,) = called(
        functools.partial(note_kernel, margin),
        none,
        [decode_ids.T, prompt_embeds],
        [shaped((EDGE, part), BF16)],
        [
            pltpu.VMEM((steps, rows), jnp.int32),
            pltpu.VMEM((2 * EDGE, part), BF16),
            pltpu.SemaphoreType.DMA((2,)),
        ],
        far=(0, 1),
    )

    def position(other):
        apart = me_c ^ other
        return sum(((apart >> k) & 1) << (len(bits) - 1 - k) for k in range(len(bits)))

    for bit in reversed(bits):
        got = swapped(notes, "ctx", bit)
        size = 2 * notes.shape[0]
        if bit > 1:
            (notes,) = called(join_kernel, none, [notes, got], [shaped((size, part), BF16)])
        else:
            notes, edge0 = called(
                last_join_kernel,
                jnp.stack([position(jnp.maximum(me_c - 1, 0)), position(groups - 1)]),
                [notes, got],
                [shaped((size, part), BF16), shaped((2 * EDGE, part), BF16)],
                [pltpu.VMEM((size, part), F32)],
            )
    edge2 = swapped(edge0, "tp", 2)
    edge1 = swapped(edge0, "tp", 1)
    e3 = swapped(e2, "tp", 1)
    edge3 = swapped(edge2, "tp", 1)
    edges = [edge0, edge1, edge2, edge3]

    half = groups * asked // 2
    chunk = min(vocab_here, 1024)
    assert vocab_here % chunk == 0
    kept, sent = called(
        functools.partial(lookup_kernel, steps, rows),
        me_c.reshape(1),
        [notes, embed_table],
        [shaped((half, part), BF16), shaped((half, part), BF16)],
        [
            pltpu.VMEM((vocab_here // chunk, chunk, part), BF16),
            pltpu.VMEM((2 * half, LANES), F32),
            pltpu.VMEM((2 * half, part), F32),
            pltpu.SemaphoreType.DMA((vocab_here // chunk,)),
        ],
        flops=4 * half * vocab_here * part,
        limit=40 if half > 512 else 16,
        far=(1,),
    )
    for bit in bits:
        got = swapped(sent, "ctx", bit)
        half = half // 2
        if bit == bits[-1]:
            (kept,) = called(fold_kernel, none, [kept, got], [shaped((asked, part), BF16)])
        else:
            kept, sent = called(
                fold_kernel,
                none,
                [kept, got],
                [shaped((half, part), BF16), shaped((half, part), BF16)],
                limit=16 if half > 512 else 4,
            )
    near = swapped(kept, "tp", 2)
    over1 = swapped(kept, "tp", 1)
    over3 = swapped(near, "tp", 1)

    weights = [
        norm_gain.reshape(PARTS, 1, part),
        x_weight,
        turned_bc,
        turned_dt,
        dt_bias.reshape(1, -1),
        decay_log.reshape(1, -1),
        conv_x,
        conv_bc.reshape(taps, 2, -1),
        skip_gain.reshape(1, -1),
    ]
    packed = state_width + 2 * EDGE
    step_lanes = 2 * LANES
    chunks = channels // step_lanes

    def front(decode, place, blocks, count):
        outs = [
            shaped((count, channels), F32),
            shaped((count, LANES), BF16),
            shaped((count, LANES), F32),
        ]
        scratch = []
        if not decode:
            outs += [
                shaped((packed, channels), BF16),
                shaped((state_width + EDGE, channels), F32),
            ]
            scratch = [pltpu.VMEM((count, part), BF16)]
        joined = margin * rows if decode else EDGE
        scratch += [
            pltpu.VMEM((PARTS, count + 2 * EDGE, part), BF16),
            pltpu.VMEM((count, channels), BF16),
            pltpu.VMEM((joined + count, step_lanes), F32),
            pltpu.VMEM((PARTS, 1, part), F32),
            pltpu.VMEM((chunks, PARTS * part, step_lanes), BF16),
        ]
        scratch += [pltpu.VMEM(w.shape, w.dtype) for w in weights[2:]]
        scratch += [pltpu.SemaphoreType.DMA((chunks + 9,))]
        return called(
            functools.partial(front_kernel, decode, rows, heads),
            place,
            edges + blocks + weights,
            outs,
            scratch,
            2 * count * PARTS * part * (channels + 2 * LANES),
            24,
            tuple(range(8, 8 + len(weights))) + (() if decode else (4,)),
        )

    y, bc, reach, message, state = front(
        False,
        jnp.stack([me_t, (me_c > 0).astype(jnp.int32)]),
        [prompt_embeds, e1, e2, e3],
        tokens,
    )

    came = state
    for bit in bits[:-1]:
        got = swapped(message, "ctx", bit)
        later = ((me_c & bit) != 0).astype(jnp.int32).reshape(1)
        message, state, came = called(
            functools.partial(step_kernel, bit == bits[0]),
            later,
            [got, state, came],
            [
                shaped((packed, channels), BF16),
                shaped((state_width + EDGE, channels), F32),
                shaped((state_width + EDGE, channels), F32),
            ],
            flops=8 * state_width * channels,
        )
    got = swapped(message, "ctx", bits[-1])
    later = ((me_c & bits[-1]) != 0).astype(jnp.int32)
    back_place = jnp.stack([me_t, later])

    def back(decode, held, y, bc, reach):
        count = y.shape[0]
        sent3, sent1, kept2, kept0 = called(
            functools.partial(back_kernel, decode, heads),
            back_place,
            [got, held, y, bc, reach, out_gain.reshape(1, -1), out_weight],
            [shaped((count, part), BF16)] * 2 + [shaped((count, part), F32)] * 2,
            [
                pltpu.VMEM((count, channels), F32),
                pltpu.VMEM((count, channels), BF16),
                pltpu.VMEM((1, channels), F32),
                pltpu.VMEM((PARTS, channels, part), BF16),
                pltpu.SemaphoreType.DMA((PARTS + 1,)),
            ],
            2 * count * channels * PARTS * part,
            16,
            (5, 6),
        )
        got3 = swapped(sent3, "tp", 1)
        got1 = swapped(sent1, "tp", 1)
        (far,) = called(far_kernel, none, [kept2, got3], [shaped((count, part), BF16)])
        far = swapped(far, "tp", 2)
        (total,) = called(total_kernel, none, [kept0, got1, far], [shaped((count, part), BF16)])
        return total

    prompt_out = back(False, came, y, bc, reach)

    dec_y, dec_bc, dec_reach = front(
        True, jnp.stack([me_t, jnp.ones((), jnp.int32)]), [kept, over1, near, over3], asked
    )
    decode_out = back(True, state, dec_y, dec_bc, dec_reach)
    decode_out = decode_out.reshape(steps, rows, part).transpose(1, 0, 2)
    return (prompt_out, decode_out)


def solution(mesh):
    return jax.shard_map(
        on_device,
        mesh=mesh,
        in_specs=(
            P("ctx", "tp"),
            P("ctx", None),
            P("ctx", "tp"),
            P(),
            P(None, "tp"),
            P(None, "tp", None, None),
            P(None, "tp"),
            P("tp"),
            P("tp"),
            P(None, "tp"),
            P(None, "tp", None, None),
            P("tp"),
            P("tp"),
            P("tp", None),
        ),
        out_specs=(P("ctx", "tp"), P("ctx", None, "tp")),
        check_vma=False,
    )
```

time: 97.2 us -> 110 us (1.13)
  Pallas kernels: 13 us -> 26.7 us
  starting transfers between devices: 20.1 us -> 25 us
  other arithmetic: 4.76 us -> 0.3 us
  local copies, waits for them, and re-layouts: 23.8 us -> 22.4 us
    pallas_call x6 -> x18, Pallas kernels: 13 us -> 26.7 us  [called(): pl.pallas_call(kernel, out_shape=outs, in_specs=[SMEM] + [ANY if at in fa...]
    ppermute x15 -> x24, starting transfers between devices: 12.9 us -> 25 us  [swapped(): return lax.ppermute(value, axis, [(i, i ^ bit) for i in range(count)])]
    all_to_all x1 -> x0, waiting for transfers between devices: 8.87 us -> none  [on_device(): lax.all_to_all(jnp.broadcast_to(note[None], (devices,) + note.shape), ('c...]
    ppermute x15 -> x24, waiting for transfers between devices: 24.9 us -> 33.6 us  [swapped(): return lax.ppermute(value, axis, [(i, i ^ bit) for i in range(count)])]
    unnamed x62 -> x64, local copies, waits for them, and re-layouts: 13.9 us -> 21.7 us
    all_to_all x1 -> x0, starting transfers between devices: 7.3 us -> none  [on_device(): lax.all_to_all(jnp.broadcast_to(note[None], (devices,) + note.shape), ('c...]
    gather x1 -> x0, local copies, waits for them, and re-layouts: 4.74 us -> none  [on_device(): picked = jnp.take(embed_table, jnp.clip(wanted, 0, vocab_here - 1), axis=0)]
    slice x6 -> x0, local copies, waits for them, and re-layouts: 2.08 us -> none  [the longest x3 1.36 us: on_device(): kept = kept[:half] + swapped(kept[half:], 'ctx', bit)]
  transfers between devices with their start and end apart: 16 -> 24, of which waited for: 10 -> 12; matrix products, arithmetic and copies ran while one was open for 12% -> 1% of each run, Pallas kernels for 13% -> 16%
where the time goes in v3:
time: 110 us; the launch traced here: 109 us
  waiting for transfers between devices  33.6 us (31%)
  Pallas kernels  26.7 us (24%)
  starting transfers between devices  25 us (23%)
  local copies, waits for them, and re-layouts  22.4 us (20%)
    ppermute x24, waiting for transfers between devices, swapped(): return lax.ppermute(value, axis, [(i, i ^ bit) for i in range(count)])  33.6 us
    pallas_call x18, Pallas kernels, called(): pl.pallas_call(kernel, out_shape=outs, in_specs=[SMEM] + [ANY if at in fa...  26.7 us
    ppermute x24, starting transfers between devices, swapped(): return lax.ppermute(value, axis, [(i, i ^ bit) for i in range(count)])  25 us
    unnamed x64, local copies, waits for them, and re-layouts  21.7 us
  transfers between devices with their start and end apart: 24, of which 12 were waited for; matrix products, arithmetic and copies ran while one was open for 1% of the time, Pallas kernels for 16%

profile of v3, /device:TPU:0, one launch (start us, length us, event | category | flops | bytes accessed | tf_op | source)
XLA Modules:
  0.0 108.8 jit_solution(18063346381038790451)
XLA Ops:
  0.6 3.0 %collective-permute-start.7 = (bf16[256,512]{1,0:T(8,128)(2,1)}, bf16[256,512]{1,0:T(8,128)(2,1)S(1)}, u32[]{:S(2)}, u32[]{:S(2)}) collective-permute-start(bf16[256,512]{1,0:T(8,128)(2,1)} %own_in.1), channel_id=1, source_target_pairs={{0,2},{1,3},{2,0},{3,1},{4,6},{5,7},{6,4},{7,5},{8,10},{9,11},{10,... | collective-permute-start | bytes 786440 | tf_op jit(solution)/shard_map/ppermute | solution.py:21
  5.1 2.7 %collective-permute-start = (bf16[8,512]{1,0:T(8,128)(2,1)S(1)}, bf16[8,512]{1,0:T(8,128)(2,1)S(1)}, u32[]{:S(2)}, u32[]{:S(2)}) collective-permute-start(bf16[8,512]{1,0:T(8,128)(2,1)S(1)} %shard_map.149.mine), channel_id=1, source_target_pairs={{0,16},{4,20},{8,24},{12,28},{16,0},{20,4},{24,8},{28,12},{1,17},{... | collective-permute-start | bytes 24584 | tf_op jit(solution)/shard_map/ppermute | solution.py:21
  7.8 2.4 %collective-permute-done.7.over2 = bf16[256,512]{1,0:T(8,128)(2,1)S(1)} collective-permute-done((bf16[256,512]{1,0:T(8,128)(2,1)}, bf16[256,512]{1,0:T(8,128)(2,1)S(1)}, u32[]{:S(2)}, u32[]{:S(2)}) %collective-permute-start.7) | collective-permute-done | bytes 262176 | tf_op jit(solution)/shard_map/ppermute | solution.py:21
  10.2 1.9 %collective-permute-start.1 = (bf16[16,512]{1,0:T(8,128)(2,1)S(1)}, bf16[16,512]{1,0:T(8,128)(2,1)S(1)}, u32[]{:S(2)}, u32[]{:S(2)}) collective-permute-start(bf16[16,512]{1,0:T(8,128)(2,1)S(1)} %shard_map.150.mine), channel_id=1, source_target_pairs={{0,8},{4,12},{8,0},{12,4},{16,24},{20,28},{24,16},{28,20},{1,9},{5... | collective-permute-start | bytes 49160 | tf_op jit(solution)/shard_map/ppermute | solution.py:21
  12.1 1.9 %collective-permute-done.1.got = bf16[16,512]{1,0:T(8,128)(2,1)S(1)} collective-permute-done((bf16[16,512]{1,0:T(8,128)(2,1)S(1)}, bf16[16,512]{1,0:T(8,128)(2,1)S(1)}, u32[]{:S(2)}, u32[]{:S(2)}) %collective-permute-start.1) | collective-permute-done | bytes 16416 | tf_op jit(solution)/shard_map/ppermute | solution.py:21
  15.8 2.1 %collective-permute-done.2.got = bf16[32,512]{1,0:T(8,128)(2,1)S(1)} collective-permute-done((bf16[32,512]{1,0:T(8,128)(2,1)S(1)}, bf16[32,512]{1,0:T(8,128)(2,1)S(1)}, u32[]{:S(2)}, u32[]{:S(2)}) %collective-permute-start.2) | collective-permute-done | bytes 32800 | tf_op jit(solution)/shard_map/ppermute | solution.py:21
  18.5 1.8 %collective-permute-start.4 = (bf16[16,512]{1,0:T(8,128)(2,1)S(1)}, bf16[16,512]{1,0:T(8,128)(2,1)S(1)}, u32[]{:S(2)}, u32[]{:S(2)}) collective-permute-start(bf16[16,512]{1,0:T(8,128)(2,1)S(1)} %get-tuple-element.32.edge0), channel_id=1, source_target_pairs={{0,2},{1,3},{2,0},{3,1},{4,6},{5,7},{6,4},{7,5},{8,10},{9,11},{10,... | collective-permute-start | bytes 49160 | tf_op jit(solution)/shard_map/ppermute | solution.py:21
  20.3 2.0 %collective-permute-done.4.edge2 = bf16[16,512]{1,0:T(8,128)(2,1)S(1)} collective-permute-done((bf16[16,512]{1,0:T(8,128)(2,1)S(1)}, bf16[16,512]{1,0:T(8,128)(2,1)S(1)}, u32[]{:S(2)}, u32[]{:S(2)}) %collective-permute-start.4) | collective-permute-done | bytes 16416 | tf_op jit(solution)/shard_map/ppermute | solution.py:21
  23.5 2.2 %copy-done = bf16[2048,1024]{1,0:T(8,128)(2,1)S(1)} copy-done((bf16[2048,1024]{1,0:T(8,128)(2,1)S(1)}, bf16[2048,1024]{1,0:T(8,128)(2,1)}, u32[]{:S(2)}) %copy-start) | copy-done | bytes 4194328
  31.6 8.9 %shard_map.153 = (f32[256,1024]{1,0:T(8,128)S(1)}, bf16[256,128]{1,0:T(8,128)(2,1)S(1)}, f32[256,128]{1,0:T(8,128)S(1)}, bf16[80,1024]{1,0:T(8,128)(2,1)S(1)}, f32[72,1024]{1,0:T(8,128)S(1)}) custom-call(s32[2]{0:T(128)S(1)} %pad_add_fusion.1.place, bf16[16,512]{1,0:T(8,128)(2,1)S(1)} %get-tuple-element.32.edge0, ...), custom_call_target="tpu_custom_call" | custom-call | flops 1342177280 | bytes 7628992 | tf_op jit(solution)/shard_map/pallas_call | solution.py:451
  43.5 4.6 %collective-permute-done.9.message = bf16[80,1024]{1,0:T(8,128)(2,1)S(1)} collective-permute-done((bf16[80,1024]{1,0:T(8,128)(2,1)S(1)}, bf16[80,1024]{1,0:T(8,128)(2,1)S(1)}, u32[]{:S(2)}, u32[]{:S(2)}) %collective-permute-start.9) | collective-permute-done | bytes 163872 | tf_op jit(solution)/shard_map/ppermute | solution.py:21
  48.2 1.9 %collective-permute-start.10 = (bf16[80,1024]{1,0:T(8,128)(2,1)S(1)}, bf16[80,1024]{1,0:T(8,128)(2,1)S(1)}, u32[]{:S(2)}, u32[]{:S(2)}) collective-permute-start(bf16[80,1024]{1,0:T(8,128)(2,1)S(1)} %get-tuple-element.35), channel_id=1, source_target_pairs={{0,8},{4,12},{8,0},{12,4},{16,24},{20,28},{24,16},{28,20},{1,9},{5... | collective-permute-start | bytes 491528 | tf_op jit(solution)/shard_map/ppermute | solution.py:21
  50.0 2.2 %copy-done.31 = bf16[4096,512]{1,0:T(8,128)(2,1)S(1)} copy-done((bf16[4096,512]{1,0:T(8,128)(2,1)S(1)}, bf16[4096,512]{1,0:T(8,128)(2,1)}, u32[]{:S(2)}) %copy-start.31) | copy-done | bytes 4194328
  52.2 3.7 %shard_map.159 = (bf16[256,512]{1,0:T(8,128)(2,1)S(1)}, bf16[256,512]{1,0:T(8,128)(2,1)}) custom-call(s32[1]{0:T(128)} %bitcast.17.place, bf16[64,512]{1,0:T(8,128)(2,1)S(1)} %get-tuple-element.48.notes, bf16[4096,512]{1,0:T(8,128)(2,1)S(1)} %copy-done.31), custom_call_target="tpu_custom_call" | custom-call | flops 2147483648 | bytes 4784128 | tf_op jit(solution)/shard_map/pallas_call | solution.py:451
  58.2 2.6 %collective-permute-start.11 = (bf16[80,1024]{1,0:T(8,128)(2,1)}, bf16[80,1024]{1,0:T(8,128)(2,1)S(1)}, u32[]{:S(2)}, u32[]{:S(2)}) collective-permute-start(bf16[80,1024]{1,0:T(8,128)(2,1)} %get-tuple-element.38), channel_id=1, source_target_pairs={{0,16},{4,20},{8,24},{12,28},{16,0},{20,4},{24,8},{28,12},{1,17},{... | collective-permute-start | bytes 491528 | tf_op jit(solution)/shard_map/ppermute | solution.py:21
  60.9 2.5 %collective-permute-done.15.got = bf16[256,512]{1,0:T(8,128)(2,1)S(1)} collective-permute-done((bf16[256,512]{1,0:T(8,128)(2,1)}, bf16[256,512]{1,0:T(8,128)(2,1)S(1)}, u32[]{:S(2)}, u32[]{:S(2)}) %collective-permute-start.15) | collective-permute-done | bytes 262176 | tf_op jit(solution)/shard_map/ppermute | solution.py:21
  63.8 3.9 %collective-permute-done.11.message = bf16[80,1024]{1,0:T(8,128)(2,1)S(1)} collective-permute-done((bf16[80,1024]{1,0:T(8,128)(2,1)}, bf16[80,1024]{1,0:T(8,128)(2,1)S(1)}, u32[]{:S(2)}, u32[]{:S(2)}) %collective-permute-start.11) | collective-permute-done | bytes 163872 | tf_op jit(solution)/shard_map/ppermute | solution.py:21
  67.7 2.2 %copy-done.2 = bf16[1024,2048]{1,0:T(8,128)(2,1)S(1)} copy-done((bf16[1024,2048]{1,0:T(8,128)(2,1)S(1)}, bf16[1024,2048]{1,0:T(8,128)(2,1)}, u32[]{:S(2)}) %copy-start.2) | copy-done | bytes 4194328
  72.3 3.6 %shard_map.156 = (bf16[256,512]{1,0:T(8,128)(2,1)S(1)}, bf16[256,512]{1,0:T(8,128)(2,1)S(1)}, f32[256,512]{1,0:T(8,128)S(1)}, f32[256,512]{1,0:T(8,128)S(1)}) custom-call(s32[2]{0:T(128)S(1)} %pad_add_fusion.place, bf16[80,1024]{1,0:T(8,128)(2,1)S(1)} %collective-permute-done.11.message, f32[72,1024]{1,0:T(8,128)S(1)} %get-tuple-element.39.held, ...), custom_call_target="tpu_custom_call" | custom-call | flops 1073741824 | bytes 7475200 | tf_op jit(solution)/shard_map/pallas_call | solution.py:451
  77.1 5.7 %collective-permute-done.17.got = bf16[64,512]{1,0:T(8,128)(2,1)S(1)} collective-permute-done((bf16[64,512]{1,0:T(8,128)(2,1)S(1)}, bf16[64,512]{1,0:T(8,128)(2,1)S(1)}, u32[]{:S(2)}, u32[]{:S(2)}) %collective-permute-start.17) | collective-permute-done | bytes 65568 | tf_op jit(solution)/shard_map/ppermute | solution.py:21
  84.4 2.7 %collective-permute-done.19.over2 = bf16[64,512]{1,0:T(8,128)(2,1)S(1)} collective-permute-done((bf16[64,512]{1,0:T(8,128)(2,1)S(1)}, bf16[64,512]{1,0:T(8,128)(2,1)S(1)}, u32[]{:S(2)}, u32[]{:S(2)}) %collective-permute-start.19) | collective-permute-done | bytes 65568 | tf_op jit(solution)/shard_map/ppermute | solution.py:21
  94.2 4.5 %shard_map.163 = (f32[64,1024]{1,0:T(8,128)S(1)}, bf16[64,128]{1,0:T(8,128)(2,1)S(1)}, f32[64,128]{1,0:T(8,128)S(1)}) custom-call(s32[2]{0:T(128)S(1)} %pad_add_fusion.3.place, bf16[16,512]{1,0:T(8,128)(2,1)S(1)} %get-tuple-element.32.edge0, bf16[16,512]{1,0:T(8,128)(2,1)S(1)} %copy-done.15, bf16[16,512]{1,0:T(8,128)(2,1)S(1)} %collective-permute-done.4.edge2, ...), custom_call_target="tpu_custom_call" | custom-call | flops 335544320 | bytes 5449920 | tf_op jit(solution)/shard_map/pallas_call | solution.py:451
  98.8 2.8 %shard_map.164 = (bf16[64,512]{1,0:T(8,128)(2,1)S(1)}, bf16[64,512]{1,0:T(8,128)(2,1)S(1)}, f32[64,512]{1,0:T(8,128)S(1)}, f32[64,512]{1,0:T(8,128)S(1)}) custom-call(s32[2]{0:T(128)S(1)} %pad_add_fusion.place, bf16[80,1024]{1,0:T(8,128)(2,1)S(1)} %collective-permute-done.11.message, f32[72,1024]{1,0:T(8,128)S(1)} %get-tuple-element.47.held, ...), custom_call_target="tpu_custom_call" | custom-call | flops 268435456 | bytes 5361664 | tf_op jit(solution)/shard_map/pallas_call | solution.py:451
  103.6 3.7 %collective-permute-done.23.far = bf16[64,512]{1,0:T(8,128)(2,1)S(1)} collective-permute-done((bf16[64,512]{1,0:T(8,128)(2,1)S(1)}, bf16[64,512]{1,0:T(8,128)(2,1)S(1)}, u32[]{:S(2)}, u32[]{:S(2)}) %collective-permute-start.23) | collective-permute-done | bytes 65568 | tf_op jit(solution)/shard_map/ppermute | solution.py:21
  (111 shorter events, 32.4 us)
Async XLA Ops:
  0.6 9.6 %collective-permute-start.7 = (bf16[256,512]{1,0:T(8,128)(2,1)}, bf16[256,512]{1,0:T(8,128)(2,1)S(1)}, u32[]{:S(2)}, u32[]{:S(2)}) collective-permute-start(bf16[256,512]{1,0:T(8,128)(2,1)} %own_in.1), channel_id=1, source_target_pairs={{0,2},{1,3},{2,0},{3,1},{4,6},{5,7},{6,4},{7,5},{8,10},{9,11},{10,... | collective-permute-start | bytes 786440 | tf_op jit(solution)/shard_map/ppermute | solution.py:21
  5.1 5.1 %collective-permute-start = (bf16[8,512]{1,0:T(8,128)(2,1)S(1)}, bf16[8,512]{1,0:T(8,128)(2,1)S(1)}, u32[]{:S(2)}, u32[]{:S(2)}) collective-permute-start(bf16[8,512]{1,0:T(8,128)(2,1)S(1)} %shard_map.149.mine), channel_id=1, source_target_pairs={{0,16},{4,20},{8,24},{12,28},{16,0},{20,4},{24,8},{28,12},{1,17},{... | collective-permute-start | bytes 24584 | tf_op jit(solution)/shard_map/ppermute | solution.py:21
  7.7 15.7 %collective-permute-start.6 = (bf16[256,512]{1,0:T(8,128)(2,1)}, bf16[256,512]{1,0:T(8,128)(2,1)S(1)}, u32[]{:S(2)}, u32[]{:S(2)}) collective-permute-start(bf16[256,512]{1,0:T(8,128)(2,1)} %own_in.1), channel_id=1, source_target_pairs={{0,1},{1,0},{2,3},{3,2},{4,5},{5,4},{6,7},{7,6},{8,9},{9,8},{10,11... | collective-permute-start | bytes 786440 | tf_op jit(solution)/shard_map/ppermute | solution.py:21
  10.2 13.3 %collective-permute-start.8 = (bf16[256,512]{1,0:T(8,128)(2,1)S(1)}, bf16[256,512]{1,0:T(8,128)(2,1)S(1)}, u32[]{:S(2)}, u32[]{:S(2)}) collective-permute-start(bf16[256,512]{1,0:T(8,128)(2,1)S(1)} %collective-permute-done.7.over2), channel_id=1, source_target_pairs={{0,1},{1,0},{2,3},{3,2},{4,5},{5,4},{6,7},{7,6},{8,9},{9,8},{10,11... | collective-permute-start | bytes 786440 | tf_op jit(solution)/shard_map/ppermute | solution.py:21
  10.2 3.8 %collective-permute-start.1 = (bf16[16,512]{1,0:T(8,128)(2,1)S(1)}, bf16[16,512]{1,0:T(8,128)(2,1)S(1)}, u32[]{:S(2)}, u32[]{:S(2)}) collective-permute-start(bf16[16,512]{1,0:T(8,128)(2,1)S(1)} %shard_map.150.mine), channel_id=1, source_target_pairs={{0,8},{4,12},{8,0},{12,4},{16,24},{20,28},{24,16},{28,20},{1,9},{5... | collective-permute-start | bytes 49160 | tf_op jit(solution)/shard_map/ppermute | solution.py:21
  14.0 3.9 %collective-permute-start.2 = (bf16[32,512]{1,0:T(8,128)(2,1)S(1)}, bf16[32,512]{1,0:T(8,128)(2,1)S(1)}, u32[]{:S(2)}, u32[]{:S(2)}) collective-permute-start(bf16[32,512]{1,0:T(8,128)(2,1)S(1)} %shard_map.151.mine), channel_id=1, source_target_pairs={{0,4},{4,0},{8,12},{12,8},{16,20},{20,16},{24,28},{28,24},{1,5},{5... | collective-permute-start | bytes 98312 | tf_op jit(solution)/shard_map/ppermute | solution.py:21
  18.5 3.8 %collective-permute-start.4 = (bf16[16,512]{1,0:T(8,128)(2,1)S(1)}, bf16[16,512]{1,0:T(8,128)(2,1)S(1)}, u32[]{:S(2)}, u32[]{:S(2)}) collective-permute-start(bf16[16,512]{1,0:T(8,128)(2,1)S(1)} %get-tuple-element.32.edge0), channel_id=1, source_target_pairs={{0,2},{1,3},{2,0},{3,1},{4,6},{5,7},{6,4},{7,5},{8,10},{9,11},{10,... | collective-permute-start | bytes 49160 | tf_op jit(solution)/shard_map/ppermute | solution.py:21
  20.3 2.1 %collective-permute-start.3 = (bf16[16,512]{1,0:T(8,128)(2,1)S(1)}, bf16[16,512]{1,0:T(8,128)(2,1)S(1)}, u32[]{:S(2)}, u32[]{:S(2)}) collective-permute-start(bf16[16,512]{1,0:T(8,128)(2,1)S(1)} %get-tuple-element.32.edge0), channel_id=1, source_target_pairs={{0,1},{1,0},{2,3},{3,2},{4,5},{5,4},{6,7},{7,6},{8,9},{9,8},{10,11... | collective-permute-start | bytes 49160 | tf_op jit(solution)/shard_map/ppermute | solution.py:21
  22.3 1.2 %collective-permute-start.5 = (bf16[16,512]{1,0:T(8,128)(2,1)S(1)}, bf16[16,512]{1,0:T(8,128)(2,1)S(1)}, u32[]{:S(2)}, u32[]{:S(2)}) collective-permute-start(bf16[16,512]{1,0:T(8,128)(2,1)S(1)} %collective-permute-done.4.edge2), channel_id=1, source_target_pairs={{0,1},{1,0},{2,3},{3,2},{4,5},{5,4},{6,7},{7,6},{8,9},{9,8},{10,11... | collective-permute-start | bytes 49160 | tf_op jit(solution)/shard_map/ppermute | solution.py:21
  41.8 6.3 %collective-permute-start.9 = (bf16[80,1024]{1,0:T(8,128)(2,1)S(1)}, bf16[80,1024]{1,0:T(8,128)(2,1)S(1)}, u32[]{:S(2)}, u32[]{:S(2)}) collective-permute-start(bf16[80,1024]{1,0:T(8,128)(2,1)S(1)} %get-tuple-element.33), channel_id=1, source_target_pairs={{0,4},{4,0},{8,12},{12,8},{16,20},{20,16},{24,28},{28,24},{1,5},{5... | collective-permute-start | bytes 491528 | tf_op jit(solution)/shard_map/ppermute | solution.py:21
  48.2 9.3 %collective-permute-start.10 = (bf16[80,1024]{1,0:T(8,128)(2,1)S(1)}, bf16[80,1024]{1,0:T(8,128)(2,1)S(1)}, u32[]{:S(2)}, u32[]{:S(2)}) collective-permute-start(bf16[80,1024]{1,0:T(8,128)(2,1)S(1)} %get-tuple-element.35), channel_id=1, source_target_pairs={{0,8},{4,12},{8,0},{12,4},{16,24},{20,28},{24,16},{28,20},{1,9},{5... | collective-permute-start | bytes 491528 | tf_op jit(solution)/shard_map/ppermute | solution.py:21
  55.9 7.5 %collective-permute-start.15 = (bf16[256,512]{1,0:T(8,128)(2,1)}, bf16[256,512]{1,0:T(8,128)(2,1)S(1)}, u32[]{:S(2)}, u32[]{:S(2)}) collective-permute-start(bf16[256,512]{1,0:T(8,128)(2,1)} %get-tuple-element.50), channel_id=1, source_target_pairs={{0,4},{4,0},{8,12},{12,8},{16,20},{20,16},{24,28},{28,24},{1,5},{5... | collective-permute-start | bytes 786440 | tf_op jit(solution)/shard_map/ppermute | solution.py:21
  58.2 9.5 %collective-permute-start.11 = (bf16[80,1024]{1,0:T(8,128)(2,1)}, bf16[80,1024]{1,0:T(8,128)(2,1)S(1)}, u32[]{:S(2)}, u32[]{:S(2)}) collective-permute-start(bf16[80,1024]{1,0:T(8,128)(2,1)} %get-tuple-element.38), channel_id=1, source_target_pairs={{0,16},{4,20},{8,24},{12,28},{16,0},{20,4},{24,8},{28,12},{1,17},{... | collective-permute-start | bytes 491528 | tf_op jit(solution)/shard_map/ppermute | solution.py:21
  63.5 12.5 %collective-permute-start.16 = (bf16[128,512]{1,0:T(8,128)(2,1)S(1)}, bf16[128,512]{1,0:T(8,128)(2,1)S(1)}, u32[]{:S(2)}, u32[]{:S(2)}) collective-permute-start(bf16[128,512]{1,0:T(8,128)(2,1)S(1)} %get-tuple-element.52), channel_id=1, source_target_pairs={{0,8},{4,12},{8,0},{12,4},{16,24},{20,28},{24,16},{28,20},{1,9},{5... | collective-permute-start | bytes 393224 | tf_op jit(solution)/shard_map/ppermute | solution.py:21
  75.9 11.8 %collective-permute-start.13 = (bf16[256,512]{1,0:T(8,128)(2,1)S(1)}, bf16[256,512]{1,0:T(8,128)(2,1)S(1)}, u32[]{:S(2)}, u32[]{:S(2)}) collective-permute-start(bf16[256,512]{1,0:T(8,128)(2,1)S(1)} %get-tuple-element.46), channel_id=1, source_target_pairs={{0,1},{1,0},{2,3},{3,2},{4,5},{5,4},{6,7},{7,6},{8,9},{9,8},{10,11... | collective-permute-start | bytes 786440 | tf_op jit(solution)/shard_map/ppermute | solution.py:21
  76.1 6.8 %collective-permute-start.17 = (bf16[64,512]{1,0:T(8,128)(2,1)S(1)}, bf16[64,512]{1,0:T(8,128)(2,1)S(1)}, u32[]{:S(2)}, u32[]{:S(2)}) collective-permute-start(bf16[64,512]{1,0:T(8,128)(2,1)S(1)} %get-tuple-element.54), channel_id=1, source_target_pairs={{0,16},{4,20},{8,24},{12,28},{16,0},{20,4},{24,8},{28,12},{1,17},{... | collective-permute-start | bytes 196616 | tf_op jit(solution)/shard_map/ppermute | solution.py:21
  82.8 4.3 %collective-permute-start.19 = (bf16[64,512]{1,0:T(8,128)(2,1)S(1)}, bf16[64,512]{1,0:T(8,128)(2,1)S(1)}, u32[]{:S(2)}, u32[]{:S(2)}) collective-permute-start(bf16[64,512]{1,0:T(8,128)(2,1)S(1)} %shard_map.162.own_in), channel_id=1, source_target_pairs={{0,2},{1,3},{2,0},{3,1},{4,6},{5,7},{6,4},{7,5},{8,10},{9,11},{10,... | collective-permute-start | bytes 196616 | tf_op jit(solution)/shard_map/ppermute | solution.py:21
  84.4 5.0 %collective-permute-start.18 = (bf16[64,512]{1,0:T(8,128)(2,1)S(1)}, bf16[64,512]{1,0:T(8,128)(2,1)S(1)}, u32[]{:S(2)}, u32[]{:S(2)}) collective-permute-start(bf16[64,512]{1,0:T(8,128)(2,1)S(1)} %shard_map.162.own_in), channel_id=1, source_target_pairs={{0,1},{1,0},{2,3},{3,2},{4,5},{5,4},{6,7},{7,6},{8,9},{9,8},{10,11... | collective-permute-start | bytes 196616 | tf_op jit(solution)/shard_map/ppermute | solution.py:21
  87.2 2.2 %collective-permute-start.20 = (bf16[64,512]{1,0:T(8,128)(2,1)S(1)}, bf16[64,512]{1,0:T(8,128)(2,1)S(1)}, u32[]{:S(2)}, u32[]{:S(2)}) collective-permute-start(bf16[64,512]{1,0:T(8,128)(2,1)S(1)} %collective-permute-done.19.over2), channel_id=1, source_target_pairs={{0,1},{1,0},{2,3},{3,2},{4,5},{5,4},{6,7},{7,6},{8,9},{9,8},{10,11... | collective-permute-start | bytes 196616 | tf_op jit(solution)/shard_map/ppermute | solution.py:21
  87.2 20.9 %collective-permute-start.12 = (bf16[256,512]{1,0:T(8,128)(2,1)S(1)}, bf16[256,512]{1,0:T(8,128)(2,1)S(1)}, u32[]{:S(2)}, u32[]{:S(2)}) collective-permute-start(bf16[256,512]{1,0:T(8,128)(2,1)S(1)} %get-tuple-element.44), channel_id=1, source_target_pairs={{0,1},{1,0},{2,3},{3,2},{4,5},{5,4},{6,7},{7,6},{8,9},{9,8},{10,11... | collective-permute-start | bytes 786440 | tf_op jit(solution)/shard_map/ppermute | solution.py:21
  87.7 20.3 %collective-permute-start.14 = (bf16[256,512]{1,0:T(8,128)(2,1)S(1)}, bf16[256,512]{1,0:T(8,128)(2,1)S(1)}, u32[]{:S(2)}, u32[]{:S(2)}) collective-permute-start(bf16[256,512]{1,0:T(8,128)(2,1)S(1)} %shard_map.157), channel_id=1, source_target_pairs={{0,2},{1,3},{2,0},{3,1},{4,6},{5,7},{6,4},{7,5},{8,10},{9,11},{10,... | collective-permute-start | bytes 786440 | tf_op jit(solution)/shard_map/ppermute | solution.py:21
  101.6 1.3 %collective-permute-start.22 = (bf16[64,512]{1,0:T(8,128)(2,1)S(1)}, bf16[64,512]{1,0:T(8,128)(2,1)S(1)}, u32[]{:S(2)}, u32[]{:S(2)}) collective-permute-start(bf16[64,512]{1,0:T(8,128)(2,1)S(1)} %get-tuple-element.61), channel_id=1, source_target_pairs={{0,1},{1,0},{2,3},{3,2},{4,5},{5,4},{6,7},{7,6},{8,9},{9,8},{10,11... | collective-permute-start | bytes 196616 | tf_op jit(solution)/shard_map/ppermute | solution.py:21
  101.7 1.8 %collective-permute-start.21 = (bf16[64,512]{1,0:T(8,128)(2,1)S(1)}, bf16[64,512]{1,0:T(8,128)(2,1)S(1)}, u32[]{:S(2)}, u32[]{:S(2)}) collective-permute-start(bf16[64,512]{1,0:T(8,128)(2,1)S(1)} %get-tuple-element.59), channel_id=1, source_target_pairs={{0,1},{1,0},{2,3},{3,2},{4,5},{5,4},{6,7},{7,6},{8,9},{9,8},{10,11... | collective-permute-start | bytes 196616 | tf_op jit(solution)/shard_map/ppermute | solution.py:21
  103.0 4.3 %collective-permute-start.23 = (bf16[64,512]{1,0:T(8,128)(2,1)S(1)}, bf16[64,512]{1,0:T(8,128)(2,1)S(1)}, u32[]{:S(2)}, u32[]{:S(2)}) collective-permute-start(bf16[64,512]{1,0:T(8,128)(2,1)S(1)} %shard_map.165), channel_id=1, source_target_pairs={{0,2},{1,3},{2,0},{3,1},{4,6},{5,7},{6,4},{7,5},{8,10},{9,11},{10,... | collective-permute-start | bytes 196616 | tf_op jit(solution)/shard_map/ppermute | solution.py:21
  (32 other events, 232.1 us)

commit v4 on v3

--- a/solution.py
+++ b/solution.py
@@ -82,76 +82,36 @@
     edge1,
     edge2,
     edge3,
-    own_in,
+    own,
     over1,
     over2,
     over3,
-    gain_in,
-    x_weight_in,
-    bc_weight_in,
-    dt_weight_in,
-    dt_bias_in,
-    decay_log_in,
-    conv_x_in,
-    conv_bc_in,
-    skip_gain_in,
+    gain,
+    x_weight,
+    bc_weight,
+    dt_weight,
+    dt_bias,
+    decay_log,
+    conv_x,
+    conv_bc,
+    skip_gain,
     y_out,
     bc_out,
     reach_out,
     *rest,
 ):
     if not decode:
-        message_out, state_out, own = rest[:3]
-        rest = rest[3:]
-    (
-        normed,
-        x_conv,
-        joined,
-        gain,
-        x_weight,
-        bc_weight,
-        dt_weight,
-        dt_bias,
-        decay_log,
-        conv_x,
-        conv_bc,
-        skip_gain,
-        sems,
-    ) = rest
-    tokens, part = over1.shape
-    chunks, _, step_lanes = x_weight.shape
-    channels = chunks * step_lanes
+        message_out, state_out = rest[:2]
+        rest = rest[2:]
+    normed, x_conv, joined = rest
+    tokens, part = own.shape
+    channels = x_weight.shape[1]
+    step_lanes = 2 * LANES
     width = channels // heads
     state_width = bc_weight.shape[0] // 2
     taps = conv_x.shape[0]
     margin = taps - 1
     me, edge_on = place[0], place[1]
-    if decode:
-        own = own_in
-        early = []
-    else:
-        early = started([(own_in, own)], sems)
-    early += started([(gain_in, gain)], sems, 1)
-    chunk_copies = started(
-        [(x_weight_in.at[:, pl.ds(c * step_lanes, step_lanes)], x_weight.at[c]) for c in range(chunks)],
-        sems,
-        2,
-    )
-    late = started(
-        [
-            (conv_x_in, conv_x),
-            (bc_weight_in, bc_weight),
-            (dt_weight_in, dt_weight),
-            (dt_bias_in, dt_bias),
-            (decay_log_in, decay_log),
-            (conv_bc_in, conv_bc),
-            (skip_gain_in, skip_gain),
-        ],
-        sems,
-        2 + chunks,
-    )
-    for copy in early:
-        copy.wait()
 
     blocks = [ref[...].astype(F32) for ref in (own, over1, over2, over3)]
     square = sum(jnp.sum(b * b, axis=1, keepdims=True) for b in blocks)
@@ -190,17 +150,12 @@
         total = sum(taps_of(k) * joined[s : s + tokens, :lanes] for k, s in enumerate(starts))
         return silu(total)
 
-    late[0].wait()
-    for c in range(chunks):
-        chunk_copies[c].wait()
-        lane = c * step_lanes
-        raw = projected(lambda j: x_weight[c, j * part : (j + 1) * part, :])
+    for lane in range(0, channels, step_lanes):
+        raw = projected(lambda j: x_weight[j * part : (j + 1) * part, lane : lane + step_lanes])
         x_conv[:, lane : lane + step_lanes] = convolved(
             raw, lambda k: conv_x[k : k + 1, lane : lane + step_lanes]
         ).astype(BF16)
 
-    for copy in late[1:]:
-        copy.wait()
     fill = jnp.zeros((LANES - heads, PARTS * part), BF16)
     side = jnp.concatenate([bc_weight[...], dt_weight[...], fill], axis=0)
     raw = sum(across(normed[j], side[:, j * part : (j + 1) * part], 1) for j in range(PARTS))
@@ -306,31 +261,19 @@
     y,
     bc,
     reach,
-    gain_in,
-    weight_in,
+    gain,
+    weight,
     sent3,
     sent1,
     kept2,
     kept0,
     full,
     mixed,
-    gain,
-    weight,
-    sems,
 ):
     me, later = place[0], place[1] > 0
     state_width = held.shape[0] - EDGE
     tokens, channels = y.shape
-    part = weight.shape[2]
-    order = (3, 1, 2, 0)
-    copies = started(
-        [(gain_in, gain)]
-        + [
-            (weight_in.at[:, pl.ds(pl.multiple_of((me ^ r) * part, part), part)], weight.at[at])
-            for at, r in enumerate(order)
-        ],
-        sems,
-    )
+    part = weight.shape[1] // PARTS
     other, other_decay = unpacked(message, state_width)
     mine, my_decay = held[:state_width, :], held[state_width : state_width + 1, :]
     if decode:
@@ -350,11 +293,10 @@
         full[:, lanes] = total
         square = square + jnp.sum(total * total, axis=1, keepdims=True)
     factor = lax.rsqrt(square / channels + EPS)
-    copies[0].wait()
     mixed[...] = (full[...] * factor * gain[...]).astype(BF16)
-    for at, out in enumerate((sent3, sent1, kept2, kept0)):
-        copies[1 + at].wait()
-        out[...] = dot(mixed[...], weight[at]).astype(out.dtype)
+    for r, out in ((3, sent3), (1, sent1), (2, kept2), (0, kept0)):
+        columns = pl.ds(pl.multiple_of((me ^ r) * part, part), part)
+        out[...] = dot(mixed[...], weight[:, columns]).astype(out.dtype)
 
 
 def far_kernel(place, kept, got, out):
@@ -394,11 +336,9 @@
     picked[...] = jnp.concatenate(edges, axis=0).astype(BF16)
 
 
-def lookup_kernel(steps, rows, place, notes, table_in, kept_out, sent_out, table, wanted, found, sems):
-    chunks, chunk, _ = table.shape
-    copies = started(
-        [(table_in.at[pl.ds(c * chunk, chunk), :], table.at[c]) for c in range(chunks)], sems
-    )
+def lookup_kernel(steps, rows, place, notes, table, kept_out, sent_out, wanted, found):
+    chunk = min(table.shape[0], 1024)
+    chunks = table.shape[0] // chunk
     first = (place[0] * (chunks * chunk)).astype(F32)
     held = notes[...].astype(F32)
     groups = held.shape[0] // EDGE
@@ -414,14 +354,13 @@
     block = min(asked, 256)
     lane = iota((block, LANES), 1).astype(F32)
     for c in range(chunks):
-        copies[c].wait()
         for at in range(0, asked, block):
             gap = wanted[at : at + block, :] - lane
             hot = [
                 jnp.where(gap == float(c * chunk + k), 1.0, 0.0).astype(BF16)
                 for k in range(0, chunk, LANES)
             ]
-            term = dot(jnp.concatenate(hot, axis=1), table[c])
+            term = dot(jnp.concatenate(hot, axis=1), table[c * chunk : (c + 1) * chunk, :])
             if c == 0:
                 found[at : at + block, :] = term
             else:
@@ -442,21 +381,36 @@
 
 VMEM = pl.BlockSpec(memory_space=pltpu.VMEM)
 SMEM = pl.BlockSpec(memory_space=pltpu.SMEM)
-ANY = pl.BlockSpec(memory_space=pl.ANY)
-
-
-def called(kernel, place, inputs, outs, scratch=(), flops=1000, limit=4, far=()):
-    moved = sum(v.size * v.dtype.itemsize for v in inputs)
-    moved += sum(o.size * o.dtype.itemsize for o in outs)
-    return pl.pallas_call(
-        kernel,
-        out_shape=outs,
-        in_specs=[SMEM] + [ANY if at in far else VMEM for at in range(len(inputs))],
-        out_specs=[VMEM] * len(outs),
-        scratch_shapes=list(scratch),
-        compiler_params=pltpu.CompilerParams(vmem_limit_bytes=limit * MEBI),
-        cost_estimate=pl.CostEstimate(flops=flops, bytes_accessed=moved, transcendentals=0),
-    )(place, *inputs)
+HBM = pl.BlockSpec(memory_space=pltpu.HBM)
+
+
+class Caller:
+    def __init__(self):
+        self.token = jnp.zeros((8, LANES), F32)
+
+    def __call__(self, kernel, place, inputs, outs, scratch=(), us=1.0, limit=4, far=()):
+        inputs = list(inputs)
+        count = len(inputs)
+
+        def ordered(place, token, *refs):
+            refs, token_out = list(refs), refs[count]
+            del refs[count]
+            kernel(place, *refs)
+            token_out[...] = jnp.zeros_like(token_out)
+
+        results = pl.pallas_call(
+            ordered,
+            out_shape=[shaped((8, LANES), F32)] + outs,
+            in_specs=[SMEM, VMEM] + [HBM if at in far else VMEM for at in range(count)],
+            out_specs=[VMEM] * (1 + len(outs)),
+            scratch_shapes=list(scratch),
+            compiler_params=pltpu.CompilerParams(vmem_limit_bytes=limit * MEBI),
+            cost_estimate=pl.CostEstimate(
+                flops=int(us * 1e9), bytes_accessed=int(us * 1e6), transcendentals=0
+            ),
+        )(place, self.token, *inputs)
+        self.token = results[0]
+        return results[1:]
 
 
 def shaped(shape, dtype):
@@ -499,6 +453,7 @@
     bits = bits_of("ctx")
     assert len(bits) >= 2
     none = jnp.zeros((1,), jnp.int32)
+    called = Caller()
 
     e2 = swapped(prompt_embeds, "tp", 2)
     e1 = swapped(prompt_embeds, "tp", 1)
@@ -513,6 +468,7 @@
             pltpu.VMEM((2 * EDGE, part), BF16),
             pltpu.SemaphoreType.DMA((2,)),
         ],
+        us=2,
         far=(0, 1),
     )
 
@@ -524,7 +480,7 @@
         got = swapped(notes, "ctx", bit)
         size = 2 * notes.shape[0]
         if bit > 1:
-            (notes,) = called(join_kernel, none, [notes, got], [shaped((size, part), BF16)])
+            (notes,) = called(join_kernel, none, [notes, got], [shaped((size, part), BF16)], us=4)
         else:
             notes, edge0 = called(
                 last_join_kernel,
@@ -532,47 +488,22 @@
                 [notes, got],
                 [shaped((size, part), BF16), shaped((2 * EDGE, part), BF16)],
                 [pltpu.VMEM((size, part), F32)],
+                us=4,
             )
-    edge2 = swapped(edge0, "tp", 2)
-    edge1 = swapped(edge0, "tp", 1)
     e3 = swapped(e2, "tp", 1)
-    edge3 = swapped(edge2, "tp", 1)
-    edges = [edge0, edge1, edge2, edge3]
+    edges = [edge0] + [swapped(edge0, "tp", r) for r in range(1, PARTS)]
 
     half = groups * asked // 2
-    chunk = min(vocab_here, 1024)
-    assert vocab_here % chunk == 0
+    assert vocab_here % min(vocab_here, 1024) == 0
     kept, sent = called(
         functools.partial(lookup_kernel, steps, rows),
         me_c.reshape(1),
         [notes, embed_table],
         [shaped((half, part), BF16), shaped((half, part), BF16)],
-        [
-            pltpu.VMEM((vocab_here // chunk, chunk, part), BF16),
-            pltpu.VMEM((2 * half, LANES), F32),
-            pltpu.VMEM((2 * half, part), F32),
-            pltpu.SemaphoreType.DMA((vocab_here // chunk,)),
-        ],
-        flops=4 * half * vocab_here * part,
-        limit=40 if half > 512 else 16,
-        far=(1,),
+        [pltpu.VMEM((2 * half, LANES), F32), pltpu.VMEM((2 * half, part), F32)],
+        us=3.5,
+        limit=32 if half > 512 else 8,
     )
-    for bit in bits:
-        got = swapped(sent, "ctx", bit)
-        half = half // 2
-        if bit == bits[-1]:
-            (kept,) = called(fold_kernel, none, [kept, got], [shaped((asked, part), BF16)])
-        else:
-            kept, sent = called(
-                fold_kernel,
-                none,
-                [kept, got],
-                [shaped((half, part), BF16), shaped((half, part), BF16)],
-                limit=16 if half > 512 else 4,
-            )
-    near = swapped(kept, "tp", 2)
-    over1 = swapped(kept, "tp", 1)
-    over3 = swapped(near, "tp", 1)
 
     weights = [
         norm_gain.reshape(PARTS, 1, part),
@@ -586,100 +517,101 @@
         skip_gain.reshape(1, -1),
     ]
     packed = state_width + 2 * EDGE
-    step_lanes = 2 * LANES
-    chunks = channels // step_lanes
-
-    def front(decode, place, blocks, count):
+
+    def front(decode, edge_on, blocks, count):
         outs = [
             shaped((count, channels), F32),
             shaped((count, LANES), BF16),
             shaped((count, LANES), F32),
         ]
-        scratch = []
         if not decode:
             outs += [
                 shaped((packed, channels), BF16),
                 shaped((state_width + EDGE, channels), F32),
             ]
-            scratch = [pltpu.VMEM((count, part), BF16)]
         joined = margin * rows if decode else EDGE
-        scratch += [
-            pltpu.VMEM((PARTS, count + 2 * EDGE, part), BF16),
-            pltpu.VMEM((count, channels), BF16),
-            pltpu.VMEM((joined + count, step_lanes), F32),
-            pltpu.VMEM((PARTS, 1, part), F32),
-            pltpu.VMEM((chunks, PARTS * part, step_lanes), BF16),
-        ]
-        scratch += [pltpu.VMEM(w.shape, w.dtype) for w in weights[2:]]
-        scratch += [pltpu.SemaphoreType.DMA((chunks + 9,))]
         return called(
             functools.partial(front_kernel, decode, rows, heads),
-            place,
+            jnp.stack([me_t, edge_on]),
             edges + blocks + weights,
             outs,
-            scratch,
-            2 * count * PARTS * part * (channels + 2 * LANES),
-            24,
-            tuple(range(8, 8 + len(weights))) + (() if decode else (4,)),
+            [
+                pltpu.VMEM((PARTS, count + 2 * EDGE, part), BF16),
+                pltpu.VMEM((count, channels), BF16),
+                pltpu.VMEM((joined + count, 2 * LANES), F32),
+            ],
+            us=2.5 if decode else 6,
+            limit=16,
         )
 
     y, bc, reach, message, state = front(
-        False,
-        jnp.stack([me_t, (me_c > 0).astype(jnp.int32)]),
-        [prompt_embeds, e1, e2, e3],
-        tokens,
+        False, (me_c > 0).astype(jnp.int32), [prompt_embeds, e1, e2, e3], tokens
     )
 
     came = state
-    for bit in bits[:-1]:
+    for bit in bits:
+        got = swapped(sent, "ctx", bit)
+        half = half // 2
+        if bit == bits[-1]:
+            (kept,) = called(fold_kernel, none, [kept, got], [shaped((asked, part), BF16)], us=3)
+        else:
+            kept, sent = called(
+                fold_kernel,
+                none,
+                [kept, got],
+                [shaped((half, part), BF16), shaped((half, part), BF16)],
+                us=3,
+                limit=16 if half > 512 else 4,
+            )
         got = swapped(message, "ctx", bit)
-        later = ((me_c & bit) != 0).astype(jnp.int32).reshape(1)
-        message, state, came = called(
-            functools.partial(step_kernel, bit == bits[0]),
-            later,
-            [got, state, came],
-            [
-                shaped((packed, channels), BF16),
-                shaped((state_width + EDGE, channels), F32),
-                shaped((state_width + EDGE, channels), F32),
-            ],
-            flops=8 * state_width * channels,
-        )
-    got = swapped(message, "ctx", bits[-1])
-    later = ((me_c & bits[-1]) != 0).astype(jnp.int32)
+        later = ((me_c & bit) != 0).astype(jnp.int32)
+        if bit != bits[-1]:
+            message, state, came = called(
+                functools.partial(step_kernel, bit == bits[0]),
+                later.reshape(1),
+                [got, state, came],
+                [
+                    shaped((packed, channels), BF16),
+                    shaped((state_width + EDGE, channels), F32),
+                    shaped((state_width + EDGE, channels), F32),
+                ],
+                us=3,
+            )
     back_place = jnp.stack([me_t, later])
+    near = swapped(kept, "tp", 2)
+    over1 = swapped(kept, "tp", 1)
+    over3 = swapped(near, "tp", 1)
 
     def back(decode, held, y, bc, reach):
         count = y.shape[0]
-        sent3, sent1, kept2, kept0 = called(
+        return called(
             functools.partial(back_kernel, decode, heads),
             back_place,
             [got, held, y, bc, reach, out_gain.reshape(1, -1), out_weight],
             [shaped((count, part), BF16)] * 2 + [shaped((count, part), F32)] * 2,
-            [
-                pltpu.VMEM((count, channels), F32),
-                pltpu.VMEM((count, channels), BF16),
-                pltpu.VMEM((1, channels), F32),
-                pltpu.VMEM((PARTS, channels, part), BF16),
-                pltpu.SemaphoreType.DMA((PARTS + 1,)),
-            ],
-            2 * count * channels * PARTS * part,
-            16,
-            (5, 6),
+            [pltpu.VMEM((count, channels), F32), pltpu.VMEM((count, channels), BF16)],
+            us=2,
+            limit=12,
         )
+
+    def crossed(sent3, sent1, kept2, kept0):
         got3 = swapped(sent3, "tp", 1)
         got1 = swapped(sent1, "tp", 1)
-        (far,) = called(far_kernel, none, [kept2, got3], [shaped((count, part), BF16)])
-        far = swapped(far, "tp", 2)
-        (total,) = called(total_kernel, none, [kept0, got1, far], [shaped((count, part), BF16)])
-        return total
-
-    prompt_out = back(False, came, y, bc, reach)
-
+        (far,) = called(far_kernel, none, [kept2, got3], [shaped(kept2.shape, BF16)])
+        return kept0, got1, swapped(far, "tp", 2)
+
+    def totalled(kept0, got1, far):
+        return called(total_kernel, none, [kept0, got1, far], [shaped(kept0.shape, BF16)])[0]
+
+    prompt_back = back(False, came, y, bc, reach)
     dec_y, dec_bc, dec_reach = front(
-        True, jnp.stack([me_t, jnp.ones((), jnp.int32)]), [kept, over1, near, over3], asked
+        True, jnp.ones((), jnp.int32), [kept, over1, near, over3], asked
     )
-    decode_out = back(True, state, dec_y, dec_bc, dec_reach)
+    prompt_crossed = crossed(*prompt_back)
+    decode_back = back(True, state, dec_y, dec_bc, dec_reach)
+    decode_crossed = crossed(*decode_back)
+    decode_out = totalled(*decode_crossed)
+    prompt_out = totalled(*prompt_crossed)
     decode_out = decode_out.reshape(steps, rows, part).transpose(1, 0, 2)
     return (prompt_out, decode_out)
 

time: 110 us -> 69.5 us (0.63)
  local copies, waits for them, and re-layouts: 22.4 us -> 1.42 us
  waiting for transfers between devices: 33.6 us -> 21.9 us
  Pallas kernels: 26.7 us -> 17.6 us
  starting transfers between devices: 25 us -> 27.2 us
    unnamed x64 -> x26, local copies, waits for them, and re-layouts: 21.7 us -> 0.74 us
    ppermute x24, waiting for transfers between devices: 33.6 us -> 21.9 us  [swapped(): return lax.ppermute(value, axis, [(i, i ^ bit) for i in range(count)])]
    pallas_call x18, Pallas kernels: 26.7 us -> 17.6 us  [__call__(): pl.pallas_call(ordered, out_shape=[shaped((8, LANES), F32)] + outs, in_sp...]
    ppermute x24, starting transfers between devices: 25 us -> 27.2 us  [swapped(): return lax.ppermute(value, axis, [(i, i ^ bit) for i in range(count)])]
  transfers between devices with their start and end apart: 24 -> 24, of which waited for: 12 -> 10; matrix products, arithmetic and copies ran while one was open for 1% -> 1% of each run, Pallas kernels for 16% -> 21%
where the time goes in v4:
time: 69.5 us; the launch traced here: 69.3 us
  starting transfers between devices  27.2 us (39%)
  waiting for transfers between devices  21.9 us (32%)
  Pallas kernels  17.6 us (25%)
  local copies, waits for them, and re-layouts  1.42 us (2%)
  between operations  0.91 us (1%)
    ppermute x24, starting transfers between devices, swapped(): return lax.ppermute(value, axis, [(i, i ^ bit) for i in range(count)])  27.2 us
    ppermute x24, waiting for transfers between devices, swapped(): return lax.ppermute(value, axis, [(i, i ^ bit) for i in range(count)])  21.9 us
    pallas_call x18, Pallas kernels, __call__(): pl.pallas_call(ordered, out_shape=[shaped((8, LANES), F32)] + outs, in_sp...  17.6 us
  transfers between devices with their start and end apart: 24, of which 10 were waited for; matrix products, arithmetic and copies ran while one was open for 1% of the time, Pallas kernels for 21%

profile of v4, /device:TPU:0, one launch (start us, length us, event | category | flops | bytes accessed | tf_op | source)
XLA Modules:
  0.0 69.3 jit_solution(7457910666538167236)
XLA Ops:
  2.1 4.1 %collective-permute-start = (bf16[8,512]{1,0:T(8,128)(2,1)S(1)}, bf16[8,512]{1,0:T(8,128)(2,1)S(1)}, u32[]{:S(2)}, u32[]{:S(2)}) collective-permute-start(bf16[8,512]{1,0:T(8,128)(2,1)S(1)} %get-tuple-element.58.refs_0_), channel_id=1, source_target_pairs={{0,16},{4,20},{8,24},{12,28},{16,0},{20,4},{24,8},{28,12},{1,17},{... | collective-permute-start | bytes 24584 | tf_op jit(solution)/shard_map/ppermute | solution.py:21
  6.2 1.5 %collective-permute-start.7 = (bf16[256,512]{1,0:T(8,128)(2,1)}, bf16[256,512]{1,0:T(8,128)(2,1)S(1)}, u32[]{:S(2)}, u32[]{:S(2)}) collective-permute-start(bf16[256,512]{1,0:T(8,128)(2,1)} %refs_4_.1), channel_id=1, source_target_pairs={{0,2},{1,3},{2,0},{3,1},{4,6},{5,7},{6,4},{7,5},{8,10},{9,11},{10,... | collective-permute-start | bytes 786440 | tf_op jit(solution)/shard_map/ppermute | solution.py:21
  7.8 1.9 %collective-permute-start.1 = (bf16[16,512]{1,0:T(8,128)(2,1)S(1)}, bf16[16,512]{1,0:T(8,128)(2,1)S(1)}, u32[]{:S(2)}, u32[]{:S(2)}) collective-permute-start(bf16[16,512]{1,0:T(8,128)(2,1)S(1)} %get-tuple-element.60.refs_0_), channel_id=1, source_target_pairs={{0,8},{4,12},{8,0},{12,4},{16,24},{20,28},{24,16},{28,20},{1,9},{5... | collective-permute-start | bytes 49160 | tf_op jit(solution)/shard_map/ppermute | solution.py:21
  9.8 1.8 %collective-permute-done.1.refs_1_ = bf16[16,512]{1,0:T(8,128)(2,1)S(1)} collective-permute-done((bf16[16,512]{1,0:T(8,128)(2,1)S(1)}, bf16[16,512]{1,0:T(8,128)(2,1)S(1)}, u32[]{:S(2)}, u32[]{:S(2)}) %collective-permute-start.1) | collective-permute-done | bytes 16416 | tf_op jit(solution)/shard_map/ppermute | solution.py:21
  11.6 1.8 %collective-permute-start.2 = (bf16[32,512]{1,0:T(8,128)(2,1)S(1)}, bf16[32,512]{1,0:T(8,128)(2,1)S(1)}, u32[]{:S(2)}, u32[]{:S(2)}) collective-permute-start(bf16[32,512]{1,0:T(8,128)(2,1)S(1)} %get-tuple-element.62.refs_0_), channel_id=1, source_target_pairs={{0,4},{4,0},{8,12},{12,8},{16,20},{20,16},{24,28},{28,24},{1,5},{5... | collective-permute-start | bytes 98312 | tf_op jit(solution)/shard_map/ppermute | solution.py:21
  13.5 2.0 %collective-permute-done.2.refs_1_ = bf16[32,512]{1,0:T(8,128)(2,1)S(1)} collective-permute-done((bf16[32,512]{1,0:T(8,128)(2,1)S(1)}, bf16[32,512]{1,0:T(8,128)(2,1)S(1)}, u32[]{:S(2)}, u32[]{:S(2)}) %collective-permute-start.2) | collective-permute-done | bytes 32800 | tf_op jit(solution)/shard_map/ppermute | solution.py:21
  16.1 1.9 %collective-permute-start.4 = (bf16[16,512]{1,0:T(8,128)(2,1)S(1)}, bf16[16,512]{1,0:T(8,128)(2,1)S(1)}, u32[]{:S(2)}, u32[]{:S(2)}) collective-permute-start(bf16[16,512]{1,0:T(8,128)(2,1)S(1)} %get-tuple-element.66.refs_0_), channel_id=1, source_target_pairs={{0,2},{1,3},{2,0},{3,1},{4,6},{5,7},{6,4},{7,5},{8,10},{9,11},{10,... | collective-permute-start | bytes 49160 | tf_op jit(solution)/shard_map/ppermute | solution.py:21
  18.4 2.4 %shard_map.153 = (f32[8,128]{1,0:T(8,128)S(1)}, bf16[256,512]{1,0:T(8,128)(2,1)S(1)}, bf16[256,512]{1,0:T(8,128)(2,1)S(1)}) custom-call(s32[1]{0:T(128)} %bitcast.5.place, f32[8,128]{1,0:T(8,128)S(1)} %get-tuple-element.63.token, bf16[64,512]{1,0:T(8,128)(2,1)S(1)} %get-tuple-element.64.refs_0_, bf16[4096,512]{1,0:T(8,128)(2,1)S(1)} %copy-done), custom_call_target="tpu_custom_call" | custom-call | flops 3500000000 | bytes 3500000 | tf_op jit(solution)/shard_map/pallas_call | solution.py:401
  20.8 1.9 %collective-permute-start.9 = (bf16[256,512]{1,0:T(8,128)(2,1)S(1)}, bf16[256,512]{1,0:T(8,128)(2,1)S(1)}, u32[]{:S(2)}, u32[]{:S(2)}) collective-permute-start(bf16[256,512]{1,0:T(8,128)(2,1)S(1)} %get-tuple-element.69), channel_id=1, source_target_pairs={{0,4},{4,0},{8,12},{12,8},{16,20},{20,16},{24,28},{28,24},{1,5},{5... | collective-permute-start | bytes 786440 | tf_op jit(solution)/shard_map/ppermute | solution.py:21
  22.8 6.2 %shard_map.154 = (f32[8,128]{1,0:T(8,128)S(1)}, f32[256,1024]{1,0:T(8,128)S(1)}, bf16[256,128]{1,0:T(8,128)(2,1)S(1)}, f32[256,128]{1,0:T(8,128)S(1)}, bf16[80,1...) custom-call(s32[2]{0:T(128)S(1)} %pad_add_fusion.2.place, f32[8,128]{1,0:T(8,128)S(1)} %get-tuple-element.65.token, ...), custom_call_target="tpu_custom_call" | custom-call | flops 6000000000 | bytes 6000000 | tf_op jit(solution)/shard_map/pallas_call | solution.py:401
  29.4 1.9 %collective-permute-start.11 = (bf16[128,512]{1,0:T(8,128)(2,1)S(1)}, bf16[128,512]{1,0:T(8,128)(2,1)S(1)}, u32[]{:S(2)}, u32[]{:S(2)}) collective-permute-start(bf16[128,512]{1,0:T(8,128)(2,1)S(1)} %get-tuple-element.75), channel_id=1, source_target_pairs={{0,8},{4,12},{8,0},{12,4},{16,24},{20,28},{24,16},{28,20},{1,9},{5... | collective-permute-start | bytes 393224 | tf_op jit(solution)/shard_map/ppermute | solution.py:21
  31.3 3.7 %collective-permute-done.10.refs_0_ = bf16[80,1024]{1,0:T(8,128)(2,1)S(1)} collective-permute-done((bf16[80,1024]{1,0:T(8,128)(2,1)S(1)}, bf16[80,1024]{1,0:T(8,128)(2,1)S(1)}, u32[]{:S(2)}, u32[]{:S(2)}) %collective-permute-start.10) | collective-permute-done | bytes 163872 | tf_op jit(solution)/shard_map/ppermute | solution.py:21
  35.2 1.6 %collective-permute-start.12 = (bf16[80,1024]{1,0:T(8,128)(2,1)S(1)}, bf16[80,1024]{1,0:T(8,128)(2,1)S(1)}, u32[]{:S(2)}, u32[]{:S(2)}) collective-permute-start(bf16[80,1024]{1,0:T(8,128)(2,1)S(1)} %get-tuple-element.77), channel_id=1, source_target_pairs={{0,8},{4,12},{8,0},{12,4},{16,24},{20,28},{24,16},{28,20},{1,9},{5... | collective-permute-start | bytes 491528 | tf_op jit(solution)/shard_map/ppermute | solution.py:21
  36.9 2.7 %collective-permute-start.13 = (bf16[64,512]{1,0:T(8,128)(2,1)S(1)}, bf16[64,512]{1,0:T(8,128)(2,1)S(1)}, u32[]{:S(2)}, u32[]{:S(2)}) collective-permute-start(bf16[64,512]{1,0:T(8,128)(2,1)S(1)} %get-tuple-element.82), channel_id=1, source_target_pairs={{0,16},{4,20},{8,24},{12,28},{16,0},{20,4},{24,8},{28,12},{1,17},{... | collective-permute-start | bytes 196616 | tf_op jit(solution)/shard_map/ppermute | solution.py:21
  39.5 1.7 %collective-permute-done.12.refs_0_ = bf16[80,1024]{1,0:T(8,128)(2,1)S(1)} collective-permute-done((bf16[80,1024]{1,0:T(8,128)(2,1)S(1)}, bf16[80,1024]{1,0:T(8,128)(2,1)S(1)}, u32[]{:S(2)}, u32[]{:S(2)}) %collective-permute-start.12) | collective-permute-done | bytes 163872 | tf_op jit(solution)/shard_map/ppermute | solution.py:21
  41.4 2.5 %collective-permute-start.14 = (bf16[80,1024]{1,0:T(8,128)(2,1)S(1)}, bf16[80,1024]{1,0:T(8,128)(2,1)S(1)}, u32[]{:S(2)}, u32[]{:S(2)}) collective-permute-start(bf16[80,1024]{1,0:T(8,128)(2,1)S(1)} %get-tuple-element.84), channel_id=1, source_target_pairs={{0,16},{4,20},{8,24},{12,28},{16,0},{20,4},{24,8},{28,12},{1,17},{... | collective-permute-start | bytes 491528 | tf_op jit(solution)/shard_map/ppermute | solution.py:21
  43.9 1.6 %collective-permute-start.16 = (bf16[64,512]{1,0:T(8,128)(2,1)S(1)}, bf16[64,512]{1,0:T(8,128)(2,1)S(1)}, u32[]{:S(2)}, u32[]{:S(2)}) collective-permute-start(bf16[64,512]{1,0:T(8,128)(2,1)S(1)} %get-tuple-element.90.refs_4_), channel_id=1, source_target_pairs={{0,2},{1,3},{2,0},{3,1},{4,6},{5,7},{6,4},{7,5},{8,10},{9,11},{10,... | collective-permute-start | bytes 196616 | tf_op jit(solution)/shard_map/ppermute | solution.py:21
  45.5 2.7 %collective-permute-done.16.refs_6_ = bf16[64,512]{1,0:T(8,128)(2,1)S(1)} collective-permute-done((bf16[64,512]{1,0:T(8,128)(2,1)S(1)}, bf16[64,512]{1,0:T(8,128)(2,1)S(1)}, u32[]{:S(2)}, u32[]{:S(2)}) %collective-permute-start.16) | collective-permute-done | bytes 65568 | tf_op jit(solution)/shard_map/ppermute | solution.py:21
  48.2 2.1 %collective-permute-done.14.refs_0_ = bf16[80,1024]{1,0:T(8,128)(2,1)S(1)} collective-permute-done((bf16[80,1024]{1,0:T(8,128)(2,1)S(1)}, bf16[80,1024]{1,0:T(8,128)(2,1)S(1)}, u32[]{:S(2)}, u32[]{:S(2)}) %collective-permute-start.14) | collective-permute-done | bytes 163872 | tf_op jit(solution)/shard_map/ppermute | solution.py:21
  50.3 2.3 %shard_map.160 = (f32[8,128]{1,0:T(8,128)S(1)}, bf16[256,512]{1,0:T(8,128)(2,1)S(1)}, bf16[256,512]{1,0:T(8,128)(2,1)S(1)}, f32[256,512]{1,0:T(8,128)S(1)}, f32[256,512]{1,0:T(8,128)S(1)}) custom-call(s32[2]{0:T(128)S(1)} %pad_add_fusion.place, f32[8,128]{1,0:T(8,128)S(1)} %get-tuple-element.83.token, bf16[80,1024]{1,0:T(8,128)(2,1)S(1)} %collective-permute-done.14.refs_0_, ...), custom_call_target="tpu_custom_call" | custom-call | flops 2000000000 | bytes 2000000 | tf_op jit(solution)/shard_map/pallas_call | solution.py:401
  52.7 2.5 %shard_map.161 = (f32[8,128]{1,0:T(8,128)S(1)}, f32[64,1024]{1,0:T(8,128)S(1)}, bf16[64,128]{1,0:T(8,128)(2,1)S(1)}, f32[64,128]{1,0:T(8,128)S(1)}) custom-call(s32[2]{0:T(128)S(1)} %pad_add_fusion.1.place, f32[8,128]{1,0:T(8,128)S(1)} %get-tuple-element.89.token, bf16[16,512]{1,0:T(8,128)(2,1)S(1)} %get-tuple-element.66.refs_0_, ...), custom_call_target="tpu_custom_call" | custom-call | flops 2500000000 | bytes 2500000 | tf_op jit(solution)/shard_map/pallas_call | solution.py:401
  55.4 1.7 %shard_map.163 = (f32[8,128]{1,0:T(8,128)S(1)}, bf16[64,512]{1,0:T(8,128)(2,1)S(1)}, bf16[64,512]{1,0:T(8,128)(2,1)S(1)}, f32[64,512]{1,0:T(8,128)S(1)}, f32[64,512]{1,0:T(8,128)S(1)}) custom-call(s32[2]{0:T(128)S(1)} %pad_add_fusion.place, f32[8,128]{1,0:T(8,128)S(1)} %get-tuple-element.94.token, bf16[80,1024]{1,0:T(8,128)(2,1)S(1)} %collective-permute-done.14.refs_0_, ...), custom_call_target="tpu_custom_call" | custom-call | flops 2000000000 | bytes 2000000 | tf_op jit(solution)/shard_map/pallas_call | solution.py:401
  57.7 1.5 %collective-permute-start.23 = (bf16[256,512]{1,0:T(8,128)(2,1)S(1)}, bf16[256,512]{1,0:T(8,128)(2,1)S(1)}, u32[]{:S(2)}, u32[]{:S(2)}) collective-permute-start(bf16[256,512]{1,0:T(8,128)(2,1)S(1)} %get-tuple-element.109), channel_id=1, source_target_pairs={{0,2},{1,3},{2,0},{3,1},{4,6},{5,7},{6,4},{7,5},{8,10},{9,11},{10,... | collective-permute-start | bytes 786440 | tf_op jit(solution)/shard_map/ppermute | solution.py:21
  60.5 7.3 %collective-permute-done.21.refs_2_ = bf16[64,512]{1,0:T(8,128)(2,1)S(1)} collective-permute-done((bf16[64,512]{1,0:T(8,128)(2,1)S(1)}, bf16[64,512]{1,0:T(8,128)(2,1)S(1)}, u32[]{:S(2)}, u32[]{:S(2)}) %collective-permute-start.21) | collective-permute-done | bytes 65568 | tf_op jit(solution)/shard_map/ppermute | solution.py:21
  (74 shorter events, 7.1 us)
Async XLA Ops:
  2.1 5.7 %collective-permute-start = (bf16[8,512]{1,0:T(8,128)(2,1)S(1)}, bf16[8,512]{1,0:T(8,128)(2,1)S(1)}, u32[]{:S(2)}, u32[]{:S(2)}) collective-permute-start(bf16[8,512]{1,0:T(8,128)(2,1)S(1)} %get-tuple-element.58.refs_0_), channel_id=1, source_target_pairs={{0,16},{4,20},{8,24},{12,28},{16,0},{20,4},{24,8},{28,12},{1,17},{... | collective-permute-start | bytes 24584 | tf_op jit(solution)/shard_map/ppermute | solution.py:21
  6.2 11.9 %collective-permute-start.7 = (bf16[256,512]{1,0:T(8,128)(2,1)}, bf16[256,512]{1,0:T(8,128)(2,1)S(1)}, u32[]{:S(2)}, u32[]{:S(2)}) collective-permute-start(bf16[256,512]{1,0:T(8,128)(2,1)} %refs_4_.1), channel_id=1, source_target_pairs={{0,2},{1,3},{2,0},{3,1},{4,6},{5,7},{6,4},{7,5},{8,10},{9,11},{10,... | collective-permute-start | bytes 786440 | tf_op jit(solution)/shard_map/ppermute | solution.py:21
  7.7 15.0 %collective-permute-start.6 = (bf16[256,512]{1,0:T(8,128)(2,1)}, bf16[256,512]{1,0:T(8,128)(2,1)S(1)}, u32[]{:S(2)}, u32[]{:S(2)}) collective-permute-start(bf16[256,512]{1,0:T(8,128)(2,1)} %refs_4_.1), channel_id=1, source_target_pairs={{0,1},{1,0},{2,3},{3,2},{4,5},{5,4},{6,7},{7,6},{8,9},{9,8},{10,11... | collective-permute-start | bytes 786440 | tf_op jit(solution)/shard_map/ppermute | solution.py:21
  7.8 3.7 %collective-permute-start.1 = (bf16[16,512]{1,0:T(8,128)(2,1)S(1)}, bf16[16,512]{1,0:T(8,128)(2,1)S(1)}, u32[]{:S(2)}, u32[]{:S(2)}) collective-permute-start(bf16[16,512]{1,0:T(8,128)(2,1)S(1)} %get-tuple-element.60.refs_0_), channel_id=1, source_target_pairs={{0,8},{4,12},{8,0},{12,4},{16,24},{20,28},{24,16},{28,20},{1,9},{5... | collective-permute-start | bytes 49160 | tf_op jit(solution)/shard_map/ppermute | solution.py:21
  11.6 3.9 %collective-permute-start.2 = (bf16[32,512]{1,0:T(8,128)(2,1)S(1)}, bf16[32,512]{1,0:T(8,128)(2,1)S(1)}, u32[]{:S(2)}, u32[]{:S(2)}) collective-permute-start(bf16[32,512]{1,0:T(8,128)(2,1)S(1)} %get-tuple-element.62.refs_0_), channel_id=1, source_target_pairs={{0,4},{4,0},{8,12},{12,8},{16,20},{20,16},{24,28},{28,24},{1,5},{5... | collective-permute-start | bytes 98312 | tf_op jit(solution)/shard_map/ppermute | solution.py:21
  16.0 4.8 %collective-permute-start.3 = (bf16[16,512]{1,0:T(8,128)(2,1)S(1)}, bf16[16,512]{1,0:T(8,128)(2,1)S(1)}, u32[]{:S(2)}, u32[]{:S(2)}) collective-permute-start(bf16[16,512]{1,0:T(8,128)(2,1)S(1)} %get-tuple-element.66.refs_0_), channel_id=1, source_target_pairs={{0,1},{1,0},{2,3},{3,2},{4,5},{5,4},{6,7},{7,6},{8,9},{9,8},{10,11... | collective-permute-start | bytes 49160 | tf_op jit(solution)/shard_map/ppermute | solution.py:21
  16.1 6.6 %collective-permute-start.4 = (bf16[16,512]{1,0:T(8,128)(2,1)S(1)}, bf16[16,512]{1,0:T(8,128)(2,1)S(1)}, u32[]{:S(2)}, u32[]{:S(2)}) collective-permute-start(bf16[16,512]{1,0:T(8,128)(2,1)S(1)} %get-tuple-element.66.refs_0_), channel_id=1, source_target_pairs={{0,2},{1,3},{2,0},{3,1},{4,6},{5,7},{6,4},{7,5},{8,10},{9,11},{10,... | collective-permute-start | bytes 49160 | tf_op jit(solution)/shard_map/ppermute | solution.py:21
  18.0 4.7 %collective-permute-start.5 = (bf16[16,512]{1,0:T(8,128)(2,1)S(1)}, bf16[16,512]{1,0:T(8,128)(2,1)S(1)}, u32[]{:S(2)}, u32[]{:S(2)}) collective-permute-start(bf16[16,512]{1,0:T(8,128)(2,1)S(1)} %get-tuple-element.66.refs_0_), channel_id=1, source_target_pairs={{0,3},{1,2},{2,1},{3,0},{4,7},{5,6},{6,5},{7,4},{8,11},{9,10},{10,... | collective-permute-start | bytes 49160 | tf_op jit(solution)/shard_map/ppermute | solution.py:21
  18.1 4.6 %collective-permute-start.8 = (bf16[256,512]{1,0:T(8,128)(2,1)S(1)}, bf16[256,512]{1,0:T(8,128)(2,1)S(1)}, u32[]{:S(2)}, u32[]{:S(2)}) collective-permute-start(bf16[256,512]{1,0:T(8,128)(2,1)S(1)} %collective-permute-done.7.refs_6_), channel_id=1, source_target_pairs={{0,1},{1,0},{2,3},{3,2},{4,5},{5,4},{6,7},{7,6},{8,9},{9,8},{10,11... | collective-permute-start | bytes 786440 | tf_op jit(solution)/shard_map/ppermute | solution.py:21
  20.8 8.6 %collective-permute-start.9 = (bf16[256,512]{1,0:T(8,128)(2,1)S(1)}, bf16[256,512]{1,0:T(8,128)(2,1)S(1)}, u32[]{:S(2)}, u32[]{:S(2)}) collective-permute-start(bf16[256,512]{1,0:T(8,128)(2,1)S(1)} %get-tuple-element.69), channel_id=1, source_target_pairs={{0,4},{4,0},{8,12},{12,8},{16,20},{20,16},{24,28},{28,24},{1,5},{5... | collective-permute-start | bytes 786440 | tf_op jit(solution)/shard_map/ppermute | solution.py:21
  29.0 6.1 %collective-permute-start.10 = (bf16[80,1024]{1,0:T(8,128)(2,1)S(1)}, bf16[80,1024]{1,0:T(8,128)(2,1)S(1)}, u32[]{:S(2)}, u32[]{:S(2)}) collective-permute-start(bf16[80,1024]{1,0:T(8,128)(2,1)S(1)} %get-tuple-element.71), channel_id=1, source_target_pairs={{0,4},{4,0},{8,12},{12,8},{16,20},{20,16},{24,28},{28,24},{1,5},{5... | collective-permute-start | bytes 491528 | tf_op jit(solution)/shard_map/ppermute | solution.py:21
  29.4 7.4 %collective-permute-start.11 = (bf16[128,512]{1,0:T(8,128)(2,1)S(1)}, bf16[128,512]{1,0:T(8,128)(2,1)S(1)}, u32[]{:S(2)}, u32[]{:S(2)}) collective-permute-start(bf16[128,512]{1,0:T(8,128)(2,1)S(1)} %get-tuple-element.75), channel_id=1, source_target_pairs={{0,8},{4,12},{8,0},{12,4},{16,24},{20,28},{24,16},{28,20},{1,9},{5... | collective-permute-start | bytes 393224 | tf_op jit(solution)/shard_map/ppermute | solution.py:21
  35.2 6.1 %collective-permute-start.12 = (bf16[80,1024]{1,0:T(8,128)(2,1)S(1)}, bf16[80,1024]{1,0:T(8,128)(2,1)S(1)}, u32[]{:S(2)}, u32[]{:S(2)}) collective-permute-start(bf16[80,1024]{1,0:T(8,128)(2,1)S(1)} %get-tuple-element.77), channel_id=1, source_target_pairs={{0,8},{4,12},{8,0},{12,4},{16,24},{20,28},{24,16},{28,20},{1,9},{5... | collective-permute-start | bytes 491528 | tf_op jit(solution)/shard_map/ppermute | solution.py:21
  36.9 7.0 %collective-permute-start.13 = (bf16[64,512]{1,0:T(8,128)(2,1)S(1)}, bf16[64,512]{1,0:T(8,128)(2,1)S(1)}, u32[]{:S(2)}, u32[]{:S(2)}) collective-permute-start(bf16[64,512]{1,0:T(8,128)(2,1)S(1)} %get-tuple-element.82), channel_id=1, source_target_pairs={{0,16},{4,20},{8,24},{12,28},{16,0},{20,4},{24,8},{28,12},{1,17},{... | collective-permute-start | bytes 196616 | tf_op jit(solution)/shard_map/ppermute | solution.py:21
  41.4 8.9 %collective-permute-start.14 = (bf16[80,1024]{1,0:T(8,128)(2,1)S(1)}, bf16[80,1024]{1,0:T(8,128)(2,1)S(1)}, u32[]{:S(2)}, u32[]{:S(2)}) collective-permute-start(bf16[80,1024]{1,0:T(8,128)(2,1)S(1)} %get-tuple-element.84), channel_id=1, source_target_pairs={{0,16},{4,20},{8,24},{12,28},{16,0},{20,4},{24,8},{28,12},{1,17},{... | collective-permute-start | bytes 491528 | tf_op jit(solution)/shard_map/ppermute | solution.py:21
  43.9 4.3 %collective-permute-start.16 = (bf16[64,512]{1,0:T(8,128)(2,1)S(1)}, bf16[64,512]{1,0:T(8,128)(2,1)S(1)}, u32[]{:S(2)}, u32[]{:S(2)}) collective-permute-start(bf16[64,512]{1,0:T(8,128)(2,1)S(1)} %get-tuple-element.90.refs_4_), channel_id=1, source_target_pairs={{0,2},{1,3},{2,0},{3,1},{4,6},{5,7},{6,4},{7,5},{8,10},{9,11},{10,... | collective-permute-start | bytes 196616 | tf_op jit(solution)/shard_map/ppermute | solution.py:21
  45.5 7.2 %collective-permute-start.15 = (bf16[64,512]{1,0:T(8,128)(2,1)S(1)}, bf16[64,512]{1,0:T(8,128)(2,1)S(1)}, u32[]{:S(2)}, u32[]{:S(2)}) collective-permute-start(bf16[64,512]{1,0:T(8,128)(2,1)S(1)} %get-tuple-element.90.refs_4_), channel_id=1, source_target_pairs={{0,1},{1,0},{2,3},{3,2},{4,5},{5,4},{6,7},{7,6},{8,9},{9,8},{10,11... | collective-permute-start | bytes 196616 | tf_op jit(solution)/shard_map/ppermute | solution.py:21
  48.2 4.5 %collective-permute-start.17 = (bf16[64,512]{1,0:T(8,128)(2,1)S(1)}, bf16[64,512]{1,0:T(8,128)(2,1)S(1)}, u32[]{:S(2)}, u32[]{:S(2)}) collective-permute-start(bf16[64,512]{1,0:T(8,128)(2,1)S(1)} %collective-permute-done.16.refs_6_), channel_id=1, source_target_pairs={{0,1},{1,0},{2,3},{3,2},{4,5},{5,4},{6,7},{7,6},{8,9},{9,8},{10,11... | collective-permute-start | bytes 196616 | tf_op jit(solution)/shard_map/ppermute | solution.py:21
  52.6 2.7 %collective-permute-start.18 = (bf16[256,512]{1,0:T(8,128)(2,1)S(1)}, bf16[256,512]{1,0:T(8,128)(2,1)S(1)}, u32[]{:S(2)}, u32[]{:S(2)}) collective-permute-start(bf16[256,512]{1,0:T(8,128)(2,1)S(1)} %get-tuple-element.93), channel_id=1, source_target_pairs={{0,1},{1,0},{2,3},{3,2},{4,5},{5,4},{6,7},{7,6},{8,9},{9,8},{10,11... | collective-permute-start | bytes 786440 | tf_op jit(solution)/shard_map/ppermute | solution.py:21
  57.1 2.3 %collective-permute-start.19 = (bf16[64,512]{1,0:T(8,128)(2,1)S(1)}, bf16[64,512]{1,0:T(8,128)(2,1)S(1)}, u32[]{:S(2)}, u32[]{:S(2)}) collective-permute-start(bf16[64,512]{1,0:T(8,128)(2,1)S(1)} %get-tuple-element.101), channel_id=1, source_target_pairs={{0,1},{1,0},{2,3},{3,2},{4,5},{5,4},{6,7},{7,6},{8,9},{9,8},{10,11... | collective-permute-start | bytes 196616 | tf_op jit(solution)/shard_map/ppermute | solution.py:21
  57.6 10.9 %collective-permute-start.22 = (bf16[256,512]{1,0:T(8,128)(2,1)S(1)}, bf16[256,512]{1,0:T(8,128)(2,1)S(1)}, u32[]{:S(2)}, u32[]{:S(2)}) collective-permute-start(bf16[256,512]{1,0:T(8,128)(2,1)S(1)} %get-tuple-element.108), channel_id=1, source_target_pairs={{0,1},{1,0},{2,3},{3,2},{4,5},{5,4},{6,7},{7,6},{8,9},{9,8},{10,11... | collective-permute-start | bytes 786440 | tf_op jit(solution)/shard_map/ppermute | solution.py:21
  57.7 10.8 %collective-permute-start.23 = (bf16[256,512]{1,0:T(8,128)(2,1)S(1)}, bf16[256,512]{1,0:T(8,128)(2,1)S(1)}, u32[]{:S(2)}, u32[]{:S(2)}) collective-permute-start(bf16[256,512]{1,0:T(8,128)(2,1)S(1)} %get-tuple-element.109), channel_id=1, source_target_pairs={{0,2},{1,3},{2,0},{3,1},{4,6},{5,7},{6,4},{7,5},{8,10},{9,11},{10,... | collective-permute-start | bytes 786440 | tf_op jit(solution)/shard_map/ppermute | solution.py:21
  59.3 1.3 %collective-permute-start.20 = (bf16[64,512]{1,0:T(8,128)(2,1)S(1)}, bf16[64,512]{1,0:T(8,128)(2,1)S(1)}, u32[]{:S(2)}, u32[]{:S(2)}) collective-permute-start(bf16[64,512]{1,0:T(8,128)(2,1)S(1)} %get-tuple-element.104), channel_id=1, source_target_pairs={{0,1},{1,0},{2,3},{3,2},{4,5},{5,4},{6,7},{7,6},{8,9},{9,8},{10,11... | collective-permute-start | bytes 196616 | tf_op jit(solution)/shard_map/ppermute | solution.py:21
  59.4 8.3 %collective-permute-start.21 = (bf16[64,512]{1,0:T(8,128)(2,1)S(1)}, bf16[64,512]{1,0:T(8,128)(2,1)S(1)}, u32[]{:S(2)}, u32[]{:S(2)}) collective-permute-start(bf16[64,512]{1,0:T(8,128)(2,1)S(1)} %get-tuple-element.105), channel_id=1, source_target_pairs={{0,2},{1,3},{2,0},{3,1},{4,6},{5,7},{6,4},{7,5},{8,10},{9,11},{10,... | collective-permute-start | bytes 196616 | tf_op jit(solution)/shard_map/ppermute | solution.py:21
  (13 other events, 56.1 us)

commit v5 on v4

v5 whole, which is shorter than its diff:
```python
import functools

import jax
import jax.numpy as jnp
from jax import lax
from jax.experimental import pallas as pl
from jax.experimental.pallas import tpu as pltpu
from jax.sharding import PartitionSpec as P

EPS = 1e-05
BF16 = jnp.bfloat16
F32 = jnp.float32
LANES = 128
PARTS = 4
EDGE = 8
MEBI = 1024 * 1024


def swapped(value, axis, bit):
    count = lax.axis_size(axis)
    return lax.ppermute(value, axis, [(i, i ^ bit) for i in range(count)])


def bits_of(axis):
    count = lax.axis_size(axis)
    assert count & (count - 1) == 0
    return [1 << k for k in range(count.bit_length() - 1)]


def dot(a, b):
    return jnp.dot(a, b, preferred_element_type=F32)


def across(a, b, axis):
    return lax.dot_general(a, b, (((axis,), (axis,)), ((), ())), preferred_element_type=F32)


def halves(value):
    high = value.astype(BF16)
    low = (value - high.astype(F32)).astype(BF16)
    return high, low


def iota(shape, axis):
    return lax.broadcasted_iota(jnp.int32, shape, axis)


def spreader(width, channels):
    head = iota((2 * LANES, channels), 0) & (LANES - 1)
    return jnp.where(head == iota((2 * LANES, channels), 1) // width, 1.0, 0.0).astype(BF16)


def widened(per_head, spread):
    high, low = halves(per_head)
    return dot(jnp.concatenate([high, low], axis=1), spread)


def padded(row):
    return jnp.concatenate([row, jnp.zeros((row.shape[0], LANES - row.shape[1]), F32)], axis=1)


def silu(value):
    return value / (1.0 + jnp.exp(-value))


def project_kernel(
    prompt,
    place,
    own,
    over1,
    over2,
    over3,
    gain,
    x_weight,
    bc_weight,
    dt_weight,
    dt_bias,
    x_out,
    bc_out,
    step_out,
    *rest,
):
    normed = rest[-1]
    me = place[0]
    tokens, part = own.shape
    channels, heads = x_weight.shape[1], dt_weight.shape[0]
    blocks = [ref[...].astype(F32) for ref in (own, over1, over2, over3)]
    square = sum(jnp.sum(b * b, axis=1, keepdims=True) for b in blocks)
    factor = lax.rsqrt(square / (PARTS * part) + EPS)
    for r in range(PARTS):
        normed[me ^ r] = (blocks[r] * factor * gain[me ^ r]).astype(BF16)
    fill = jnp.zeros((LANES - heads, PARTS * part), BF16)
    side = jnp.concatenate([bc_weight[...], dt_weight[...], fill], axis=0)
    raw = sum(across(normed[j], side[:, j * part : (j + 1) * part], 1) for j in range(PARTS))
    bc_out[...] = raw[:, :LANES].astype(BF16)
    pre = raw[:, LANES:] + padded(dt_bias[...])
    step_out[...] = jnp.maximum(pre, 0.0) + jnp.log1p(jnp.exp(-jnp.abs(pre)))
    last = 2 * EDGE
    if prompt:
        rest[0][:, channels:] = raw[tokens - last :, :LANES].astype(BF16)
        rest[1][...] = x_weight[...]
    for lane in range(0, channels, 2 * LANES):
        lanes = slice(lane, lane + 2 * LANES)
        raw = sum(dot(normed[j], x_weight[j * part : (j + 1) * part, lanes]) for j in range(PARTS))
        x_out[:, lanes] = raw.astype(BF16)
        if prompt:
            rest[0][:, lanes] = raw[tokens - last :].astype(BF16)


def summed_logs(step_size, decay_log, mask):
    logs = step_size * -jnp.exp(padded(decay_log[...]))
    high, low = halves(logs)
    lowest = (logs - high.astype(F32) - low.astype(F32)).astype(BF16)
    sums = dot(
        jnp.where(mask, 1.0, 0.0).astype(BF16), jnp.concatenate([high, low, lowest], axis=1)
    )
    return sums[:, :LANES] + sums[:, LANES : 2 * LANES] + sums[:, 2 * LANES :]


def joined_taps(conv_bc):
    return jnp.concatenate([conv_bc[:, 0, :], conv_bc[:, 1, :]], axis=1)


def block_mask(tokens, rows):
    t_at = iota((tokens, tokens), 0)
    s_at = iota((tokens, tokens), 1)
    mask = t_at >= s_at
    return mask if rows == 1 else jnp.logical_and(mask, t_at % rows == s_at % rows)


def mixed_rows(rows, heads, x_conv, bc_conv, step_size, cum_log, skip_gain, y_out):
    tokens, channels = x_conv.shape
    width = channels // heads
    state_width = bc_conv.shape[1] // 2
    mask = block_mask(tokens, rows)
    b_rows = bc_conv[:, :state_width].astype(BF16)
    c_rows = bc_conv[:, state_width:].astype(BF16)
    cum_across = cum_log.T
    step_across = step_size.T
    scores = across(c_rows, b_rows, 1)
    spread = spreader(width, channels)
    skip_row = widened(jnp.broadcast_to(padded(skip_gain[...]), (EDGE, LANES)), spread)[:1]
    per_tile = LANES // width
    lane_head = iota((tokens, LANES), 1) // width
    for tile in range(channels // LANES):
        lanes = slice(tile * LANES, (tile + 1) * LANES)
        x_tile = x_conv[:, lanes].astype(F32)
        within = skip_row[:, lanes] * x_tile
        for k in range(per_tile):
            h = tile * per_tile + k
            gaps = cum_log[:, h : h + 1] - cum_across[h : h + 1, :]
            decays = jnp.exp(jnp.where(mask, gaps, -1e30))
            mixing = (scores * decays * step_across[h : h + 1, :]).astype(BF16)
            within += dot(mixing, jnp.where(lane_head == k, x_tile, 0.0).astype(BF16))
        y_out[:, lanes] = within


def packed_message(message_out, total, side):
    state_width, channels = total.shape
    message_out[:state_width, :] = total.astype(BF16)
    high, low = halves(side[:1])
    at = iota((EDGE, channels), 0)
    rows = jnp.where(at == 0, high.astype(F32), jnp.where(at == 1, low.astype(F32), side))
    message_out[state_width:, :] = jnp.concatenate([rows, jnp.zeros_like(rows)], axis=0).astype(BF16)


def unpacked(message, state_width):
    other = message[:state_width, :].astype(F32)
    side = message[state_width:, :].astype(F32)[:EDGE]
    return other, side[0:1] + side[1:2], side


def convolved(joined, edge, raw, taps_of, taps):
    count, lanes = raw.shape
    margin = taps - 1
    joined[:EDGE, :lanes] = edge
    joined[EDGE : EDGE + count, :lanes] = raw
    starts = [EDGE - margin + k for k in range(taps)]
    return silu(sum(taps_of(k) * joined[s : s + count, :lanes] for k, s in enumerate(starts)))


def state_kernel(
    heads,
    place,
    x_raw,
    bc_raw,
    step_size,
    decay_log,
    conv_x,
    conv_bc,
    x_out,
    bc_out,
    cum_out,
    state_out,
    joined,
):
    tokens, channels = x_raw.shape
    state_width = bc_raw.shape[1] // 2
    taps = conv_x.shape[0]
    margin = taps - 1
    bc_taps = joined_taps(conv_bc)
    step_lanes = 2 * LANES
    raw = bc_raw[...].astype(F32)
    none = jnp.zeros((EDGE, step_lanes), F32)
    bc_conv = convolved(joined, none[:, :LANES], raw, lambda k: bc_taps[k : k + 1], taps)
    bc_out[...] = bc_conv.astype(BF16)
    cum_log = summed_logs(step_size[...], decay_log, block_mask(tokens, 1))
    cum_out[...] = cum_log
    spread = spreader(channels // heads, channels)
    to_end = jnp.exp(cum_log[tokens - 1 : tokens] - cum_log) * step_size[...]
    b_turned = bc_conv.T[:state_width]
    b_turned = jnp.where(iota(b_turned.shape, 1) >= margin, b_turned, 0.0).astype(BF16)
    for lane in range(0, channels, step_lanes):
        lanes = slice(lane, lane + step_lanes)
        raw = x_raw[:, lanes].astype(F32)
        x_conv = convolved(joined, none, raw, lambda k: conv_x[k : k + 1, lanes], taps).astype(BF16)
        x_out[:, lanes] = x_conv
        scale = widened(to_end, spread[:, lanes])
        weighted = (x_conv.astype(F32) * scale).astype(BF16)
        state_out[:, lanes] = dot(b_turned, weighted)


def fix_kernel(
    heads,
    place,
    halo,
    x_raw,
    bc_raw,
    step_size,
    cum_log,
    conv_x,
    conv_bc,
    partial,
    x_out,
    bc_out,
    message_out,
    state_out,
    joined,
):
    tokens, channels = x_raw.shape
    state_width = bc_raw.shape[1] // 2
    taps = conv_x.shape[0]
    margin = taps - 1
    last = 2 * EDGE
    edge = halo[...].astype(F32)[EDGE:]
    bc_taps = joined_taps(conv_bc)
    raw = bc_raw[:last, :].astype(F32)
    bc_conv = convolved(joined, edge[:, channels:], raw, lambda k: bc_taps[k : k + 1], taps)
    bc_out[...] = bc_conv.astype(BF16)
    raw = x_raw[:last, :].astype(F32)
    x_conv = convolved(joined, edge[:, :channels], raw, lambda k: conv_x[k : k + 1], taps)
    x_conv = x_conv.astype(BF16)
    x_out[...] = x_conv
    spread = spreader(channels // heads, channels)
    final = cum_log[tokens - 1 : tokens, :]
    to_end = jnp.exp(final - cum_log[:last, :]) * step_size[:last, :]
    both = jnp.concatenate([to_end, jnp.broadcast_to(jnp.exp(final), (last, LANES))], axis=0)
    both = widened(both, spread)
    weighted = (x_conv.astype(F32) * both[:last]).astype(BF16).astype(F32)
    fill = jnp.zeros((LANES - last, LANES), F32)
    b_turned = jnp.concatenate([bc_conv, fill], axis=0).T[:state_width]
    b_turned = jnp.where(iota(b_turned.shape, 1) < margin, b_turned, 0.0).astype(BF16)
    fill = jnp.zeros((LANES - last, channels), F32)
    weighted = jnp.concatenate([weighted, fill], axis=0).astype(BF16)
    total = partial[...] + dot(b_turned, weighted)
    bc_tail = bc_raw[tokens - last :, :].astype(F32)[last - margin :]
    bc_tail = jnp.concatenate([bc_tail, jnp.zeros((margin, channels - LANES), F32)], axis=1)
    x_tail = x_raw[tokens - last :, :].astype(F32)[last - margin :]
    blank = jnp.zeros((EDGE - 1 - 2 * margin, channels), F32)
    side = jnp.concatenate([both[last : last + 1], blank, x_tail, bc_tail], axis=0)
    state_out[:state_width, :] = total
    state_out[state_width:, :] = side
    packed_message(message_out, total, side)


def mix_kernel(
    heads, place, x_head, bc_head, x_rest, bc_rest, step_size, cum_log, skip_gain, y_out, reach_out, bc_out, x_conv
):
    first = x_head.shape[0]
    x_conv[:first, :] = x_head[...]
    x_conv[first:, :] = x_rest[first:, :]
    bc_out[:first, :] = bc_head[...]
    bc_out[first:, :] = bc_rest[first:, :]
    cum_log = cum_log[...]
    reach_out[...] = jnp.exp(cum_log)
    mixed_rows(1, heads, x_conv, bc_out[...].astype(F32), step_size[...], cum_log, skip_gain, y_out)


def step_kernel(first, place, message, state, came, message_out, state_out, came_out):
    later = place[0] > 0
    state_width = state.shape[0] - EDGE
    channels = state.shape[1]
    other, other_decay, other_side = unpacked(message, state_width)
    mine, my_side = state[:state_width, :], state[state_width:, :]
    my_decay = my_side[:1]
    if first:
        before, passed = jnp.zeros_like(mine), jnp.ones_like(my_decay)
    else:
        before, passed = came[:state_width, :], came[state_width : state_width + 1, :]
    came_out[:state_width, :] = jnp.where(later, passed * other + before, before)
    passed = jnp.where(later, passed * other_decay, passed)
    came_out[state_width:, :] = jnp.broadcast_to(passed, (EDGE, channels))
    total = jnp.where(later, my_decay * other + mine, other_decay * mine + other)
    state_out[:state_width, :] = total
    side = jnp.where(later, my_side, other_side)
    side = jnp.where(iota((EDGE, channels), 0) == 0, my_decay * other_decay, side)
    state_out[state_width:, :] = side
    packed_message(message_out, total, side)


def finished(heads, me, incoming, y, bc, reach, gain, weight, outs, full, mixed):
    tokens, channels = y.shape
    part = weight.shape[1] // PARTS
    high, low = halves(incoming)
    blank = jnp.zeros_like(high)
    table = jnp.concatenate([blank, high, blank, low], axis=0)
    twice = jnp.concatenate([bc, bc], axis=1)
    spread = spreader(channels // heads, channels)
    step_lanes = 2 * LANES
    square = jnp.zeros((tokens, 1), F32)
    for lane in range(0, channels, step_lanes):
        lanes = slice(lane, lane + step_lanes)
        total = y[:, lanes] + dot(twice, table[:, lanes]) * widened(reach, spread[:, lanes])
        full[:, lanes] = total
        square = square + jnp.sum(total * total, axis=1, keepdims=True)
    factor = lax.rsqrt(square / channels + EPS)
    mixed[...] = (full[...] * factor * gain[...]).astype(BF16)
    for r, out in zip((3, 1, 2, 0), outs):
        columns = pl.ds(pl.multiple_of((me ^ r) * part, part), part)
        out[...] = dot(mixed[...], weight[:, columns]).astype(out.dtype)


def prompt_back_kernel(
    heads, place, message, came, y, bc, reach, gain, weight, sent3, sent1, kept2, kept0, full, mixed
):
    me, later = place[0], place[1] > 0
    state_width = came.shape[0] - EDGE
    other, _, _ = unpacked(message, state_width)
    before, passed = came[:state_width, :], came[state_width : state_width + 1, :]
    incoming = jnp.where(later, passed * other + before, before)
    outs = (sent3, sent1, kept2, kept0)
    finished(heads, me, incoming, y, bc[...], reach[...], gain, weight, outs, full, mixed)


def decode_back_kernel(
    rows,
    heads,
    place,
    message,
    state,
    x_raw,
    bc_raw,
    step_size,
    decay_log,
    conv_x,
    conv_bc,
    skip_gain,
    gain,
    weight,
    sent3,
    sent1,
    kept2,
    kept0,
    full,
    mixed,
    joined,
    x_conv,
    y,
):
    me, later = place[0], place[1] > 0
    state_width = state.shape[0] - EDGE
    tokens, channels = x_raw.shape
    taps = conv_x.shape[0]
    margin = taps - 1
    other, other_decay, other_side = unpacked(message, state_width)
    mine, my_side = state[:state_width, :], state[state_width:, :]
    incoming = jnp.where(later, my_side[:1] * other + mine, other_decay * mine + other)
    side = jnp.where(later, my_side, other_side)
    x_tail = side[EDGE - 2 * margin : EDGE - margin]
    bc_tail = side[EDGE - margin :, :LANES]

    def convolved(raw, tail, taps_of):
        lanes = raw.shape[1]
        for m in range(margin):
            joined[m * rows : (m + 1) * rows, :lanes] = jnp.broadcast_to(
                tail[m : m + 1], (rows, lanes)
            )
        joined[margin * rows :, :lanes] = raw
        return silu(
            sum(taps_of(k) * joined[k * rows : k * rows + tokens, :lanes] for k in range(taps))
        )

    bc_taps = joined_taps(conv_bc)
    bc_conv = convolved(bc_raw[...].astype(F32), bc_tail, lambda k: bc_taps[k : k + 1])
    step_lanes = 2 * LANES
    for lane in range(0, channels, step_lanes):
        lanes = slice(lane, lane + step_lanes)
        x_conv[:, lanes] = convolved(
            x_raw[:, lanes].astype(F32), x_tail[:, lanes], lambda k: conv_x[k : k + 1, lanes]
        ).astype(BF16)
    cum_log = summed_logs(step_size[...], decay_log, block_mask(tokens, rows))
    mixed_rows(rows, heads, x_conv, bc_conv, step_size[...], cum_log, skip_gain, y)
    bc = bc_conv.astype(BF16)
    outs = (sent3, sent1, kept2, kept0)
    finished(heads, me, incoming, y, bc, jnp.exp(cum_log), gain, weight, outs, full, mixed)


def far_kernel(place, kept, got, out):
    out[...] = (kept[...] + got[...].astype(F32)).astype(BF16)


def total_kernel(rows, place, kept, got, far, dec_kept, dec_got, dec_far, out, dec_out):
    out[...] = (kept[...] + got[...].astype(F32) + far[...].astype(F32)).astype(BF16)
    total = dec_kept[...] + dec_got[...].astype(F32) + dec_far[...].astype(F32)
    asked = total.shape[0]
    steps = asked // rows
    at = iota((asked, asked), 0)
    order = (at % steps) * rows + at // steps == iota((asked, asked), 1)
    total = dot(jnp.where(order, 1.0, 0.0).astype(BF16), total.astype(BF16))
    for r in range(rows):
        dec_out[r] = total[r * steps : (r + 1) * steps].astype(BF16)


def note_kernel(place, ids, note):
    steps = ids.shape[0]
    ids = ids[...]
    digits = [padded(d.astype(F32)) for d in (ids & 255, (ids >> 8) & 255, ids >> 16)]
    top = jnp.concatenate(digits, axis=1)
    note[...] = jnp.concatenate([top, jnp.zeros((EDGE - steps, 3 * LANES), F32)], axis=0).astype(BF16)


def join_kernel(place, mine, got, out):
    out[...] = jnp.concatenate([mine[...].astype(F32), got[...].astype(F32)], axis=0).astype(BF16)


def started(pairs, sems):
    copies = [
        pltpu.make_async_copy(source, target, sems.at[at])
        for at, (source, target) in enumerate(pairs)
    ]
    for copy in copies:
        copy.start()
    return copies


def lookup_kernel(
    steps, rows, place, notes, got, ahead, table_in, kept_out, sent_out, wanted, found, table, sems
):
    chunks, chunk, _ = table.shape
    copies = started(
        [(table_in.at[pl.ds(c * chunk, chunk), :], table.at[c]) for c in range(chunks)], sems
    )
    first = (place[0] * (chunks * chunk)).astype(F32)
    held = jnp.concatenate([notes[...].astype(F32), got[...].astype(F32)], axis=0)
    groups = held.shape[0] // EDGE
    digits = held[:, :LANES] + held[:, LANES : 2 * LANES] * 256.0 + held[:, 2 * LANES : 3 * LANES] * 65536.0
    same = iota((rows, LANES), 0) == iota((rows, LANES), 1)
    for q in range(groups):
        for s in range(steps):
            line = jnp.broadcast_to(digits[q * EDGE + s : q * EDGE + s + 1], (rows, LANES))
            column = jnp.sum(jnp.where(same, line, 0.0), axis=1, keepdims=True) - first
            at = (q * steps + s) * rows
            wanted[at : at + rows, :] = jnp.broadcast_to(column, (rows, LANES))
    asked = groups * steps * rows
    block = min(asked, 256)
    lane = iota((block, LANES), 1).astype(F32)
    for c in range(chunks):
        copies[c].wait()
        for at in range(0, asked, block):
            gap = wanted[at : at + block, :] - lane
            hot = [
                jnp.where(gap == float(c * chunk + k), 1.0, 0.0).astype(BF16)
                for k in range(0, chunk, LANES)
            ]
            term = dot(jnp.concatenate(hot, axis=1), table[c])
            if c == 0:
                found[at : at + block, :] = term
            else:
                found[at : at + block, :] += term
    kept_out[...] = found[: asked // 2, :].astype(BF16)
    sent_out[...] = found[asked // 2 :, :].astype(BF16)


def fold_kernel(place, kept, got, kept_out, sent_out):
    total = (kept[...].astype(F32) + got[...].astype(F32)).astype(BF16)
    half = kept_out.shape[0]
    kept_out[...] = total[:half]
    sent_out[...] = total[half:]


def last_fold_kernel(place, kept, got, out):
    out[...] = (kept[...].astype(F32) + got[...].astype(F32)).astype(BF16)


VMEM = pl.BlockSpec(memory_space=pltpu.VMEM)
SMEM = pl.BlockSpec(memory_space=pltpu.SMEM)
HBM = pl.BlockSpec(memory_space=pltpu.HBM)


class Caller:
    def __init__(self):
        self.token = jnp.zeros((8, LANES), F32)

    def __call__(self, kernel, place, inputs, outs, scratch=(), us=1.0, limit=4, far=()):
        inputs = list(inputs)
        count = len(inputs)

        def ordered(place, token, *refs):
            refs, token_out = list(refs), refs[count]
            del refs[count]
            kernel(place, *refs)
            token_out[...] = jnp.zeros_like(token_out)

        results = pl.pallas_call(
            ordered,
            out_shape=[shaped((8, LANES), F32)] + outs,
            in_specs=[SMEM, VMEM] + [HBM if at in far else VMEM for at in range(count)],
            out_specs=[VMEM] * (1 + len(outs)),
            scratch_shapes=list(scratch),
            compiler_params=pltpu.CompilerParams(vmem_limit_bytes=limit * MEBI),
            cost_estimate=pl.CostEstimate(
                flops=int(us * 1e9), bytes_accessed=int(us * 1e6), transcendentals=0
            ),
        )(place, self.token, *inputs)
        self.token = results[0]
        return results[1:]


def shaped(shape, dtype):
    return jax.ShapeDtypeStruct(shape, dtype)


def on_device(
    prompt_embeds,
    decode_ids,
    embed_table,
    norm_gain,
    x_weight,
    bc_weight,
    dt_weight,
    dt_bias,
    decay_log,
    conv_x,
    conv_bc,
    skip_gain,
    out_gain,
    out_weight,
):
    heads = dt_weight.shape[1]
    assert bc_weight.shape[1] == 1 and lax.axis_size("tp") == PARTS
    channels = x_weight.shape[1]
    taps = conv_x.shape[0]
    margin = taps - 1
    turned_bc = bc_weight.transpose(1, 2, 3, 0).reshape(-1, bc_weight.shape[0])
    turned_dt = dt_weight.T
    state_width = turned_bc.shape[0] // 2
    assert turned_bc.shape[0] == LANES
    tokens, part = prompt_embeds.shape
    rows, steps = decode_ids.shape
    assert steps <= EDGE and rows <= LANES and 2 * margin < EDGE
    asked = rows * steps
    groups = lax.axis_size("ctx")
    me_c = lax.axis_index("ctx").astype(jnp.int32)
    me_t = lax.axis_index("tp").astype(jnp.int32)
    vocab_here = embed_table.shape[0]
    bits = bits_of("ctx")
    assert len(bits) >= 2
    none = jnp.zeros((1,), jnp.int32)
    called = Caller()

    e2 = swapped(prompt_embeds, "tp", 2)
    e1 = swapped(prompt_embeds, "tp", 1)

    e3 = swapped(e2, "tp", 1)

    (notes,) = called(
        note_kernel, none, [decode_ids.T], [shaped((EDGE, 3 * LANES), BF16)], us=2
    )
    halving = [bits[1], bits[0]] + bits[2:]
    for bit in reversed(halving):
        got = swapped(notes, "ctx", bit)
        if bit != halving[0]:
            size = 2 * notes.shape[0]
            (notes,) = called(
                join_kernel, none, [notes, got], [shaped((size, notes.shape[1]), BF16)]
            )

    half = groups * asked // 2
    chunk = max(LANES, vocab_here // 8)
    assert vocab_here % chunk == 0
    kept, sent = called(
        functools.partial(lookup_kernel, steps, rows),
        me_c.reshape(1),
        [notes, got, e2, embed_table],
        [shaped((half, part), BF16), shaped((half, part), BF16)],
        [
            pltpu.VMEM((2 * half, LANES), F32),
            pltpu.VMEM((2 * half, part), F32),
            pltpu.VMEM((vocab_here // chunk, chunk, part), BF16),
            pltpu.SemaphoreType.DMA((vocab_here // chunk,)),
        ],
        us=3.5,
        limit=50,
        far=(3,),
    )

    project_weights = [
        norm_gain.reshape(PARTS, 1, part),
        x_weight,
        turned_bc,
        turned_dt,
        dt_bias.reshape(1, -1),
    ]
    conv_weights = [decay_log.reshape(1, -1), conv_x, conv_bc.reshape(taps, 2, -1)]
    skip_row, gain_row = skip_gain.reshape(1, -1), out_gain.reshape(1, -1)
    packed = state_width + 2 * EDGE

    def project(prompt, blocks, us):
        count = blocks[0].shape[0]
        outs = [
            shaped((count, channels), BF16),
            shaped((count, LANES), BF16),
            shaped((count, LANES), F32),
        ]
        if prompt:
            outs.append(shaped((2 * EDGE, channels + LANES), BF16))
            outs.append(shaped(x_weight.shape, BF16))
        return called(
            functools.partial(project_kernel, prompt),
            me_t.reshape(1),
            blocks + project_weights,
            outs,
            [pltpu.VMEM((PARTS, count, part), BF16)],
            us=us,
            limit=12,
        )

    x_raw, bc_raw, step_size, halo, project_weights[1] = project(True, [prompt_embeds, e1, e2, e3], 3)
    halo = lax.ppermute(halo, "ctx", [(c, c + 1) for c in range(groups - 1)])

    x_rest, bc_rest, cum_log, partial = called(
        functools.partial(state_kernel, heads),
        none,
        [x_raw, bc_raw, step_size] + conv_weights,
        [
            shaped((tokens, channels), BF16),
            shaped((tokens, LANES), BF16),
            shaped((tokens, LANES), F32),
            shaped((state_width, channels), F32),
        ],
        [pltpu.VMEM((EDGE + tokens, 2 * LANES), F32)],
        us=2,
        limit=8,
    )
    x_head, bc_head, message, state = called(
        functools.partial(fix_kernel, heads),
        none,
        [halo, x_raw, bc_raw, step_size, cum_log] + conv_weights[1:] + [partial],
        [
            shaped((2 * EDGE, channels), BF16),
            shaped((2 * EDGE, LANES), BF16),
            shaped((packed, channels), BF16),
            shaped((state_width + EDGE, channels), F32),
        ],
        [pltpu.VMEM((3 * EDGE, channels), F32)],
        limit=8,
    )
    came = state
    def folded(kept, got):
        half = kept.shape[0] // 2
        return called(
            fold_kernel,
            none,
            [kept, got],
            [shaped((half, part), BF16), shaped((half, part), BF16)],
            limit=16 if half > 512 else 4,
        )

    y, reach, bc = called(
        functools.partial(mix_kernel, heads),
        none,
        [x_head, bc_head, x_rest, bc_rest, step_size, cum_log, skip_row],
        [
            shaped((tokens, channels), F32),
            shaped((tokens, LANES), F32),
            shaped((tokens, LANES), BF16),
        ],
        [pltpu.VMEM((tokens, channels), BF16)],
        us=2.5,
        limit=8,
    )

    for bit, halved in zip(bits, halving):
        embeds = swapped(sent, "ctx", halved)
        if halved == halving[-1]:
            (kept,) = called(last_fold_kernel, none, [kept, embeds], [shaped((asked, part), BF16)])
        else:
            kept, sent = folded(kept, embeds)
        got = swapped(message, "ctx", bit)
        later = ((me_c & bit) != 0).astype(jnp.int32)
        if bit != bits[-1]:
            message, state, came = called(
                functools.partial(step_kernel, bit == bits[0]),
                later.reshape(1),
                [got, state, came],
                [
                    shaped((packed, channels), BF16),
                    shaped((state_width + EDGE, channels), F32),
                    shaped((state_width + EDGE, channels), F32),
                ],
            )
    back_place = jnp.stack([me_t, later])
    near = swapped(kept, "tp", 2)
    over1 = swapped(kept, "tp", 1)
    over3 = swapped(near, "tp", 1)

    def back(kernel, count, inputs, scratch, us):
        return called(
            kernel,
            back_place,
            [got] + inputs + [gain_row, out_weight],
            [shaped((count, part), BF16)] * 2 + [shaped((count, part), F32)] * 2,
            [pltpu.VMEM((count, channels), F32), pltpu.VMEM((count, channels), BF16)] + scratch,
            us=us,
            limit=12,
        )

    def crossed(sent3, sent1, kept2, kept0):
        got3 = swapped(sent3, "tp", 1)
        got1 = swapped(sent1, "tp", 1)
        (far,) = called(far_kernel, none, [kept2, got3], [shaped(kept2.shape, BF16)])
        return kept0, got1, swapped(far, "tp", 2)

    prompt_back = back(
        functools.partial(prompt_back_kernel, heads), tokens, [came, y, bc, reach], [], 2
    )
    dec_x_raw, dec_bc_raw, dec_step = project(False, [kept, over1, near, over3], 1.5)
    prompt_crossed = crossed(*prompt_back)
    decode_back = back(
        functools.partial(decode_back_kernel, rows, heads),
        asked,
        [state, dec_x_raw, dec_bc_raw, dec_step] + conv_weights + [skip_row],
        [
            pltpu.VMEM((margin * rows + asked, 2 * LANES), F32),
            pltpu.VMEM((asked, channels), BF16),
            pltpu.VMEM((asked, channels), F32),
        ],
        2.5,
    )
    decode_crossed = crossed(*decode_back)
    prompt_out, decode_out = called(
        functools.partial(total_kernel, rows),
        none,
        [*prompt_crossed, *decode_crossed],
        [shaped((tokens, part), BF16), shaped((rows, steps, part), BF16)],
    )
    return (prompt_out, decode_out)


def solution(mesh):
    return jax.shard_map(
        on_device,
        mesh=mesh,
        in_specs=(
            P("ctx", "tp"),
            P("ctx", None),
            P("ctx", "tp"),
            P(),
            P(None, "tp"),
            P(None, "tp", None, None),
            P(None, "tp"),
            P("tp"),
            P("tp"),
            P(None, "tp"),
            P(None, "tp", None, None),
            P("tp"),
            P("tp"),
            P("tp", None),
        ),
        out_specs=(P("ctx", "tp"), P("ctx", None, "tp")),
        check_vma=False,
    )
```

time: 69.5 us -> 67.2 us (0.967)
  waiting for transfers between devices: 21.9 us -> 19.9 us
  starting transfers between devices: 27.2 us -> 28.3 us
    ppermute x0 -> x1, starting transfers between devices: none -> 3.59 us  [on_device(): halo = lax.ppermute(halo, 'ctx', [(c, c + 1) for c in range(groups - 1)])]
    ppermute x24 -> x21, starting transfers between devices: 27.2 us -> 24.7 us  [swapped(): return lax.ppermute(value, axis, [(i, i ^ bit) for i in range(count)])]
    ppermute x24 -> x21, waiting for transfers between devices: 21.9 us -> 19.9 us  [swapped(): return lax.ppermute(value, axis, [(i, i ^ bit) for i in range(count)])]
    pallas_call x18 -> x19, Pallas kernels: 17.6 us -> 17.1 us  [__call__(): pl.pallas_call(ordered, out_shape=[shaped((8, LANES), F32)] + outs, in_sp...]
  transfers between devices with their start and end apart: 24 -> 22, of which waited for: 10 -> 11; matrix products, arithmetic and copies ran while one was open for 1% -> 0% of each run, Pallas kernels for 21% -> 24%
where the time goes in v5:
time: 67.2 us; the launch traced here: 67 us
  starting transfers between devices  28.3 us (42%)
  waiting for transfers between devices  19.9 us (30%)
  Pallas kernels  17.1 us (25%)
  between operations  0.93 us (1%)
  local copies, waits for them, and re-layouts  0.75 us (1%)
    ppermute x21, starting transfers between devices, swapped(): return lax.ppermute(value, axis, [(i, i ^ bit) for i in range(count)])  24.7 us
    ppermute x21, waiting for transfers between devices, swapped(): return lax.ppermute(value, axis, [(i, i ^ bit) for i in range(count)])  19.9 us
    pallas_call x19, Pallas kernels, __call__(): pl.pallas_call(ordered, out_shape=[shaped((8, LANES), F32)] + outs, in_sp...  17.1 us
    ppermute x1, starting transfers between devices, on_device(): halo = lax.ppermute(halo, 'ctx', [(c, c + 1) for c in range(groups - 1)])  3.59 us
  transfers between devices with their start and end apart: 22, of which 11 were waited for; matrix products, arithmetic and copies ran while one was open for 0% of the time, Pallas kernels for 24%

profile of v5, /device:TPU:0, one launch (start us, length us, event | category | flops | bytes accessed | tf_op | source)
XLA Modules:
  0.0 67.0 jit_solution(9092007997291197280)
XLA Ops:
  0.6 3.0 %collective-permute-start.3 = (bf16[256,512]{1,0:T(8,128)(2,1)}, bf16[256,512]{1,0:T(8,128)(2,1)S(1)}, u32[]{:S(2)}, u32[]{:S(2)}) collective-permute-start(bf16[256,512]{1,0:T(8,128)(2,1)} %refs_0_.1), channel_id=1, source_target_pairs={{0,2},{1,3},{2,0},{3,1},{4,6},{5,7},{6,4},{7,5},{8,10},{9,11},{10,... | collective-permute-start | bytes 786440 | tf_op jit(solution)/shard_map/ppermute | solution.py:21
  4.4 2.7 %collective-permute-start = (bf16[8,384]{1,0:T(8,128)(2,1)S(1)}, bf16[8,384]{1,0:T(8,128)(2,1)S(1)}, u32[]{:S(2)}, u32[]{:S(2)}) collective-permute-start(bf16[8,384]{1,0:T(8,128)(2,1)S(1)} %get-tuple-element.68.refs_0_), channel_id=1, source_target_pairs={{0,16},{4,20},{8,24},{12,28},{16,0},{20,4},{24,8},{28,12},{1,17},{... | collective-permute-start | bytes 18440 | tf_op jit(solution)/shard_map/ppermute | solution.py:21
  7.0 1.9 %collective-permute-done.refs_1_ = bf16[8,384]{1,0:T(8,128)(2,1)S(1)} collective-permute-done((bf16[8,384]{1,0:T(8,128)(2,1)S(1)}, bf16[8,384]{1,0:T(8,128)(2,1)S(1)}, u32[]{:S(2)}, u32[]{:S(2)}) %collective-permute-start) | collective-permute-done | bytes 6176 | tf_op jit(solution)/shard_map/ppermute | solution.py:21
  9.0 1.5 %collective-permute-start.1 = (bf16[16,384]{1,0:T(8,128)(2,1)S(1)}, bf16[16,384]{1,0:T(8,128)(2,1)S(1)}, u32[]{:S(2)}, u32[]{:S(2)}) collective-permute-start(bf16[16,384]{1,0:T(8,128)(2,1)S(1)} %get-tuple-element.70.refs_0_), channel_id=1, source_target_pairs={{0,4},{4,0},{8,12},{12,8},{16,20},{20,16},{24,28},{28,24},{1,5},{5... | collective-permute-start | bytes 36872 | tf_op jit(solution)/shard_map/ppermute | solution.py:21
  10.4 2.2 %collective-permute-done.1.refs_1_ = bf16[16,384]{1,0:T(8,128)(2,1)S(1)} collective-permute-done((bf16[16,384]{1,0:T(8,128)(2,1)S(1)}, bf16[16,384]{1,0:T(8,128)(2,1)S(1)}, u32[]{:S(2)}, u32[]{:S(2)}) %collective-permute-start.1) | collective-permute-done | bytes 12320 | tf_op jit(solution)/shard_map/ppermute | solution.py:21
  12.7 1.6 %collective-permute-start.2 = (bf16[32,384]{1,0:T(8,128)(2,1)S(1)}, bf16[32,384]{1,0:T(8,128)(2,1)S(1)}, u32[]{:S(2)}, u32[]{:S(2)}) collective-permute-start(bf16[32,384]{1,0:T(8,128)(2,1)S(1)} %get-tuple-element.72.refs_0_), channel_id=1, source_target_pairs={{0,8},{4,12},{8,0},{12,4},{16,24},{20,28},{24,16},{28,20},{1,9},{5... | collective-permute-start | bytes 73736 | tf_op jit(solution)/shard_map/ppermute | solution.py:21
  14.7 1.7 %collective-permute-done.2.refs_1_ = bf16[32,384]{1,0:T(8,128)(2,1)S(1)} collective-permute-done((bf16[32,384]{1,0:T(8,128)(2,1)S(1)}, bf16[32,384]{1,0:T(8,128)(2,1)S(1)}, u32[]{:S(2)}, u32[]{:S(2)}) %collective-permute-start.2) | collective-permute-done | bytes 24608 | tf_op jit(solution)/shard_map/ppermute | solution.py:21
  16.5 4.0 %shard_map.152 = (f32[8,128]{1,0:T(8,128)S(1)}, bf16[256,512]{1,0:T(8,128)(2,1)S(1)}, bf16[256,512]{1,0:T(8,128)(2,1)S(1)}) custom-call(s32[1]{0:T(128)} %bitcast.4.place, f32[8,128]{1,0:T(8,128)S(1)} %get-tuple-element.71.token, bf16[32,384]{1,0:T(8,128)(2,1)S(1)} %get-tuple-element.72.refs_0_, bf16[32,384]{1,0:T(8,128)(2,1)S(1)} %collective-permute-done.2.refs_1_, ...), custom_call_target="tpu_custom_call" | custom-call | flops 3500000000 | bytes 3500000 | tf_op jit(solution)/shard_map/pallas_call | solution.py:514
  20.5 1.6 %collective-permute-start.7 = (bf16[256,512]{1,0:T(8,128)(2,1)S(1)}, bf16[256,512]{1,0:T(8,128)(2,1)S(1)}, u32[]{:S(2)}, u32[]{:S(2)}) collective-permute-start(bf16[256,512]{1,0:T(8,128)(2,1)S(1)} %get-tuple-element.89), channel_id=1, source_target_pairs={{0,8},{4,12},{8,0},{12,4},{16,24},{20,28},{24,16},{28,20},{1,9},{5... | collective-permute-start | bytes 786440 | tf_op jit(solution)/shard_map/ppermute | solution.py:21
  22.2 2.4 %shard_map.153 = (f32[8,128]{1,0:T(8,128)S(1)}, bf16[256,1024]{1,0:T(8,128)(2,1)S(1)}, bf16[256,128]{1,0:T(8,128)(2,1)S(1)}, f32[256,128]{1,0:T(8,128)S(1)}, bf1...) custom-call(s32[1]{0:T(128)} %bitcast.place, f32[8,128]{1,0:T(8,128)S(1)} %get-tuple-element.73.token, ...), custom_call_target="tpu_custom_call" | custom-call | flops 3000000000 | bytes 3000000 | tf_op jit(solution)/shard_map/pallas_call | solution.py:514
  24.6 3.6 %collective-permute-start.6 = (bf16[16,1152]{1,0:T(8,128)(2,1)S(1)}, bf16[16,1152]{1,0:T(8,128)(2,1)S(1)}, u32[]{:S(2)}, u32[]{:S(2)}) collective-permute-start(bf16[16,1152]{1,0:T(8,128)(2,1)S(1)} %get-tuple-element.79), channel_id=1, source_target_pairs={{0,4},{4,8},{8,12},{12,16},{16,20},{20,24},{24,28},{1,5},{5,9},{9,... | collective-permute-start | bytes 110600 | tf_op jit(solution)/shard_map/ppermute | solution.py:639
  28.2 1.9 %shard_map.154 = (f32[8,128]{1,0:T(8,128)S(1)}, bf16[256,1024]{1,0:T(8,128)(2,1)S(1)}, bf16[256,128]{1,0:T(8,128)(2,1)S(1)}, f32[256,128]{1,0:T(8,128)S(1)}, f32[64,1024]{1,0:T(8,128)S(1)}) custom-call(s32[1]{0:T(128)} %constant.3.clone.1.place, f32[8,128]{1,0:T(8,128)S(1)} %get-tuple-element.74.token, ...), custom_call_target="tpu_custom_call" | custom-call | flops 2000000000 | bytes 2000000 | tf_op jit(solution)/shard_map/pallas_call | solution.py:514
  30.5 2.2 %collective-permute-start.8 = (bf16[80,1024]{1,0:T(8,128)(2,1)S(1)}, bf16[80,1024]{1,0:T(8,128)(2,1)S(1)}, u32[]{:S(2)}, u32[]{:S(2)}) collective-permute-start(bf16[80,1024]{1,0:T(8,128)(2,1)S(1)} %get-tuple-element.91), channel_id=1, source_target_pairs={{0,4},{4,0},{8,12},{12,8},{16,20},{20,16},{24,28},{28,24},{1,5},{5... | collective-permute-start | bytes 491528 | tf_op jit(solution)/shard_map/ppermute | solution.py:21
  32.8 1.4 %shard_map.156 = (f32[8,128]{1,0:T(8,128)S(1)}, f32[256,1024]{1,0:T(8,128)S(1)}, f32[256,128]{1,0:T(8,128)S(1)}, bf16[256,128]{1,0:T(8,128)(2,1)S(1)}) custom-call(s32[1]{0:T(128)} %constant.3.clone.1.place, f32[8,128]{1,0:T(8,128)S(1)} %get-tuple-element.82.token, bf16[16,1024]{1,0:T(8,128)(2,1)S(1)} %get-tuple-element.83.refs_0_, ...), custom_call_target="tpu_custom_call" | custom-call | flops 2500000000 | bytes 2500000 | tf_op jit(solution)/shard_map/pallas_call | solution.py:514
  34.4 1.7 %collective-permute-done.8.refs_0_ = bf16[80,1024]{1,0:T(8,128)(2,1)S(1)} collective-permute-done((bf16[80,1024]{1,0:T(8,128)(2,1)S(1)}, bf16[80,1024]{1,0:T(8,128)(2,1)S(1)}, u32[]{:S(2)}, u32[]{:S(2)}) %collective-permute-start.8) | collective-permute-done | bytes 163872 | tf_op jit(solution)/shard_map/ppermute | solution.py:21
  36.2 1.5 %collective-permute-start.10 = (bf16[80,1024]{1,0:T(8,128)(2,1)S(1)}, bf16[80,1024]{1,0:T(8,128)(2,1)S(1)}, u32[]{:S(2)}, u32[]{:S(2)}) collective-permute-start(bf16[80,1024]{1,0:T(8,128)(2,1)S(1)} %get-tuple-element.97), channel_id=1, source_target_pairs={{0,8},{4,12},{8,0},{12,4},{16,24},{20,28},{24,16},{28,20},{1,9},{5... | collective-permute-start | bytes 491528 | tf_op jit(solution)/shard_map/ppermute | solution.py:21
  37.7 1.6 %collective-permute-done.9.refs_1_ = bf16[128,512]{1,0:T(8,128)(2,1)S(1)} collective-permute-done((bf16[128,512]{1,0:T(8,128)(2,1)S(1)}, bf16[128,512]{1,0:T(8,128)(2,1)S(1)}, u32[]{:S(2)}, u32[]{:S(2)}) %collective-permute-start.9) | collective-permute-done | bytes 131104 | tf_op jit(solution)/shard_map/ppermute | solution.py:21
  39.4 2.6 %collective-permute-start.11 = (bf16[64,512]{1,0:T(8,128)(2,1)S(1)}, bf16[64,512]{1,0:T(8,128)(2,1)S(1)}, u32[]{:S(2)}, u32[]{:S(2)}) collective-permute-start(bf16[64,512]{1,0:T(8,128)(2,1)S(1)} %get-tuple-element.102), channel_id=1, source_target_pairs={{0,16},{4,20},{8,24},{12,28},{16,0},{20,4},{24,8},{28,12},{1,17},{... | collective-permute-start | bytes 196616 | tf_op jit(solution)/shard_map/ppermute | solution.py:21
  42.8 3.0 %collective-permute-start.12 = (bf16[80,1024]{1,0:T(8,128)(2,1)S(1)}, bf16[80,1024]{1,0:T(8,128)(2,1)S(1)}, u32[]{:S(2)}, u32[]{:S(2)}) collective-permute-start(bf16[80,1024]{1,0:T(8,128)(2,1)S(1)} %get-tuple-element.104), channel_id=1, source_target_pairs={{0,16},{4,20},{8,24},{12,28},{16,0},{20,4},{24,8},{28,12},{1,17},{... | collective-permute-start | bytes 491528 | tf_op jit(solution)/shard_map/ppermute | solution.py:21
  46.5 4.4 %collective-permute-done.12.refs_0_ = bf16[80,1024]{1,0:T(8,128)(2,1)S(1)} collective-permute-done((bf16[80,1024]{1,0:T(8,128)(2,1)S(1)}, bf16[80,1024]{1,0:T(8,128)(2,1)S(1)}, u32[]{:S(2)}, u32[]{:S(2)}) %collective-permute-start.12) | collective-permute-done | bytes 163872 | tf_op jit(solution)/shard_map/ppermute | solution.py:21
  50.9 2.3 %shard_map.162 = (f32[8,128]{1,0:T(8,128)S(1)}, bf16[256,512]{1,0:T(8,128)(2,1)S(1)}, bf16[256,512]{1,0:T(8,128)(2,1)S(1)}, f32[256,512]{1,0:T(8,128)S(1)}, f32[256,512]{1,0:T(8,128)S(1)}) custom-call(s32[2]{0:T(128)S(1)} %pad_add_fusion.place, f32[8,128]{1,0:T(8,128)S(1)} %get-tuple-element.103.token, bf16[80,1024]{1,0:T(8,128)(2,1)S(1)} %collective-permute-done.12.refs_0_, ...), custom_call_target="tpu_custom_call" | custom-call | flops 2000000000 | bytes 2000000 | tf_op jit(solution)/shard_map/pallas_call | solution.py:514
  56.8 2.2 %shard_map.165 = (f32[8,128]{1,0:T(8,128)S(1)}, bf16[64,512]{1,0:T(8,128)(2,1)S(1)}, bf16[64,512]{1,0:T(8,128)(2,1)S(1)}, f32[64,512]{1,0:T(8,128)S(1)}, f32[64,512]{1,0:T(8,128)S(1)}) custom-call(s32[2]{0:T(128)S(1)} %pad_add_fusion.place, f32[8,128]{1,0:T(8,128)S(1)} %get-tuple-element.115.token, bf16[80,1024]{1,0:T(8,128)(2,1)S(1)} %collective-permute-done.12.refs_0_, ...), custom_call_target="tpu_custom_call" | custom-call | flops 2500000000 | bytes 2500000 | tf_op jit(solution)/shard_map/pallas_call | solution.py:514
  60.3 1.6 %collective-permute-start.21 = (bf16[64,512]{1,0:T(8,128)(2,1)S(1)}, bf16[64,512]{1,0:T(8,128)(2,1)S(1)}, u32[]{:S(2)}, u32[]{:S(2)}) collective-permute-start(bf16[64,512]{1,0:T(8,128)(2,1)S(1)} %get-tuple-element.129), channel_id=1, source_target_pairs={{0,2},{1,3},{2,0},{3,1},{4,6},{5,7},{6,4},{7,5},{8,10},{9,11},{10,... | collective-permute-start | bytes 196616 | tf_op jit(solution)/shard_map/ppermute | solution.py:21
  61.9 4.1 %collective-permute-done.21.refs_5_ = bf16[64,512]{1,0:T(8,128)(2,1)S(1)} collective-permute-done((bf16[64,512]{1,0:T(8,128)(2,1)S(1)}, bf16[64,512]{1,0:T(8,128)(2,1)S(1)}, u32[]{:S(2)}, u32[]{:S(2)}) %collective-permute-start.21) | collective-permute-done | bytes 65568 | tf_op jit(solution)/shard_map/ppermute | solution.py:21
  (71 shorter events, 9.3 us)
Async XLA Ops:
  0.6 13.6 %collective-permute-start.3 = (bf16[256,512]{1,0:T(8,128)(2,1)}, bf16[256,512]{1,0:T(8,128)(2,1)S(1)}, u32[]{:S(2)}, u32[]{:S(2)}) collective-permute-start(bf16[256,512]{1,0:T(8,128)(2,1)} %refs_0_.1), channel_id=1, source_target_pairs={{0,2},{1,3},{2,0},{3,1},{4,6},{5,7},{6,4},{7,5},{8,10},{9,11},{10,... | collective-permute-start | bytes 786440 | tf_op jit(solution)/shard_map/ppermute | solution.py:21
  4.4 4.6 %collective-permute-start = (bf16[8,384]{1,0:T(8,128)(2,1)S(1)}, bf16[8,384]{1,0:T(8,128)(2,1)S(1)}, u32[]{:S(2)}, u32[]{:S(2)}) collective-permute-start(bf16[8,384]{1,0:T(8,128)(2,1)S(1)} %get-tuple-element.68.refs_0_), channel_id=1, source_target_pairs={{0,16},{4,20},{8,24},{12,28},{16,0},{20,4},{24,8},{28,12},{1,17},{... | collective-permute-start | bytes 18440 | tf_op jit(solution)/shard_map/ppermute | solution.py:21
  9.0 3.7 %collective-permute-start.1 = (bf16[16,384]{1,0:T(8,128)(2,1)S(1)}, bf16[16,384]{1,0:T(8,128)(2,1)S(1)}, u32[]{:S(2)}, u32[]{:S(2)}) collective-permute-start(bf16[16,384]{1,0:T(8,128)(2,1)S(1)} %get-tuple-element.70.refs_0_), channel_id=1, source_target_pairs={{0,4},{4,0},{8,12},{12,8},{16,20},{20,16},{24,28},{28,24},{1,5},{5... | collective-permute-start | bytes 36872 | tf_op jit(solution)/shard_map/ppermute | solution.py:21
  12.7 3.8 %collective-permute-start.2 = (bf16[32,384]{1,0:T(8,128)(2,1)S(1)}, bf16[32,384]{1,0:T(8,128)(2,1)S(1)}, u32[]{:S(2)}, u32[]{:S(2)}) collective-permute-start(bf16[32,384]{1,0:T(8,128)(2,1)S(1)} %get-tuple-element.72.refs_0_), channel_id=1, source_target_pairs={{0,8},{4,12},{8,0},{12,4},{16,24},{20,28},{24,16},{28,20},{1,9},{5... | collective-permute-start | bytes 73736 | tf_op jit(solution)/shard_map/ppermute | solution.py:21
  14.2 7.9 %collective-permute-start.4 = (bf16[256,512]{1,0:T(8,128)(2,1)S(1)}, bf16[256,512]{1,0:T(8,128)(2,1)S(1)}, u32[]{:S(2)}, u32[]{:S(2)}) collective-permute-start(bf16[256,512]{1,0:T(8,128)(2,1)S(1)} %copy-done.3), channel_id=1, source_target_pairs={{0,1},{1,0},{2,3},{3,2},{4,5},{5,4},{6,7},{7,6},{8,9},{9,8},{10,11... | collective-permute-start | bytes 786440 | tf_op jit(solution)/shard_map/ppermute | solution.py:21
  14.2 7.9 %collective-permute-start.5 = (bf16[256,512]{1,0:T(8,128)(2,1)S(1)}, bf16[256,512]{1,0:T(8,128)(2,1)S(1)}, u32[]{:S(2)}, u32[]{:S(2)}) collective-permute-start(bf16[256,512]{1,0:T(8,128)(2,1)S(1)} %collective-permute-done.3.refs_2_), channel_id=1, source_target_pairs={{0,1},{1,0},{2,3},{3,2},{4,5},{5,4},{6,7},{7,6},{8,9},{9,8},{10,11... | collective-permute-start | bytes 786440 | tf_op jit(solution)/shard_map/ppermute | solution.py:21
  20.5 13.7 %collective-permute-start.7 = (bf16[256,512]{1,0:T(8,128)(2,1)S(1)}, bf16[256,512]{1,0:T(8,128)(2,1)S(1)}, u32[]{:S(2)}, u32[]{:S(2)}) collective-permute-start(bf16[256,512]{1,0:T(8,128)(2,1)S(1)} %get-tuple-element.89), channel_id=1, source_target_pairs={{0,8},{4,12},{8,0},{12,4},{16,24},{20,28},{24,16},{28,20},{1,9},{5... | collective-permute-start | bytes 786440 | tf_op jit(solution)/shard_map/ppermute | solution.py:21
  24.6 5.6 %collective-permute-start.6 = (bf16[16,1152]{1,0:T(8,128)(2,1)S(1)}, bf16[16,1152]{1,0:T(8,128)(2,1)S(1)}, u32[]{:S(2)}, u32[]{:S(2)}) collective-permute-start(bf16[16,1152]{1,0:T(8,128)(2,1)S(1)} %get-tuple-element.79), channel_id=1, source_target_pairs={{0,4},{4,8},{8,12},{12,16},{16,20},{20,24},{24,28},{1,5},{5,9},{9,... | collective-permute-start | bytes 110600 | tf_op jit(solution)/shard_map/ppermute | solution.py:639
  30.5 5.5 %collective-permute-start.8 = (bf16[80,1024]{1,0:T(8,128)(2,1)S(1)}, bf16[80,1024]{1,0:T(8,128)(2,1)S(1)}, u32[]{:S(2)}, u32[]{:S(2)}) collective-permute-start(bf16[80,1024]{1,0:T(8,128)(2,1)S(1)} %get-tuple-element.91), channel_id=1, source_target_pairs={{0,4},{4,0},{8,12},{12,8},{16,20},{20,16},{24,28},{28,24},{1,5},{5... | collective-permute-start | bytes 491528 | tf_op jit(solution)/shard_map/ppermute | solution.py:21
  34.3 5.0 %collective-permute-start.9 = (bf16[128,512]{1,0:T(8,128)(2,1)S(1)}, bf16[128,512]{1,0:T(8,128)(2,1)S(1)}, u32[]{:S(2)}, u32[]{:S(2)}) collective-permute-start(bf16[128,512]{1,0:T(8,128)(2,1)S(1)} %get-tuple-element.95), channel_id=1, source_target_pairs={{0,4},{4,0},{8,12},{12,8},{16,20},{20,16},{24,28},{28,24},{1,5},{5... | collective-permute-start | bytes 393224 | tf_op jit(solution)/shard_map/ppermute | solution.py:21
  36.2 6.5 %collective-permute-start.10 = (bf16[80,1024]{1,0:T(8,128)(2,1)S(1)}, bf16[80,1024]{1,0:T(8,128)(2,1)S(1)}, u32[]{:S(2)}, u32[]{:S(2)}) collective-permute-start(bf16[80,1024]{1,0:T(8,128)(2,1)S(1)} %get-tuple-element.97), channel_id=1, source_target_pairs={{0,8},{4,12},{8,0},{12,4},{16,24},{20,28},{24,16},{28,20},{1,9},{5... | collective-permute-start | bytes 491528 | tf_op jit(solution)/shard_map/ppermute | solution.py:21
  39.3 11.5 %copy-start.1 = (bf16[1024,2048]{1,0:T(8,128)(2,1)S(1)}, bf16[1024,2048]{1,0:T(8,128)(2,1)}, u32[]{:S(2)}) copy-start(bf16[1024,2048]{1,0:T(8,128)(2,1)} %refs_10_.1) | copy-start | bytes 12582916
  39.4 11.5 %copy-start.8 = (f32[1024]{0:T(1024)S(1)}, f32[1024]{0:T(1024)}, u32[]{:S(2)}) copy-start(f32[1024]{0:T(1024)} %param.26) | copy-start | bytes 12292
  39.4 6.5 %collective-permute-start.11 = (bf16[64,512]{1,0:T(8,128)(2,1)S(1)}, bf16[64,512]{1,0:T(8,128)(2,1)S(1)}, u32[]{:S(2)}, u32[]{:S(2)}) collective-permute-start(bf16[64,512]{1,0:T(8,128)(2,1)S(1)} %get-tuple-element.102), channel_id=1, source_target_pairs={{0,16},{4,20},{8,24},{12,28},{16,0},{20,4},{24,8},{28,12},{1,17},{... | collective-permute-start | bytes 196616 | tf_op jit(solution)/shard_map/ppermute | solution.py:21
  42.8 8.0 %collective-permute-start.12 = (bf16[80,1024]{1,0:T(8,128)(2,1)S(1)}, bf16[80,1024]{1,0:T(8,128)(2,1)S(1)}, u32[]{:S(2)}, u32[]{:S(2)}) collective-permute-start(bf16[80,1024]{1,0:T(8,128)(2,1)S(1)} %get-tuple-element.104), channel_id=1, source_target_pairs={{0,16},{4,20},{8,24},{12,28},{16,0},{20,4},{24,8},{28,12},{1,17},{... | collective-permute-start | bytes 491528 | tf_op jit(solution)/shard_map/ppermute | solution.py:21
  45.9 7.8 %collective-permute-start.14 = (bf16[64,512]{1,0:T(8,128)(2,1)S(1)}, bf16[64,512]{1,0:T(8,128)(2,1)S(1)}, u32[]{:S(2)}, u32[]{:S(2)}) collective-permute-start(bf16[64,512]{1,0:T(8,128)(2,1)S(1)} %get-tuple-element.110.refs_0_), channel_id=1, source_target_pairs={{0,2},{1,3},{2,0},{3,1},{4,6},{5,7},{6,4},{7,5},{8,10},{9,11},{10,... | collective-permute-start | bytes 196616 | tf_op jit(solution)/shard_map/ppermute | solution.py:21
  53.1 3.0 %collective-permute-start.16 = (bf16[256,512]{1,0:T(8,128)(2,1)S(1)}, bf16[256,512]{1,0:T(8,128)(2,1)S(1)}, u32[]{:S(2)}, u32[]{:S(2)}) collective-permute-start(bf16[256,512]{1,0:T(8,128)(2,1)S(1)} %get-tuple-element.114), channel_id=1, source_target_pairs={{0,1},{1,0},{2,3},{3,2},{4,5},{5,4},{6,7},{7,6},{8,9},{9,8},{10,11... | collective-permute-start | bytes 786440 | tf_op jit(solution)/shard_map/ppermute | solution.py:21
  53.2 1.6 %collective-permute-start.13 = (bf16[64,512]{1,0:T(8,128)(2,1)S(1)}, bf16[64,512]{1,0:T(8,128)(2,1)S(1)}, u32[]{:S(2)}, u32[]{:S(2)}) collective-permute-start(bf16[64,512]{1,0:T(8,128)(2,1)S(1)} %get-tuple-element.110.refs_0_), channel_id=1, source_target_pairs={{0,1},{1,0},{2,3},{3,2},{4,5},{5,4},{6,7},{7,6},{8,9},{9,8},{10,11... | collective-permute-start | bytes 196616 | tf_op jit(solution)/shard_map/ppermute | solution.py:21
  53.7 1.3 %collective-permute-start.15 = (bf16[64,512]{1,0:T(8,128)(2,1)S(1)}, bf16[64,512]{1,0:T(8,128)(2,1)S(1)}, u32[]{:S(2)}, u32[]{:S(2)}) collective-permute-start(bf16[64,512]{1,0:T(8,128)(2,1)S(1)} %collective-permute-done.14.refs_2_), channel_id=1, source_target_pairs={{0,1},{1,0},{2,3},{3,2},{4,5},{5,4},{6,7},{7,6},{8,9},{9,8},{10,11... | collective-permute-start | bytes 196616 | tf_op jit(solution)/shard_map/ppermute | solution.py:21
  53.8 8.1 %collective-permute-start.18 = (bf16[256,512]{1,0:T(8,128)(2,1)S(1)}, bf16[256,512]{1,0:T(8,128)(2,1)S(1)}, u32[]{:S(2)}, u32[]{:S(2)}) collective-permute-start(bf16[256,512]{1,0:T(8,128)(2,1)S(1)} %get-tuple-element.125), channel_id=1, source_target_pairs={{0,1},{1,0},{2,3},{3,2},{4,5},{5,4},{6,7},{7,6},{8,9},{9,8},{10,11... | collective-permute-start | bytes 786440 | tf_op jit(solution)/shard_map/ppermute | solution.py:21
  56.2 9.8 %collective-permute-start.19 = (bf16[256,512]{1,0:T(8,128)(2,1)S(1)}, bf16[256,512]{1,0:T(8,128)(2,1)S(1)}, u32[]{:S(2)}, u32[]{:S(2)}) collective-permute-start(bf16[256,512]{1,0:T(8,128)(2,1)S(1)} %get-tuple-element.126), channel_id=1, source_target_pairs={{0,2},{1,3},{2,0},{3,1},{4,6},{5,7},{6,4},{7,5},{8,10},{9,11},{10,... | collective-permute-start | bytes 786440 | tf_op jit(solution)/shard_map/ppermute | solution.py:21
  59.0 1.3 %collective-permute-start.17 = (bf16[64,512]{1,0:T(8,128)(2,1)S(1)}, bf16[64,512]{1,0:T(8,128)(2,1)S(1)}, u32[]{:S(2)}, u32[]{:S(2)}) collective-permute-start(bf16[64,512]{1,0:T(8,128)(2,1)S(1)} %get-tuple-element.122), channel_id=1, source_target_pairs={{0,1},{1,0},{2,3},{3,2},{4,5},{5,4},{6,7},{7,6},{8,9},{9,8},{10,11... | collective-permute-start | bytes 196616 | tf_op jit(solution)/shard_map/ppermute | solution.py:21
  59.1 2.9 %collective-permute-start.20 = (bf16[64,512]{1,0:T(8,128)(2,1)S(1)}, bf16[64,512]{1,0:T(8,128)(2,1)S(1)}, u32[]{:S(2)}, u32[]{:S(2)}) collective-permute-start(bf16[64,512]{1,0:T(8,128)(2,1)S(1)} %get-tuple-element.128), channel_id=1, source_target_pairs={{0,1},{1,0},{2,3},{3,2},{4,5},{5,4},{6,7},{7,6},{8,9},{9,8},{10,11... | collective-permute-start | bytes 196616 | tf_op jit(solution)/shard_map/ppermute | solution.py:21
  60.3 5.7 %collective-permute-start.21 = (bf16[64,512]{1,0:T(8,128)(2,1)S(1)}, bf16[64,512]{1,0:T(8,128)(2,1)S(1)}, u32[]{:S(2)}, u32[]{:S(2)}) collective-permute-start(bf16[64,512]{1,0:T(8,128)(2,1)S(1)} %get-tuple-element.129), channel_id=1, source_target_pairs={{0,2},{1,3},{2,0},{3,1},{4,6},{5,7},{6,4},{7,5},{8,10},{9,11},{10,... | collective-permute-start | bytes 196616 | tf_op jit(solution)/shard_map/ppermute | solution.py:21
  (13 other events, 76.5 us)

commit v6 on v5

--- a/solution.py
+++ b/solution.py
@@ -61,6 +61,16 @@
 
 def silu(value):
     return value / (1.0 + jnp.exp(-value))
+
+
+def started(pairs, sems):
+    copies = [
+        pltpu.make_async_copy(source, target, sems.at[at])
+        for at, (source, target) in enumerate(pairs)
+    ]
+    for copy in copies:
+        copy.start()
+    return copies
 
 
 def project_kernel(
@@ -80,7 +90,14 @@
     step_out,
     *rest,
 ):
-    normed = rest[-1]
+    if prompt:
+        halo_out, normed, chunks, total, sems = rest
+        copies = started(
+            [(x_weight.at[pl.ds(j * chunks.shape[1], chunks.shape[1]), :], chunks.at[j]) for j in range(PARTS)],
+            sems,
+        )
+    else:
+        (normed,) = rest
     me = place[0]
     tokens, part = own.shape
     channels, heads = x_weight.shape[1], dt_weight.shape[0]
@@ -96,15 +113,26 @@
     pre = raw[:, LANES:] + padded(dt_bias[...])
     step_out[...] = jnp.maximum(pre, 0.0) + jnp.log1p(jnp.exp(-jnp.abs(pre)))
     last = 2 * EDGE
-    if prompt:
-        rest[0][:, channels:] = raw[tokens - last :, :LANES].astype(BF16)
-        rest[1][...] = x_weight[...]
-    for lane in range(0, channels, 2 * LANES):
-        lanes = slice(lane, lane + 2 * LANES)
-        raw = sum(dot(normed[j], x_weight[j * part : (j + 1) * part, lanes]) for j in range(PARTS))
-        x_out[:, lanes] = raw.astype(BF16)
-        if prompt:
-            rest[0][:, lanes] = raw[tokens - last :].astype(BF16)
+    step_lanes = 2 * LANES
+    if not prompt:
+        for lane in range(0, channels, step_lanes):
+            lanes = slice(lane, lane + step_lanes)
+            terms = [dot(normed[j], x_weight[j * part : (j + 1) * part, lanes]) for j in range(PARTS)]
+            x_out[:, lanes] = sum(terms).astype(BF16)
+        return
+    halo_out[:, channels:] = raw[tokens - last :, :LANES].astype(BF16)
+    for j in range(PARTS):
+        copies[j].wait()
+        for lane in range(0, channels, step_lanes):
+            lanes = slice(lane, lane + step_lanes)
+            term = dot(normed[j], chunks[j, :, lanes])
+            if j > 0:
+                term = total[:, lanes] + term
+            if j < PARTS - 1:
+                total[:, lanes] = term
+            else:
+                x_out[:, lanes] = term.astype(BF16)
+                halo_out[:, lanes] = term[tokens - last :].astype(BF16)
 
 
 def summed_logs(step_size, decay_log, mask):
@@ -156,18 +184,16 @@
 
 
 def packed_message(message_out, total, side):
-    state_width, channels = total.shape
-    message_out[:state_width, :] = total.astype(BF16)
     high, low = halves(side[:1])
-    at = iota((EDGE, channels), 0)
+    at = iota(side.shape, 0)
     rows = jnp.where(at == 0, high.astype(F32), jnp.where(at == 1, low.astype(F32), side))
-    message_out[state_width:, :] = jnp.concatenate([rows, jnp.zeros_like(rows)], axis=0).astype(BF16)
+    message_out[...] = jnp.concatenate([total, rows], axis=0).astype(BF16)
 
 
 def unpacked(message, state_width):
-    other = message[:state_width, :].astype(F32)
-    side = message[state_width:, :].astype(F32)[:EDGE]
-    return other, side[0:1] + side[1:2], side
+    whole = message[...].astype(F32)
+    side = whole[state_width:]
+    return whole[:state_width], side[0:1] + side[1:2], side
 
 
 def convolved(joined, edge, raw, taps_of, taps):
@@ -310,7 +336,6 @@
 
 def finished(heads, me, incoming, y, bc, reach, gain, weight, outs, full, mixed):
     tokens, channels = y.shape
-    part = weight.shape[1] // PARTS
     high, low = halves(incoming)
     blank = jnp.zeros_like(high)
     table = jnp.concatenate([blank, high, blank, low], axis=0)
@@ -325,21 +350,29 @@
         square = square + jnp.sum(total * total, axis=1, keepdims=True)
     factor = lax.rsqrt(square / channels + EPS)
     mixed[...] = (full[...] * factor * gain[...]).astype(BF16)
-    for r, out in zip((3, 1, 2, 0), outs):
+    sent(me, mixed, weight, zip((3, 1, 2, 0), outs))
+
+
+def sent(me, mixed, weight, wanted):
+    part = weight.shape[1] // PARTS
+    for r, out in wanted:
         columns = pl.ds(pl.multiple_of((me ^ r) * part, part), part)
         out[...] = dot(mixed[...], weight[:, columns]).astype(out.dtype)
 
 
+def rest_kernel(place, mixed, weight, sent1, kept2, kept0):
+    sent(place[0], mixed, weight, ((1, sent1), (2, kept2), (0, kept0)))
+
+
 def prompt_back_kernel(
-    heads, place, message, came, y, bc, reach, gain, weight, sent3, sent1, kept2, kept0, full, mixed
+    heads, place, message, came, y, bc, reach, gain, weight, sent3, mixed, full
 ):
     me, later = place[0], place[1] > 0
     state_width = came.shape[0] - EDGE
     other, _, _ = unpacked(message, state_width)
     before, passed = came[:state_width, :], came[state_width : state_width + 1, :]
     incoming = jnp.where(later, passed * other + before, before)
-    outs = (sent3, sent1, kept2, kept0)
-    finished(heads, me, incoming, y, bc[...], reach[...], gain, weight, outs, full, mixed)
+    finished(heads, me, incoming, y, bc[...], reach[...], gain, weight, (sent3,), full, mixed)
 
 
 def decode_back_kernel(
@@ -433,23 +466,13 @@
     out[...] = jnp.concatenate([mine[...].astype(F32), got[...].astype(F32)], axis=0).astype(BF16)
 
 
-def started(pairs, sems):
-    copies = [
-        pltpu.make_async_copy(source, target, sems.at[at])
-        for at, (source, target) in enumerate(pairs)
-    ]
-    for copy in copies:
-        copy.start()
-    return copies
-
-
-def lookup_kernel(
-    steps, rows, place, notes, got, ahead, table_in, kept_out, sent_out, wanted, found, table, sems
-):
-    chunks, chunk, _ = table.shape
-    copies = started(
-        [(table_in.at[pl.ds(c * chunk, chunk), :], table.at[c]) for c in range(chunks)], sems
-    )
+def hand_kernel(place, mine, got, given, ahead, out, handed):
+    join_kernel(place, mine, got, out)
+
+
+def lookup_kernel(steps, rows, place, notes, got, table, kept_out, sent_out, wanted, found):
+    chunk = min(table.shape[0], 1024)
+    chunks = table.shape[0] // chunk
     first = (place[0] * (chunks * chunk)).astype(F32)
     held = jnp.concatenate([notes[...].astype(F32), got[...].astype(F32)], axis=0)
     groups = held.shape[0] // EDGE
@@ -465,14 +488,13 @@
     block = min(asked, 256)
     lane = iota((block, LANES), 1).astype(F32)
     for c in range(chunks):
-        copies[c].wait()
         for at in range(0, asked, block):
             gap = wanted[at : at + block, :] - lane
             hot = [
                 jnp.where(gap == float(c * chunk + k), 1.0, 0.0).astype(BF16)
                 for k in range(0, chunk, LANES)
             ]
-            term = dot(jnp.concatenate(hot, axis=1), table[c])
+            term = dot(jnp.concatenate(hot, axis=1), table[c * chunk : (c + 1) * chunk, :])
             if c == 0:
                 found[at : at + block, :] = term
             else:
@@ -501,7 +523,7 @@
     def __init__(self):
         self.token = jnp.zeros((8, LANES), F32)
 
-    def __call__(self, kernel, place, inputs, outs, scratch=(), us=1.0, limit=4, far=()):
+    def __call__(self, kernel, place, inputs, outs, scratch=(), us=1.0, limit=4, far=(), same=()):
         inputs = list(inputs)
         count = len(inputs)
 
@@ -517,6 +539,7 @@
             in_specs=[SMEM, VMEM] + [HBM if at in far else VMEM for at in range(count)],
             out_specs=[VMEM] * (1 + len(outs)),
             scratch_shapes=list(scratch),
+            input_output_aliases={2 + at: 1 + out for at, out in same},
             compiler_params=pltpu.CompilerParams(vmem_limit_bytes=limit * MEBI),
             cost_estimate=pl.CostEstimate(
                 flops=int(us * 1e9), bytes_accessed=int(us * 1e6), transcendentals=0
@@ -571,7 +594,6 @@
     e2 = swapped(prompt_embeds, "tp", 2)
     e1 = swapped(prompt_embeds, "tp", 1)
 
-    e3 = swapped(e2, "tp", 1)
 
     (notes,) = called(
         note_kernel, none, [decode_ids.T], [shaped((EDGE, 3 * LANES), BF16)], us=2
@@ -579,30 +601,20 @@
     halving = [bits[1], bits[0]] + bits[2:]
     for bit in reversed(halving):
         got = swapped(notes, "ctx", bit)
-        if bit != halving[0]:
-            size = 2 * notes.shape[0]
-            (notes,) = called(
-                join_kernel, none, [notes, got], [shaped((size, notes.shape[1]), BF16)]
+        joined = shaped((2 * notes.shape[0], notes.shape[1]), BF16)
+        if bit == halving[1]:
+            notes, e2 = called(
+                hand_kernel,
+                none,
+                [notes, got, e2, embed_table],
+                [joined, shaped(e2.shape, BF16)],
+                limit=50,
+                far=(3,),
+                same=((2, 1),),
             )
-
-    half = groups * asked // 2
-    chunk = max(LANES, vocab_here // 8)
-    assert vocab_here % chunk == 0
-    kept, sent = called(
-        functools.partial(lookup_kernel, steps, rows),
-        me_c.reshape(1),
-        [notes, got, e2, embed_table],
-        [shaped((half, part), BF16), shaped((half, part), BF16)],
-        [
-            pltpu.VMEM((2 * half, LANES), F32),
-            pltpu.VMEM((2 * half, part), F32),
-            pltpu.VMEM((vocab_here // chunk, chunk, part), BF16),
-            pltpu.SemaphoreType.DMA((vocab_here // chunk,)),
-        ],
-        us=3.5,
-        limit=50,
-        far=(3,),
-    )
+        elif bit != halving[0]:
+            (notes,) = called(join_kernel, none, [notes, got], [joined])
+    e3 = swapped(e2, "tp", 1)
 
     project_weights = [
         norm_gain.reshape(PARTS, 1, part),
@@ -613,10 +625,11 @@
     ]
     conv_weights = [decay_log.reshape(1, -1), conv_x, conv_bc.reshape(taps, 2, -1)]
     skip_row, gain_row = skip_gain.reshape(1, -1), out_gain.reshape(1, -1)
-    packed = state_width + 2 * EDGE
+    packed = state_width + EDGE
 
     def project(prompt, blocks, us):
         count = blocks[0].shape[0]
+        scratch = []
         outs = [
             shaped((count, channels), BF16),
             shaped((count, LANES), BF16),
@@ -624,19 +637,36 @@
         ]
         if prompt:
             outs.append(shaped((2 * EDGE, channels + LANES), BF16))
-            outs.append(shaped(x_weight.shape, BF16))
+            scratch = [
+                pltpu.VMEM((PARTS, part, channels), BF16),
+                pltpu.VMEM((count, channels), F32),
+                pltpu.SemaphoreType.DMA((PARTS,)),
+            ]
         return called(
             functools.partial(project_kernel, prompt),
             me_t.reshape(1),
             blocks + project_weights,
             outs,
-            [pltpu.VMEM((PARTS, count, part), BF16)],
+            [pltpu.VMEM((PARTS, count, part), BF16)] + scratch,
             us=us,
-            limit=12,
+            limit=50 if prompt else 12,
+            far=(5,) if prompt else (),
         )
 
-    x_raw, bc_raw, step_size, halo, project_weights[1] = project(True, [prompt_embeds, e1, e2, e3], 3)
+    x_raw, bc_raw, step_size, halo = project(True, [prompt_embeds, e1, e2, e3], 3)
     halo = lax.ppermute(halo, "ctx", [(c, c + 1) for c in range(groups - 1)])
+
+    half = groups * asked // 2
+    assert vocab_here % min(vocab_here, 1024) == 0
+    kept, sent = called(
+        functools.partial(lookup_kernel, steps, rows),
+        me_c.reshape(1),
+        [notes, got, embed_table],
+        [shaped((half, part), BF16), shaped((half, part), BF16)],
+        [pltpu.VMEM((2 * half, LANES), F32), pltpu.VMEM((2 * half, part), F32)],
+        us=2.5,
+        limit=32 if half > 512 else 8,
+    )
 
     x_rest, bc_rest, cum_log, partial = called(
         functools.partial(state_kernel, heads),
@@ -731,11 +761,23 @@
         (far,) = called(far_kernel, none, [kept2, got3], [shaped(kept2.shape, BF16)])
         return kept0, got1, swapped(far, "tp", 2)
 
-    prompt_back = back(
-        functools.partial(prompt_back_kernel, heads), tokens, [came, y, bc, reach], [], 2
+    prompt_sent3, prompt_mixed = called(
+        functools.partial(prompt_back_kernel, heads),
+        back_place,
+        [got, came, y, bc, reach, gain_row, out_weight],
+        [shaped((tokens, part), BF16), shaped((tokens, channels), BF16)],
+        [pltpu.VMEM((tokens, channels), F32)],
+        us=1.5,
+        limit=12,
+    )
+    prompt_rest = called(
+        rest_kernel,
+        back_place,
+        [prompt_mixed, out_weight],
+        [shaped((tokens, part), BF16)] + [shaped((tokens, part), F32)] * 2,
     )
     dec_x_raw, dec_bc_raw, dec_step = project(False, [kept, over1, near, over3], 1.5)
-    prompt_crossed = crossed(*prompt_back)
+    prompt_crossed = crossed(prompt_sent3, *prompt_rest)
     decode_back = back(
         functools.partial(decode_back_kernel, rows, heads),
         asked,

time: 67.2 us -> 65.6 us (0.976)
  waiting for transfers between devices: 19.9 us -> 17.6 us
    ppermute x21, waiting for transfers between devices: 19.9 us -> 17.6 us  [swapped(): return lax.ppermute(value, axis, [(i, i ^ bit) for i in range(count)])]
    pallas_call x19 -> x20, Pallas kernels: 17.1 us -> 17.6 us  [__call__(): pl.pallas_call(ordered, out_shape=[shaped((8, LANES), F32)] + outs, in_sp...]
  transfers between devices with their start and end apart: 22 -> 22, of which waited for: 11 -> 8; matrix products, arithmetic and copies ran while one was open for 0% -> 0% of each run, Pallas kernels for 24% -> 25%
where the time goes in v6:
time: 65.6 us; the launch traced here: 65.4 us
  starting transfers between devices  28.4 us (43%)
  Pallas kernels  17.6 us (27%)
  waiting for transfers between devices  17.6 us (27%)
  between operations  0.93 us (1%)
  local copies, waits for them, and re-layouts  0.76 us (1%)
    ppermute x21, starting transfers between devices, swapped(): return lax.ppermute(value, axis, [(i, i ^ bit) for i in range(count)])  24.9 us
    pallas_call x20, Pallas kernels, __call__(): pl.pallas_call(ordered, out_shape=[shaped((8, LANES), F32)] + outs, in_sp...  17.6 us
    ppermute x21, waiting for transfers between devices, swapped(): return lax.ppermute(value, axis, [(i, i ^ bit) for i in range(count)])  17.6 us
    ppermute x1, starting transfers between devices, on_device(): halo = lax.ppermute(halo, 'ctx', [(c, c + 1) for c in range(groups - 1)])  3.58 us
  transfers between devices with their start and end apart: 22, of which 8 were waited for; matrix products, arithmetic and copies ran while one was open for 0% of the time, Pallas kernels for 25%

profile of v6, /device:TPU:0, one launch (start us, length us, event | category | flops | bytes accessed | tf_op | source)
XLA Modules:
  0.0 65.4 jit_solution(3654974200208194284)
XLA Ops:
  0.6 3.0 %collective-permute-start.2 = (bf16[256,512]{1,0:T(8,128)(2,1)}, bf16[256,512]{1,0:T(8,128)(2,1)S(1)}, u32[]{:S(2)}, u32[]{:S(2)}) collective-permute-start(bf16[256,512]{1,0:T(8,128)(2,1)} %refs_0_.1), channel_id=1, source_target_pairs={{0,2},{1,3},{2,0},{3,1},{4,6},{5,7},{6,4},{7,5},{8,10},{9,11},{10,... | collective-permute-start | bytes 786440 | tf_op jit(solution)/shard_map/ppermute | solution.py:21
  4.4 2.7 %collective-permute-start = (bf16[8,384]{1,0:T(8,128)(2,1)S(1)}, bf16[8,384]{1,0:T(8,128)(2,1)S(1)}, u32[]{:S(2)}, u32[]{:S(2)}) collective-permute-start(bf16[8,384]{1,0:T(8,128)(2,1)S(1)} %get-tuple-element.70.refs_0_), channel_id=1, source_target_pairs={{0,16},{4,20},{8,24},{12,28},{16,0},{20,4},{24,8},{28,12},{1,17},{... | collective-permute-start | bytes 18440 | tf_op jit(solution)/shard_map/ppermute | solution.py:21
  7.1 1.9 %collective-permute-done.refs_1_ = bf16[8,384]{1,0:T(8,128)(2,1)S(1)} collective-permute-done((bf16[8,384]{1,0:T(8,128)(2,1)S(1)}, bf16[8,384]{1,0:T(8,128)(2,1)S(1)}, u32[]{:S(2)}, u32[]{:S(2)}) %collective-permute-start) | collective-permute-done | bytes 6176 | tf_op jit(solution)/shard_map/ppermute | solution.py:21
  9.0 1.5 %collective-permute-start.1 = (bf16[16,384]{1,0:T(8,128)(2,1)S(1)}, bf16[16,384]{1,0:T(8,128)(2,1)S(1)}, u32[]{:S(2)}, u32[]{:S(2)}) collective-permute-start(bf16[16,384]{1,0:T(8,128)(2,1)S(1)} %get-tuple-element.72.refs_0_), channel_id=1, source_target_pairs={{0,4},{4,0},{8,12},{12,8},{16,20},{20,16},{24,28},{28,24},{1,5},{5... | collective-permute-start | bytes 36872 | tf_op jit(solution)/shard_map/ppermute | solution.py:21
  10.5 2.2 %collective-permute-done.1.refs_1_ = bf16[16,384]{1,0:T(8,128)(2,1)S(1)} collective-permute-done((bf16[16,384]{1,0:T(8,128)(2,1)S(1)}, bf16[16,384]{1,0:T(8,128)(2,1)S(1)}, u32[]{:S(2)}, u32[]{:S(2)}) %collective-permute-start.1) | collective-permute-done | bytes 12320 | tf_op jit(solution)/shard_map/ppermute | solution.py:21
  12.8 1.6 %collective-permute-start.5 = (bf16[32,384]{1,0:T(8,128)(2,1)S(1)}, bf16[32,384]{1,0:T(8,128)(2,1)S(1)}, u32[]{:S(2)}, u32[]{:S(2)}) collective-permute-start(bf16[32,384]{1,0:T(8,128)(2,1)S(1)} %get-tuple-element.76.refs_0_), channel_id=1, source_target_pairs={{0,8},{4,12},{8,0},{12,4},{16,24},{20,28},{24,16},{28,20},{1,9},{5... | collective-permute-start | bytes 73736 | tf_op jit(solution)/shard_map/ppermute | solution.py:21
  14.5 3.8 %shard_map.152 = (f32[8,128]{1,0:T(8,128)S(1)}, bf16[256,1024]{1,0:T(8,128)(2,1)S(1)}, bf16[256,128]{1,0:T(8,128)(2,1)S(1)}, f32[256,128]{1,0:T(8,128)S(1)}, bf16[16,1152]{1,0:T(8,128)(2,1)S(1)}) custom-call(s32[1]{0:T(128)} %bitcast.place, f32[8,128]{1,0:T(8,128)S(1)} %get-tuple-element.73.token, bf16[256,512]{1,0:T(8,128)(2,1)S(1)} %copy-done.5, ...), custom_call_target="tpu_custom_call" | custom-call | flops 3000000000 | bytes 3000000 | tf_op jit(solution)/shard_map/pallas_call | solution.py:536
  18.3 3.6 %collective-permute-start.6 = (bf16[16,1152]{1,0:T(8,128)(2,1)S(1)}, bf16[16,1152]{1,0:T(8,128)(2,1)S(1)}, u32[]{:S(2)}, u32[]{:S(2)}) collective-permute-start(bf16[16,1152]{1,0:T(8,128)(2,1)S(1)} %get-tuple-element.82), channel_id=1, source_target_pairs={{0,4},{4,8},{8,12},{12,16},{16,20},{20,24},{24,28},{1,5},{5,9},{9,... | collective-permute-start | bytes 110600 | tf_op jit(solution)/shard_map/ppermute | solution.py:657
  21.9 2.4 %shard_map.153 = (f32[8,128]{1,0:T(8,128)S(1)}, bf16[256,512]{1,0:T(8,128)(2,1)S(1)}, bf16[256,512]{1,0:T(8,128)(2,1)S(1)}) custom-call(s32[1]{0:T(128)} %bitcast.4.place, f32[8,128]{1,0:T(8,128)S(1)} %get-tuple-element.75.token, bf16[32,384]{1,0:T(8,128)(2,1)S(1)} %get-tuple-element.76.refs_0_, bf16[32,384]{1,0:T(8,128)(2,1)S(1)} %collective-permute-done.5.refs_1_, ...), custom_call_target="tpu_custom_call" | custom-call | flops 2500000000 | bytes 2500000 | tf_op jit(solution)/shard_map/pallas_call | solution.py:536
  24.3 1.5 %collective-permute-start.7 = (bf16[256,512]{1,0:T(8,128)(2,1)S(1)}, bf16[256,512]{1,0:T(8,128)(2,1)S(1)}, u32[]{:S(2)}, u32[]{:S(2)}) collective-permute-start(bf16[256,512]{1,0:T(8,128)(2,1)S(1)} %get-tuple-element.92), channel_id=1, source_target_pairs={{0,8},{4,12},{8,0},{12,4},{16,24},{20,28},{24,16},{28,20},{1,9},{5... | collective-permute-start | bytes 786440 | tf_op jit(solution)/shard_map/ppermute | solution.py:21
  25.8 1.9 %shard_map.154 = (f32[8,128]{1,0:T(8,128)S(1)}, bf16[256,1024]{1,0:T(8,128)(2,1)S(1)}, bf16[256,128]{1,0:T(8,128)(2,1)S(1)}, f32[256,128]{1,0:T(8,128)S(1)}, f32[64,1024]{1,0:T(8,128)S(1)}) custom-call(s32[1]{0:T(128)} %constant.3.clone.1.place, f32[8,128]{1,0:T(8,128)S(1)} %get-tuple-element.77.token, ...), custom_call_target="tpu_custom_call" | custom-call | flops 2000000000 | bytes 2000000 | tf_op jit(solution)/shard_map/pallas_call | solution.py:536
  28.1 1.8 %collective-permute-start.8 = (bf16[72,1024]{1,0:T(8,128)(2,1)S(1)}, bf16[72,1024]{1,0:T(8,128)(2,1)S(1)}, u32[]{:S(2)}, u32[]{:S(2)}) collective-permute-start(bf16[72,1024]{1,0:T(8,128)(2,1)S(1)} %get-tuple-element.94), channel_id=1, source_target_pairs={{0,4},{4,0},{8,12},{12,8},{16,20},{20,16},{24,28},{28,24},{1,5},{5... | collective-permute-start | bytes 442376 | tf_op jit(solution)/shard_map/ppermute | solution.py:21
  32.6 1.4 %collective-permute-start.9 = (bf16[128,512]{1,0:T(8,128)(2,1)S(1)}, bf16[128,512]{1,0:T(8,128)(2,1)S(1)}, u32[]{:S(2)}, u32[]{:S(2)}) collective-permute-start(bf16[128,512]{1,0:T(8,128)(2,1)S(1)} %get-tuple-element.98), channel_id=1, source_target_pairs={{0,4},{4,0},{8,12},{12,8},{16,20},{20,16},{24,28},{28,24},{1,5},{5... | collective-permute-start | bytes 393224 | tf_op jit(solution)/shard_map/ppermute | solution.py:21
  34.1 1.8 %collective-permute-start.10 = (bf16[72,1024]{1,0:T(8,128)(2,1)S(1)}, bf16[72,1024]{1,0:T(8,128)(2,1)S(1)}, u32[]{:S(2)}, u32[]{:S(2)}) collective-permute-start(bf16[72,1024]{1,0:T(8,128)(2,1)S(1)} %get-tuple-element.100), channel_id=1, source_target_pairs={{0,8},{4,12},{8,0},{12,4},{16,24},{20,28},{24,16},{28,20},{1,9},{5... | collective-permute-start | bytes 442376 | tf_op jit(solution)/shard_map/ppermute | solution.py:21
  35.9 1.7 %collective-permute-done.9.refs_1_ = bf16[128,512]{1,0:T(8,128)(2,1)S(1)} collective-permute-done((bf16[128,512]{1,0:T(8,128)(2,1)S(1)}, bf16[128,512]{1,0:T(8,128)(2,1)S(1)}, u32[]{:S(2)}, u32[]{:S(2)}) %collective-permute-start.9) | collective-permute-done | bytes 131104 | tf_op jit(solution)/shard_map/ppermute | solution.py:21
  37.7 2.6 %collective-permute-start.11 = (bf16[64,512]{1,0:T(8,128)(2,1)S(1)}, bf16[64,512]{1,0:T(8,128)(2,1)S(1)}, u32[]{:S(2)}, u32[]{:S(2)}) collective-permute-start(bf16[64,512]{1,0:T(8,128)(2,1)S(1)} %get-tuple-element.105), channel_id=1, source_target_pairs={{0,16},{4,20},{8,24},{12,28},{16,0},{20,4},{24,8},{28,12},{1,17},{... | collective-permute-start | bytes 196616 | tf_op jit(solution)/shard_map/ppermute | solution.py:21
  40.4 2.4 %collective-permute-start.12 = (bf16[72,1024]{1,0:T(8,128)(2,1)S(1)}, bf16[72,1024]{1,0:T(8,128)(2,1)S(1)}, u32[]{:S(2)}, u32[]{:S(2)}) collective-permute-start(bf16[72,1024]{1,0:T(8,128)(2,1)S(1)} %get-tuple-element.107), channel_id=1, source_target_pairs={{0,16},{4,20},{8,24},{12,28},{16,0},{20,4},{24,8},{28,12},{1,17},{... | collective-permute-start | bytes 442376 | tf_op jit(solution)/shard_map/ppermute | solution.py:21
  42.9 3.0 %collective-permute-done.11.refs_1_ = bf16[64,512]{1,0:T(8,128)(2,1)S(1)} collective-permute-done((bf16[64,512]{1,0:T(8,128)(2,1)S(1)}, bf16[64,512]{1,0:T(8,128)(2,1)S(1)}, u32[]{:S(2)}, u32[]{:S(2)}) %collective-permute-start.11) | collective-permute-done | bytes 65568 | tf_op jit(solution)/shard_map/ppermute | solution.py:21
  46.4 2.9 %collective-permute-done.12.refs_0_ = bf16[72,1024]{1,0:T(8,128)(2,1)S(1)} collective-permute-done((bf16[72,1024]{1,0:T(8,128)(2,1)S(1)}, bf16[72,1024]{1,0:T(8,128)(2,1)S(1)}, u32[]{:S(2)}, u32[]{:S(2)}) %collective-permute-start.12) | collective-permute-done | bytes 147488 | tf_op jit(solution)/shard_map/ppermute | solution.py:21
  49.3 1.4 %shard_map.162 = (f32[8,128]{1,0:T(8,128)S(1)}, bf16[256,512]{1,0:T(8,128)(2,1)S(1)}, bf16[256,1024]{1,0:T(8,128)(2,1)S(1)}) custom-call(s32[2]{0:T(128)S(1)} %pad_add_fusion.place, f32[8,128]{1,0:T(8,128)S(1)} %get-tuple-element.106.token, bf16[72,1024]{1,0:T(8,128)(2,1)S(1)} %collective-permute-done.12.refs_0_, f32[72,1024]{1,0:T(8,128)S(1)} %get-tuple-element.108.refs_1_, ...), custom_call_target="tpu_custom_call" | custom-call | flops 1500000000 | bytes 1500000 | tf_op jit(solution)/shard_map/pallas_call | solution.py:536
  51.4 1.5 %shard_map.163 = (f32[8,128]{1,0:T(8,128)S(1)}, bf16[256,512]{1,0:T(8,128)(2,1)S(1)}, f32[256,512]{1,0:T(8,128)S(1)}, f32[256,512]{1,0:T(8,128)S(1)}) custom-call(s32[2]{0:T(128)S(1)} %pad_add_fusion.place, f32[8,128]{1,0:T(8,128)S(1)} %get-tuple-element.112.token, bf16[256,1024]{1,0:T(8,128)(2,1)S(1)} %get-tuple-element.113.refs_0_, ...), custom_call_target="tpu_custom_call" | custom-call | flops 1000000000 | bytes 1000000 | tf_op jit(solution)/shard_map/pallas_call | solution.py:536
  55.2 2.2 %shard_map.166 = (f32[8,128]{1,0:T(8,128)S(1)}, bf16[64,512]{1,0:T(8,128)(2,1)S(1)}, bf16[64,512]{1,0:T(8,128)(2,1)S(1)}, f32[64,512]{1,0:T(8,128)S(1)}, f32[64,512]{1,0:T(8,128)S(1)}) custom-call(s32[2]{0:T(128)S(1)} %pad_add_fusion.place, f32[8,128]{1,0:T(8,128)S(1)} %get-tuple-element.119.token, bf16[72,1024]{1,0:T(8,128)(2,1)S(1)} %collective-permute-done.12.refs_0_, ...), custom_call_target="tpu_custom_call" | custom-call | flops 2500000000 | bytes 2500000 | tf_op jit(solution)/shard_map/pallas_call | solution.py:536
  58.8 1.6 %collective-permute-start.21 = (bf16[64,512]{1,0:T(8,128)(2,1)S(1)}, bf16[64,512]{1,0:T(8,128)(2,1)S(1)}, u32[]{:S(2)}, u32[]{:S(2)}) collective-permute-start(bf16[64,512]{1,0:T(8,128)(2,1)S(1)} %get-tuple-element.133), channel_id=1, source_target_pairs={{0,2},{1,3},{2,0},{3,1},{4,6},{5,7},{6,4},{7,5},{8,10},{9,11},{10,... | collective-permute-start | bytes 196616 | tf_op jit(solution)/shard_map/ppermute | solution.py:21
  60.4 4.0 %collective-permute-done.21.refs_5_ = bf16[64,512]{1,0:T(8,128)(2,1)S(1)} collective-permute-done((bf16[64,512]{1,0:T(8,128)(2,1)S(1)}, bf16[64,512]{1,0:T(8,128)(2,1)S(1)}, u32[]{:S(2)}, u32[]{:S(2)}) %collective-permute-start.21) | collective-permute-done | bytes 65568 | tf_op jit(solution)/shard_map/ppermute | solution.py:21
  (70 shorter events, 10.0 us)
Async XLA Ops:
  0.6 12.1 %collective-permute-start.2 = (bf16[256,512]{1,0:T(8,128)(2,1)}, bf16[256,512]{1,0:T(8,128)(2,1)S(1)}, u32[]{:S(2)}, u32[]{:S(2)}) collective-permute-start(bf16[256,512]{1,0:T(8,128)(2,1)} %refs_0_.1), channel_id=1, source_target_pairs={{0,2},{1,3},{2,0},{3,1},{4,6},{5,7},{6,4},{7,5},{8,10},{9,11},{10,... | collective-permute-start | bytes 786440 | tf_op jit(solution)/shard_map/ppermute | solution.py:21
  4.4 4.6 %collective-permute-start = (bf16[8,384]{1,0:T(8,128)(2,1)S(1)}, bf16[8,384]{1,0:T(8,128)(2,1)S(1)}, u32[]{:S(2)}, u32[]{:S(2)}) collective-permute-start(bf16[8,384]{1,0:T(8,128)(2,1)S(1)} %get-tuple-element.70.refs_0_), channel_id=1, source_target_pairs={{0,16},{4,20},{8,24},{12,28},{16,0},{20,4},{24,8},{28,12},{1,17},{... | collective-permute-start | bytes 18440 | tf_op jit(solution)/shard_map/ppermute | solution.py:21
  9.0 3.7 %collective-permute-start.1 = (bf16[16,384]{1,0:T(8,128)(2,1)S(1)}, bf16[16,384]{1,0:T(8,128)(2,1)S(1)}, u32[]{:S(2)}, u32[]{:S(2)}) collective-permute-start(bf16[16,384]{1,0:T(8,128)(2,1)S(1)} %get-tuple-element.72.refs_0_), channel_id=1, source_target_pairs={{0,4},{4,0},{8,12},{12,8},{16,20},{20,16},{24,28},{28,24},{1,5},{5... | collective-permute-start | bytes 36872 | tf_op jit(solution)/shard_map/ppermute | solution.py:21
  10.5 3.9 %collective-permute-start.3 = (bf16[256,512]{1,0:T(8,128)(2,1)S(1)}, bf16[256,512]{1,0:T(8,128)(2,1)S(1)}, u32[]{:S(2)}, u32[]{:S(2)}) collective-permute-start(bf16[256,512]{1,0:T(8,128)(2,1)S(1)} %copy-done.5), channel_id=1, source_target_pairs={{0,1},{1,0},{2,3},{3,2},{4,5},{5,4},{6,7},{7,6},{8,9},{9,8},{10,11... | collective-permute-start | bytes 786440 | tf_op jit(solution)/shard_map/ppermute | solution.py:21
  12.7 1.7 %collective-permute-start.4 = (bf16[256,512]{1,0:T(8,128)(2,1)S(1)}, bf16[256,512]{1,0:T(8,128)(2,1)S(1)}, u32[]{:S(2)}, u32[]{:S(2)}) collective-permute-start(bf16[256,512]{1,0:T(8,128)(2,1)S(1)} %get-tuple-element.74.refs_2_), channel_id=1, source_target_pairs={{0,1},{1,0},{2,3},{3,2},{4,5},{5,4},{6,7},{7,6},{8,9},{9,8},{10,11... | collective-permute-start | bytes 786440 | tf_op jit(solution)/shard_map/ppermute | solution.py:21
  12.8 9.1 %collective-permute-start.5 = (bf16[32,384]{1,0:T(8,128)(2,1)S(1)}, bf16[32,384]{1,0:T(8,128)(2,1)S(1)}, u32[]{:S(2)}, u32[]{:S(2)}) collective-permute-start(bf16[32,384]{1,0:T(8,128)(2,1)S(1)} %get-tuple-element.76.refs_0_), channel_id=1, source_target_pairs={{0,8},{4,12},{8,0},{12,4},{16,24},{20,28},{24,16},{28,20},{1,9},{5... | collective-permute-start | bytes 73736 | tf_op jit(solution)/shard_map/ppermute | solution.py:21
  18.3 9.5 %collective-permute-start.6 = (bf16[16,1152]{1,0:T(8,128)(2,1)S(1)}, bf16[16,1152]{1,0:T(8,128)(2,1)S(1)}, u32[]{:S(2)}, u32[]{:S(2)}) collective-permute-start(bf16[16,1152]{1,0:T(8,128)(2,1)S(1)} %get-tuple-element.82), channel_id=1, source_target_pairs={{0,4},{4,8},{8,12},{12,16},{16,20},{20,24},{24,28},{1,5},{5,9},{9,... | collective-permute-start | bytes 110600 | tf_op jit(solution)/shard_map/ppermute | solution.py:657
  24.3 8.1 %collective-permute-start.7 = (bf16[256,512]{1,0:T(8,128)(2,1)S(1)}, bf16[256,512]{1,0:T(8,128)(2,1)S(1)}, u32[]{:S(2)}, u32[]{:S(2)}) collective-permute-start(bf16[256,512]{1,0:T(8,128)(2,1)S(1)} %get-tuple-element.92), channel_id=1, source_target_pairs={{0,8},{4,12},{8,0},{12,4},{16,24},{20,28},{24,16},{28,20},{1,9},{5... | collective-permute-start | bytes 786440 | tf_op jit(solution)/shard_map/ppermute | solution.py:21
  28.1 5.9 %collective-permute-start.8 = (bf16[72,1024]{1,0:T(8,128)(2,1)S(1)}, bf16[72,1024]{1,0:T(8,128)(2,1)S(1)}, u32[]{:S(2)}, u32[]{:S(2)}) collective-permute-start(bf16[72,1024]{1,0:T(8,128)(2,1)S(1)} %get-tuple-element.94), channel_id=1, source_target_pairs={{0,4},{4,0},{8,12},{12,8},{16,20},{20,16},{24,28},{28,24},{1,5},{5... | collective-permute-start | bytes 442376 | tf_op jit(solution)/shard_map/ppermute | solution.py:21
  32.6 5.0 %collective-permute-start.9 = (bf16[128,512]{1,0:T(8,128)(2,1)S(1)}, bf16[128,512]{1,0:T(8,128)(2,1)S(1)}, u32[]{:S(2)}, u32[]{:S(2)}) collective-permute-start(bf16[128,512]{1,0:T(8,128)(2,1)S(1)} %get-tuple-element.98), channel_id=1, source_target_pairs={{0,4},{4,0},{8,12},{12,8},{16,20},{20,16},{24,28},{28,24},{1,5},{5... | collective-permute-start | bytes 393224 | tf_op jit(solution)/shard_map/ppermute | solution.py:21
  34.1 6.2 %collective-permute-start.10 = (bf16[72,1024]{1,0:T(8,128)(2,1)S(1)}, bf16[72,1024]{1,0:T(8,128)(2,1)S(1)}, u32[]{:S(2)}, u32[]{:S(2)}) collective-permute-start(bf16[72,1024]{1,0:T(8,128)(2,1)S(1)} %get-tuple-element.100), channel_id=1, source_target_pairs={{0,8},{4,12},{8,0},{12,4},{16,24},{20,28},{24,16},{28,20},{1,9},{5... | collective-permute-start | bytes 442376 | tf_op jit(solution)/shard_map/ppermute | solution.py:21
  37.6 11.7 %copy-start = (bf16[1024,2048]{1,0:T(8,128)(2,1)S(1)}, bf16[1024,2048]{1,0:T(8,128)(2,1)}, u32[]{:S(2)}) copy-start(bf16[1024,2048]{1,0:T(8,128)(2,1)} %refs_10_.1) | copy-start | bytes 12582916
  37.6 11.7 %copy-start.2 = (f32[1024]{0:T(1024)S(1)}, f32[1024]{0:T(1024)}, u32[]{:S(2)}) copy-start(f32[1024]{0:T(1024)} %param.26) | copy-start | bytes 12292
  37.7 8.2 %collective-permute-start.11 = (bf16[64,512]{1,0:T(8,128)(2,1)S(1)}, bf16[64,512]{1,0:T(8,128)(2,1)S(1)}, u32[]{:S(2)}, u32[]{:S(2)}) collective-permute-start(bf16[64,512]{1,0:T(8,128)(2,1)S(1)} %get-tuple-element.105), channel_id=1, source_target_pairs={{0,16},{4,20},{8,24},{12,28},{16,0},{20,4},{24,8},{28,12},{1,17},{... | collective-permute-start | bytes 196616 | tf_op jit(solution)/shard_map/ppermute | solution.py:21
  40.4 8.9 %collective-permute-start.12 = (bf16[72,1024]{1,0:T(8,128)(2,1)S(1)}, bf16[72,1024]{1,0:T(8,128)(2,1)S(1)}, u32[]{:S(2)}, u32[]{:S(2)}) collective-permute-start(bf16[72,1024]{1,0:T(8,128)(2,1)S(1)} %get-tuple-element.107), channel_id=1, source_target_pairs={{0,16},{4,20},{8,24},{12,28},{16,0},{20,4},{24,8},{28,12},{1,17},{... | collective-permute-start | bytes 442376 | tf_op jit(solution)/shard_map/ppermute | solution.py:21
  45.9 5.5 %collective-permute-start.14 = (bf16[64,512]{1,0:T(8,128)(2,1)S(1)}, bf16[64,512]{1,0:T(8,128)(2,1)S(1)}, u32[]{:S(2)}, u32[]{:S(2)}) collective-permute-start(bf16[64,512]{1,0:T(8,128)(2,1)S(1)} %get-tuple-element.115.refs_0_), channel_id=1, source_target_pairs={{0,2},{1,3},{2,0},{3,1},{4,6},{5,7},{6,4},{7,5},{8,10},{9,11},{10,... | collective-permute-start | bytes 196616 | tf_op jit(solution)/shard_map/ppermute | solution.py:21
  50.8 3.9 %collective-permute-start.16 = (bf16[256,512]{1,0:T(8,128)(2,1)S(1)}, bf16[256,512]{1,0:T(8,128)(2,1)S(1)}, u32[]{:S(2)}, u32[]{:S(2)}) collective-permute-start(bf16[256,512]{1,0:T(8,128)(2,1)S(1)} %get-tuple-element.118), channel_id=1, source_target_pairs={{0,1},{1,0},{2,3},{3,2},{4,5},{5,4},{6,7},{7,6},{8,9},{9,8},{10,11... | collective-permute-start | bytes 786440 | tf_op jit(solution)/shard_map/ppermute | solution.py:21
  50.8 2.6 %collective-permute-start.13 = (bf16[64,512]{1,0:T(8,128)(2,1)S(1)}, bf16[64,512]{1,0:T(8,128)(2,1)S(1)}, u32[]{:S(2)}, u32[]{:S(2)}) collective-permute-start(bf16[64,512]{1,0:T(8,128)(2,1)S(1)} %get-tuple-element.115.refs_0_), channel_id=1, source_target_pairs={{0,1},{1,0},{2,3},{3,2},{4,5},{5,4},{6,7},{7,6},{8,9},{9,8},{10,11... | collective-permute-start | bytes 196616 | tf_op jit(solution)/shard_map/ppermute | solution.py:21
  51.3 2.1 %collective-permute-start.15 = (bf16[64,512]{1,0:T(8,128)(2,1)S(1)}, bf16[64,512]{1,0:T(8,128)(2,1)S(1)}, u32[]{:S(2)}, u32[]{:S(2)}) collective-permute-start(bf16[64,512]{1,0:T(8,128)(2,1)S(1)} %collective-permute-done.14.refs_2_), channel_id=1, source_target_pairs={{0,1},{1,0},{2,3},{3,2},{4,5},{5,4},{6,7},{7,6},{8,9},{9,8},{10,11... | collective-permute-start | bytes 196616 | tf_op jit(solution)/shard_map/ppermute | solution.py:21
  52.9 7.5 %collective-permute-start.18 = (bf16[256,512]{1,0:T(8,128)(2,1)S(1)}, bf16[256,512]{1,0:T(8,128)(2,1)S(1)}, u32[]{:S(2)}, u32[]{:S(2)}) collective-permute-start(bf16[256,512]{1,0:T(8,128)(2,1)S(1)} %get-tuple-element.129), channel_id=1, source_target_pairs={{0,1},{1,0},{2,3},{3,2},{4,5},{5,4},{6,7},{7,6},{8,9},{9,8},{10,11... | collective-permute-start | bytes 786440 | tf_op jit(solution)/shard_map/ppermute | solution.py:21
  54.7 9.8 %collective-permute-start.19 = (bf16[256,512]{1,0:T(8,128)(2,1)S(1)}, bf16[256,512]{1,0:T(8,128)(2,1)S(1)}, u32[]{:S(2)}, u32[]{:S(2)}) collective-permute-start(bf16[256,512]{1,0:T(8,128)(2,1)S(1)} %get-tuple-element.130), channel_id=1, source_target_pairs={{0,2},{1,3},{2,0},{3,1},{4,6},{5,7},{6,4},{7,5},{8,10},{9,11},{10,... | collective-permute-start | bytes 786440 | tf_op jit(solution)/shard_map/ppermute | solution.py:21
  57.5 1.3 %collective-permute-start.17 = (bf16[64,512]{1,0:T(8,128)(2,1)S(1)}, bf16[64,512]{1,0:T(8,128)(2,1)S(1)}, u32[]{:S(2)}, u32[]{:S(2)}) collective-permute-start(bf16[64,512]{1,0:T(8,128)(2,1)S(1)} %get-tuple-element.126), channel_id=1, source_target_pairs={{0,1},{1,0},{2,3},{3,2},{4,5},{5,4},{6,7},{7,6},{8,9},{9,8},{10,11... | collective-permute-start | bytes 196616 | tf_op jit(solution)/shard_map/ppermute | solution.py:21
  57.6 2.9 %collective-permute-start.20 = (bf16[64,512]{1,0:T(8,128)(2,1)S(1)}, bf16[64,512]{1,0:T(8,128)(2,1)S(1)}, u32[]{:S(2)}, u32[]{:S(2)}) collective-permute-start(bf16[64,512]{1,0:T(8,128)(2,1)S(1)} %get-tuple-element.132), channel_id=1, source_target_pairs={{0,1},{1,0},{2,3},{3,2},{4,5},{5,4},{6,7},{7,6},{8,9},{9,8},{10,11... | collective-permute-start | bytes 196616 | tf_op jit(solution)/shard_map/ppermute | solution.py:21
  58.8 5.6 %collective-permute-start.21 = (bf16[64,512]{1,0:T(8,128)(2,1)S(1)}, bf16[64,512]{1,0:T(8,128)(2,1)S(1)}, u32[]{:S(2)}, u32[]{:S(2)}) collective-permute-start(bf16[64,512]{1,0:T(8,128)(2,1)S(1)} %get-tuple-element.133), channel_id=1, source_target_pairs={{0,2},{1,3},{2,0},{3,1},{4,6},{5,7},{6,4},{7,5},{8,10},{9,11},{10,... | collective-permute-start | bytes 196616 | tf_op jit(solution)/shard_map/ppermute | solution.py:21
  (12 other events, 74.5 us)

commit v7 on v6

--- a/solution.py
+++ b/solution.py
@@ -466,13 +466,17 @@
     out[...] = jnp.concatenate([mine[...].astype(F32), got[...].astype(F32)], axis=0).astype(BF16)
 
 
-def hand_kernel(place, mine, got, given, ahead, out, handed):
-    join_kernel(place, mine, got, out)
-
-
-def lookup_kernel(steps, rows, place, notes, got, table, kept_out, sent_out, wanted, found):
-    chunk = min(table.shape[0], 1024)
-    chunks = table.shape[0] // chunk
+def hand_kernel(place, given, handed):
+    del given, handed
+
+
+def lookup_kernel(
+    steps, rows, place, notes, got, table_in, kept_out, sent_out, wanted, found, table, sems
+):
+    chunks, chunk, _ = table.shape
+    copies = started(
+        [(table_in.at[pl.ds(c * chunk, chunk), :], table.at[c]) for c in range(chunks)], sems
+    )
     first = (place[0] * (chunks * chunk)).astype(F32)
     held = jnp.concatenate([notes[...].astype(F32), got[...].astype(F32)], axis=0)
     groups = held.shape[0] // EDGE
@@ -488,13 +492,14 @@
     block = min(asked, 256)
     lane = iota((block, LANES), 1).astype(F32)
     for c in range(chunks):
+        copies[c].wait()
         for at in range(0, asked, block):
             gap = wanted[at : at + block, :] - lane
             hot = [
                 jnp.where(gap == float(c * chunk + k), 1.0, 0.0).astype(BF16)
                 for k in range(0, chunk, LANES)
             ]
-            term = dot(jnp.concatenate(hot, axis=1), table[c * chunk : (c + 1) * chunk, :])
+            term = dot(jnp.concatenate(hot, axis=1), table[c])
             if c == 0:
                 found[at : at + block, :] = term
             else:
@@ -599,21 +604,15 @@
         note_kernel, none, [decode_ids.T], [shaped((EDGE, 3 * LANES), BF16)], us=2
     )
     halving = [bits[1], bits[0]] + bits[2:]
-    for bit in reversed(halving):
-        got = swapped(notes, "ctx", bit)
-        joined = shaped((2 * notes.shape[0], notes.shape[1]), BF16)
-        if bit == halving[1]:
-            notes, e2 = called(
-                hand_kernel,
-                none,
-                [notes, got, e2, embed_table],
-                [joined, shaped(e2.shape, BF16)],
-                limit=50,
-                far=(3,),
-                same=((2, 1),),
-            )
-        elif bit != halving[0]:
-            (notes,) = called(join_kernel, none, [notes, got], [joined])
+
+    def joined(notes, bit):
+        out = shaped((2 * notes.shape[0], notes.shape[1]), BF16)
+        return called(join_kernel, none, [notes, swapped(notes, "ctx", bit)], [out], us=0.05)[0]
+
+    notes = joined(notes, halving[-1])
+    (e2,) = called(
+        hand_kernel, none, [e2], [shaped(e2.shape, BF16)], us=0.05, same=((0, 0),)
+    )
     e3 = swapped(e2, "tp", 1)
 
     project_weights = [
@@ -654,18 +653,28 @@
         )
 
     x_raw, bc_raw, step_size, halo = project(True, [prompt_embeds, e1, e2, e3], 3)
+    for bit in reversed(halving[1:-1]):
+        notes = joined(notes, bit)
+    got = swapped(notes, "ctx", halving[0])
     halo = lax.ppermute(halo, "ctx", [(c, c + 1) for c in range(groups - 1)])
 
     half = groups * asked // 2
-    assert vocab_here % min(vocab_here, 1024) == 0
+    chunk = max(LANES, vocab_here // 4)
+    assert vocab_here % chunk == 0
     kept, sent = called(
         functools.partial(lookup_kernel, steps, rows),
         me_c.reshape(1),
         [notes, got, embed_table],
         [shaped((half, part), BF16), shaped((half, part), BF16)],
-        [pltpu.VMEM((2 * half, LANES), F32), pltpu.VMEM((2 * half, part), F32)],
-        us=2.5,
-        limit=32 if half > 512 else 8,
+        [
+            pltpu.VMEM((2 * half, LANES), F32),
+            pltpu.VMEM((2 * half, part), F32),
+            pltpu.VMEM((vocab_here // chunk, chunk, part), BF16),
+            pltpu.SemaphoreType.DMA((vocab_here // chunk,)),
+        ],
+        us=3.5,
+        limit=50,
+        far=(2,),
     )
 
     x_rest, bc_rest, cum_log, partial = called(

time: 65.6 us -> 65.3 us (level)
  waiting for transfers between devices: 17.6 us -> 15.7 us
  Pallas kernels: 17.6 us -> 18.8 us
    ppermute x21, waiting for transfers between devices: 17.6 us -> 15.7 us  [swapped(): return lax.ppermute(value, axis, [(i, i ^ bit) for i in range(count)])]
    pallas_call x20 -> x21, Pallas kernels: 17.6 us -> 18.8 us  [__call__(): pl.pallas_call(ordered, out_shape=[shaped((8, LANES), F32)] + outs, in_sp...]
  transfers between devices with their start and end apart: 22 -> 22, of which waited for: 8 -> 8; matrix products, arithmetic and copies ran while one was open for 0% -> 0% of each run, Pallas kernels for 25% -> 27%
where the time goes in v7:
time: 65.3 us; the launch traced here: 65.1 us
  starting transfers between devices  28.8 us (44%)
  Pallas kernels  18.8 us (29%)
  waiting for transfers between devices  15.7 us (24%)
  between operations  0.92 us (1%)
  local copies, waits for them, and re-layouts  0.74 us (1%)
    ppermute x21, starting transfers between devices, swapped(): return lax.ppermute(value, axis, [(i, i ^ bit) for i in range(count)])  25.3 us
    pallas_call x21, Pallas kernels, __call__(): pl.pallas_call(ordered, out_shape=[shaped((8, LANES), F32)] + outs, in_sp...  18.8 us
    ppermute x21, waiting for transfers between devices, swapped(): return lax.ppermute(value, axis, [(i, i ^ bit) for i in range(count)])  15.7 us
    ppermute x1, starting transfers between devices, on_device(): halo = lax.ppermute(halo, 'ctx', [(c, c + 1) for c in range(groups - 1)])  3.57 us
  transfers between devices with their start and end apart: 22, of which 8 were waited for; matrix products, arithmetic and copies ran while one was open for 0% of the time, Pallas kernels for 27%

profile of v7, /device:TPU:0, one launch (start us, length us, event | category | flops | bytes accessed | tf_op | source)
XLA Modules:
  0.0 65.1 jit_solution(17186349360759653945)
XLA Ops:
  0.7 3.0 %collective-permute-start.1 = (bf16[256,512]{1,0:T(8,128)(2,1)}, bf16[256,512]{1,0:T(8,128)(2,1)S(1)}, u32[]{:S(2)}, u32[]{:S(2)}) collective-permute-start(bf16[256,512]{1,0:T(8,128)(2,1)} %refs_0_.1), channel_id=1, source_target_pairs={{0,2},{1,3},{2,0},{3,1},{4,6},{5,7},{6,4},{7,5},{8,10},{9,11},{10,... | collective-permute-start | bytes 786440 | tf_op jit(solution)/shard_map/ppermute | solution.py:21
  4.4 2.7 %collective-permute-start = (bf16[8,384]{1,0:T(8,128)(2,1)S(1)}, bf16[8,384]{1,0:T(8,128)(2,1)S(1)}, u32[]{:S(2)}, u32[]{:S(2)}) collective-permute-start(bf16[8,384]{1,0:T(8,128)(2,1)S(1)} %get-tuple-element.71.refs_0_), channel_id=1, source_target_pairs={{0,16},{4,20},{8,24},{12,28},{16,0},{20,4},{24,8},{28,12},{1,17},{... | collective-permute-start | bytes 18440 | tf_op jit(solution)/shard_map/ppermute | solution.py:21
  7.1 1.9 %collective-permute-done.refs_1_ = bf16[8,384]{1,0:T(8,128)(2,1)S(1)} collective-permute-done((bf16[8,384]{1,0:T(8,128)(2,1)S(1)}, bf16[8,384]{1,0:T(8,128)(2,1)S(1)}, u32[]{:S(2)}, u32[]{:S(2)}) %collective-permute-start) | collective-permute-done | bytes 6176 | tf_op jit(solution)/shard_map/ppermute | solution.py:21
  10.2 1.7 %collective-permute-start.4 = (bf16[16,384]{1,0:T(8,128)(2,1)S(1)}, bf16[16,384]{1,0:T(8,128)(2,1)S(1)}, u32[]{:S(2)}, u32[]{:S(2)}) collective-permute-start(bf16[16,384]{1,0:T(8,128)(2,1)S(1)} %get-tuple-element.76.refs_0_), channel_id=1, source_target_pairs={{0,4},{4,0},{8,12},{12,8},{16,20},{20,16},{24,28},{28,24},{1,5},{5... | collective-permute-start | bytes 36872 | tf_op jit(solution)/shard_map/ppermute | solution.py:21
  12.0 3.7 %shard_map.152 = (f32[8,128]{1,0:T(8,128)S(1)}, bf16[256,1024]{1,0:T(8,128)(2,1)S(1)}, bf16[256,128]{1,0:T(8,128)(2,1)S(1)}, f32[256,128]{1,0:T(8,128)S(1)}, bf16[16,1152]{1,0:T(8,128)(2,1)S(1)}) custom-call(s32[1]{0:T(128)} %bitcast.place, f32[8,128]{1,0:T(8,128)S(1)} %get-tuple-element.73.token, bf16[256,512]{1,0:T(8,128)(2,1)S(1)} %copy-done.4, ...), custom_call_target="tpu_custom_call" | custom-call | flops 3000000000 | bytes 3000000 | tf_op jit(solution)/shard_map/pallas_call | solution.py:541
  15.7 1.7 %collective-permute-start.5 = (bf16[32,384]{1,0:T(8,128)(2,1)S(1)}, bf16[32,384]{1,0:T(8,128)(2,1)S(1)}, u32[]{:S(2)}, u32[]{:S(2)}) collective-permute-start(bf16[32,384]{1,0:T(8,128)(2,1)S(1)} %get-tuple-element.78.refs_0_), channel_id=1, source_target_pairs={{0,8},{4,12},{8,0},{12,4},{16,24},{20,28},{24,16},{28,20},{1,9},{5... | collective-permute-start | bytes 73736 | tf_op jit(solution)/shard_map/ppermute | solution.py:21
  17.3 3.6 %collective-permute-start.6 = (bf16[16,1152]{1,0:T(8,128)(2,1)S(1)}, bf16[16,1152]{1,0:T(8,128)(2,1)S(1)}, u32[]{:S(2)}, u32[]{:S(2)}) collective-permute-start(bf16[16,1152]{1,0:T(8,128)(2,1)S(1)} %get-tuple-element.84), channel_id=1, source_target_pairs={{0,4},{4,8},{8,12},{12,16},{16,20},{20,24},{24,28},{1,5},{5,9},{9,... | collective-permute-start | bytes 110600 | tf_op jit(solution)/shard_map/ppermute | solution.py:659
  21.0 3.8 %shard_map.154 = (f32[8,128]{1,0:T(8,128)S(1)}, bf16[256,512]{1,0:T(8,128)(2,1)S(1)}, bf16[256,512]{1,0:T(8,128)(2,1)S(1)}) custom-call(s32[1]{0:T(128)} %bitcast.4.place, f32[8,128]{1,0:T(8,128)S(1)} %get-tuple-element.77.token, bf16[32,384]{1,0:T(8,128)(2,1)S(1)} %get-tuple-element.78.refs_0_, bf16[32,384]{1,0:T(8,128)(2,1)S(1)} %collective-permute-done.5.refs_1_, ...), custom_call_target="tpu_custom_call" | custom-call | flops 3500000000 | bytes 3500000 | tf_op jit(solution)/shard_map/pallas_call | solution.py:541
  25.3 1.9 %shard_map.155 = (f32[8,128]{1,0:T(8,128)S(1)}, bf16[256,1024]{1,0:T(8,128)(2,1)S(1)}, bf16[256,128]{1,0:T(8,128)(2,1)S(1)}, f32[256,128]{1,0:T(8,128)S(1)}, f32[64,1024]{1,0:T(8,128)S(1)}) custom-call(s32[1]{0:T(128)} %constant.3.clone.1.place, f32[8,128]{1,0:T(8,128)S(1)} %get-tuple-element.79.token, ...), custom_call_target="tpu_custom_call" | custom-call | flops 2000000000 | bytes 2000000 | tf_op jit(solution)/shard_map/pallas_call | solution.py:541
  27.6 2.7 %collective-permute-start.8 = (bf16[72,1024]{1,0:T(8,128)(2,1)S(1)}, bf16[72,1024]{1,0:T(8,128)(2,1)S(1)}, u32[]{:S(2)}, u32[]{:S(2)}) collective-permute-start(bf16[72,1024]{1,0:T(8,128)(2,1)S(1)} %get-tuple-element.96), channel_id=1, source_target_pairs={{0,4},{4,0},{8,12},{12,8},{16,20},{20,16},{24,28},{28,24},{1,5},{5... | collective-permute-start | bytes 442376 | tf_op jit(solution)/shard_map/ppermute | solution.py:21
  30.3 1.4 %shard_map.157 = (f32[8,128]{1,0:T(8,128)S(1)}, f32[256,1024]{1,0:T(8,128)S(1)}, f32[256,128]{1,0:T(8,128)S(1)}, bf16[256,128]{1,0:T(8,128)(2,1)S(1)}) custom-call(s32[1]{0:T(128)} %constant.3.clone.1.place, f32[8,128]{1,0:T(8,128)S(1)} %get-tuple-element.87.token, bf16[16,1024]{1,0:T(8,128)(2,1)S(1)} %get-tuple-element.88.refs_0_, ...), custom_call_target="tpu_custom_call" | custom-call | flops 2500000000 | bytes 2500000 | tf_op jit(solution)/shard_map/pallas_call | solution.py:541
  32.6 1.5 %collective-permute-start.9 = (bf16[128,512]{1,0:T(8,128)(2,1)S(1)}, bf16[128,512]{1,0:T(8,128)(2,1)S(1)}, u32[]{:S(2)}, u32[]{:S(2)}) collective-permute-start(bf16[128,512]{1,0:T(8,128)(2,1)S(1)} %get-tuple-element.100), channel_id=1, source_target_pairs={{0,4},{4,0},{8,12},{12,8},{16,20},{20,16},{24,28},{28,24},{1,5},{5... | collective-permute-start | bytes 393224 | tf_op jit(solution)/shard_map/ppermute | solution.py:21
  34.3 1.8 %collective-permute-start.10 = (bf16[72,1024]{1,0:T(8,128)(2,1)S(1)}, bf16[72,1024]{1,0:T(8,128)(2,1)S(1)}, u32[]{:S(2)}, u32[]{:S(2)}) collective-permute-start(bf16[72,1024]{1,0:T(8,128)(2,1)S(1)} %get-tuple-element.102), channel_id=1, source_target_pairs={{0,8},{4,12},{8,0},{12,4},{16,24},{20,28},{24,16},{28,20},{1,9},{5... | collective-permute-start | bytes 442376 | tf_op jit(solution)/shard_map/ppermute | solution.py:21
  36.1 1.6 %collective-permute-done.9.refs_1_ = bf16[128,512]{1,0:T(8,128)(2,1)S(1)} collective-permute-done((bf16[128,512]{1,0:T(8,128)(2,1)S(1)}, bf16[128,512]{1,0:T(8,128)(2,1)S(1)}, u32[]{:S(2)}, u32[]{:S(2)}) %collective-permute-start.9) | collective-permute-done | bytes 131104 | tf_op jit(solution)/shard_map/ppermute | solution.py:21
  37.7 2.7 %collective-permute-start.11 = (bf16[64,512]{1,0:T(8,128)(2,1)S(1)}, bf16[64,512]{1,0:T(8,128)(2,1)S(1)}, u32[]{:S(2)}, u32[]{:S(2)}) collective-permute-start(bf16[64,512]{1,0:T(8,128)(2,1)S(1)} %get-tuple-element.107), channel_id=1, source_target_pairs={{0,16},{4,20},{8,24},{12,28},{16,0},{20,4},{24,8},{28,12},{1,17},{... | collective-permute-start | bytes 196616 | tf_op jit(solution)/shard_map/ppermute | solution.py:21
  40.5 1.5 %collective-permute-start.12 = (bf16[72,1024]{1,0:T(8,128)(2,1)S(1)}, bf16[72,1024]{1,0:T(8,128)(2,1)S(1)}, u32[]{:S(2)}, u32[]{:S(2)}) collective-permute-start(bf16[72,1024]{1,0:T(8,128)(2,1)S(1)} %get-tuple-element.109), channel_id=1, source_target_pairs={{0,16},{4,20},{8,24},{12,28},{16,0},{20,4},{24,8},{28,12},{1,17},{... | collective-permute-start | bytes 442376 | tf_op jit(solution)/shard_map/ppermute | solution.py:21
  42.1 3.6 %collective-permute-done.11.refs_1_ = bf16[64,512]{1,0:T(8,128)(2,1)S(1)} collective-permute-done((bf16[64,512]{1,0:T(8,128)(2,1)S(1)}, bf16[64,512]{1,0:T(8,128)(2,1)S(1)}, u32[]{:S(2)}, u32[]{:S(2)}) %collective-permute-start.11) | collective-permute-done | bytes 65568 | tf_op jit(solution)/shard_map/ppermute | solution.py:21
  45.8 1.6 %collective-permute-start.14 = (bf16[64,512]{1,0:T(8,128)(2,1)S(1)}, bf16[64,512]{1,0:T(8,128)(2,1)S(1)}, u32[]{:S(2)}, u32[]{:S(2)}) collective-permute-start(bf16[64,512]{1,0:T(8,128)(2,1)S(1)} %get-tuple-element.117.refs_0_), channel_id=1, source_target_pairs={{0,2},{1,3},{2,0},{3,1},{4,6},{5,7},{6,4},{7,5},{8,10},{9,11},{10,... | collective-permute-start | bytes 196616 | tf_op jit(solution)/shard_map/ppermute | solution.py:21
  47.3 1.7 %collective-permute-done.12.refs_0_ = bf16[72,1024]{1,0:T(8,128)(2,1)S(1)} collective-permute-done((bf16[72,1024]{1,0:T(8,128)(2,1)S(1)}, bf16[72,1024]{1,0:T(8,128)(2,1)S(1)}, u32[]{:S(2)}, u32[]{:S(2)}) %collective-permute-start.12) | collective-permute-done | bytes 147488 | tf_op jit(solution)/shard_map/ppermute | solution.py:21
  49.0 1.4 %shard_map.163 = (f32[8,128]{1,0:T(8,128)S(1)}, bf16[256,512]{1,0:T(8,128)(2,1)S(1)}, bf16[256,1024]{1,0:T(8,128)(2,1)S(1)}) custom-call(s32[2]{0:T(128)S(1)} %pad_add_fusion.place, f32[8,128]{1,0:T(8,128)S(1)} %get-tuple-element.108.token, bf16[72,1024]{1,0:T(8,128)(2,1)S(1)} %collective-permute-done.12.refs_0_, f32[72,1024]{1,0:T(8,128)S(1)} %get-tuple-element.110.refs_1_, ...), custom_call_target="tpu_custom_call" | custom-call | flops 1500000000 | bytes 1500000 | tf_op jit(solution)/shard_map/pallas_call | solution.py:541
  51.1 1.5 %shard_map.164 = (f32[8,128]{1,0:T(8,128)S(1)}, bf16[256,512]{1,0:T(8,128)(2,1)S(1)}, f32[256,512]{1,0:T(8,128)S(1)}, f32[256,512]{1,0:T(8,128)S(1)}) custom-call(s32[2]{0:T(128)S(1)} %pad_add_fusion.place, f32[8,128]{1,0:T(8,128)S(1)} %get-tuple-element.114.token, bf16[256,1024]{1,0:T(8,128)(2,1)S(1)} %get-tuple-element.115.refs_0_, ...), custom_call_target="tpu_custom_call" | custom-call | flops 1000000000 | bytes 1000000 | tf_op jit(solution)/shard_map/pallas_call | solution.py:541
  54.4 1.6 %collective-permute-start.19 = (bf16[256,512]{1,0:T(8,128)(2,1)S(1)}, bf16[256,512]{1,0:T(8,128)(2,1)S(1)}, u32[]{:S(2)}, u32[]{:S(2)}) collective-permute-start(bf16[256,512]{1,0:T(8,128)(2,1)S(1)} %get-tuple-element.132), channel_id=1, source_target_pairs={{0,2},{1,3},{2,0},{3,1},{4,6},{5,7},{6,4},{7,5},{8,10},{9,11},{10,... | collective-permute-start | bytes 786440 | tf_op jit(solution)/shard_map/ppermute | solution.py:21
  56.0 2.2 %shard_map.167 = (f32[8,128]{1,0:T(8,128)S(1)}, bf16[64,512]{1,0:T(8,128)(2,1)S(1)}, bf16[64,512]{1,0:T(8,128)(2,1)S(1)}, f32[64,512]{1,0:T(8,128)S(1)}, f32[64,512]{1,0:T(8,128)S(1)}) custom-call(s32[2]{0:T(128)S(1)} %pad_add_fusion.place, f32[8,128]{1,0:T(8,128)S(1)} %get-tuple-element.121.token, bf16[72,1024]{1,0:T(8,128)(2,1)S(1)} %collective-permute-done.12.refs_0_, ...), custom_call_target="tpu_custom_call" | custom-call | flops 2500000000 | bytes 2500000 | tf_op jit(solution)/shard_map/pallas_call | solution.py:541
  60.1 4.0 %collective-permute-done.21.refs_5_ = bf16[64,512]{1,0:T(8,128)(2,1)S(1)} collective-permute-done((bf16[64,512]{1,0:T(8,128)(2,1)S(1)}, bf16[64,512]{1,0:T(8,128)(2,1)S(1)}, u32[]{:S(2)}, u32[]{:S(2)}) %collective-permute-start.21) | collective-permute-done | bytes 65568 | tf_op jit(solution)/shard_map/ppermute | solution.py:21
  (69 shorter events, 9.3 us)
Async XLA Ops:
  0.7 9.5 %collective-permute-start.1 = (bf16[256,512]{1,0:T(8,128)(2,1)}, bf16[256,512]{1,0:T(8,128)(2,1)S(1)}, u32[]{:S(2)}, u32[]{:S(2)}) collective-permute-start(bf16[256,512]{1,0:T(8,128)(2,1)} %refs_0_.1), channel_id=1, source_target_pairs={{0,2},{1,3},{2,0},{3,1},{4,6},{5,7},{6,4},{7,5},{8,10},{9,11},{10,... | collective-permute-start | bytes 786440 | tf_op jit(solution)/shard_map/ppermute | solution.py:21
  4.4 4.6 %collective-permute-start = (bf16[8,384]{1,0:T(8,128)(2,1)S(1)}, bf16[8,384]{1,0:T(8,128)(2,1)S(1)}, u32[]{:S(2)}, u32[]{:S(2)}) collective-permute-start(bf16[8,384]{1,0:T(8,128)(2,1)S(1)} %get-tuple-element.71.refs_0_), channel_id=1, source_target_pairs={{0,16},{4,20},{8,24},{12,28},{16,0},{20,4},{24,8},{28,12},{1,17},{... | collective-permute-start | bytes 18440 | tf_op jit(solution)/shard_map/ppermute | solution.py:21
  7.1 4.9 %collective-permute-start.2 = (bf16[256,512]{1,0:T(8,128)(2,1)S(1)}, bf16[256,512]{1,0:T(8,128)(2,1)S(1)}, u32[]{:S(2)}, u32[]{:S(2)}) collective-permute-start(bf16[256,512]{1,0:T(8,128)(2,1)S(1)} %copy-done.4), channel_id=1, source_target_pairs={{0,1},{1,0},{2,3},{3,2},{4,5},{5,4},{6,7},{7,6},{8,9},{9,8},{10,11... | collective-permute-start | bytes 786440 | tf_op jit(solution)/shard_map/ppermute | solution.py:21
  10.2 1.7 %collective-permute-start.3 = (bf16[256,512]{1,0:T(8,128)(2,1)S(1)}, bf16[256,512]{1,0:T(8,128)(2,1)S(1)}, u32[]{:S(2)}, u32[]{:S(2)}) collective-permute-start(bf16[256,512]{1,0:T(8,128)(2,1)S(1)} %get-tuple-element.74.refs_2_), channel_id=1, source_target_pairs={{0,1},{1,0},{2,3},{3,2},{4,5},{5,4},{6,7},{7,6},{8,9},{9,8},{10,11... | collective-permute-start | bytes 786440 | tf_op jit(solution)/shard_map/ppermute | solution.py:21
  10.2 5.4 %collective-permute-start.4 = (bf16[16,384]{1,0:T(8,128)(2,1)S(1)}, bf16[16,384]{1,0:T(8,128)(2,1)S(1)}, u32[]{:S(2)}, u32[]{:S(2)}) collective-permute-start(bf16[16,384]{1,0:T(8,128)(2,1)S(1)} %get-tuple-element.76.refs_0_), channel_id=1, source_target_pairs={{0,4},{4,0},{8,12},{12,8},{16,20},{20,16},{24,28},{28,24},{1,5},{5... | collective-permute-start | bytes 36872 | tf_op jit(solution)/shard_map/ppermute | solution.py:21
  15.7 5.2 %collective-permute-start.5 = (bf16[32,384]{1,0:T(8,128)(2,1)S(1)}, bf16[32,384]{1,0:T(8,128)(2,1)S(1)}, u32[]{:S(2)}, u32[]{:S(2)}) collective-permute-start(bf16[32,384]{1,0:T(8,128)(2,1)S(1)} %get-tuple-element.78.refs_0_), channel_id=1, source_target_pairs={{0,8},{4,12},{8,0},{12,4},{16,24},{20,28},{24,16},{28,20},{1,9},{5... | collective-permute-start | bytes 73736 | tf_op jit(solution)/shard_map/ppermute | solution.py:21
  17.3 9.9 %collective-permute-start.6 = (bf16[16,1152]{1,0:T(8,128)(2,1)S(1)}, bf16[16,1152]{1,0:T(8,128)(2,1)S(1)}, u32[]{:S(2)}, u32[]{:S(2)}) collective-permute-start(bf16[16,1152]{1,0:T(8,128)(2,1)S(1)} %get-tuple-element.84), channel_id=1, source_target_pairs={{0,4},{4,8},{8,12},{12,16},{16,20},{20,24},{24,28},{1,5},{5,9},{9,... | collective-permute-start | bytes 110600 | tf_op jit(solution)/shard_map/ppermute | solution.py:659
  24.7 7.8 %collective-permute-start.7 = (bf16[256,512]{1,0:T(8,128)(2,1)S(1)}, bf16[256,512]{1,0:T(8,128)(2,1)S(1)}, u32[]{:S(2)}, u32[]{:S(2)}) collective-permute-start(bf16[256,512]{1,0:T(8,128)(2,1)S(1)} %get-tuple-element.94), channel_id=1, source_target_pairs={{0,8},{4,12},{8,0},{12,4},{16,24},{20,28},{24,16},{28,20},{1,9},{5... | collective-permute-start | bytes 786440 | tf_op jit(solution)/shard_map/ppermute | solution.py:21
  27.6 6.6 %collective-permute-start.8 = (bf16[72,1024]{1,0:T(8,128)(2,1)S(1)}, bf16[72,1024]{1,0:T(8,128)(2,1)S(1)}, u32[]{:S(2)}, u32[]{:S(2)}) collective-permute-start(bf16[72,1024]{1,0:T(8,128)(2,1)S(1)} %get-tuple-element.96), channel_id=1, source_target_pairs={{0,4},{4,0},{8,12},{12,8},{16,20},{20,16},{24,28},{28,24},{1,5},{5... | collective-permute-start | bytes 442376 | tf_op jit(solution)/shard_map/ppermute | solution.py:21
  32.6 5.0 %collective-permute-start.9 = (bf16[128,512]{1,0:T(8,128)(2,1)S(1)}, bf16[128,512]{1,0:T(8,128)(2,1)S(1)}, u32[]{:S(2)}, u32[]{:S(2)}) collective-permute-start(bf16[128,512]{1,0:T(8,128)(2,1)S(1)} %get-tuple-element.100), channel_id=1, source_target_pairs={{0,4},{4,0},{8,12},{12,8},{16,20},{20,16},{24,28},{28,24},{1,5},{5... | collective-permute-start | bytes 393224 | tf_op jit(solution)/shard_map/ppermute | solution.py:21
  34.3 6.1 %collective-permute-start.10 = (bf16[72,1024]{1,0:T(8,128)(2,1)S(1)}, bf16[72,1024]{1,0:T(8,128)(2,1)S(1)}, u32[]{:S(2)}, u32[]{:S(2)}) collective-permute-start(bf16[72,1024]{1,0:T(8,128)(2,1)S(1)} %get-tuple-element.102), channel_id=1, source_target_pairs={{0,8},{4,12},{8,0},{12,4},{16,24},{20,28},{24,16},{28,20},{1,9},{5... | collective-permute-start | bytes 442376 | tf_op jit(solution)/shard_map/ppermute | solution.py:21
  37.7 11.3 %copy-start = (bf16[1024,2048]{1,0:T(8,128)(2,1)S(1)}, bf16[1024,2048]{1,0:T(8,128)(2,1)}, u32[]{:S(2)}) copy-start(bf16[1024,2048]{1,0:T(8,128)(2,1)} %refs_10_.1) | copy-start | bytes 12582916
  37.7 11.3 %copy-start.1 = (f32[1024]{0:T(1024)S(1)}, f32[1024]{0:T(1024)}, u32[]{:S(2)}) copy-start(f32[1024]{0:T(1024)} %param.26) | copy-start | bytes 12292
  37.7 8.0 %collective-permute-start.11 = (bf16[64,512]{1,0:T(8,128)(2,1)S(1)}, bf16[64,512]{1,0:T(8,128)(2,1)S(1)}, u32[]{:S(2)}, u32[]{:S(2)}) collective-permute-start(bf16[64,512]{1,0:T(8,128)(2,1)S(1)} %get-tuple-element.107), channel_id=1, source_target_pairs={{0,16},{4,20},{8,24},{12,28},{16,0},{20,4},{24,8},{28,12},{1,17},{... | collective-permute-start | bytes 196616 | tf_op jit(solution)/shard_map/ppermute | solution.py:21
  40.5 8.5 %collective-permute-start.12 = (bf16[72,1024]{1,0:T(8,128)(2,1)S(1)}, bf16[72,1024]{1,0:T(8,128)(2,1)S(1)}, u32[]{:S(2)}, u32[]{:S(2)}) collective-permute-start(bf16[72,1024]{1,0:T(8,128)(2,1)S(1)} %get-tuple-element.109), channel_id=1, source_target_pairs={{0,16},{4,20},{8,24},{12,28},{16,0},{20,4},{24,8},{28,12},{1,17},{... | collective-permute-start | bytes 442376 | tf_op jit(solution)/shard_map/ppermute | solution.py:21
  45.8 5.3 %collective-permute-start.14 = (bf16[64,512]{1,0:T(8,128)(2,1)S(1)}, bf16[64,512]{1,0:T(8,128)(2,1)S(1)}, u32[]{:S(2)}, u32[]{:S(2)}) collective-permute-start(bf16[64,512]{1,0:T(8,128)(2,1)S(1)} %get-tuple-element.117.refs_0_), channel_id=1, source_target_pairs={{0,2},{1,3},{2,0},{3,1},{4,6},{5,7},{6,4},{7,5},{8,10},{9,11},{10,... | collective-permute-start | bytes 196616 | tf_op jit(solution)/shard_map/ppermute | solution.py:21
  50.5 3.9 %collective-permute-start.16 = (bf16[256,512]{1,0:T(8,128)(2,1)S(1)}, bf16[256,512]{1,0:T(8,128)(2,1)S(1)}, u32[]{:S(2)}, u32[]{:S(2)}) collective-permute-start(bf16[256,512]{1,0:T(8,128)(2,1)S(1)} %get-tuple-element.120), channel_id=1, source_target_pairs={{0,1},{1,0},{2,3},{3,2},{4,5},{5,4},{6,7},{7,6},{8,9},{9,8},{10,11... | collective-permute-start | bytes 786440 | tf_op jit(solution)/shard_map/ppermute | solution.py:21
  50.6 2.6 %collective-permute-start.13 = (bf16[64,512]{1,0:T(8,128)(2,1)S(1)}, bf16[64,512]{1,0:T(8,128)(2,1)S(1)}, u32[]{:S(2)}, u32[]{:S(2)}) collective-permute-start(bf16[64,512]{1,0:T(8,128)(2,1)S(1)} %get-tuple-element.117.refs_0_), channel_id=1, source_target_pairs={{0,1},{1,0},{2,3},{3,2},{4,5},{5,4},{6,7},{7,6},{8,9},{9,8},{10,11... | collective-permute-start | bytes 196616 | tf_op jit(solution)/shard_map/ppermute | solution.py:21
  51.1 2.1 %collective-permute-start.15 = (bf16[64,512]{1,0:T(8,128)(2,1)S(1)}, bf16[64,512]{1,0:T(8,128)(2,1)S(1)}, u32[]{:S(2)}, u32[]{:S(2)}) collective-permute-start(bf16[64,512]{1,0:T(8,128)(2,1)S(1)} %collective-permute-done.14.refs_2_), channel_id=1, source_target_pairs={{0,1},{1,0},{2,3},{3,2},{4,5},{5,4},{6,7},{7,6},{8,9},{9,8},{10,11... | collective-permute-start | bytes 196616 | tf_op jit(solution)/shard_map/ppermute | solution.py:21
  52.7 7.5 %collective-permute-start.18 = (bf16[256,512]{1,0:T(8,128)(2,1)S(1)}, bf16[256,512]{1,0:T(8,128)(2,1)S(1)}, u32[]{:S(2)}, u32[]{:S(2)}) collective-permute-start(bf16[256,512]{1,0:T(8,128)(2,1)S(1)} %get-tuple-element.131), channel_id=1, source_target_pairs={{0,1},{1,0},{2,3},{3,2},{4,5},{5,4},{6,7},{7,6},{8,9},{9,8},{10,11... | collective-permute-start | bytes 786440 | tf_op jit(solution)/shard_map/ppermute | solution.py:21
  54.4 9.8 %collective-permute-start.19 = (bf16[256,512]{1,0:T(8,128)(2,1)S(1)}, bf16[256,512]{1,0:T(8,128)(2,1)S(1)}, u32[]{:S(2)}, u32[]{:S(2)}) collective-permute-start(bf16[256,512]{1,0:T(8,128)(2,1)S(1)} %get-tuple-element.132), channel_id=1, source_target_pairs={{0,2},{1,3},{2,0},{3,1},{4,6},{5,7},{6,4},{7,5},{8,10},{9,11},{10,... | collective-permute-start | bytes 786440 | tf_op jit(solution)/shard_map/ppermute | solution.py:21
  58.2 1.3 %collective-permute-start.17 = (bf16[64,512]{1,0:T(8,128)(2,1)S(1)}, bf16[64,512]{1,0:T(8,128)(2,1)S(1)}, u32[]{:S(2)}, u32[]{:S(2)}) collective-permute-start(bf16[64,512]{1,0:T(8,128)(2,1)S(1)} %get-tuple-element.128), channel_id=1, source_target_pairs={{0,1},{1,0},{2,3},{3,2},{4,5},{5,4},{6,7},{7,6},{8,9},{9,8},{10,11... | collective-permute-start | bytes 196616 | tf_op jit(solution)/shard_map/ppermute | solution.py:21
  58.3 1.8 %collective-permute-start.20 = (bf16[64,512]{1,0:T(8,128)(2,1)S(1)}, bf16[64,512]{1,0:T(8,128)(2,1)S(1)}, u32[]{:S(2)}, u32[]{:S(2)}) collective-permute-start(bf16[64,512]{1,0:T(8,128)(2,1)S(1)} %get-tuple-element.134), channel_id=1, source_target_pairs={{0,1},{1,0},{2,3},{3,2},{4,5},{5,4},{6,7},{7,6},{8,9},{9,8},{10,11... | collective-permute-start | bytes 196616 | tf_op jit(solution)/shard_map/ppermute | solution.py:21
  59.6 4.6 %collective-permute-start.21 = (bf16[64,512]{1,0:T(8,128)(2,1)S(1)}, bf16[64,512]{1,0:T(8,128)(2,1)S(1)}, u32[]{:S(2)}, u32[]{:S(2)}) collective-permute-start(bf16[64,512]{1,0:T(8,128)(2,1)S(1)} %get-tuple-element.135), channel_id=1, source_target_pairs={{0,2},{1,3},{2,0},{3,1},{4,6},{5,7},{6,4},{7,5},{8,10},{9,11},{10,... | collective-permute-start | bytes 196616 | tf_op jit(solution)/shard_map/ppermute | solution.py:21
  (11 other events, 70.8 us)

commit v8 on v7

--- a/solution.py
+++ b/solution.py
@@ -360,8 +360,8 @@
         out[...] = dot(mixed[...], weight[:, columns]).astype(out.dtype)
 
 
-def rest_kernel(place, mixed, weight, sent1, kept2, kept0):
-    sent(place[0], mixed, weight, ((1, sent1), (2, kept2), (0, kept0)))
+def rest_kernel(blocks, place, mixed, weight, *outs):
+    sent(place[0], mixed, weight, zip(blocks, outs))
 
 
 def prompt_back_kernel(
@@ -388,12 +388,14 @@
     conv_x,
     conv_bc,
     skip_gain,
+    prompt_mixed,
     gain,
     weight,
     sent3,
     sent1,
     kept2,
     kept0,
+    prompt_kept0,
     full,
     mixed,
     joined,
@@ -436,6 +438,7 @@
     bc = bc_conv.astype(BF16)
     outs = (sent3, sent1, kept2, kept0)
     finished(heads, me, incoming, y, bc, jnp.exp(cum_log), gain, weight, outs, full, mixed)
+    sent(me, prompt_mixed, weight, ((0, prompt_kept0),))
 
 
 def far_kernel(place, kept, got, out):
@@ -758,7 +761,9 @@
             kernel,
             back_place,
             [got] + inputs + [gain_row, out_weight],
-            [shaped((count, part), BF16)] * 2 + [shaped((count, part), F32)] * 2,
+            [shaped((count, part), BF16)] * 2
+            + [shaped((count, part), F32)] * 2
+            + [shaped((tokens, part), F32)],
             [pltpu.VMEM((count, channels), F32), pltpu.VMEM((count, channels), BF16)] + scratch,
             us=us,
             limit=12,
@@ -779,18 +784,24 @@
         us=1.5,
         limit=12,
     )
-    prompt_rest = called(
-        rest_kernel,
+    prompt_sent1, prompt_kept2 = called(
+        functools.partial(rest_kernel, (1, 2)),
         back_place,
         [prompt_mixed, out_weight],
-        [shaped((tokens, part), BF16)] + [shaped((tokens, part), F32)] * 2,
+        [shaped((tokens, part), BF16), shaped((tokens, part), F32)],
     )
     dec_x_raw, dec_bc_raw, dec_step = project(False, [kept, over1, near, over3], 1.5)
-    prompt_crossed = crossed(prompt_sent3, *prompt_rest)
-    decode_back = back(
+    (far,) = called(
+        far_kernel,
+        none,
+        [prompt_kept2, swapped(prompt_sent3, "tp", 1)],
+        [shaped((tokens, part), BF16)],
+    )
+    far = swapped(far, "tp", 2)
+    *decode_back, prompt_kept0 = back(
         functools.partial(decode_back_kernel, rows, heads),
         asked,
-        [state, dec_x_raw, dec_bc_raw, dec_step] + conv_weights + [skip_row],
+        [state, dec_x_raw, dec_bc_raw, dec_step] + conv_weights + [skip_row, prompt_mixed],
         [
             pltpu.VMEM((margin * rows + asked, 2 * LANES), F32),
             pltpu.VMEM((asked, channels), BF16),
@@ -802,7 +813,7 @@
     prompt_out, decode_out = called(
         functools.partial(total_kernel, rows),
         none,
-        [*prompt_crossed, *decode_crossed],
+        [prompt_kept0, swapped(prompt_sent1, "tp", 1), far, *decode_crossed],
         [shaped((tokens, part), BF16), shaped((rows, steps, part), BF16)],
     )
     return (prompt_out, decode_out)

time: 65.3 us -> 65.1 us (level)
  transfers between devices with their start and end apart: 22 -> 22, of which waited for: 8 -> 8; matrix products, arithmetic and copies ran while one was open for 0% -> 0% of each run, Pallas kernels for 27% -> 28%
where the time goes in v8:
time: 65.1 us; the launch traced here: 64.9 us
  starting transfers between devices  28.8 us (44%)
  Pallas kernels  18.9 us (29%)
  waiting for transfers between devices  15.5 us (24%)
  between operations  0.91 us (1%)
  local copies, waits for them, and re-layouts  0.74 us (1%)
    ppermute x21, starting transfers between devices, swapped(): return lax.ppermute(value, axis, [(i, i ^ bit) for i in range(count)])  25.3 us
    pallas_call x21, Pallas kernels, __call__(): pl.pallas_call(ordered, out_shape=[shaped((8, LANES), F32)] + outs, in_sp...  18.9 us
    ppermute x21, waiting for transfers between devices, swapped(): return lax.ppermute(value, axis, [(i, i ^ bit) for i in range(count)])  15.5 us
    ppermute x1, starting transfers between devices, on_device(): halo = lax.ppermute(halo, 'ctx', [(c, c + 1) for c in range(groups - 1)])  3.57 us
  transfers between devices with their start and end apart: 22, of which 8 were waited for; matrix products, arithmetic and copies ran while one was open for 0% of the time, Pallas kernels for 28%

profile of v8, /device:TPU:0, one launch (start us, length us, event | category | flops | bytes accessed | tf_op | source)
XLA Modules:
  0.0 64.9 jit_solution(17032447396193606854)
XLA Ops:
  0.7 3.0 %collective-permute-start.1 = (bf16[256,512]{1,0:T(8,128)(2,1)}, bf16[256,512]{1,0:T(8,128)(2,1)S(1)}, u32[]{:S(2)}, u32[]{:S(2)}) collective-permute-start(bf16[256,512]{1,0:T(8,128)(2,1)} %refs_0_.1), channel_id=1, source_target_pairs={{0,2},{1,3},{2,0},{3,1},{4,6},{5,7},{6,4},{7,5},{8,10},{9,11},{10,... | collective-permute-start | bytes 786440 | tf_op jit(solution)/shard_map/ppermute | solution.py:21
  4.4 2.7 %collective-permute-start = (bf16[8,384]{1,0:T(8,128)(2,1)S(1)}, bf16[8,384]{1,0:T(8,128)(2,1)S(1)}, u32[]{:S(2)}, u32[]{:S(2)}) collective-permute-start(bf16[8,384]{1,0:T(8,128)(2,1)S(1)} %get-tuple-element.71.refs_0_), channel_id=1, source_target_pairs={{0,16},{4,20},{8,24},{12,28},{16,0},{20,4},{24,8},{28,12},{1,17},{... | collective-permute-start | bytes 18440 | tf_op jit(solution)/shard_map/ppermute | solution.py:21
  7.1 1.9 %collective-permute-done.refs_1_ = bf16[8,384]{1,0:T(8,128)(2,1)S(1)} collective-permute-done((bf16[8,384]{1,0:T(8,128)(2,1)S(1)}, bf16[8,384]{1,0:T(8,128)(2,1)S(1)}, u32[]{:S(2)}, u32[]{:S(2)}) %collective-permute-start) | collective-permute-done | bytes 6176 | tf_op jit(solution)/shard_map/ppermute | solution.py:21
  10.2 1.7 %collective-permute-start.4 = (bf16[16,384]{1,0:T(8,128)(2,1)S(1)}, bf16[16,384]{1,0:T(8,128)(2,1)S(1)}, u32[]{:S(2)}, u32[]{:S(2)}) collective-permute-start(bf16[16,384]{1,0:T(8,128)(2,1)S(1)} %get-tuple-element.76.refs_0_), channel_id=1, source_target_pairs={{0,4},{4,0},{8,12},{12,8},{16,20},{20,16},{24,28},{28,24},{1,5},{5... | collective-permute-start | bytes 36872 | tf_op jit(solution)/shard_map/ppermute | solution.py:21
  12.0 3.7 %shard_map.152 = (f32[8,128]{1,0:T(8,128)S(1)}, bf16[256,1024]{1,0:T(8,128)(2,1)S(1)}, bf16[256,128]{1,0:T(8,128)(2,1)S(1)}, f32[256,128]{1,0:T(8,128)S(1)}, bf16[16,1152]{1,0:T(8,128)(2,1)S(1)}) custom-call(s32[1]{0:T(128)} %bitcast.place, f32[8,128]{1,0:T(8,128)S(1)} %get-tuple-element.73.token, bf16[256,512]{1,0:T(8,128)(2,1)S(1)} %copy-done.4, ...), custom_call_target="tpu_custom_call" | custom-call | flops 3000000000 | bytes 3000000 | tf_op jit(solution)/shard_map/pallas_call | solution.py:544
  15.7 1.7 %collective-permute-start.5 = (bf16[32,384]{1,0:T(8,128)(2,1)S(1)}, bf16[32,384]{1,0:T(8,128)(2,1)S(1)}, u32[]{:S(2)}, u32[]{:S(2)}) collective-permute-start(bf16[32,384]{1,0:T(8,128)(2,1)S(1)} %get-tuple-element.78.refs_0_), channel_id=1, source_target_pairs={{0,8},{4,12},{8,0},{12,4},{16,24},{20,28},{24,16},{28,20},{1,9},{5... | collective-permute-start | bytes 73736 | tf_op jit(solution)/shard_map/ppermute | solution.py:21
  17.3 3.6 %collective-permute-start.6 = (bf16[16,1152]{1,0:T(8,128)(2,1)S(1)}, bf16[16,1152]{1,0:T(8,128)(2,1)S(1)}, u32[]{:S(2)}, u32[]{:S(2)}) collective-permute-start(bf16[16,1152]{1,0:T(8,128)(2,1)S(1)} %get-tuple-element.84), channel_id=1, source_target_pairs={{0,4},{4,8},{8,12},{12,16},{16,20},{20,24},{24,28},{1,5},{5,9},{9,... | collective-permute-start | bytes 110600 | tf_op jit(solution)/shard_map/ppermute | solution.py:662
  21.0 3.8 %shard_map.154 = (f32[8,128]{1,0:T(8,128)S(1)}, bf16[256,512]{1,0:T(8,128)(2,1)S(1)}, bf16[256,512]{1,0:T(8,128)(2,1)S(1)}) custom-call(s32[1]{0:T(128)} %bitcast.4.place, f32[8,128]{1,0:T(8,128)S(1)} %get-tuple-element.77.token, bf16[32,384]{1,0:T(8,128)(2,1)S(1)} %get-tuple-element.78.refs_0_, bf16[32,384]{1,0:T(8,128)(2,1)S(1)} %collective-permute-done.5.refs_1_, ...), custom_call_target="tpu_custom_call" | custom-call | flops 3500000000 | bytes 3500000 | tf_op jit(solution)/shard_map/pallas_call | solution.py:544
  25.3 1.9 %shard_map.155 = (f32[8,128]{1,0:T(8,128)S(1)}, bf16[256,1024]{1,0:T(8,128)(2,1)S(1)}, bf16[256,128]{1,0:T(8,128)(2,1)S(1)}, f32[256,128]{1,0:T(8,128)S(1)}, f32[64,1024]{1,0:T(8,128)S(1)}) custom-call(s32[1]{0:T(128)} %constant.3.clone.1.place, f32[8,128]{1,0:T(8,128)S(1)} %get-tuple-element.79.token, ...), custom_call_target="tpu_custom_call" | custom-call | flops 2000000000 | bytes 2000000 | tf_op jit(solution)/shard_map/pallas_call | solution.py:544
  27.6 2.7 %collective-permute-start.8 = (bf16[72,1024]{1,0:T(8,128)(2,1)S(1)}, bf16[72,1024]{1,0:T(8,128)(2,1)S(1)}, u32[]{:S(2)}, u32[]{:S(2)}) collective-permute-start(bf16[72,1024]{1,0:T(8,128)(2,1)S(1)} %get-tuple-element.96), channel_id=1, source_target_pairs={{0,4},{4,0},{8,12},{12,8},{16,20},{20,16},{24,28},{28,24},{1,5},{5... | collective-permute-start | bytes 442376 | tf_op jit(solution)/shard_map/ppermute | solution.py:21
  30.3 1.4 %shard_map.157 = (f32[8,128]{1,0:T(8,128)S(1)}, f32[256,1024]{1,0:T(8,128)S(1)}, f32[256,128]{1,0:T(8,128)S(1)}, bf16[256,128]{1,0:T(8,128)(2,1)S(1)}) custom-call(s32[1]{0:T(128)} %constant.3.clone.1.place, f32[8,128]{1,0:T(8,128)S(1)} %get-tuple-element.87.token, bf16[16,1024]{1,0:T(8,128)(2,1)S(1)} %get-tuple-element.88.refs_0_, ...), custom_call_target="tpu_custom_call" | custom-call | flops 2500000000 | bytes 2500000 | tf_op jit(solution)/shard_map/pallas_call | solution.py:544
  32.6 1.5 %collective-permute-start.9 = (bf16[128,512]{1,0:T(8,128)(2,1)S(1)}, bf16[128,512]{1,0:T(8,128)(2,1)S(1)}, u32[]{:S(2)}, u32[]{:S(2)}) collective-permute-start(bf16[128,512]{1,0:T(8,128)(2,1)S(1)} %get-tuple-element.100), channel_id=1, source_target_pairs={{0,4},{4,0},{8,12},{12,8},{16,20},{20,16},{24,28},{28,24},{1,5},{5... | collective-permute-start | bytes 393224 | tf_op jit(solution)/shard_map/ppermute | solution.py:21
  34.3 1.8 %collective-permute-start.10 = (bf16[72,1024]{1,0:T(8,128)(2,1)S(1)}, bf16[72,1024]{1,0:T(8,128)(2,1)S(1)}, u32[]{:S(2)}, u32[]{:S(2)}) collective-permute-start(bf16[72,1024]{1,0:T(8,128)(2,1)S(1)} %get-tuple-element.102), channel_id=1, source_target_pairs={{0,8},{4,12},{8,0},{12,4},{16,24},{20,28},{24,16},{28,20},{1,9},{5... | collective-permute-start | bytes 442376 | tf_op jit(solution)/shard_map/ppermute | solution.py:21
  36.1 1.6 %collective-permute-done.9.refs_1_ = bf16[128,512]{1,0:T(8,128)(2,1)S(1)} collective-permute-done((bf16[128,512]{1,0:T(8,128)(2,1)S(1)}, bf16[128,512]{1,0:T(8,128)(2,1)S(1)}, u32[]{:S(2)}, u32[]{:S(2)}) %collective-permute-start.9) | collective-permute-done | bytes 131104 | tf_op jit(solution)/shard_map/ppermute | solution.py:21
  37.7 2.7 %collective-permute-start.11 = (bf16[64,512]{1,0:T(8,128)(2,1)S(1)}, bf16[64,512]{1,0:T(8,128)(2,1)S(1)}, u32[]{:S(2)}, u32[]{:S(2)}) collective-permute-start(bf16[64,512]{1,0:T(8,128)(2,1)S(1)} %get-tuple-element.107), channel_id=1, source_target_pairs={{0,16},{4,20},{8,24},{12,28},{16,0},{20,4},{24,8},{28,12},{1,17},{... | collective-permute-start | bytes 196616 | tf_op jit(solution)/shard_map/ppermute | solution.py:21
  40.5 1.5 %collective-permute-start.12 = (bf16[72,1024]{1,0:T(8,128)(2,1)S(1)}, bf16[72,1024]{1,0:T(8,128)(2,1)S(1)}, u32[]{:S(2)}, u32[]{:S(2)}) collective-permute-start(bf16[72,1024]{1,0:T(8,128)(2,1)S(1)} %get-tuple-element.109), channel_id=1, source_target_pairs={{0,16},{4,20},{8,24},{12,28},{16,0},{20,4},{24,8},{28,12},{1,17},{... | collective-permute-start | bytes 442376 | tf_op jit(solution)/shard_map/ppermute | solution.py:21
  42.1 3.6 %collective-permute-done.11.refs_1_ = bf16[64,512]{1,0:T(8,128)(2,1)S(1)} collective-permute-done((bf16[64,512]{1,0:T(8,128)(2,1)S(1)}, bf16[64,512]{1,0:T(8,128)(2,1)S(1)}, u32[]{:S(2)}, u32[]{:S(2)}) %collective-permute-start.11) | collective-permute-done | bytes 65568 | tf_op jit(solution)/shard_map/ppermute | solution.py:21
  45.8 1.6 %collective-permute-start.14 = (bf16[64,512]{1,0:T(8,128)(2,1)S(1)}, bf16[64,512]{1,0:T(8,128)(2,1)S(1)}, u32[]{:S(2)}, u32[]{:S(2)}) collective-permute-start(bf16[64,512]{1,0:T(8,128)(2,1)S(1)} %get-tuple-element.117.refs_0_), channel_id=1, source_target_pairs={{0,2},{1,3},{2,0},{3,1},{4,6},{5,7},{6,4},{7,5},{8,10},{9,11},{10,... | collective-permute-start | bytes 196616 | tf_op jit(solution)/shard_map/ppermute | solution.py:21
  47.3 1.7 %collective-permute-done.12.refs_0_ = bf16[72,1024]{1,0:T(8,128)(2,1)S(1)} collective-permute-done((bf16[72,1024]{1,0:T(8,128)(2,1)S(1)}, bf16[72,1024]{1,0:T(8,128)(2,1)S(1)}, u32[]{:S(2)}, u32[]{:S(2)}) %collective-permute-start.12) | collective-permute-done | bytes 147488 | tf_op jit(solution)/shard_map/ppermute | solution.py:21
  49.0 1.4 %shard_map.163 = (f32[8,128]{1,0:T(8,128)S(1)}, bf16[256,512]{1,0:T(8,128)(2,1)S(1)}, bf16[256,1024]{1,0:T(8,128)(2,1)S(1)}) custom-call(s32[2]{0:T(128)S(1)} %pad_add_fusion.place, f32[8,128]{1,0:T(8,128)S(1)} %get-tuple-element.108.token, bf16[72,1024]{1,0:T(8,128)(2,1)S(1)} %collective-permute-done.12.refs_0_, f32[72,1024]{1,0:T(8,128)S(1)} %get-tuple-element.110.refs_1_, ...), custom_call_target="tpu_custom_call" | custom-call | flops 1500000000 | bytes 1500000 | tf_op jit(solution)/shard_map/pallas_call | solution.py:544
  51.1 1.2 %shard_map.164 = (f32[8,128]{1,0:T(8,128)S(1)}, bf16[256,512]{1,0:T(8,128)(2,1)S(1)}, f32[256,512]{1,0:T(8,128)S(1)}) custom-call(s32[2]{0:T(128)S(1)} %pad_add_fusion.place, f32[8,128]{1,0:T(8,128)S(1)} %get-tuple-element.114.token, bf16[256,1024]{1,0:T(8,128)(2,1)S(1)} %get-tuple-element.115.refs_0_.refs_9_, bf16[1024,2048]{1,0:T(8,128)(2,1)S(1)} %copy-done), custom_call_target="tpu_custom_call" | custom-call | flops 1000000000 | bytes 1000000 | tf_op jit(solution)/shard_map/pallas_call | solution.py:544
  54.1 1.6 %collective-permute-start.19 = (bf16[256,512]{1,0:T(8,128)(2,1)S(1)}, bf16[256,512]{1,0:T(8,128)(2,1)S(1)}, u32[]{:S(2)}, u32[]{:S(2)}) collective-permute-start(bf16[256,512]{1,0:T(8,128)(2,1)S(1)} %get-tuple-element.132), channel_id=1, source_target_pairs={{0,2},{1,3},{2,0},{3,1},{4,6},{5,7},{6,4},{7,5},{8,10},{9,11},{10,... | collective-permute-start | bytes 786440 | tf_op jit(solution)/shard_map/ppermute | solution.py:21
  55.7 2.5 %shard_map.167 = (f32[8,128]{1,0:T(8,128)S(1)}, bf16[64,512]{1,0:T(8,128)(2,1)S(1)}, bf16[64,512]{1,0:T(8,128)(2,1)S(1)}, f32[64,512]{1,0:T(8,128)S(1)}, f32[64,512]{1,0:T(8,128)S(1)}, /*index=5*/f32[256,512]{1,0:T(8,128)S(1)}) custom-call(s32[2]{0:T(128)S(1)} %pad_add_fusion.place, f32[8,128]{1,0:T(8,128)S(1)} %get-tuple-element.121.token, ...), custom_call_target="tpu_custom_call" | custom-call | flops 2500000000 | bytes 2500000 | tf_op jit(solution)/shard_map/pallas_call | solution.py:544
  60.2 3.8 %collective-permute-done.21.refs_5_ = bf16[64,512]{1,0:T(8,128)(2,1)S(1)} collective-permute-done((bf16[64,512]{1,0:T(8,128)(2,1)S(1)}, bf16[64,512]{1,0:T(8,128)(2,1)S(1)}, u32[]{:S(2)}, u32[]{:S(2)}) %collective-permute-start.21) | collective-permute-done | bytes 65568 | tf_op jit(solution)/shard_map/ppermute | solution.py:21
  (69 shorter events, 9.4 us)
Async XLA Ops:
  0.7 9.5 %collective-permute-start.1 = (bf16[256,512]{1,0:T(8,128)(2,1)}, bf16[256,512]{1,0:T(8,128)(2,1)S(1)}, u32[]{:S(2)}, u32[]{:S(2)}) collective-permute-start(bf16[256,512]{1,0:T(8,128)(2,1)} %refs_0_.1), channel_id=1, source_target_pairs={{0,2},{1,3},{2,0},{3,1},{4,6},{5,7},{6,4},{7,5},{8,10},{9,11},{10,... | collective-permute-start | bytes 786440 | tf_op jit(solution)/shard_map/ppermute | solution.py:21
  4.4 4.6 %collective-permute-start = (bf16[8,384]{1,0:T(8,128)(2,1)S(1)}, bf16[8,384]{1,0:T(8,128)(2,1)S(1)}, u32[]{:S(2)}, u32[]{:S(2)}) collective-permute-start(bf16[8,384]{1,0:T(8,128)(2,1)S(1)} %get-tuple-element.71.refs_0_), channel_id=1, source_target_pairs={{0,16},{4,20},{8,24},{12,28},{16,0},{20,4},{24,8},{28,12},{1,17},{... | collective-permute-start | bytes 18440 | tf_op jit(solution)/shard_map/ppermute | solution.py:21
  7.1 4.9 %collective-permute-start.2 = (bf16[256,512]{1,0:T(8,128)(2,1)S(1)}, bf16[256,512]{1,0:T(8,128)(2,1)S(1)}, u32[]{:S(2)}, u32[]{:S(2)}) collective-permute-start(bf16[256,512]{1,0:T(8,128)(2,1)S(1)} %copy-done.4), channel_id=1, source_target_pairs={{0,1},{1,0},{2,3},{3,2},{4,5},{5,4},{6,7},{7,6},{8,9},{9,8},{10,11... | collective-permute-start | bytes 786440 | tf_op jit(solution)/shard_map/ppermute | solution.py:21
  10.2 1.7 %collective-permute-start.3 = (bf16[256,512]{1,0:T(8,128)(2,1)S(1)}, bf16[256,512]{1,0:T(8,128)(2,1)S(1)}, u32[]{:S(2)}, u32[]{:S(2)}) collective-permute-start(bf16[256,512]{1,0:T(8,128)(2,1)S(1)} %get-tuple-element.74.refs_2_), channel_id=1, source_target_pairs={{0,1},{1,0},{2,3},{3,2},{4,5},{5,4},{6,7},{7,6},{8,9},{9,8},{10,11... | collective-permute-start | bytes 786440 | tf_op jit(solution)/shard_map/ppermute | solution.py:21
  10.2 5.4 %collective-permute-start.4 = (bf16[16,384]{1,0:T(8,128)(2,1)S(1)}, bf16[16,384]{1,0:T(8,128)(2,1)S(1)}, u32[]{:S(2)}, u32[]{:S(2)}) collective-permute-start(bf16[16,384]{1,0:T(8,128)(2,1)S(1)} %get-tuple-element.76.refs_0_), channel_id=1, source_target_pairs={{0,4},{4,0},{8,12},{12,8},{16,20},{20,16},{24,28},{28,24},{1,5},{5... | collective-permute-start | bytes 36872 | tf_op jit(solution)/shard_map/ppermute | solution.py:21
  15.7 5.2 %collective-permute-start.5 = (bf16[32,384]{1,0:T(8,128)(2,1)S(1)}, bf16[32,384]{1,0:T(8,128)(2,1)S(1)}, u32[]{:S(2)}, u32[]{:S(2)}) collective-permute-start(bf16[32,384]{1,0:T(8,128)(2,1)S(1)} %get-tuple-element.78.refs_0_), channel_id=1, source_target_pairs={{0,8},{4,12},{8,0},{12,4},{16,24},{20,28},{24,16},{28,20},{1,9},{5... | collective-permute-start | bytes 73736 | tf_op jit(solution)/shard_map/ppermute | solution.py:21
  17.3 9.9 %collective-permute-start.6 = (bf16[16,1152]{1,0:T(8,128)(2,1)S(1)}, bf16[16,1152]{1,0:T(8,128)(2,1)S(1)}, u32[]{:S(2)}, u32[]{:S(2)}) collective-permute-start(bf16[16,1152]{1,0:T(8,128)(2,1)S(1)} %get-tuple-element.84), channel_id=1, source_target_pairs={{0,4},{4,8},{8,12},{12,16},{16,20},{20,24},{24,28},{1,5},{5,9},{9,... | collective-permute-start | bytes 110600 | tf_op jit(solution)/shard_map/ppermute | solution.py:662
  24.7 7.8 %collective-permute-start.7 = (bf16[256,512]{1,0:T(8,128)(2,1)S(1)}, bf16[256,512]{1,0:T(8,128)(2,1)S(1)}, u32[]{:S(2)}, u32[]{:S(2)}) collective-permute-start(bf16[256,512]{1,0:T(8,128)(2,1)S(1)} %get-tuple-element.94), channel_id=1, source_target_pairs={{0,8},{4,12},{8,0},{12,4},{16,24},{20,28},{24,16},{28,20},{1,9},{5... | collective-permute-start | bytes 786440 | tf_op jit(solution)/shard_map/ppermute | solution.py:21
  27.6 6.6 %collective-permute-start.8 = (bf16[72,1024]{1,0:T(8,128)(2,1)S(1)}, bf16[72,1024]{1,0:T(8,128)(2,1)S(1)}, u32[]{:S(2)}, u32[]{:S(2)}) collective-permute-start(bf16[72,1024]{1,0:T(8,128)(2,1)S(1)} %get-tuple-element.96), channel_id=1, source_target_pairs={{0,4},{4,0},{8,12},{12,8},{16,20},{20,16},{24,28},{28,24},{1,5},{5... | collective-permute-start | bytes 442376 | tf_op jit(solution)/shard_map/ppermute | solution.py:21
  32.6 5.0 %collective-permute-start.9 = (bf16[128,512]{1,0:T(8,128)(2,1)S(1)}, bf16[128,512]{1,0:T(8,128)(2,1)S(1)}, u32[]{:S(2)}, u32[]{:S(2)}) collective-permute-start(bf16[128,512]{1,0:T(8,128)(2,1)S(1)} %get-tuple-element.100), channel_id=1, source_target_pairs={{0,4},{4,0},{8,12},{12,8},{16,20},{20,16},{24,28},{28,24},{1,5},{5... | collective-permute-start | bytes 393224 | tf_op jit(solution)/shard_map/ppermute | solution.py:21
  34.3 6.1 %collective-permute-start.10 = (bf16[72,1024]{1,0:T(8,128)(2,1)S(1)}, bf16[72,1024]{1,0:T(8,128)(2,1)S(1)}, u32[]{:S(2)}, u32[]{:S(2)}) collective-permute-start(bf16[72,1024]{1,0:T(8,128)(2,1)S(1)} %get-tuple-element.102), channel_id=1, source_target_pairs={{0,8},{4,12},{8,0},{12,4},{16,24},{20,28},{24,16},{28,20},{1,9},{5... | collective-permute-start | bytes 442376 | tf_op jit(solution)/shard_map/ppermute | solution.py:21
  37.7 11.3 %copy-start = (bf16[1024,2048]{1,0:T(8,128)(2,1)S(1)}, bf16[1024,2048]{1,0:T(8,128)(2,1)}, u32[]{:S(2)}) copy-start(bf16[1024,2048]{1,0:T(8,128)(2,1)} %refs_11_.1) | copy-start | bytes 12582916
  37.7 11.3 %copy-start.1 = (f32[1024]{0:T(1024)S(1)}, f32[1024]{0:T(1024)}, u32[]{:S(2)}) copy-start(f32[1024]{0:T(1024)} %param.26) | copy-start | bytes 12292
  37.7 8.0 %collective-permute-start.11 = (bf16[64,512]{1,0:T(8,128)(2,1)S(1)}, bf16[64,512]{1,0:T(8,128)(2,1)S(1)}, u32[]{:S(2)}, u32[]{:S(2)}) collective-permute-start(bf16[64,512]{1,0:T(8,128)(2,1)S(1)} %get-tuple-element.107), channel_id=1, source_target_pairs={{0,16},{4,20},{8,24},{12,28},{16,0},{20,4},{24,8},{28,12},{1,17},{... | collective-permute-start | bytes 196616 | tf_op jit(solution)/shard_map/ppermute | solution.py:21
  40.5 8.5 %collective-permute-start.12 = (bf16[72,1024]{1,0:T(8,128)(2,1)S(1)}, bf16[72,1024]{1,0:T(8,128)(2,1)S(1)}, u32[]{:S(2)}, u32[]{:S(2)}) collective-permute-start(bf16[72,1024]{1,0:T(8,128)(2,1)S(1)} %get-tuple-element.109), channel_id=1, source_target_pairs={{0,16},{4,20},{8,24},{12,28},{16,0},{20,4},{24,8},{28,12},{1,17},{... | collective-permute-start | bytes 442376 | tf_op jit(solution)/shard_map/ppermute | solution.py:21
  45.8 5.3 %collective-permute-start.14 = (bf16[64,512]{1,0:T(8,128)(2,1)S(1)}, bf16[64,512]{1,0:T(8,128)(2,1)S(1)}, u32[]{:S(2)}, u32[]{:S(2)}) collective-permute-start(bf16[64,512]{1,0:T(8,128)(2,1)S(1)} %get-tuple-element.117.refs_0_), channel_id=1, source_target_pairs={{0,2},{1,3},{2,0},{3,1},{4,6},{5,7},{6,4},{7,5},{8,10},{9,11},{10,... | collective-permute-start | bytes 196616 | tf_op jit(solution)/shard_map/ppermute | solution.py:21
  50.5 3.6 %collective-permute-start.16 = (bf16[256,512]{1,0:T(8,128)(2,1)S(1)}, bf16[256,512]{1,0:T(8,128)(2,1)S(1)}, u32[]{:S(2)}, u32[]{:S(2)}) collective-permute-start(bf16[256,512]{1,0:T(8,128)(2,1)S(1)} %get-tuple-element.120), channel_id=1, source_target_pairs={{0,1},{1,0},{2,3},{3,2},{4,5},{5,4},{6,7},{7,6},{8,9},{9,8},{10,11... | collective-permute-start | bytes 786440 | tf_op jit(solution)/shard_map/ppermute | solution.py:21
  50.6 2.3 %collective-permute-start.13 = (bf16[64,512]{1,0:T(8,128)(2,1)S(1)}, bf16[64,512]{1,0:T(8,128)(2,1)S(1)}, u32[]{:S(2)}, u32[]{:S(2)}) collective-permute-start(bf16[64,512]{1,0:T(8,128)(2,1)S(1)} %get-tuple-element.117.refs_0_), channel_id=1, source_target_pairs={{0,1},{1,0},{2,3},{3,2},{4,5},{5,4},{6,7},{7,6},{8,9},{9,8},{10,11... | collective-permute-start | bytes 196616 | tf_op jit(solution)/shard_map/ppermute | solution.py:21
  51.1 1.8 %collective-permute-start.15 = (bf16[64,512]{1,0:T(8,128)(2,1)S(1)}, bf16[64,512]{1,0:T(8,128)(2,1)S(1)}, u32[]{:S(2)}, u32[]{:S(2)}) collective-permute-start(bf16[64,512]{1,0:T(8,128)(2,1)S(1)} %collective-permute-done.14.refs_2_), channel_id=1, source_target_pairs={{0,1},{1,0},{2,3},{3,2},{4,5},{5,4},{6,7},{7,6},{8,9},{9,8},{10,11... | collective-permute-start | bytes 196616 | tf_op jit(solution)/shard_map/ppermute | solution.py:21
  52.4 7.8 %collective-permute-start.18 = (bf16[256,512]{1,0:T(8,128)(2,1)S(1)}, bf16[256,512]{1,0:T(8,128)(2,1)S(1)}, u32[]{:S(2)}, u32[]{:S(2)}) collective-permute-start(bf16[256,512]{1,0:T(8,128)(2,1)S(1)} %get-tuple-element.131), channel_id=1, source_target_pairs={{0,1},{1,0},{2,3},{3,2},{4,5},{5,4},{6,7},{7,6},{8,9},{9,8},{10,11... | collective-permute-start | bytes 786440 | tf_op jit(solution)/shard_map/ppermute | solution.py:21
  54.1 9.8 %collective-permute-start.19 = (bf16[256,512]{1,0:T(8,128)(2,1)S(1)}, bf16[256,512]{1,0:T(8,128)(2,1)S(1)}, u32[]{:S(2)}, u32[]{:S(2)}) collective-permute-start(bf16[256,512]{1,0:T(8,128)(2,1)S(1)} %get-tuple-element.132), channel_id=1, source_target_pairs={{0,2},{1,3},{2,0},{3,1},{4,6},{5,7},{6,4},{7,5},{8,10},{9,11},{10,... | collective-permute-start | bytes 786440 | tf_op jit(solution)/shard_map/ppermute | solution.py:21
  58.3 1.3 %collective-permute-start.17 = (bf16[64,512]{1,0:T(8,128)(2,1)S(1)}, bf16[64,512]{1,0:T(8,128)(2,1)S(1)}, u32[]{:S(2)}, u32[]{:S(2)}) collective-permute-start(bf16[64,512]{1,0:T(8,128)(2,1)S(1)} %get-tuple-element.128), channel_id=1, source_target_pairs={{0,1},{1,0},{2,3},{3,2},{4,5},{5,4},{6,7},{7,6},{8,9},{9,8},{10,11... | collective-permute-start | bytes 196616 | tf_op jit(solution)/shard_map/ppermute | solution.py:21
  58.4 1.8 %collective-permute-start.20 = (bf16[64,512]{1,0:T(8,128)(2,1)S(1)}, bf16[64,512]{1,0:T(8,128)(2,1)S(1)}, u32[]{:S(2)}, u32[]{:S(2)}) collective-permute-start(bf16[64,512]{1,0:T(8,128)(2,1)S(1)} %get-tuple-element.134), channel_id=1, source_target_pairs={{0,1},{1,0},{2,3},{3,2},{4,5},{5,4},{6,7},{7,6},{8,9},{9,8},{10,11... | collective-permute-start | bytes 196616 | tf_op jit(solution)/shard_map/ppermute | solution.py:21
  59.6 4.3 %collective-permute-start.21 = (bf16[64,512]{1,0:T(8,128)(2,1)S(1)}, bf16[64,512]{1,0:T(8,128)(2,1)S(1)}, u32[]{:S(2)}, u32[]{:S(2)}) collective-permute-start(bf16[64,512]{1,0:T(8,128)(2,1)S(1)} %get-tuple-element.135), channel_id=1, source_target_pairs={{0,2},{1,3},{2,0},{3,1},{4,6},{5,7},{6,4},{7,5},{8,10},{9,11},{10,... | collective-permute-start | bytes 196616 | tf_op jit(solution)/shard_map/ppermute | solution.py:21
  (11 other events, 70.5 us)

commit v9 on v7

--- a/solution.py
+++ b/solution.py
@@ -442,8 +442,11 @@
     out[...] = (kept[...] + got[...].astype(F32)).astype(BF16)
 
 
-def total_kernel(rows, place, kept, got, far, dec_kept, dec_got, dec_far, out, dec_out):
+def total_kernel(place, kept, got, far, out):
     out[...] = (kept[...] + got[...].astype(F32) + far[...].astype(F32)).astype(BF16)
+
+
+def decode_total_kernel(rows, place, dec_kept, dec_got, dec_far, dec_out):
     total = dec_kept[...] + dec_got[...].astype(F32) + dec_far[...].astype(F32)
     asked = total.shape[0]
     steps = asked // rows
@@ -799,11 +802,14 @@
         2.5,
     )
     decode_crossed = crossed(*decode_back)
-    prompt_out, decode_out = called(
-        functools.partial(total_kernel, rows),
+    (prompt_out,) = called(
+        total_kernel, none, [*prompt_crossed], [shaped((tokens, part), BF16)]
+    )
+    (decode_out,) = called(
+        functools.partial(decode_total_kernel, rows),
         none,
-        [*prompt_crossed, *decode_crossed],
-        [shaped((tokens, part), BF16), shaped((rows, steps, part), BF16)],
+        [*decode_crossed],
+        [shaped((rows, steps, part), BF16)],
     )
     return (prompt_out, decode_out)
 

time: 65.3 us -> 65.1 us (level)
  waiting for transfers between devices: 15.7 us -> 14.9 us
    ppermute x21, waiting for transfers between devices: 15.7 us -> 14.9 us  [swapped(): return lax.ppermute(value, axis, [(i, i ^ bit) for i in range(count)])]
    pallas_call x21 -> x22, Pallas kernels: 18.8 us -> 19.4 us  [__call__(): pl.pallas_call(ordered, out_shape=[shaped((8, LANES), F32)] + outs, in_sp...]
  transfers between devices with their start and end apart: 22 -> 22, of which waited for: 8 -> 9; matrix products, arithmetic and copies ran while one was open for 0% -> 0% of each run, Pallas kernels for 27% -> 29%
where the time goes in v9:
time: 65.1 us; the launch traced here: 65 us
  starting transfers between devices  28.8 us (44%)
  Pallas kernels  19.4 us (30%)
  waiting for transfers between devices  14.9 us (23%)
  between operations  0.92 us (1%)
  local copies, waits for them, and re-layouts  0.74 us (1%)
    ppermute x21, starting transfers between devices, swapped(): return lax.ppermute(value, axis, [(i, i ^ bit) for i in range(count)])  25.3 us
    pallas_call x22, Pallas kernels, __call__(): pl.pallas_call(ordered, out_shape=[shaped((8, LANES), F32)] + outs, in_sp...  19.4 us
    ppermute x21, waiting for transfers between devices, swapped(): return lax.ppermute(value, axis, [(i, i ^ bit) for i in range(count)])  14.9 us
    ppermute x1, starting transfers between devices, on_device(): halo = lax.ppermute(halo, 'ctx', [(c, c + 1) for c in range(groups - 1)])  3.57 us
  transfers between devices with their start and end apart: 22, of which 9 were waited for; matrix products, arithmetic and copies ran while one was open for 0% of the time, Pallas kernels for 29%

profile of v9, /device:TPU:0, one launch (start us, length us, event | category | flops | bytes accessed | tf_op | source)
XLA Modules:
  0.0 65.0 jit_solution(10040134895944421902)
XLA Ops:
  0.7 3.0 %collective-permute-start.1 = (bf16[256,512]{1,0:T(8,128)(2,1)}, bf16[256,512]{1,0:T(8,128)(2,1)S(1)}, u32[]{:S(2)}, u32[]{:S(2)}) collective-permute-start(bf16[256,512]{1,0:T(8,128)(2,1)} %refs_0_.1), channel_id=1, source_target_pairs={{0,2},{1,3},{2,0},{3,1},{4,6},{5,7},{6,4},{7,5},{8,10},{9,11},{10,... | collective-permute-start | bytes 786440 | tf_op jit(solution)/shard_map/ppermute | solution.py:21
  4.4 2.7 %collective-permute-start = (bf16[8,384]{1,0:T(8,128)(2,1)S(1)}, bf16[8,384]{1,0:T(8,128)(2,1)S(1)}, u32[]{:S(2)}, u32[]{:S(2)}) collective-permute-start(bf16[8,384]{1,0:T(8,128)(2,1)S(1)} %get-tuple-element.72.refs_0_), channel_id=1, source_target_pairs={{0,16},{4,20},{8,24},{12,28},{16,0},{20,4},{24,8},{28,12},{1,17},{... | collective-permute-start | bytes 18440 | tf_op jit(solution)/shard_map/ppermute | solution.py:21
  7.1 1.9 %collective-permute-done.refs_1_ = bf16[8,384]{1,0:T(8,128)(2,1)S(1)} collective-permute-done((bf16[8,384]{1,0:T(8,128)(2,1)S(1)}, bf16[8,384]{1,0:T(8,128)(2,1)S(1)}, u32[]{:S(2)}, u32[]{:S(2)}) %collective-permute-start) | collective-permute-done | bytes 6176 | tf_op jit(solution)/shard_map/ppermute | solution.py:21
  10.2 1.7 %collective-permute-start.4 = (bf16[16,384]{1,0:T(8,128)(2,1)S(1)}, bf16[16,384]{1,0:T(8,128)(2,1)S(1)}, u32[]{:S(2)}, u32[]{:S(2)}) collective-permute-start(bf16[16,384]{1,0:T(8,128)(2,1)S(1)} %get-tuple-element.77.refs_0_), channel_id=1, source_target_pairs={{0,4},{4,0},{8,12},{12,8},{16,20},{20,16},{24,28},{28,24},{1,5},{5... | collective-permute-start | bytes 36872 | tf_op jit(solution)/shard_map/ppermute | solution.py:21
  12.0 3.7 %shard_map.152 = (f32[8,128]{1,0:T(8,128)S(1)}, bf16[256,1024]{1,0:T(8,128)(2,1)S(1)}, bf16[256,128]{1,0:T(8,128)(2,1)S(1)}, f32[256,128]{1,0:T(8,128)S(1)}, bf16[16,1152]{1,0:T(8,128)(2,1)S(1)}) custom-call(s32[1]{0:T(128)} %bitcast.place, f32[8,128]{1,0:T(8,128)S(1)} %get-tuple-element.74.token, bf16[256,512]{1,0:T(8,128)(2,1)S(1)} %copy-done.4, ...), custom_call_target="tpu_custom_call" | custom-call | flops 3000000000 | bytes 3000000 | tf_op jit(solution)/shard_map/pallas_call | solution.py:544
  15.7 1.7 %collective-permute-start.5 = (bf16[32,384]{1,0:T(8,128)(2,1)S(1)}, bf16[32,384]{1,0:T(8,128)(2,1)S(1)}, u32[]{:S(2)}, u32[]{:S(2)}) collective-permute-start(bf16[32,384]{1,0:T(8,128)(2,1)S(1)} %get-tuple-element.79.refs_0_), channel_id=1, source_target_pairs={{0,8},{4,12},{8,0},{12,4},{16,24},{20,28},{24,16},{28,20},{1,9},{5... | collective-permute-start | bytes 73736 | tf_op jit(solution)/shard_map/ppermute | solution.py:21
  17.3 3.6 %collective-permute-start.6 = (bf16[16,1152]{1,0:T(8,128)(2,1)S(1)}, bf16[16,1152]{1,0:T(8,128)(2,1)S(1)}, u32[]{:S(2)}, u32[]{:S(2)}) collective-permute-start(bf16[16,1152]{1,0:T(8,128)(2,1)S(1)} %get-tuple-element.85), channel_id=1, source_target_pairs={{0,4},{4,8},{8,12},{12,16},{16,20},{20,24},{24,28},{1,5},{5,9},{9,... | collective-permute-start | bytes 110600 | tf_op jit(solution)/shard_map/ppermute | solution.py:662
  21.0 3.8 %shard_map.154 = (f32[8,128]{1,0:T(8,128)S(1)}, bf16[256,512]{1,0:T(8,128)(2,1)S(1)}, bf16[256,512]{1,0:T(8,128)(2,1)S(1)}) custom-call(s32[1]{0:T(128)} %bitcast.4.place, f32[8,128]{1,0:T(8,128)S(1)} %get-tuple-element.78.token, bf16[32,384]{1,0:T(8,128)(2,1)S(1)} %get-tuple-element.79.refs_0_, bf16[32,384]{1,0:T(8,128)(2,1)S(1)} %collective-permute-done.5.refs_1_, ...), custom_call_target="tpu_custom_call" | custom-call | flops 3500000000 | bytes 3500000 | tf_op jit(solution)/shard_map/pallas_call | solution.py:544
  25.3 1.9 %shard_map.155 = (f32[8,128]{1,0:T(8,128)S(1)}, bf16[256,1024]{1,0:T(8,128)(2,1)S(1)}, bf16[256,128]{1,0:T(8,128)(2,1)S(1)}, f32[256,128]{1,0:T(8,128)S(1)}, f32[64,1024]{1,0:T(8,128)S(1)}) custom-call(s32[1]{0:T(128)} %constant.3.clone.1.place, f32[8,128]{1,0:T(8,128)S(1)} %get-tuple-element.80.token, ...), custom_call_target="tpu_custom_call" | custom-call | flops 2000000000 | bytes 2000000 | tf_op jit(solution)/shard_map/pallas_call | solution.py:544
  27.6 2.7 %collective-permute-start.8 = (bf16[72,1024]{1,0:T(8,128)(2,1)S(1)}, bf16[72,1024]{1,0:T(8,128)(2,1)S(1)}, u32[]{:S(2)}, u32[]{:S(2)}) collective-permute-start(bf16[72,1024]{1,0:T(8,128)(2,1)S(1)} %get-tuple-element.97), channel_id=1, source_target_pairs={{0,4},{4,0},{8,12},{12,8},{16,20},{20,16},{24,28},{28,24},{1,5},{5... | collective-permute-start | bytes 442376 | tf_op jit(solution)/shard_map/ppermute | solution.py:21
  30.3 1.4 %shard_map.157 = (f32[8,128]{1,0:T(8,128)S(1)}, f32[256,1024]{1,0:T(8,128)S(1)}, f32[256,128]{1,0:T(8,128)S(1)}, bf16[256,128]{1,0:T(8,128)(2,1)S(1)}) custom-call(s32[1]{0:T(128)} %constant.3.clone.1.place, f32[8,128]{1,0:T(8,128)S(1)} %get-tuple-element.88.token, bf16[16,1024]{1,0:T(8,128)(2,1)S(1)} %get-tuple-element.89.refs_0_, ...), custom_call_target="tpu_custom_call" | custom-call | flops 2500000000 | bytes 2500000 | tf_op jit(solution)/shard_map/pallas_call | solution.py:544
  32.6 1.5 %collective-permute-start.9 = (bf16[128,512]{1,0:T(8,128)(2,1)S(1)}, bf16[128,512]{1,0:T(8,128)(2,1)S(1)}, u32[]{:S(2)}, u32[]{:S(2)}) collective-permute-start(bf16[128,512]{1,0:T(8,128)(2,1)S(1)} %get-tuple-element.101), channel_id=1, source_target_pairs={{0,4},{4,0},{8,12},{12,8},{16,20},{20,16},{24,28},{28,24},{1,5},{5... | collective-permute-start | bytes 393224 | tf_op jit(solution)/shard_map/ppermute | solution.py:21
  34.3 1.8 %collective-permute-start.10 = (bf16[72,1024]{1,0:T(8,128)(2,1)S(1)}, bf16[72,1024]{1,0:T(8,128)(2,1)S(1)}, u32[]{:S(2)}, u32[]{:S(2)}) collective-permute-start(bf16[72,1024]{1,0:T(8,128)(2,1)S(1)} %get-tuple-element.103), channel_id=1, source_target_pairs={{0,8},{4,12},{8,0},{12,4},{16,24},{20,28},{24,16},{28,20},{1,9},{5... | collective-permute-start | bytes 442376 | tf_op jit(solution)/shard_map/ppermute | solution.py:21
  36.1 1.6 %collective-permute-done.9.refs_1_ = bf16[128,512]{1,0:T(8,128)(2,1)S(1)} collective-permute-done((bf16[128,512]{1,0:T(8,128)(2,1)S(1)}, bf16[128,512]{1,0:T(8,128)(2,1)S(1)}, u32[]{:S(2)}, u32[]{:S(2)}) %collective-permute-start.9) | collective-permute-done | bytes 131104 | tf_op jit(solution)/shard_map/ppermute | solution.py:21
  37.7 2.7 %collective-permute-start.11 = (bf16[64,512]{1,0:T(8,128)(2,1)S(1)}, bf16[64,512]{1,0:T(8,128)(2,1)S(1)}, u32[]{:S(2)}, u32[]{:S(2)}) collective-permute-start(bf16[64,512]{1,0:T(8,128)(2,1)S(1)} %get-tuple-element.108), channel_id=1, source_target_pairs={{0,16},{4,20},{8,24},{12,28},{16,0},{20,4},{24,8},{28,12},{1,17},{... | collective-permute-start | bytes 196616 | tf_op jit(solution)/shard_map/ppermute | solution.py:21
  40.5 1.5 %collective-permute-start.12 = (bf16[72,1024]{1,0:T(8,128)(2,1)S(1)}, bf16[72,1024]{1,0:T(8,128)(2,1)S(1)}, u32[]{:S(2)}, u32[]{:S(2)}) collective-permute-start(bf16[72,1024]{1,0:T(8,128)(2,1)S(1)} %get-tuple-element.110), channel_id=1, source_target_pairs={{0,16},{4,20},{8,24},{12,28},{16,0},{20,4},{24,8},{28,12},{1,17},{... | collective-permute-start | bytes 442376 | tf_op jit(solution)/shard_map/ppermute | solution.py:21
  42.1 3.6 %collective-permute-done.11.refs_1_ = bf16[64,512]{1,0:T(8,128)(2,1)S(1)} collective-permute-done((bf16[64,512]{1,0:T(8,128)(2,1)S(1)}, bf16[64,512]{1,0:T(8,128)(2,1)S(1)}, u32[]{:S(2)}, u32[]{:S(2)}) %collective-permute-start.11) | collective-permute-done | bytes 65568 | tf_op jit(solution)/shard_map/ppermute | solution.py:21
  45.8 1.6 %collective-permute-start.14 = (bf16[64,512]{1,0:T(8,128)(2,1)S(1)}, bf16[64,512]{1,0:T(8,128)(2,1)S(1)}, u32[]{:S(2)}, u32[]{:S(2)}) collective-permute-start(bf16[64,512]{1,0:T(8,128)(2,1)S(1)} %get-tuple-element.118.refs_0_), channel_id=1, source_target_pairs={{0,2},{1,3},{2,0},{3,1},{4,6},{5,7},{6,4},{7,5},{8,10},{9,11},{10,... | collective-permute-start | bytes 196616 | tf_op jit(solution)/shard_map/ppermute | solution.py:21
  47.3 1.7 %collective-permute-done.12.refs_0_ = bf16[72,1024]{1,0:T(8,128)(2,1)S(1)} collective-permute-done((bf16[72,1024]{1,0:T(8,128)(2,1)S(1)}, bf16[72,1024]{1,0:T(8,128)(2,1)S(1)}, u32[]{:S(2)}, u32[]{:S(2)}) %collective-permute-start.12) | collective-permute-done | bytes 147488 | tf_op jit(solution)/shard_map/ppermute | solution.py:21
  49.0 1.4 %shard_map.163 = (f32[8,128]{1,0:T(8,128)S(1)}, bf16[256,512]{1,0:T(8,128)(2,1)S(1)}, bf16[256,1024]{1,0:T(8,128)(2,1)S(1)}) custom-call(s32[2]{0:T(128)S(1)} %pad_add_fusion.place, f32[8,128]{1,0:T(8,128)S(1)} %get-tuple-element.109.token, bf16[72,1024]{1,0:T(8,128)(2,1)S(1)} %collective-permute-done.12.refs_0_, f32[72,1024]{1,0:T(8,128)S(1)} %get-tuple-element.111.refs_1_, ...), custom_call_target="tpu_custom_call" | custom-call | flops 1500000000 | bytes 1500000 | tf_op jit(solution)/shard_map/pallas_call | solution.py:544
  51.1 1.5 %shard_map.164 = (f32[8,128]{1,0:T(8,128)S(1)}, bf16[256,512]{1,0:T(8,128)(2,1)S(1)}, f32[256,512]{1,0:T(8,128)S(1)}, f32[256,512]{1,0:T(8,128)S(1)}) custom-call(s32[2]{0:T(128)S(1)} %pad_add_fusion.place, f32[8,128]{1,0:T(8,128)S(1)} %get-tuple-element.115.token, bf16[256,1024]{1,0:T(8,128)(2,1)S(1)} %get-tuple-element.116.refs_0_, ...), custom_call_target="tpu_custom_call" | custom-call | flops 1000000000 | bytes 1000000 | tf_op jit(solution)/shard_map/pallas_call | solution.py:544
  54.4 1.6 %collective-permute-start.19 = (bf16[256,512]{1,0:T(8,128)(2,1)S(1)}, bf16[256,512]{1,0:T(8,128)(2,1)S(1)}, u32[]{:S(2)}, u32[]{:S(2)}) collective-permute-start(bf16[256,512]{1,0:T(8,128)(2,1)S(1)} %get-tuple-element.133), channel_id=1, source_target_pairs={{0,2},{1,3},{2,0},{3,1},{4,6},{5,7},{6,4},{7,5},{8,10},{9,11},{10,... | collective-permute-start | bytes 786440 | tf_op jit(solution)/shard_map/ppermute | solution.py:21
  56.0 2.2 %shard_map.167 = (f32[8,128]{1,0:T(8,128)S(1)}, bf16[64,512]{1,0:T(8,128)(2,1)S(1)}, bf16[64,512]{1,0:T(8,128)(2,1)S(1)}, f32[64,512]{1,0:T(8,128)S(1)}, f32[64,512]{1,0:T(8,128)S(1)}) custom-call(s32[2]{0:T(128)S(1)} %pad_add_fusion.place, f32[8,128]{1,0:T(8,128)S(1)} %get-tuple-element.122.token, bf16[72,1024]{1,0:T(8,128)(2,1)S(1)} %collective-permute-done.12.refs_0_, ...), custom_call_target="tpu_custom_call" | custom-call | flops 2500000000 | bytes 2500000 | tf_op jit(solution)/shard_map/pallas_call | solution.py:544
  60.1 2.9 %collective-permute-done.19.refs_2_ = bf16[256,512]{1,0:T(8,128)(2,1)S(1)} collective-permute-done((bf16[256,512]{1,0:T(8,128)(2,1)S(1)}, bf16[256,512]{1,0:T(8,128)(2,1)S(1)}, u32[]{:S(2)}, u32[]{:S(2)}) %collective-permute-start.19) | collective-permute-done | bytes 262176 | tf_op jit(solution)/shard_map/ppermute | solution.py:21
  (70 shorter events, 10.3 us)
Async XLA Ops:
  0.7 9.5 %collective-permute-start.1 = (bf16[256,512]{1,0:T(8,128)(2,1)}, bf16[256,512]{1,0:T(8,128)(2,1)S(1)}, u32[]{:S(2)}, u32[]{:S(2)}) collective-permute-start(bf16[256,512]{1,0:T(8,128)(2,1)} %refs_0_.1), channel_id=1, source_target_pairs={{0,2},{1,3},{2,0},{3,1},{4,6},{5,7},{6,4},{7,5},{8,10},{9,11},{10,... | collective-permute-start | bytes 786440 | tf_op jit(solution)/shard_map/ppermute | solution.py:21
  4.4 4.6 %collective-permute-start = (bf16[8,384]{1,0:T(8,128)(2,1)S(1)}, bf16[8,384]{1,0:T(8,128)(2,1)S(1)}, u32[]{:S(2)}, u32[]{:S(2)}) collective-permute-start(bf16[8,384]{1,0:T(8,128)(2,1)S(1)} %get-tuple-element.72.refs_0_), channel_id=1, source_target_pairs={{0,16},{4,20},{8,24},{12,28},{16,0},{20,4},{24,8},{28,12},{1,17},{... | collective-permute-start | bytes 18440 | tf_op jit(solution)/shard_map/ppermute | solution.py:21
  7.1 4.9 %collective-permute-start.2 = (bf16[256,512]{1,0:T(8,128)(2,1)S(1)}, bf16[256,512]{1,0:T(8,128)(2,1)S(1)}, u32[]{:S(2)}, u32[]{:S(2)}) collective-permute-start(bf16[256,512]{1,0:T(8,128)(2,1)S(1)} %copy-done.4), channel_id=1, source_target_pairs={{0,1},{1,0},{2,3},{3,2},{4,5},{5,4},{6,7},{7,6},{8,9},{9,8},{10,11... | collective-permute-start | bytes 786440 | tf_op jit(solution)/shard_map/ppermute | solution.py:21
  10.2 1.7 %collective-permute-start.3 = (bf16[256,512]{1,0:T(8,128)(2,1)S(1)}, bf16[256,512]{1,0:T(8,128)(2,1)S(1)}, u32[]{:S(2)}, u32[]{:S(2)}) collective-permute-start(bf16[256,512]{1,0:T(8,128)(2,1)S(1)} %get-tuple-element.75.refs_2_), channel_id=1, source_target_pairs={{0,1},{1,0},{2,3},{3,2},{4,5},{5,4},{6,7},{7,6},{8,9},{9,8},{10,11... | collective-permute-start | bytes 786440 | tf_op jit(solution)/shard_map/ppermute | solution.py:21
  10.2 5.4 %collective-permute-start.4 = (bf16[16,384]{1,0:T(8,128)(2,1)S(1)}, bf16[16,384]{1,0:T(8,128)(2,1)S(1)}, u32[]{:S(2)}, u32[]{:S(2)}) collective-permute-start(bf16[16,384]{1,0:T(8,128)(2,1)S(1)} %get-tuple-element.77.refs_0_), channel_id=1, source_target_pairs={{0,4},{4,0},{8,12},{12,8},{16,20},{20,16},{24,28},{28,24},{1,5},{5... | collective-permute-start | bytes 36872 | tf_op jit(solution)/shard_map/ppermute | solution.py:21
  15.7 5.2 %collective-permute-start.5 = (bf16[32,384]{1,0:T(8,128)(2,1)S(1)}, bf16[32,384]{1,0:T(8,128)(2,1)S(1)}, u32[]{:S(2)}, u32[]{:S(2)}) collective-permute-start(bf16[32,384]{1,0:T(8,128)(2,1)S(1)} %get-tuple-element.79.refs_0_), channel_id=1, source_target_pairs={{0,8},{4,12},{8,0},{12,4},{16,24},{20,28},{24,16},{28,20},{1,9},{5... | collective-permute-start | bytes 73736 | tf_op jit(solution)/shard_map/ppermute | solution.py:21
  17.3 9.9 %collective-permute-start.6 = (bf16[16,1152]{1,0:T(8,128)(2,1)S(1)}, bf16[16,1152]{1,0:T(8,128)(2,1)S(1)}, u32[]{:S(2)}, u32[]{:S(2)}) collective-permute-start(bf16[16,1152]{1,0:T(8,128)(2,1)S(1)} %get-tuple-element.85), channel_id=1, source_target_pairs={{0,4},{4,8},{8,12},{12,16},{16,20},{20,24},{24,28},{1,5},{5,9},{9,... | collective-permute-start | bytes 110600 | tf_op jit(solution)/shard_map/ppermute | solution.py:662
  24.7 7.8 %collective-permute-start.7 = (bf16[256,512]{1,0:T(8,128)(2,1)S(1)}, bf16[256,512]{1,0:T(8,128)(2,1)S(1)}, u32[]{:S(2)}, u32[]{:S(2)}) collective-permute-start(bf16[256,512]{1,0:T(8,128)(2,1)S(1)} %get-tuple-element.95), channel_id=1, source_target_pairs={{0,8},{4,12},{8,0},{12,4},{16,24},{20,28},{24,16},{28,20},{1,9},{5... | collective-permute-start | bytes 786440 | tf_op jit(solution)/shard_map/ppermute | solution.py:21
  27.6 6.6 %collective-permute-start.8 = (bf16[72,1024]{1,0:T(8,128)(2,1)S(1)}, bf16[72,1024]{1,0:T(8,128)(2,1)S(1)}, u32[]{:S(2)}, u32[]{:S(2)}) collective-permute-start(bf16[72,1024]{1,0:T(8,128)(2,1)S(1)} %get-tuple-element.97), channel_id=1, source_target_pairs={{0,4},{4,0},{8,12},{12,8},{16,20},{20,16},{24,28},{28,24},{1,5},{5... | collective-permute-start | bytes 442376 | tf_op jit(solution)/shard_map/ppermute | solution.py:21
  32.6 5.0 %collective-permute-start.9 = (bf16[128,512]{1,0:T(8,128)(2,1)S(1)}, bf16[128,512]{1,0:T(8,128)(2,1)S(1)}, u32[]{:S(2)}, u32[]{:S(2)}) collective-permute-start(bf16[128,512]{1,0:T(8,128)(2,1)S(1)} %get-tuple-element.101), channel_id=1, source_target_pairs={{0,4},{4,0},{8,12},{12,8},{16,20},{20,16},{24,28},{28,24},{1,5},{5... | collective-permute-start | bytes 393224 | tf_op jit(solution)/shard_map/ppermute | solution.py:21
  34.3 6.1 %collective-permute-start.10 = (bf16[72,1024]{1,0:T(8,128)(2,1)S(1)}, bf16[72,1024]{1,0:T(8,128)(2,1)S(1)}, u32[]{:S(2)}, u32[]{:S(2)}) collective-permute-start(bf16[72,1024]{1,0:T(8,128)(2,1)S(1)} %get-tuple-element.103), channel_id=1, source_target_pairs={{0,8},{4,12},{8,0},{12,4},{16,24},{20,28},{24,16},{28,20},{1,9},{5... | collective-permute-start | bytes 442376 | tf_op jit(solution)/shard_map/ppermute | solution.py:21
  37.7 11.3 %copy-start = (bf16[1024,2048]{1,0:T(8,128)(2,1)S(1)}, bf16[1024,2048]{1,0:T(8,128)(2,1)}, u32[]{:S(2)}) copy-start(bf16[1024,2048]{1,0:T(8,128)(2,1)} %refs_10_.1) | copy-start | bytes 12582916
  37.7 11.3 %copy-start.1 = (f32[1024]{0:T(1024)S(1)}, f32[1024]{0:T(1024)}, u32[]{:S(2)}) copy-start(f32[1024]{0:T(1024)} %param.26) | copy-start | bytes 12292
  37.7 8.0 %collective-permute-start.11 = (bf16[64,512]{1,0:T(8,128)(2,1)S(1)}, bf16[64,512]{1,0:T(8,128)(2,1)S(1)}, u32[]{:S(2)}, u32[]{:S(2)}) collective-permute-start(bf16[64,512]{1,0:T(8,128)(2,1)S(1)} %get-tuple-element.108), channel_id=1, source_target_pairs={{0,16},{4,20},{8,24},{12,28},{16,0},{20,4},{24,8},{28,12},{1,17},{... | collective-permute-start | bytes 196616 | tf_op jit(solution)/shard_map/ppermute | solution.py:21
  40.5 8.5 %collective-permute-start.12 = (bf16[72,1024]{1,0:T(8,128)(2,1)S(1)}, bf16[72,1024]{1,0:T(8,128)(2,1)S(1)}, u32[]{:S(2)}, u32[]{:S(2)}) collective-permute-start(bf16[72,1024]{1,0:T(8,128)(2,1)S(1)} %get-tuple-element.110), channel_id=1, source_target_pairs={{0,16},{4,20},{8,24},{12,28},{16,0},{20,4},{24,8},{28,12},{1,17},{... | collective-permute-start | bytes 442376 | tf_op jit(solution)/shard_map/ppermute | solution.py:21
  45.8 5.3 %collective-permute-start.14 = (bf16[64,512]{1,0:T(8,128)(2,1)S(1)}, bf16[64,512]{1,0:T(8,128)(2,1)S(1)}, u32[]{:S(2)}, u32[]{:S(2)}) collective-permute-start(bf16[64,512]{1,0:T(8,128)(2,1)S(1)} %get-tuple-element.118.refs_0_), channel_id=1, source_target_pairs={{0,2},{1,3},{2,0},{3,1},{4,6},{5,7},{6,4},{7,5},{8,10},{9,11},{10,... | collective-permute-start | bytes 196616 | tf_op jit(solution)/shard_map/ppermute | solution.py:21
  50.5 3.9 %collective-permute-start.16 = (bf16[256,512]{1,0:T(8,128)(2,1)S(1)}, bf16[256,512]{1,0:T(8,128)(2,1)S(1)}, u32[]{:S(2)}, u32[]{:S(2)}) collective-permute-start(bf16[256,512]{1,0:T(8,128)(2,1)S(1)} %get-tuple-element.121), channel_id=1, source_target_pairs={{0,1},{1,0},{2,3},{3,2},{4,5},{5,4},{6,7},{7,6},{8,9},{9,8},{10,11... | collective-permute-start | bytes 786440 | tf_op jit(solution)/shard_map/ppermute | solution.py:21
  50.6 2.6 %collective-permute-start.13 = (bf16[64,512]{1,0:T(8,128)(2,1)S(1)}, bf16[64,512]{1,0:T(8,128)(2,1)S(1)}, u32[]{:S(2)}, u32[]{:S(2)}) collective-permute-start(bf16[64,512]{1,0:T(8,128)(2,1)S(1)} %get-tuple-element.118.refs_0_), channel_id=1, source_target_pairs={{0,1},{1,0},{2,3},{3,2},{4,5},{5,4},{6,7},{7,6},{8,9},{9,8},{10,11... | collective-permute-start | bytes 196616 | tf_op jit(solution)/shard_map/ppermute | solution.py:21
  51.1 2.1 %collective-permute-start.15 = (bf16[64,512]{1,0:T(8,128)(2,1)S(1)}, bf16[64,512]{1,0:T(8,128)(2,1)S(1)}, u32[]{:S(2)}, u32[]{:S(2)}) collective-permute-start(bf16[64,512]{1,0:T(8,128)(2,1)S(1)} %collective-permute-done.14.refs_2_), channel_id=1, source_target_pairs={{0,1},{1,0},{2,3},{3,2},{4,5},{5,4},{6,7},{7,6},{8,9},{9,8},{10,11... | collective-permute-start | bytes 196616 | tf_op jit(solution)/shard_map/ppermute | solution.py:21
  52.7 7.5 %collective-permute-start.18 = (bf16[256,512]{1,0:T(8,128)(2,1)S(1)}, bf16[256,512]{1,0:T(8,128)(2,1)S(1)}, u32[]{:S(2)}, u32[]{:S(2)}) collective-permute-start(bf16[256,512]{1,0:T(8,128)(2,1)S(1)} %get-tuple-element.132), channel_id=1, source_target_pairs={{0,1},{1,0},{2,3},{3,2},{4,5},{5,4},{6,7},{7,6},{8,9},{9,8},{10,11... | collective-permute-start | bytes 786440 | tf_op jit(solution)/shard_map/ppermute | solution.py:21
  54.4 8.6 %collective-permute-start.19 = (bf16[256,512]{1,0:T(8,128)(2,1)S(1)}, bf16[256,512]{1,0:T(8,128)(2,1)S(1)}, u32[]{:S(2)}, u32[]{:S(2)}) collective-permute-start(bf16[256,512]{1,0:T(8,128)(2,1)S(1)} %get-tuple-element.133), channel_id=1, source_target_pairs={{0,2},{1,3},{2,0},{3,1},{4,6},{5,7},{6,4},{7,5},{8,10},{9,11},{10,... | collective-permute-start | bytes 786440 | tf_op jit(solution)/shard_map/ppermute | solution.py:21
  58.2 1.3 %collective-permute-start.17 = (bf16[64,512]{1,0:T(8,128)(2,1)S(1)}, bf16[64,512]{1,0:T(8,128)(2,1)S(1)}, u32[]{:S(2)}, u32[]{:S(2)}) collective-permute-start(bf16[64,512]{1,0:T(8,128)(2,1)S(1)} %get-tuple-element.129), channel_id=1, source_target_pairs={{0,1},{1,0},{2,3},{3,2},{4,5},{5,4},{6,7},{7,6},{8,9},{9,8},{10,11... | collective-permute-start | bytes 196616 | tf_op jit(solution)/shard_map/ppermute | solution.py:21
  58.3 5.5 %collective-permute-start.20 = (bf16[64,512]{1,0:T(8,128)(2,1)S(1)}, bf16[64,512]{1,0:T(8,128)(2,1)S(1)}, u32[]{:S(2)}, u32[]{:S(2)}) collective-permute-start(bf16[64,512]{1,0:T(8,128)(2,1)S(1)} %get-tuple-element.137), channel_id=1, source_target_pairs={{0,1},{1,0},{2,3},{3,2},{4,5},{5,4},{6,7},{7,6},{8,9},{9,8},{10,11... | collective-permute-start | bytes 196616 | tf_op jit(solution)/shard_map/ppermute | solution.py:21
  59.6 4.6 %collective-permute-start.21 = (bf16[64,512]{1,0:T(8,128)(2,1)S(1)}, bf16[64,512]{1,0:T(8,128)(2,1)S(1)}, u32[]{:S(2)}, u32[]{:S(2)}) collective-permute-start(bf16[64,512]{1,0:T(8,128)(2,1)S(1)} %get-tuple-element.138), channel_id=1, source_target_pairs={{0,2},{1,3},{2,0},{3,1},{4,6},{5,7},{6,4},{7,5},{8,10},{9,11},{10,... | collective-permute-start | bytes 196616 | tf_op jit(solution)/shard_map/ppermute | solution.py:21
  (11 other events, 70.8 us)
